TPU v7x, 32 devices: a whole 2x2x4 slice. The times are simulated.
32 devices in a mesh: groups: 2 (over y), seq: 4 (over z), head: 2 (over x), inner: 2 (over core).
Axes of the slice: x: 2, y: 2, z: 4, core: 2. Of those that a mesh axis runs over, the one named last changes fastest.
Arguments:
- query_rows: bfloat16 [16, 640, 1024], P(('groups', 'seq'), 'inner', 'head'), parts along dimension 0, may hold values from -100 to 100
- key_rows: bfloat16 [16, 640, 128], P(('groups', 'seq')), parts along dimension 0, may hold values from -5 to 5
- value_rows: bfloat16 [16, 640, 128], P(('groups', 'seq')), parts along dimension 0, may hold values from -6 to 6
- slot_block: int32 [8], replicated, may hold values from 0 to 7, as said below
Outputs:
- attended: bfloat16 [16, 640, 1024], P(('groups', 'seq'), 'inner', 'head'), parts along dimension 0
- log_total: float32 [16, 8, 640], P(('groups', 'seq'), 'head', 'inner'), parts along dimension 0
There are 2 independent parts, one for each index of `groups`. A program takes and returns all parts, laid end to end along the dimension named above; an argument that names none is the same for every part. Nothing has to cross between parts.
Inputs may be any that keep to these rules, and one draw needn't show every extreme that they name: slot_block is a permutation of 0 .. 7; slots 2 s and 2 s + 1 hold blocks b and 7 - b.
All inputs are finite; a program needn't handle non-finite values.
Results may differ from a plain program's by a relative error of at most 0.017.
Values may be sent and summed in bfloat16 or wider, within the bound.
No kernel may reach another device: no remote copies, remote signals or barrier semaphores. Data moves between devices by JAX's collectives and lax.ppermute only.
A program may use at most 64 MiB of HBM per device.

v0:
```python
import functools
import math

import jax
import jax.numpy as jnp
from jax import lax
from jax.experimental import pallas as pl
from jax.experimental.pallas import tpu as pltpu
from jax.sharding import PartitionSpec as P

NEG = -1e30
SUM_LIMIT = 1e36
LO, HI = 0, 1
TILE = 256


def score_dot(q, k):
    return lax.dot_general(q, k, (((1,), (1,)), ((), ())), preferred_element_type=jnp.float32)


def value_dot(p, v):
    return jnp.dot(p, v, preferred_element_type=jnp.float32)


def widen(x, width):
    return jnp.concatenate([x] * (width // x.shape[1]), axis=1)


def with_ones(x):
    return jnp.concatenate([x, jnp.ones_like(x)], axis=1)


def is_power(count):
    return count & (count - 1) == 0


def source_of(index, distance, count):
    if is_power(count):
        return index ^ distance
    return lax.rem(index - distance + count, count)


def blocks_of(sb, seq_index):
    b0, b1 = sb[2 * seq_index], sb[2 * seq_index + 1]
    return jnp.where(b1 > b0, 1, 0), jnp.minimum(b0, b1), jnp.maximum(b0, b1)


def minus_columns(top):
    high = top.astype(jnp.bfloat16)
    rest = top - high.astype(jnp.float32)
    middle = rest.astype(jnp.bfloat16)
    low = (rest - middle.astype(jnp.float32)).astype(jnp.bfloat16)
    lane = lax.broadcasted_iota(jnp.int32, top.shape, 1)
    high, middle, low = (x.astype(jnp.float32) for x in (high, middle, low))
    picked = jnp.where(lane == 0, high, jnp.where(lane == 1, middle, jnp.where(lane == 2, low, 0.0)))
    return (-picked).astype(jnp.bfloat16)


def key_tiles(count):
    return [(start, min(TILE, count - start)) for start in range(0, count, TILE)]


def load_kernel(q_hbm, k_hbm, v_hbm, sb_hbm, piece, q_out, k_out, v_out, sb_out, sems):
    half = piece.shape[1]
    rows, width = q_hbm.shape[1], q_out.shape[2]
    inner = lax.axis_index("inner")
    mine = pl.ds(pl.multiple_of(lax.rem(lax.axis_index("head"), 2) * half, half), half)
    for value, src in enumerate((k_hbm, v_hbm)):

        @pl.when(inner == value)
        def _():
            pltpu.make_async_copy(src.at[:, mine], piece, sems.at[0]).start()

    copies = [pltpu.make_async_copy(k_hbm.at[:, mine], piece, sems.at[0])]
    pairs = [(k_hbm, k_out), (v_hbm, v_out), (sb_hbm, sb_out)]
    for h in range(q_hbm.shape[2] // width):
        pairs.append((q_hbm.at[:, :, pl.ds(h * width, width)], q_out.at[:, pl.ds(h * rows, rows)]))
    for place, (src, dst) in enumerate(pairs):
        copy = pltpu.make_async_copy(src, dst, sems.at[1 + place])
        copy.start()
        copies.append(copy)
    for copy in copies:
        copy.wait()


def scaled_exp(coef, s):
    return jnp.exp2(s * coef).astype(jnp.bfloat16)


def in_turn(coef, chunks, score, finish):
    ready = score(*chunks[0])
    for place, chunk in enumerate(chunks):
        now = ready
        if place + 1 < len(chunks):
            ready = score(*chunks[place + 1])
        finish(scaled_exp(coef, now), *chunk)


def local_kernel(coef, rows, sb, q_ref, k_ref, v_ref, qx_ref, acc_ref):
    _, all_rows, width = q_ref.shape
    block_len = k_ref.shape[1]
    heads = all_rows // rows
    hi, _, _ = blocks_of(sb, lax.axis_index("seq"))
    slots = {HI: hi, LO: 1 - hi}
    tiles = key_tiles(block_len)

    def keys(slot, start, size):
        return k_ref[slot, pl.ds(start, size)]

    def values(slot, start, size):
        return with_ones(v_ref[slot, pl.ds(start, size)])

    def masked(order, start, size):
        row = lax.broadcasted_iota(jnp.int32, (rows, size), 0) + lax.axis_index("inner") * rows
        col = lax.broadcasted_iota(jnp.int32, (rows, size), 1) + start
        bias = jnp.where(col <= row, 0.0, NEG)
        s = score_dot(q_ref[slots[order]], keys(slots[order], start, size))
        return s + jnp.concatenate([bias] * heads, axis=0)

    def highest(scores):
        parts = [s[:, at : at + width] for s in scores for at in range(0, s.shape[1], width)]
        top = functools.reduce(jnp.maximum, parts)
        return jnp.broadcast_to(jnp.max(top, axis=1, keepdims=True), (all_rows, width))

    def settle(order, scores, top):
        total = None
        for (start, size), s in zip(tiles, scores):
            p = scaled_exp(coef, s - widen(top, size))
            part = value_dot(p, values(slots[order], start, size))
            total = part if total is None else total + part
        acc_ref[order] = total

    def extend(order, top):
        qx_ref[order] = jnp.concatenate([q_ref[slots[order]], minus_columns(top)], axis=1)

    diag = [masked(HI, *tile) for tile in tiles]
    top = highest(diag)
    extend(HI, top)
    low = [masked(LO, *tile) for tile in tiles]
    settle(HI, diag, top)
    top = highest(low)
    extend(LO, top)

    def score(start, size):
        return score_dot(qx_ref[HI], with_ones(keys(slots[LO], start, size)))

    def finish(p, start, size):
        acc_ref[HI] += value_dot(p, values(slots[LO], start, size))

    settle(LO, low, top)
    in_turn(coef, tiles, score, finish)


def place_pieces(parts, own_half, k_buf, v_buf):
    inner = lax.axis_index("inner")
    for value, (own_buf, twin_buf) in enumerate([(k_buf, v_buf), (v_buf, k_buf)]):

        @pl.when(inner == value)
        def _():
            for turn, pair in enumerate(parts):
                half = own_half if turn == 0 else 1 - own_half
                for piece, buf in zip(pair, (own_buf, twin_buf)):
                    size = piece.shape[1]
                    for slot in range(2):
                        start = pl.multiple_of((slot * len(parts) + half) * size, size)
                        buf[pl.ds(start, size)] = piece[slot]


def visit(coef, distance, parts, sb, qx_ref, acc_ref, buffers, group, store):
    all_rows = qx_ref.shape[1]
    count = lax.axis_size("seq")
    me = lax.axis_index("seq")
    k_buf, v_buf = buffers[:2] if len(parts) == 2 else buffers[2:]
    own_half = lax.rem(lax.axis_index("head"), 2) if len(parts) == 2 else 0
    place_pieces(parts, own_half, k_buf, v_buf)
    keys_here = k_buf.shape[0] // 2

    _, _, top_block = blocks_of(sb, me)
    other_hi, _, other_top = blocks_of(sb, source_of(me, distance, count))
    above = top_block > other_top

    def run(orders, first_key, key_count):
        tiles = key_tiles(key_count)
        totals = {}

        def chosen(buf, start, size):
            return with_ones(buf[pl.ds(first_key + start, size)])

        def score(order, row, start, size):
            return score_dot(qx_ref[order, pl.ds(row, group)], chosen(k_buf, start, size))

        def finish(p, order, row, start, size):
            part = value_dot(p, chosen(v_buf, start, size))
            before = acc_ref[order, pl.ds(row, group)] if start == 0 else totals[order, row]
            totals[order, row] = before + part
            if start == tiles[-1][0]:
                store(order, row, totals[order, row])

        chunks = [(order, row, *tile) for row in range(0, all_rows, group) for order in orders for tile in tiles]
        in_turn(coef, chunks, score, finish)

    @pl.when(above)
    def _():
        for row in range(0, all_rows, group):
            store(LO, row, None)
        run((HI,), 0, 2 * keys_here)

    @pl.when(jnp.logical_not(above))
    def _():
        run((HI, LO), pl.multiple_of((1 - other_hi) * keys_here, keys_here), keys_here)


def first_row(x):
    return jnp.transpose(x)[:1]


def middle_kernel(coef, visits, rows, sb, qx_ref, acc_in, *refs):
    taken = []
    for distance, pairs in visits:
        taken.append((distance, [refs[2 * i : 2 * i + 2] for i in range(pairs)]))
        refs = refs[2 * pairs :]
    acc_ref, tops, buffers = refs[0], refs[1:-4], refs[-4:]
    _, all_rows, double = qx_ref.shape

    def store(order, row, value):
        if value is not None:
            acc_ref[order, pl.ds(row, all_rows)] = value

    for distance, parts in taken:
        visit(coef, distance, parts, sb, qx_ref, acc_ref, buffers, all_rows, store)
    for top_ref in tops:
        for order in (LO, HI):
            for h in range(all_rows // rows):
                columns = qx_ref[order, pl.ds(h * rows, rows), pl.ds(double // 2, double // 2)]
                columns = jnp.transpose(columns.astype(jnp.float32))
                top_ref[order, h : h + 1, :] = -(columns[0:1] + columns[1:2] + columns[2:3])


def last_kernel(coef, distances, sb, qx_ref, acc_ref, top_ref, *refs):
    parts, every, rest = [refs[:2]], refs[2 : 4 * len(distances) + 4], refs[4 * len(distances) + 4 :]
    out_hbm, lse_hbm, out_buf, lse_ref, *buffers, worst, run_top, run_acc, sem, out_sems = rest
    rows = out_buf.shape[1]
    all_rows = qx_ref.shape[1]
    heads = all_rows // rows
    k_buf, v_buf = buffers[:2]
    block_len, width = k_buf.shape[0] // 2, k_buf.shape[1]
    half_len = block_len // 2
    count = lax.axis_size("seq")
    me = lax.axis_index("seq")
    own_half = lax.rem(lax.axis_index("head"), 2)
    inner = lax.axis_index("inner")
    hi, lo_block, hi_block = blocks_of(sb, me)
    lse_copy = pltpu.make_async_copy(lse_ref, lse_hbm, sem)

    def out_copy(h):
        columns = pl.ds(h * width, width)
        return pltpu.make_async_copy(out_buf.at[:, :, columns], out_hbm.at[:, :, columns], out_sems.at[h])

    def emit(order, h, value, top_row):
        slot = hi if order == HI else 1 - hi
        sums = value[:, width:]
        out_buf[slot, :, h * width : (h + 1) * width] = (value[:, :width] / sums).astype(out_buf.dtype)
        lse_ref[slot, h : h + 1, :] = top_row * (coef * math.log(2.0)) + jnp.log(first_row(sums))
        return sums

    worst[...] = jnp.zeros_like(worst)

    def store(order, row, value):
        group = all_rows // 2 if heads > 1 else all_rows
        if value is None:
            value = acc_ref[order, pl.ds(row, group)]
        for at in range(0, group, rows):
            h = (row + at) // rows
            sums = emit(order, h, value[at : at + rows], top_ref[order, h : h + 1, :])
            worst[...] = jnp.maximum(worst[...], sums)

    visit(coef, distances[-1], parts, sb, qx_ref, acc_ref, buffers, all_rows // 2 if heads > 1 else all_rows, store)
    for h in range(heads):
        out_copy(h).start()
    lse_copy.start()
    for h in range(heads):
        out_copy(h).wait()
    lse_copy.wait()

    @pl.when(jnp.logical_not(jnp.max(worst[...]) < SUM_LIMIT))
    def _():
        def fetch(src, dst):
            copy = pltpu.make_async_copy(src, dst, sem)
            copy.start()
            copy.wait()

        def online(source):
            @pl.loop(0, 4 * heads)
            def _(i):
                h, slot, order = i // 4, lax.rem(i, 4) // 2, lax.rem(i, 2)
                own_block = jnp.where(order == HI, hi_block, lo_block)
                shift = (own_block - sb[2 * source + slot]) * block_len + inner * rows

                @pl.when(shift + rows > 0)
                def _():
                    queries = qx_ref[order, pl.ds(pl.multiple_of(h * rows, rows), rows), pl.ds(0, width)]
                    at = pl.ds(pl.multiple_of(slot * block_len, block_len), block_len)
                    s = score_dot(queries, k_buf[at])
                    row = lax.broadcasted_iota(jnp.int32, s.shape, 0) + shift
                    allowed = lax.broadcasted_iota(jnp.int32, s.shape, 1) <= row
                    s = jnp.where(allowed, s, NEG)
                    before = run_top[order, h]
                    top = jnp.maximum(before, jnp.broadcast_to(jnp.max(s, axis=1, keepdims=True), before.shape))
                    p = jnp.where(allowed, jnp.exp2((s - widen(top, block_len)) * coef), 0.0)
                    run_top[order, h] = top
                    shrink = widen(jnp.exp2((before - top) * coef), 2 * width)
                    fresh = value_dot(p.astype(jnp.bfloat16), with_ones(v_buf[at]))
                    run_acc[order, h] = run_acc[order, h] * shrink + fresh

        run_top[...] = jnp.full_like(run_top, NEG)
        run_acc[...] = jnp.zeros_like(run_acc)
        def rows_of(slot, half):
            return pl.ds(pl.multiple_of((slot * 2 + half) * half_len, half_len), half_len)

        for slot in range(2):
            fetch(every[0].at[slot], k_buf.at[pl.ds(slot * block_len, block_len)])
            fetch(every[1].at[slot], v_buf.at[pl.ds(slot * block_len, block_len)])
        online(me)
        for place, other in enumerate(distances):
            others = every[2 + 4 * place : 6 + 4 * place]
            for value, (own_buf, twin_buf) in enumerate([(k_buf, v_buf), (v_buf, k_buf)]):

                @pl.when(inner == value)
                def _():
                    for turn in range(2):
                        half = own_half if turn == 0 else 1 - own_half
                        for slot in range(2):
                            fetch(others[2 * turn].at[slot], own_buf.at[rows_of(slot, half)])
                            fetch(others[2 * turn + 1].at[slot], twin_buf.at[rows_of(slot, half)])

            online(source_of(me, other, count))
        for h in range(heads):
            for order in (LO, HI):
                emit(order, h, run_acc[order, h], first_row(run_top[order, h]))
            out_copy(h).start()
            out_copy(h).wait()
        lse_copy.start()
        lse_copy.wait()


def body(query_rows, key_rows, value_rows, slot_block):
    _, block_len, width = key_rows.shape
    _, rows, feats = query_rows.shape
    heads = feats // width
    all_rows = heads * rows
    count = lax.axis_size("seq")
    coef = math.log2(math.e) / math.sqrt(width)
    distances = list(range(1, count))

    def along_seq(block, distance):
        if is_power(count):
            route = [(i, i ^ distance) for i in range(count)]
        else:
            route = [(i, (i + distance) % count) for i in range(count)]
        with jax.named_scope("along_seq"):
            return lax.ppermute(block, "seq", route)

    def along_head(block):
        with jax.named_scope("along_head"):
            return lax.ppermute(block, "head", [(i, i ^ 1) for i in range(lax.axis_size("head"))])

    def along_inner(block):
        with jax.named_scope("along_inner"):
            return lax.ppermute(block, "inner", [(0, 1), (1, 0)])

    whole = pl.BlockSpec(memory_space=pltpu.VMEM)
    anywhere = pl.BlockSpec(memory_space=pl.ANY)
    scalars = pl.BlockSpec(memory_space=pltpu.SMEM)
    acc_shape = jax.ShapeDtypeStruct((2, all_rows, 2 * width), jnp.float32)
    qx_shape = jax.ShapeDtypeStruct(acc_shape.shape, jnp.bfloat16)
    top_shape = jax.ShapeDtypeStruct((2, heads, rows), jnp.float32)
    params = pltpu.CompilerParams(vmem_limit_bytes=40 * 1024 * 1024)
    unit = rows * heads * block_len * width * 4
    exps = rows * heads * block_len

    def cost(units, size):
        return pl.CostEstimate(flops=int(2 * units * unit), bytes_accessed=size, transcendentals=int(units * exps))

    in_hbm = [
        pltpu.with_memory_space_constraint(x, pltpu.HBM) for x in (query_rows, key_rows, value_rows, slot_block)
    ]
    half_shape = jax.ShapeDtypeStruct((2, block_len // 2, width), key_rows.dtype)
    piece, q_here, k_here, v_here, sb_here = pl.pallas_call(
        load_kernel,
        in_specs=[anywhere] * 4,
        out_specs=[whole] * 5,
        out_shape=[half_shape, jax.ShapeDtypeStruct((2, all_rows, width), query_rows.dtype)]
        + [jax.ShapeDtypeStruct(x.shape, x.dtype) for x in in_hbm[1:]],
        scratch_shapes=[pltpu.SemaphoreType.DMA((4 + heads,))],
        cost_estimate=pl.CostEstimate(flops=0, bytes_accessed=3_000_000, transcendentals=0),
        compiler_params=params,
        name="load",
    )(*in_hbm)
    arrived, across, beside, beside_across = {}, {}, {}, {}
    for distance in distances:
        if not is_power(count) or is_power(distance):
            arrived[distance] = along_seq(piece, distance)

    qx, acc = pl.pallas_call(
        functools.partial(local_kernel, coef, rows),
        in_specs=[scalars] + [whole] * 3,
        out_specs=[whole] * 2,
        out_shape=[qx_shape, acc_shape],
        cost_estimate=cost(3, 6_000_000),
        compiler_params=params,
        name="local_part",
    )(sb_here, q_here, k_here, v_here)
    kv_buffers = [pltpu.VMEM((2 * block_len, width), jnp.bfloat16)] * 2
    kv_buffers += [pltpu.VMEM((block_len, width), jnp.bfloat16)] * 2

    def attend(acc, visits, with_tops):
        pieces = [part for _, pairs in visits for pair in pairs for part in pair]
        return pl.pallas_call(
            functools.partial(middle_kernel, coef, [(distance, len(pairs)) for distance, pairs in visits], rows),
            in_specs=[scalars] + [whole] * (2 + len(pieces)),
            out_specs=[whole] * (1 + with_tops),
            out_shape=[acc_shape] + [top_shape] * with_tops,
            scratch_shapes=kv_buffers,
            input_output_aliases={2: 0},
            cost_estimate=cost(len(pieces) / 2, 7_000_000),
            compiler_params=params,
            name=f"visitors_from_{visits[0][0]}",
        )(sb_here, qx, acc, *pieces)

    def relay(distance):
        if distance in distances and distance not in arrived:
            near = distance & -distance
            arrived[distance] = along_seq(arrived[distance ^ near], near)

    def spread(distance):
        if distance in distances:
            across[distance] = along_head(arrived[distance])
            beside[distance] = along_inner(arrived[distance])

    def own_pair(distance):
        return arrived[distance], beside[distance]

    def far_pair(distance):
        beside_across[distance] = along_inner(across[distance])
        return across[distance], beside_across[distance]

    last = distances[-1]
    first, acc = lax.optimization_barrier((dict(arrived), acc))
    arrived.update(first)
    spread(1)
    relay(3)
    spread(2)
    for distance in distances[:-1]:
        ahead = distance + 2
        tied = lax.optimization_barrier((across[distance], arrived.get(ahead), acc))
        across[distance], arrived_ahead, acc = tied
        if ahead in distances:
            arrived[ahead] = arrived_ahead
        visits = [(distance, [own_pair(distance), far_pair(distance)])]
        if distance + 1 == last:
            visits.append((last, [own_pair(last)]))
        acc, *tops = attend(acc, visits, int(distance + 1 == last))
        relay(ahead + 1)
        spread(ahead)
    across[last], acc = lax.optimization_barrier((across[last], acc))
    far_pair(last)

    pairs = [(arrived[d], beside[d], across[d], beside_across[d]) for d in distances]
    flat = [part for pair in pairs for part in pair]
    attended, log_total = pl.pallas_call(
        functools.partial(last_kernel, coef, distances),
        in_specs=[scalars] + [whole] * 5 + [anywhere] * (2 + len(flat)),
        out_specs=[anywhere, anywhere],
        out_shape=[jax.ShapeDtypeStruct(query_rows.shape, query_rows.dtype), top_shape],
        scratch_shapes=[
            pltpu.VMEM(query_rows.shape, query_rows.dtype),
            pltpu.VMEM(top_shape.shape, jnp.float32),
        ]
        + kv_buffers
        + [
            pltpu.VMEM((rows, width), jnp.float32),
            pltpu.VMEM((2, heads, rows, width), jnp.float32),
            pltpu.VMEM((2, heads, rows, 2 * width), jnp.float32),
            pltpu.SemaphoreType.DMA,
            pltpu.SemaphoreType.DMA((heads,)),
        ],
        cost_estimate=cost(1, 7_000_000),
        compiler_params=params,
        name="last_visitor",
    )(sb_here, qx, acc, *tops, *flat[-2:], in_hbm[1], in_hbm[2], *flat)
    return attended, log_total


def solution(mesh):
    placed = (
        P(("groups", "seq"), "inner", "head"),
        P(("groups", "seq"), None, None),
        P(("groups", "seq"), None, None),
        P(),
    )
    return jax.shard_map(
        body,
        mesh=mesh,
        in_specs=placed,
        out_specs=(P(("groups", "seq"), "inner", "head"), P(("groups", "seq"), "head", "inner")),
        check_vma=False,
    )
```

profile of v0, /device:TPU:0, one launch (start us, length us, event | category | flops | bytes accessed | tf_op | source)
XLA Modules:
  0.0 39.3 jit_solution(13203344034767419997)
XLA Ops:
  0.6 1.5 %load.1 = (bf16[2,320,128]{2,1,0:T(8,128)(2,1)S(1)}, bf16[2,1280,128]{2,1,0:T(8,128)(2,1)S(1)}, bf16[2,640,128]{2,1,0:T(8,128)(2,1)S(1)}, bf16[2,640,128]{2,1,0:T(8,128)(2,1)S(1)}, s32[8]{0:T(128)S(1)}) custom-call(bf16[2,320,512]{2,1,0:T(8,128)(2,1)} %q_hbm.1, bf16[2,640,128]{2,1,0:T(8,128)(2,1)} %refs_2_.1, bf16[2,640,128]{2,1,0:T(8,128)(2,1)} %refs_3_.1, ...), custom_call_target="tpu_custom_call" | custom-call | bytes 3000000 | tf_op jit(solution)/shard_map/load/pallas_call | solution.py:388
  2.1 4.1 %collective-permute-start.1 = (bf16[2,320,128]{2,1,0:T(8,128)(2,1)S(1)}, bf16[2,320,128]{2,1,0:T(8,128)(2,1)S(1)}, u32[]{:S(2)}, u32[]{:S(2)}) collective-permute-start(bf16[2,320,128]{2,1,0:T(8,128)(2,1)S(1)} %get-tuple-element.26), channel_id=1, source_target_pairs={{0,8},{4,12},{8,0},{12,4},{1,9},{5,13},{9,1},{13,5},{2,10},{6,14},... | collective-permute-start | bytes 491528 | tf_op jit(solution)/shard_map/along_seq/ppermute | solution.py:361
  6.2 1.6 %collective-permute-start = (bf16[2,320,128]{2,1,0:T(8,128)(2,1)S(1)}, bf16[2,320,128]{2,1,0:T(8,128)(2,1)S(1)}, u32[]{:S(2)}, u32[]{:S(2)}) collective-permute-start(bf16[2,320,128]{2,1,0:T(8,128)(2,1)S(1)} %get-tuple-element.26), channel_id=1, source_target_pairs={{0,4},{4,0},{8,12},{12,8},{1,5},{5,1},{9,13},{13,9},{2,6},{6,2},{1... | collective-permute-start | bytes 491528 | tf_op jit(solution)/shard_map/along_seq/ppermute | solution.py:361
  7.8 4.6 %local_part.1 = (bf16[2,1280,256]{2,1,0:T(8,128)(2,1)S(1)}, f32[2,1280,256]{2,1,0:T(8,128)S(1)}) custom-call(s32[8]{0:T(128)S(1)} %get-tuple-element.21.sb, bf16[2,1280,128]{2,1,0:T(8,128)(2,1)S(1)} %get-tuple-element.22.q_ref, bf16[2,640,128]{2,1,0:T(8,128)(2,1)S(1)} %get-tuple-element.23.k_ref, bf16[2,640,128]{2,1,0:T(8,128)(2,1)S(1)} %get-tuple-element.24.v_ref), custom_call_target="tpu_custom_call" | custom-call | flops 2516582400 | bytes 6000000 | tf_op jit(solution)/shard_map/local_part/pallas_call | solution.py:404
  12.4 1.6 %collective-permute-done.1.refs_0_.refs_8_ = bf16[2,320,128]{2,1,0:T(8,128)(2,1)S(1)} collective-permute-done((bf16[2,320,128]{2,1,0:T(8,128)(2,1)S(1)}, bf16[2,320,128]{2,1,0:T(8,128)(2,1)S(1)}, u32[]{:S(2)}, u32[]{:S(2)}) %collective-permute-start.1) | collective-permute-done | bytes 163872 | tf_op jit(solution)/shard_map/along_seq/ppermute | solution.py:361
  14.0 0.2 collective-permute-done.refs_0_.refs_4_
  14.2 1.5 %collective-permute-start.2 = (bf16[2,320,128]{2,1,0:T(8,128)(2,1)S(1)}, bf16[2,320,128]{2,1,0:T(8,128)(2,1)S(1)}, u32[]{:S(2)}, u32[]{:S(2)}) collective-permute-start(bf16[2,320,128]{2,1,0:T(8,128)(2,1)S(1)} %collective-permute-done.refs_0_.refs_4_), channel_id=1, source_target_pairs={{0,2},{2,0},{1,3},{3,1},{4,6},{6,4},{5,7},{7,5},{8,10},{10,8},{9,1... | collective-permute-start | bytes 491528 | tf_op jit(solution)/shard_map/along_head/ppermute | solution.py:365
  15.8 1.4 %collective-permute-start.3 = (bf16[2,320,128]{2,1,0:T(8,128)(2,1)S(1)}, bf16[2,320,128]{2,1,0:T(8,128)(2,1)S(1)}, u32[]{:S(2)}, u32[]{:S(2)}) collective-permute-start(bf16[2,320,128]{2,1,0:T(8,128)(2,1)S(1)} %collective-permute-done.1.refs_0_.refs_8_), channel_id=1, source_target_pairs={{0,4},{4,0},{8,12},{12,8},{1,5},{5,1},{9,13},{13,9},{2,6},{6,2},{1... | collective-permute-start | bytes 491528 | tf_op jit(solution)/shard_map/along_seq/ppermute | solution.py:361
  17.2 0.0 collective-permute-start.6
  17.2 2.3 %collective-permute-done.2.refs_2_.refs_6_ = bf16[2,320,128]{2,1,0:T(8,128)(2,1)S(1)} collective-permute-done((bf16[2,320,128]{2,1,0:T(8,128)(2,1)S(1)}, bf16[2,320,128]{2,1,0:T(8,128)(2,1)S(1)}, u32[]{:S(2)}, u32[]{:S(2)}) %collective-permute-start.2) | collective-permute-done | bytes 163872 | tf_op jit(solution)/shard_map/along_head/ppermute | solution.py:365
  19.5 1.5 %collective-permute-done.3.refs_4_.refs_12_ = bf16[2,320,128]{2,1,0:T(8,128)(2,1)S(1)} collective-permute-done((bf16[2,320,128]{2,1,0:T(8,128)(2,1)S(1)}, bf16[2,320,128]{2,1,0:T(8,128)(2,1)S(1)}, u32[]{:S(2)}, u32[]{:S(2)}) %collective-permute-start.3) | collective-permute-done | bytes 163872 | tf_op jit(solution)/shard_map/along_seq/ppermute | solution.py:361
  21.1 0.0 collective-permute-start.7
  21.1 0.5 %collective-permute-start.5 = (bf16[2,320,128]{2,1,0:T(8,128)(2,1)S(1)}, bf16[2,320,128]{2,1,0:T(8,128)(2,1)S(1)}, u32[]{:S(2)}, u32[]{:S(2)}) collective-permute-start(bf16[2,320,128]{2,1,0:T(8,128)(2,1)S(1)} %collective-permute-done.1.refs_0_.refs_8_), channel_id=1, source_target_pairs={{0,2},{2,0},{1,3},{3,1},{4,6},{6,4},{5,7},{7,5},{8,10},{10,8},{9,1... | collective-permute-start | bytes 491528 | tf_op jit(solution)/shard_map/along_head/ppermute | solution.py:365
  21.6 0.2 collective-permute-start.8
  21.8 0.3 collective-permute-start.10
  22.1 0.0 collective-permute-done.6.refs_1_.refs_5_
  22.1 0.4 collective-permute-done.7.refs_3_.refs_7_
  22.5 3.0 %visitors_from_1.1.acc_in = f32[2,1280,256]{2,1,0:T(8,128)S(1)} custom-call(s32[8]{0:T(128)S(1)} %get-tuple-element.21.sb, bf16[2,1280,256]{2,1,0:T(8,128)(2,1)S(1)} %get-tuple-element.25.qx_ref, f32[2,1280,256]{2,1,0:T(8,128)S(1)} %get-tuple-element.32.acc_in, ...), custom_call_target="tpu_custom_call", output_to_operand_aliasing={{}: (2, {})} | custom-call | flops 1677721600 | bytes 7000000 | tf_op jit(solution)/shard_map/visitors_from_1/pallas_call | solution.py:418
  25.5 2.2 %collective-permute-done.5.refs_2_.refs_10_ = bf16[2,320,128]{2,1,0:T(8,128)(2,1)S(1)} collective-permute-done((bf16[2,320,128]{2,1,0:T(8,128)(2,1)S(1)}, bf16[2,320,128]{2,1,0:T(8,128)(2,1)S(1)}, u32[]{:S(2)}, u32[]{:S(2)}) %collective-permute-start.5) | collective-permute-done | bytes 163872 | tf_op jit(solution)/shard_map/along_head/ppermute | solution.py:365
  27.7 0.0 collective-permute-start.9
  27.7 0.5 %collective-permute-start.4 = (bf16[2,320,128]{2,1,0:T(8,128)(2,1)S(1)}, bf16[2,320,128]{2,1,0:T(8,128)(2,1)S(1)}, u32[]{:S(2)}, u32[]{:S(2)}) collective-permute-start(bf16[2,320,128]{2,1,0:T(8,128)(2,1)S(1)} %collective-permute-done.3.refs_4_.refs_12_), channel_id=1, source_target_pairs={{0,2},{2,0},{1,3},{3,1},{4,6},{6,4},{5,7},{7,5},{8,10},{10,8},{9,1... | collective-permute-start | bytes 491528 | tf_op jit(solution)/shard_map/along_head/ppermute | solution.py:365
  28.2 0.0 collective-permute-done.8.refs_1_.refs_9_
  28.2 0.0 collective-permute-done.10.refs_5_.refs_13_
  28.2 0.9 %collective-permute-done.9.refs_3_.refs_11_ = bf16[2,320,128]{2,1,0:T(8,128)(2,1)S(1)} collective-permute-done((bf16[2,320,128]{2,1,0:T(8,128)(2,1)S(1)}, bf16[2,320,128]{2,1,0:T(8,128)(2,1)S(1)}, u32[]{:S(2)}, u32[]{:S(2)}) %collective-permute-start.9) | collective-permute-done | bytes 163872 | tf_op jit(solution)/shard_map/along_inner/ppermute | solution.py:369
  29.1 5.1 %visitors_from_2.1 = (f32[2,1280,256]{2,1,0:T(8,128)S(1)}, f32[2,4,320]{2,1,0:T(4,128)S(1)}) custom-call(s32[8]{0:T(128)S(1)} %get-tuple-element.21.sb, bf16[2,1280,256]{2,1,0:T(8,128)(2,1)S(1)} %get-tuple-element.25.qx_ref, f32[2,1280,256]{2,1,0:T(8,128)S(1)} %visitors_from_1.1.acc_in, ...), custom_call_target="tpu_custom_call", output_to_operand_aliasing={{0}: (2, {})} | custom-call | flops 2516582400 | bytes 7000000 | tf_op jit(solution)/shard_map/visitors_from_2/pallas_call | solution.py:418
  34.2 0.1 collective-permute-done.4.refs_0_.refs_14_
  34.3 0.1 collective-permute-start.11
  34.5 1.3 %collective-permute-done.11.refs_1_.refs_15_ = bf16[2,320,128]{2,1,0:T(8,128)(2,1)S(1)} collective-permute-done((bf16[2,320,128]{2,1,0:T(8,128)(2,1)S(1)}, bf16[2,320,128]{2,1,0:T(8,128)(2,1)S(1)}, u32[]{:S(2)}, u32[]{:S(2)}) %collective-permute-start.11) | collective-permute-done | bytes 163872 | tf_op jit(solution)/shard_map/along_inner/ppermute | solution.py:369
  35.7 3.4 %last_visitor.1 = (bf16[2,320,512]{2,1,0:T(8,128)(2,1)}, f32[2,4,320]{2,1,0:T(4,128)}) custom-call(s32[8]{0:T(128)S(1)} %get-tuple-element.21.sb, bf16[2,1280,256]{2,1,0:T(8,128)(2,1)S(1)} %get-tuple-element.25.qx_ref, f32[2,1280,256]{2,1,0:T(8,128)S(1)} %get-tuple-element.37.acc_ref, f32[2,4,320]{2,1,0:T(4,128)S(1)} %get-tuple-element.38.top_ref, ...), custom_call_target="tpu_custom_call" | custom-call | flops 838860800 | bytes 7000000 | tf_op jit(solution)/shard_map/last_visitor/pallas_call | solution.py:470
Async XLA Ops:
  2.1 11.9 %collective-permute-start.1 = (bf16[2,320,128]{2,1,0:T(8,128)(2,1)S(1)}, bf16[2,320,128]{2,1,0:T(8,128)(2,1)S(1)}, u32[]{:S(2)}, u32[]{:S(2)}) collective-permute-start(bf16[2,320,128]{2,1,0:T(8,128)(2,1)S(1)} %get-tuple-element.26), channel_id=1, source_target_pairs={{0,8},{4,12},{8,0},{12,4},{1,9},{5,13},{9,1},{13,5},{2,10},{6,14},... | collective-permute-start | bytes 491528 | tf_op jit(solution)/shard_map/along_seq/ppermute | solution.py:361
  6.2 8.0 %collective-permute-start = (bf16[2,320,128]{2,1,0:T(8,128)(2,1)S(1)}, bf16[2,320,128]{2,1,0:T(8,128)(2,1)S(1)}, u32[]{:S(2)}, u32[]{:S(2)}) collective-permute-start(bf16[2,320,128]{2,1,0:T(8,128)(2,1)S(1)} %get-tuple-element.26), channel_id=1, source_target_pairs={{0,4},{4,0},{8,12},{12,8},{1,5},{5,1},{9,13},{13,9},{2,6},{6,2},{1... | collective-permute-start | bytes 491528 | tf_op jit(solution)/shard_map/along_seq/ppermute | solution.py:361
  14.2 5.3 %collective-permute-start.2 = (bf16[2,320,128]{2,1,0:T(8,128)(2,1)S(1)}, bf16[2,320,128]{2,1,0:T(8,128)(2,1)S(1)}, u32[]{:S(2)}, u32[]{:S(2)}) collective-permute-start(bf16[2,320,128]{2,1,0:T(8,128)(2,1)S(1)} %collective-permute-done.refs_0_.refs_4_), channel_id=1, source_target_pairs={{0,2},{2,0},{1,3},{3,1},{4,6},{6,4},{5,7},{7,5},{8,10},{10,8},{9,1... | collective-permute-start | bytes 491528 | tf_op jit(solution)/shard_map/along_head/ppermute | solution.py:365
  15.8 5.3 %collective-permute-start.3 = (bf16[2,320,128]{2,1,0:T(8,128)(2,1)S(1)}, bf16[2,320,128]{2,1,0:T(8,128)(2,1)S(1)}, u32[]{:S(2)}, u32[]{:S(2)}) collective-permute-start(bf16[2,320,128]{2,1,0:T(8,128)(2,1)S(1)} %collective-permute-done.1.refs_0_.refs_8_), channel_id=1, source_target_pairs={{0,4},{4,0},{8,12},{12,8},{1,5},{5,1},{9,13},{13,9},{2,6},{6,2},{1... | collective-permute-start | bytes 491528 | tf_op jit(solution)/shard_map/along_seq/ppermute | solution.py:361
  17.2 4.9 %collective-permute-start.6 = (bf16[2,320,128]{2,1,0:T(8,128)(2,1)S(1)}, bf16[2,320,128]{2,1,0:T(8,128)(2,1)S(1)}, u32[]{:S(2)}, u32[]{:S(2)}) collective-permute-start(bf16[2,320,128]{2,1,0:T(8,128)(2,1)S(1)} %collective-permute-done.refs_0_.refs_4_), channel_id=1, source_target_pairs={{0,1},{1,0},{2,3},{3,2},{4,5},{5,4},{6,7},{7,6},{8,9},{9,8},{10,11... | collective-permute-start | bytes 491528 | tf_op jit(solution)/shard_map/along_inner/ppermute | solution.py:369
  21.1 1.4 %collective-permute-start.7 = (bf16[2,320,128]{2,1,0:T(8,128)(2,1)S(1)}, bf16[2,320,128]{2,1,0:T(8,128)(2,1)S(1)}, u32[]{:S(2)}, u32[]{:S(2)}) collective-permute-start(bf16[2,320,128]{2,1,0:T(8,128)(2,1)S(1)} %collective-permute-done.2.refs_2_.refs_6_), channel_id=1, source_target_pairs={{0,1},{1,0},{2,3},{3,2},{4,5},{5,4},{6,7},{7,6},{8,9},{9,8},{10,11... | collective-permute-start | bytes 491528 | tf_op jit(solution)/shard_map/along_inner/ppermute | solution.py:369
  21.1 6.6 %collective-permute-start.5 = (bf16[2,320,128]{2,1,0:T(8,128)(2,1)S(1)}, bf16[2,320,128]{2,1,0:T(8,128)(2,1)S(1)}, u32[]{:S(2)}, u32[]{:S(2)}) collective-permute-start(bf16[2,320,128]{2,1,0:T(8,128)(2,1)S(1)} %collective-permute-done.1.refs_0_.refs_8_), channel_id=1, source_target_pairs={{0,2},{2,0},{1,3},{3,1},{4,6},{6,4},{5,7},{7,5},{8,10},{10,8},{9,1... | collective-permute-start | bytes 491528 | tf_op jit(solution)/shard_map/along_head/ppermute | solution.py:365
  21.6 6.6 %collective-permute-start.8 = (bf16[2,320,128]{2,1,0:T(8,128)(2,1)S(1)}, bf16[2,320,128]{2,1,0:T(8,128)(2,1)S(1)}, u32[]{:S(2)}, u32[]{:S(2)}) collective-permute-start(bf16[2,320,128]{2,1,0:T(8,128)(2,1)S(1)} %collective-permute-done.1.refs_0_.refs_8_), channel_id=1, source_target_pairs={{0,1},{1,0},{2,3},{3,2},{4,5},{5,4},{6,7},{7,6},{8,9},{9,8},{10,11... | collective-permute-start | bytes 491528 | tf_op jit(solution)/shard_map/along_inner/ppermute | solution.py:369
  21.8 6.4 %collective-permute-start.10 = (bf16[2,320,128]{2,1,0:T(8,128)(2,1)S(1)}, bf16[2,320,128]{2,1,0:T(8,128)(2,1)S(1)}, u32[]{:S(2)}, u32[]{:S(2)}) collective-permute-start(bf16[2,320,128]{2,1,0:T(8,128)(2,1)S(1)} %collective-permute-done.3.refs_4_.refs_12_), channel_id=1, source_target_pairs={{0,1},{1,0},{2,3},{3,2},{4,5},{5,4},{6,7},{7,6},{8,9},{9,8},{10,11... | collective-permute-start | bytes 491528 | tf_op jit(solution)/shard_map/along_inner/ppermute | solution.py:369
  27.7 1.4 %collective-permute-start.9 = (bf16[2,320,128]{2,1,0:T(8,128)(2,1)S(1)}, bf16[2,320,128]{2,1,0:T(8,128)(2,1)S(1)}, u32[]{:S(2)}, u32[]{:S(2)}) collective-permute-start(bf16[2,320,128]{2,1,0:T(8,128)(2,1)S(1)} %collective-permute-done.5.refs_2_.refs_10_), channel_id=1, source_target_pairs={{0,1},{1,0},{2,3},{3,2},{4,5},{5,4},{6,7},{7,6},{8,9},{9,8},{10,11... | collective-permute-start | bytes 491528 | tf_op jit(solution)/shard_map/along_inner/ppermute | solution.py:369
  27.7 6.6 %collective-permute-start.4 = (bf16[2,320,128]{2,1,0:T(8,128)(2,1)S(1)}, bf16[2,320,128]{2,1,0:T(8,128)(2,1)S(1)}, u32[]{:S(2)}, u32[]{:S(2)}) collective-permute-start(bf16[2,320,128]{2,1,0:T(8,128)(2,1)S(1)} %collective-permute-done.3.refs_4_.refs_12_), channel_id=1, source_target_pairs={{0,2},{2,0},{1,3},{3,1},{4,6},{6,4},{5,7},{7,5},{8,10},{10,8},{9,1... | collective-permute-start | bytes 491528 | tf_op jit(solution)/shard_map/along_head/ppermute | solution.py:365
  34.3 1.4 %collective-permute-start.11 = (bf16[2,320,128]{2,1,0:T(8,128)(2,1)S(1)}, bf16[2,320,128]{2,1,0:T(8,128)(2,1)S(1)}, u32[]{:S(2)}, u32[]{:S(2)}) collective-permute-start(bf16[2,320,128]{2,1,0:T(8,128)(2,1)S(1)} %collective-permute-done.4.refs_0_.refs_14_), channel_id=1, source_target_pairs={{0,1},{1,0},{2,3},{3,2},{4,5},{5,4},{6,7},{7,6},{8,9},{9,8},{10,11... | collective-permute-start | bytes 491528 | tf_op jit(solution)/shard_map/along_inner/ppermute | solution.py:369
where the time goes:
time: 39.2 us; the launch traced here: 39.3 us
  Pallas kernels  17.6 us (45%)
  waiting for transfers between devices  10.5 us (27%)
  starting transfers between devices  10.3 us (26%)
  between operations  0.83 us (2%)
    pallas_call x2, Pallas kernels, attend(): pl.pallas_call(functools.partial(middle_kernel, coef, [(distance, len(pai...  8.15 us
    ppermute x3, starting transfers between devices, along_seq(): return lax.ppermute(block, 'seq', route)  7.11 us
    pallas_call x1, Pallas kernels, body(): pl.pallas_call(functools.partial(local_kernel, coef, rows), in_specs=[sca...  4.62 us
    ppermute x3, waiting for transfers between devices, along_head(): lax.ppermute(block, 'head', [(i, i ^ 1) for i in range(lax.axis_size('hea...  4.62 us
    pallas_call x1, Pallas kernels, body(): pl.pallas_call(functools.partial(last_kernel, coef, distances), in_specs=...  3.38 us
    ppermute x3, waiting for transfers between devices, along_seq(): return lax.ppermute(block, 'seq', route)  3.34 us
    ppermute x6, waiting for transfers between devices, along_inner(): return lax.ppermute(block, 'inner', [(0, 1), (1, 0)])  2.56 us
    ppermute x3, starting transfers between devices, along_head(): lax.ppermute(block, 'head', [(i, i ^ 1) for i in range(lax.axis_size('hea...  2.51 us
  transfers between devices with their start and end apart: 12, of which 9 were waited for; matrix products, arithmetic and copies ran while one was open for 0% of the time, Pallas kernels for 32%

commit v1 on v0

v1 whole, which is shorter than its diff:
```python
import functools
import math

import jax
import jax.numpy as jnp
from jax import lax
from jax.experimental import pallas as pl
from jax.experimental.pallas import tpu as pltpu
from jax.sharding import PartitionSpec as P

NEG = -1e30
SUM_LIMIT = 1e36
LO, HI = 0, 1


def score_dot(q, k):
    return lax.dot_general(q, k, (((1,), (1,)), ((), ())), preferred_element_type=jnp.float32)


def value_dot(p, v):
    return jnp.dot(p, v, preferred_element_type=jnp.float32)


def widen(x, width):
    return jnp.concatenate([x] * (width // x.shape[1]), axis=1)


def with_ones(x):
    return jnp.concatenate([x, jnp.ones_like(x)], axis=1)


def is_power(count):
    return count & (count - 1) == 0


def source_of(index, distance, count):
    if is_power(count):
        return index ^ distance
    return lax.rem(index - distance + count, count)


def blocks_of(sb, seq_index):
    b0, b1 = sb[2 * seq_index], sb[2 * seq_index + 1]
    return jnp.where(b1 > b0, 1, 0), jnp.minimum(b0, b1), jnp.maximum(b0, b1)


def minus_columns(top):
    high = top.astype(jnp.bfloat16)
    rest = top - high.astype(jnp.float32)
    middle = rest.astype(jnp.bfloat16)
    low = (rest - middle.astype(jnp.float32)).astype(jnp.bfloat16)
    lane = lax.broadcasted_iota(jnp.int32, top.shape, 1)
    high, middle, low = (x.astype(jnp.float32) for x in (high, middle, low))
    picked = jnp.where(lane == 0, high, jnp.where(lane == 1, middle, jnp.where(lane == 2, low, 0.0)))
    return (-picked).astype(jnp.bfloat16)


def load_kernel(q_hbm, k_hbm, v_hbm, sb_hbm, piece, q_out, k_out, v_out, sb_out, sems):
    half = piece.shape[1]
    rows, width = q_hbm.shape[1], q_out.shape[2]
    inner = lax.axis_index("inner")
    mine = pl.ds(pl.multiple_of(lax.rem(lax.axis_index("head"), 2) * half, half), half)
    for value, src in enumerate((k_hbm, v_hbm)):

        @pl.when(inner == value)
        def _():
            pltpu.make_async_copy(src.at[:, mine], piece, sems.at[0]).start()

    copies = [pltpu.make_async_copy(k_hbm.at[:, mine], piece, sems.at[0])]
    pairs = [(k_hbm, k_out), (v_hbm, v_out), (sb_hbm, sb_out)]
    for h in range(q_hbm.shape[2] // width):
        pairs.append((q_hbm.at[:, :, pl.ds(h * width, width)], q_out.at[:, pl.ds(h * rows, rows)]))
    for place, (src, dst) in enumerate(pairs):
        copy = pltpu.make_async_copy(src, dst, sems.at[1 + place])
        copy.start()
        copies.append(copy)
    for copy in copies:
        copy.wait()


def scaled_exp(coef, s):
    return jnp.exp2(s * coef).astype(jnp.bfloat16)


def pipelined(steps, buffers, score, finish, done=None):
    even, odd = buffers
    score(0, even)
    if steps == 1:
        finish(0, even)
        return

    @pl.loop(0, steps // 2)
    def _(pair):
        first = 2 * pair
        score(first + 1, odd)
        finish(first, even)
        score(jnp.minimum(first + 2, steps - 1), even)
        finish(first + 1, odd)
        if done is not None:
            done(pair)


def sweep(coef, steps, chunk, rows, block_len, qx_ref, acc_ref, k_ref, v_ref, buffers, done=None):
    def place(i):
        order, row, start = chunk(i)
        return order, pl.ds(pl.multiple_of(row, rows), rows), pl.ds(pl.multiple_of(start, block_len), block_len)

    def score(i, buf):
        order, mine, keys = place(i)
        buf[...] = score_dot(qx_ref[order, mine], with_ones(k_ref[keys]))

    def finish(i, buf):
        order, mine, keys = place(i)
        acc_ref[order, mine] += value_dot(scaled_exp(coef, buf[...]), with_ones(v_ref[keys]))

    pipelined(steps, buffers, score, finish, done)


def diagonal_kernel(coef, rows, sb, q_ref, k_ref, v_ref, qx_ref, acc_ref, bias, *buffers):
    _, all_rows, width = q_ref.shape
    block_len = bias.shape[1]
    hi, _, _ = blocks_of(sb, lax.axis_index("seq"))
    row = lax.broadcasted_iota(jnp.int32, bias.shape, 0) + lax.axis_index("inner") * rows
    bias[...] = jnp.where(lax.broadcasted_iota(jnp.int32, bias.shape, 1) <= row, 0.0, NEG)

    def place(i):
        order = lax.rem(i, 2)
        slot = jnp.where(order == HI, hi, 1 - hi)
        return order, slot, pl.ds(pl.multiple_of(i // 2 * rows, rows), rows)

    def keys_of(slot):
        return pl.ds(pl.multiple_of(slot * block_len, block_len), block_len)

    def score(i, buf):
        _, slot, mine = place(i)
        buf[...] = score_dot(q_ref[slot, mine], k_ref[keys_of(slot)]) + bias[...]

    def finish(i, buf):
        order, slot, mine = place(i)
        parts = [buf[:, at : at + width] for at in range(0, block_len, width)]
        top = jnp.max(functools.reduce(jnp.maximum, parts), axis=1, keepdims=True)
        top = jnp.broadcast_to(top, (rows, width))
        p = scaled_exp(coef, buf[...] - widen(top, block_len))
        acc_ref[order, mine] = value_dot(p, with_ones(v_ref[keys_of(slot)]))
        qx_ref[order, mine] = jnp.concatenate([q_ref[slot, mine], minus_columns(top)], axis=1)

    pipelined(2 * all_rows // rows, buffers, score, finish)


def past_kernel(coef, rows, sb, qx_ref, acc_in, k_ref, v_ref, acc_ref, *buffers):
    block_len = buffers[0].shape[1]
    hi, _, _ = blocks_of(sb, lax.axis_index("seq"))

    def chunk(i):
        return HI, i * rows, (1 - hi) * block_len

    sweep(coef, qx_ref.shape[1] // rows, chunk, rows, block_len, qx_ref, acc_ref, k_ref, v_ref, buffers)


def place_pieces(parts, k_buf, v_buf):
    inner = lax.axis_index("inner")
    own_half = lax.rem(lax.axis_index("head"), 2)
    for value, (own_buf, twin_buf) in enumerate([(k_buf, v_buf), (v_buf, k_buf)]):

        @pl.when(inner == value)
        def _():
            for turn in range(2):
                half = own_half if turn == 0 else 1 - own_half
                for piece, buf in zip(parts[2 * turn : 2 * turn + 2], (own_buf, twin_buf)):
                    size = piece.shape[1]
                    for slot in range(2):
                        buf[pl.ds(pl.multiple_of((slot * 2 + half) * size, size), size)] = piece[slot]


def visit(coef, distance, rows, parts, sb, qx_ref, acc_ref, k_buf, v_buf, buffers, done=None):
    me = lax.axis_index("seq")
    block_len = buffers[0].shape[1]
    place_pieces(parts, k_buf, v_buf)
    _, _, top_block = blocks_of(sb, me)
    other_hi, _, other_top = blocks_of(sb, source_of(me, distance, lax.axis_size("seq")))
    above = top_block > other_top

    def chunk(i):
        turn = lax.rem(i, 2)
        order = jnp.where(above, HI, turn)
        slot = jnp.where(above, turn, 1 - other_hi)
        return order, i // 2 * rows, slot * block_len

    steps = 2 * qx_ref.shape[1] // rows
    sweep(coef, steps, chunk, rows, block_len, qx_ref, acc_ref, k_buf, v_buf, buffers, done)


def first_row(x):
    return jnp.transpose(x)[:1]


def middle_kernel(coef, distance, rows, sb, qx_ref, acc_in, p0, p1, p2, p3, acc_ref, *refs):
    *tops, k_buf, v_buf, even, odd = refs
    _, all_rows, double = qx_ref.shape
    visit(coef, distance, rows, (p0, p1, p2, p3), sb, qx_ref, acc_ref, k_buf, v_buf, (even, odd))
    for top_ref in tops:
        for order in (LO, HI):
            for h in range(all_rows // rows):
                columns = qx_ref[order, pl.ds(h * rows, rows), pl.ds(double // 2, double // 2)]
                columns = jnp.transpose(columns.astype(jnp.float32))
                top_ref[order, h : h + 1, :] = -(columns[0:1] + columns[1:2] + columns[2:3])


def last_kernel(coef, distances, sb, qx_ref, acc_ref, top_ref, *refs):
    parts, every, rest = refs[:4], refs[4 : 4 * len(distances) + 6], refs[4 * len(distances) + 6 :]
    out_hbm, lse_hbm, out_buf, lse_ref, k_buf, v_buf, even, odd, worst, run_top, run_acc, sem, out_sems = rest
    rows = out_buf.shape[1]
    all_rows = qx_ref.shape[1]
    heads = all_rows // rows
    block_len, width = k_buf.shape[0] // 2, k_buf.shape[1]
    half_len = block_len // 2
    count = lax.axis_size("seq")
    me = lax.axis_index("seq")
    own_half = lax.rem(lax.axis_index("head"), 2)
    inner = lax.axis_index("inner")
    hi, lo_block, hi_block = blocks_of(sb, me)
    lse_copy = pltpu.make_async_copy(lse_ref, lse_hbm, sem)

    def out_copy(h):
        columns = pl.ds(pl.multiple_of(h * width, width), width)
        return pltpu.make_async_copy(out_buf.at[:, :, columns], out_hbm.at[:, :, columns], out_sems.at[h])

    def emit(order, h, value, top_row):
        slot = hi if order == HI else 1 - hi
        sums = value[:, width:]
        columns = pl.ds(pl.multiple_of(h * width, width), width)
        out_buf[slot, :, columns] = (value[:, :width] / sums).astype(out_buf.dtype)
        lse_ref[slot, pl.ds(h, 1), :] = top_row * (coef * math.log(2.0)) + jnp.log(first_row(sums))
        return sums

    worst[...] = jnp.zeros_like(worst)

    def done(h):
        mine = pl.ds(pl.multiple_of(h * rows, rows), rows)
        for order in (LO, HI):
            sums = emit(order, h, acc_ref[order, mine], top_ref[order, pl.ds(h, 1), :])
            worst[...] = jnp.maximum(worst[...], sums)
        out_copy(h).start()

    visit(coef, distances[-1], rows, parts, sb, qx_ref, acc_ref, k_buf, v_buf, (even, odd), done)
    lse_copy.start()
    for h in range(heads):
        out_copy(h).wait()
    lse_copy.wait()

    @pl.when(jnp.logical_not(jnp.max(worst[...]) < SUM_LIMIT))
    def _():
        def fetch(src, dst):
            copy = pltpu.make_async_copy(src, dst, sem)
            copy.start()
            copy.wait()

        def online(source):
            @pl.loop(0, 4 * heads)
            def _(i):
                h, slot, order = i // 4, lax.rem(i, 4) // 2, lax.rem(i, 2)
                own_block = jnp.where(order == HI, hi_block, lo_block)
                shift = (own_block - sb[2 * source + slot]) * block_len + inner * rows

                @pl.when(shift + rows > 0)
                def _():
                    queries = qx_ref[order, pl.ds(pl.multiple_of(h * rows, rows), rows), pl.ds(0, width)]
                    at = pl.ds(pl.multiple_of(slot * block_len, block_len), block_len)
                    s = score_dot(queries, k_buf[at])
                    row = lax.broadcasted_iota(jnp.int32, s.shape, 0) + shift
                    allowed = lax.broadcasted_iota(jnp.int32, s.shape, 1) <= row
                    s = jnp.where(allowed, s, NEG)
                    before = run_top[order, h]
                    top = jnp.maximum(before, jnp.broadcast_to(jnp.max(s, axis=1, keepdims=True), before.shape))
                    p = jnp.where(allowed, jnp.exp2((s - widen(top, block_len)) * coef), 0.0)
                    run_top[order, h] = top
                    shrink = widen(jnp.exp2((before - top) * coef), 2 * width)
                    fresh = value_dot(p.astype(jnp.bfloat16), with_ones(v_buf[at]))
                    run_acc[order, h] = run_acc[order, h] * shrink + fresh

        run_top[...] = jnp.full_like(run_top, NEG)
        run_acc[...] = jnp.zeros_like(run_acc)
        def rows_of(slot, half):
            return pl.ds(pl.multiple_of((slot * 2 + half) * half_len, half_len), half_len)

        for slot in range(2):
            fetch(every[0].at[slot], k_buf.at[pl.ds(slot * block_len, block_len)])
            fetch(every[1].at[slot], v_buf.at[pl.ds(slot * block_len, block_len)])
        online(me)
        for place, other in enumerate(distances):
            others = every[2 + 4 * place : 6 + 4 * place]
            for value, (own_buf, twin_buf) in enumerate([(k_buf, v_buf), (v_buf, k_buf)]):

                @pl.when(inner == value)
                def _():
                    for turn in range(2):
                        half = own_half if turn == 0 else 1 - own_half
                        for slot in range(2):
                            fetch(others[2 * turn].at[slot], own_buf.at[rows_of(slot, half)])
                            fetch(others[2 * turn + 1].at[slot], twin_buf.at[rows_of(slot, half)])

            online(source_of(me, other, count))
        for h in range(heads):
            for order in (LO, HI):
                emit(order, h, run_acc[order, h], first_row(run_top[order, h]))
            out_copy(h).start()
            out_copy(h).wait()
        lse_copy.start()
        lse_copy.wait()


def body(query_rows, key_rows, value_rows, slot_block):
    _, block_len, width = key_rows.shape
    _, rows, feats = query_rows.shape
    heads = feats // width
    all_rows = heads * rows
    count = lax.axis_size("seq")
    coef = math.log2(math.e) / math.sqrt(width)
    distances = list(range(1, count))

    def along_seq(block, distance):
        if is_power(count):
            route = [(i, i ^ distance) for i in range(count)]
        else:
            route = [(i, (i + distance) % count) for i in range(count)]
        with jax.named_scope("along_seq"):
            return lax.ppermute(block, "seq", route)

    def along_head(block):
        with jax.named_scope("along_head"):
            return lax.ppermute(block, "head", [(i, i ^ 1) for i in range(lax.axis_size("head"))])

    def along_inner(block):
        with jax.named_scope("along_inner"):
            return lax.ppermute(block, "inner", [(0, 1), (1, 0)])

    whole = pl.BlockSpec(memory_space=pltpu.VMEM)
    anywhere = pl.BlockSpec(memory_space=pl.ANY)
    scalars = pl.BlockSpec(memory_space=pltpu.SMEM)
    acc_shape = jax.ShapeDtypeStruct((2, all_rows, 2 * width), jnp.float32)
    qx_shape = jax.ShapeDtypeStruct(acc_shape.shape, jnp.bfloat16)
    top_shape = jax.ShapeDtypeStruct((2, heads, rows), jnp.float32)
    params = pltpu.CompilerParams(vmem_limit_bytes=40 * 1024 * 1024)
    unit = rows * heads * block_len * width * 4
    exps = rows * heads * block_len

    def cost(units, size):
        return pl.CostEstimate(flops=int(2 * units * unit), bytes_accessed=size, transcendentals=int(units * exps))

    in_hbm = [
        pltpu.with_memory_space_constraint(x, pltpu.HBM) for x in (query_rows, key_rows, value_rows, slot_block)
    ]
    half_shape = jax.ShapeDtypeStruct((2, block_len // 2, width), key_rows.dtype)
    piece, q_here, k_here, v_here, sb_here = pl.pallas_call(
        load_kernel,
        in_specs=[anywhere] * 4,
        out_specs=[whole] * 5,
        out_shape=[half_shape, jax.ShapeDtypeStruct((2, all_rows, width), query_rows.dtype)]
        + [jax.ShapeDtypeStruct(x.shape, x.dtype) for x in in_hbm[1:]],
        scratch_shapes=[pltpu.SemaphoreType.DMA((4 + heads,))],
        cost_estimate=pl.CostEstimate(flops=0, bytes_accessed=3_000_000, transcendentals=0),
        compiler_params=params,
        name="load",
    )(*in_hbm)
    arrived, across, beside, beside_across = {}, {}, {}, {}
    for distance in distances:
        if not is_power(count) or is_power(distance):
            arrived[distance] = along_seq(piece, distance)

    k_flat, v_flat = (x.reshape(2 * block_len, width) for x in (k_here, v_here))
    score_buffers = [pltpu.VMEM((rows, block_len), jnp.float32)] * 2
    qx, acc = pl.pallas_call(
        functools.partial(diagonal_kernel, coef, rows),
        in_specs=[scalars] + [whole] * 3,
        out_specs=[whole] * 2,
        out_shape=[qx_shape, acc_shape],
        scratch_shapes=[pltpu.VMEM((rows, block_len), jnp.float32)] + score_buffers,
        cost_estimate=cost(2, 6_000_000),
        compiler_params=params,
        name="diagonal",
    )(sb_here, q_here, k_flat, v_flat)
    kv_buffers = [pltpu.VMEM((2 * block_len, width), jnp.bfloat16)] * 2

    def spread(distance):
        if distance in distances:
            across[distance] = along_head(arrived[distance])
            beside[distance] = along_inner(arrived[distance])

    def relay(distance):
        if distance in distances and distance not in arrived:
            near = distance & -distance
            arrived[distance] = along_seq(arrived[distance ^ near], near)

    def attend(acc, distance, with_tops):
        return pl.pallas_call(
            functools.partial(middle_kernel, coef, distance, rows),
            in_specs=[scalars] + [whole] * 6,
            out_specs=[whole] * (1 + with_tops),
            out_shape=[acc_shape] + [top_shape] * with_tops,
            scratch_shapes=kv_buffers + score_buffers,
            input_output_aliases={2: 0},
            cost_estimate=cost(2, 7_000_000),
            compiler_params=params,
            name=f"visitor_{distance}",
        )(sb_here, qx, acc, arrived[distance], beside[distance], across[distance], beside_across[distance])

    last = distances[-1]
    arrived[1], acc = lax.optimization_barrier((arrived[1], acc))
    spread(1)
    acc = pl.pallas_call(
        functools.partial(past_kernel, coef, rows),
        in_specs=[scalars] + [whole] * 4,
        out_specs=whole,
        out_shape=acc_shape,
        scratch_shapes=score_buffers,
        input_output_aliases={2: 0},
        cost_estimate=cost(1, 6_000_000),
        compiler_params=params,
        name="past",
    )(sb_here, qx, acc, k_flat, v_flat)
    for distance in distances[:-1]:
        following = distance + 1
        tied = lax.optimization_barrier((across[distance], arrived[following], acc))
        across[distance], arrived[following], acc = tied
        relay(following + 1)
        spread(following)
        beside_across[distance] = along_inner(across[distance])
        acc, *tops = attend(acc, distance, int(following == last))
    across[last], acc = lax.optimization_barrier((across[last], acc))
    beside_across[last] = along_inner(across[last])

    flat = [part[d] for d in distances for part in (arrived, beside, across, beside_across)]
    attended, log_total = pl.pallas_call(
        functools.partial(last_kernel, coef, distances),
        in_specs=[scalars] + [whole] * 7 + [anywhere] * (2 + len(flat)),
        out_specs=[anywhere, anywhere],
        out_shape=[jax.ShapeDtypeStruct(query_rows.shape, query_rows.dtype), top_shape],
        scratch_shapes=[
            pltpu.VMEM(query_rows.shape, query_rows.dtype),
            pltpu.VMEM(top_shape.shape, jnp.float32),
        ]
        + kv_buffers
        + score_buffers
        + [
            pltpu.VMEM((rows, width), jnp.float32),
            pltpu.VMEM((2, heads, rows, width), jnp.float32),
            pltpu.VMEM((2, heads, rows, 2 * width), jnp.float32),
            pltpu.SemaphoreType.DMA,
            pltpu.SemaphoreType.DMA((heads,)),
        ],
        cost_estimate=cost(1, 7_000_000),
        compiler_params=params,
        name="last_visitor",
    )(sb_here, qx, acc, *tops, *flat[-4:], in_hbm[1], in_hbm[2], *flat)
    return attended, log_total


def solution(mesh):
    placed = (
        P(("groups", "seq"), "inner", "head"),
        P(("groups", "seq"), None, None),
        P(("groups", "seq"), None, None),
        P(),
    )
    return jax.shard_map(
        body,
        mesh=mesh,
        in_specs=placed,
        out_specs=(P(("groups", "seq"), "inner", "head"), P(("groups", "seq"), "head", "inner")),
        check_vma=False,
    )
```

time: 39.2 us -> 39.4 us (level)
  Pallas kernels: 17.6 us -> 21.8 us
  waiting for transfers between devices: 10.5 us -> 6.83 us
    pallas_call x3 -> x4, Pallas kernels: 12.8 us -> 15.2 us  [the longest x2 7.82 us: attend(): pl.pallas_call(functools.partial(middle_kernel, coef, distance, rows), in...]
    ppermute x3, waiting for transfers between devices: 3.34 us -> 1.21 us  [along_seq(): return lax.ppermute(block, 'seq', route)]
    pallas_call x1, Pallas kernels: 3.38 us -> 5.07 us  [body(): pl.pallas_call(functools.partial(last_kernel, coef, distances), in_specs=...]
    ppermute x3, starting transfers between devices: 2.51 us -> 3.6 us  [along_head(): lax.ppermute(block, 'head', [(i, i ^ 1) for i in range(lax.axis_size('hea...]
    ppermute x3, waiting for transfers between devices: 4.62 us -> 3.59 us  [along_head(): lax.ppermute(block, 'head', [(i, i ^ 1) for i in range(lax.axis_size('hea...]
    ppermute x3, starting transfers between devices: 7.11 us -> 6.13 us  [along_seq(): return lax.ppermute(block, 'seq', route)]
    ppermute x6, waiting for transfers between devices: 2.56 us -> 2.02 us  [along_inner(): return lax.ppermute(block, 'inner', [(0, 1), (1, 0)])]
    ppermute x6, starting transfers between devices: 0.65 us -> 0.24 us  [along_inner(): return lax.ppermute(block, 'inner', [(0, 1), (1, 0)])]
  transfers between devices with their start and end apart: 12 -> 12, of which waited for: 9 -> 6; matrix products, arithmetic and copies ran while one was open for 0% -> 0% of each run, Pallas kernels for 32% -> 39%
where the time goes in v1:
time: 39.4 us; the launch traced here: 39.2 us
  Pallas kernels  21.8 us (55%)
  starting transfers between devices  9.96 us (25%)
  waiting for transfers between devices  6.83 us (17%)
  between operations  0.69 us (2%)
    pallas_call x2, Pallas kernels, attend(): pl.pallas_call(functools.partial(middle_kernel, coef, distance, rows), in...  7.82 us
    ppermute x3, starting transfers between devices, along_seq(): return lax.ppermute(block, 'seq', route)  6.13 us
    pallas_call x1, Pallas kernels, body(): pl.pallas_call(functools.partial(diagonal_kernel, coef, rows), in_specs=[...  5.07 us
    pallas_call x1, Pallas kernels, body(): pl.pallas_call(functools.partial(last_kernel, coef, distances), in_specs=...  5.07 us
    ppermute x3, starting transfers between devices, along_head(): lax.ppermute(block, 'head', [(i, i ^ 1) for i in range(lax.axis_size('hea...  3.6 us
    ppermute x3, waiting for transfers between devices, along_head(): lax.ppermute(block, 'head', [(i, i ^ 1) for i in range(lax.axis_size('hea...  3.59 us
    pallas_call x1, Pallas kernels, body(): pl.pallas_call(functools.partial(past_kernel, coef, rows), in_specs=[scal...  2.32 us
    ppermute x6, waiting for transfers between devices, along_inner(): return lax.ppermute(block, 'inner', [(0, 1), (1, 0)])  2.02 us
  transfers between devices with their start and end apart: 12, of which 6 were waited for; matrix products, arithmetic and copies ran while one was open for 0% of the time, Pallas kernels for 39%

profile of v1, /device:TPU:0, one launch (start us, length us, event | category | flops | bytes accessed | tf_op | source)
XLA Modules:
  0.0 39.2 jit_solution(3869216787358210097)
XLA Ops:
  0.6 1.5 %load.1 = (bf16[2,320,128]{2,1,0:T(8,128)(2,1)S(1)}, bf16[2,1280,128]{2,1,0:T(8,128)(2,1)S(1)}, bf16[2,640,128]{2,1,0:T(8,128)(2,1)S(1)}, bf16[2,640,128]{2,1,0:T(8,128)(2,1)S(1)}, s32[8]{0:T(128)S(1)}) custom-call(bf16[2,320,512]{2,1,0:T(8,128)(2,1)} %q_hbm.1, bf16[2,640,128]{2,1,0:T(8,128)(2,1)} %refs_4_.1, bf16[2,640,128]{2,1,0:T(8,128)(2,1)} %refs_5_.1, ...), custom_call_target="tpu_custom_call" | custom-call | bytes 3000000 | tf_op jit(solution)/shard_map/load/pallas_call | solution.py:354
  2.1 3.1 %collective-permute-start = (bf16[2,320,128]{2,1,0:T(8,128)(2,1)S(1)}, bf16[2,320,128]{2,1,0:T(8,128)(2,1)S(1)}, u32[]{:S(2)}, u32[]{:S(2)}) collective-permute-start(bf16[2,320,128]{2,1,0:T(8,128)(2,1)S(1)} %get-tuple-element.26), channel_id=1, source_target_pairs={{0,4},{4,0},{8,12},{12,8},{1,5},{5,1},{9,13},{13,9},{2,6},{6,2},{1... | collective-permute-start | bytes 491528 | tf_op jit(solution)/shard_map/along_seq/ppermute | solution.py:327
  5.2 2.6 %collective-permute-start.2 = (bf16[2,320,128]{2,1,0:T(8,128)(2,1)S(1)}, bf16[2,320,128]{2,1,0:T(8,128)(2,1)S(1)}, u32[]{:S(2)}, u32[]{:S(2)}) collective-permute-start(bf16[2,320,128]{2,1,0:T(8,128)(2,1)S(1)} %get-tuple-element.26), channel_id=1, source_target_pairs={{0,8},{4,12},{8,0},{12,4},{1,9},{5,13},{9,1},{13,5},{2,10},{6,14},... | collective-permute-start | bytes 491528 | tf_op jit(solution)/shard_map/along_seq/ppermute | solution.py:327
  7.8 5.1 %diagonal.1 = (bf16[2,1280,256]{2,1,0:T(8,128)(2,1)S(1)}, f32[2,1280,256]{2,1,0:T(8,128)S(1)}) custom-call(s32[8]{0:T(128)S(1)} %get-tuple-element.21.sb, bf16[2,1280,128]{2,1,0:T(8,128)(2,1)S(1)} %get-tuple-element.22.q_ref, bf16[1280,128]{1,0:T(8,128)(2,1)S(1)} %bitcast.2, bf16[1280,128]{1,0:T(8,128)(2,1)S(1)} %bitcast.4), custom_call_target="tpu_custom_call" | custom-call | flops 1677721600 | bytes 6000000 | tf_op jit(solution)/shard_map/diagonal/pallas_call | solution.py:372
  12.9 0.0 collective-permute-done.p0.refs_6_
  12.9 1.6 %collective-permute-start.1 = (bf16[2,320,128]{2,1,0:T(8,128)(2,1)S(1)}, bf16[2,320,128]{2,1,0:T(8,128)(2,1)S(1)}, u32[]{:S(2)}, u32[]{:S(2)}) collective-permute-start(bf16[2,320,128]{2,1,0:T(8,128)(2,1)S(1)} %collective-permute-done.p0.refs_6_), channel_id=1, source_target_pairs={{0,2},{2,0},{1,3},{3,1},{4,6},{6,4},{5,7},{7,5},{8,10},{10,8},{9,1... | collective-permute-start | bytes 491528 | tf_op jit(solution)/shard_map/along_head/ppermute | solution.py:331
  14.5 0.0 collective-permute-start.5
  14.5 2.3 %past.1.acc_in = f32[2,1280,256]{2,1,0:T(8,128)S(1)} custom-call(s32[8]{0:T(128)S(1)} %get-tuple-element.21.sb, bf16[2,1280,256]{2,1,0:T(8,128)(2,1)S(1)} %get-tuple-element.25.qx_ref, f32[2,1280,256]{2,1,0:T(8,128)S(1)} %get-tuple-element.29.acc_in, bf16[1280,128]{1,0:T(8,128)(2,1)S(1)} %bitcast.3, ...), custom_call_target="tpu_custom_call", output_to_operand_aliasing={{}: (2, {})} | custom-call | flops 838860800 | bytes 6000000 | tf_op jit(solution)/shard_map/past/pallas_call | solution.py:410
  16.8 0.0 collective-permute-done.2.p0.refs_10_
  16.8 1.5 %collective-permute-done.1.p2.refs_8_ = bf16[2,320,128]{2,1,0:T(8,128)(2,1)S(1)} collective-permute-done((bf16[2,320,128]{2,1,0:T(8,128)(2,1)S(1)}, bf16[2,320,128]{2,1,0:T(8,128)(2,1)S(1)}, u32[]{:S(2)}, u32[]{:S(2)}) %collective-permute-start.1) | collective-permute-done | bytes 163872 | tf_op jit(solution)/shard_map/along_head/ppermute | solution.py:331
  18.3 0.0 collective-permute-start.6
  18.3 1.5 %collective-permute-start.3 = (bf16[2,320,128]{2,1,0:T(8,128)(2,1)S(1)}, bf16[2,320,128]{2,1,0:T(8,128)(2,1)S(1)}, u32[]{:S(2)}, u32[]{:S(2)}) collective-permute-start(bf16[2,320,128]{2,1,0:T(8,128)(2,1)S(1)} %collective-permute-done.2.p0.refs_10_), channel_id=1, source_target_pairs={{0,2},{2,0},{1,3},{3,1},{4,6},{6,4},{5,7},{7,5},{8,10},{10,8},{9,1... | collective-permute-start | bytes 491528 | tf_op jit(solution)/shard_map/along_head/ppermute | solution.py:331
  19.8 0.4 %collective-permute-start.4 = (bf16[2,320,128]{2,1,0:T(8,128)(2,1)S(1)}, bf16[2,320,128]{2,1,0:T(8,128)(2,1)S(1)}, u32[]{:S(2)}, u32[]{:S(2)}) collective-permute-start(bf16[2,320,128]{2,1,0:T(8,128)(2,1)S(1)} %collective-permute-done.2.p0.refs_10_), channel_id=1, source_target_pairs={{0,4},{4,0},{8,12},{12,8},{1,5},{5,1},{9,13},{13,9},{2,6},{6,2},{1... | collective-permute-start | bytes 491528 | tf_op jit(solution)/shard_map/along_seq/ppermute | solution.py:327
  20.3 0.0 collective-permute-start.8
  20.3 0.0 collective-permute-done.5.p1.refs_7_
  20.3 0.0 collective-permute-done.6.p3.refs_9_
  20.3 3.8 %visitor_1.1.acc_in = f32[2,1280,256]{2,1,0:T(8,128)S(1)} custom-call(s32[8]{0:T(128)S(1)} %get-tuple-element.21.sb, bf16[2,1280,256]{2,1,0:T(8,128)(2,1)S(1)} %get-tuple-element.25.qx_ref, f32[2,1280,256]{2,1,0:T(8,128)S(1)} %past.1.acc_in, bf16[2,320,128]{2,1,0:T(8,128)(2,1)S(1)} %collective-permute-done.p0.refs_6_, ...), custom_call_target="tpu_custom_call", output_to_operand_aliasing={{}: (2, {})} | custom-call | flops 1677721600 | bytes 7000000 | tf_op jit(solution)/shard_map/visitor_1/pallas_call | solution.py:395
  24.1 0.8 %collective-permute-done.3.p2.refs_12_ = bf16[2,320,128]{2,1,0:T(8,128)(2,1)S(1)} collective-permute-done((bf16[2,320,128]{2,1,0:T(8,128)(2,1)S(1)}, bf16[2,320,128]{2,1,0:T(8,128)(2,1)S(1)}, u32[]{:S(2)}, u32[]{:S(2)}) %collective-permute-start.3) | collective-permute-done | bytes 163872 | tf_op jit(solution)/shard_map/along_head/ppermute | solution.py:331
  24.9 1.2 %collective-permute-done.4.refs_0_.refs_14_ = bf16[2,320,128]{2,1,0:T(8,128)(2,1)S(1)} collective-permute-done((bf16[2,320,128]{2,1,0:T(8,128)(2,1)S(1)}, bf16[2,320,128]{2,1,0:T(8,128)(2,1)S(1)}, u32[]{:S(2)}, u32[]{:S(2)}) %collective-permute-start.4) | collective-permute-done | bytes 163872 | tf_op jit(solution)/shard_map/along_seq/ppermute | solution.py:327
  26.2 0.0 collective-permute-start.9
  26.2 0.5 %collective-permute-start.7 = (bf16[2,320,128]{2,1,0:T(8,128)(2,1)S(1)}, bf16[2,320,128]{2,1,0:T(8,128)(2,1)S(1)}, u32[]{:S(2)}, u32[]{:S(2)}) collective-permute-start(bf16[2,320,128]{2,1,0:T(8,128)(2,1)S(1)} %collective-permute-done.4.refs_0_.refs_14_), channel_id=1, source_target_pairs={{0,2},{2,0},{1,3},{3,1},{4,6},{6,4},{5,7},{7,5},{8,10},{10,8},{9,1... | collective-permute-start | bytes 491528 | tf_op jit(solution)/shard_map/along_head/ppermute | solution.py:331
  26.7 0.2 collective-permute-start.10
  26.9 0.0 collective-permute-done.8.p1.refs_11_
  26.9 0.6 %collective-permute-done.9.p3.refs_13_ = bf16[2,320,128]{2,1,0:T(8,128)(2,1)S(1)} collective-permute-done((bf16[2,320,128]{2,1,0:T(8,128)(2,1)S(1)}, bf16[2,320,128]{2,1,0:T(8,128)(2,1)S(1)}, u32[]{:S(2)}, u32[]{:S(2)}) %collective-permute-start.9) | collective-permute-done | bytes 163872 | tf_op jit(solution)/shard_map/along_inner/ppermute | solution.py:335
  27.6 4.0 %visitor_2.1 = (f32[2,1280,256]{2,1,0:T(8,128)S(1)}, f32[2,4,320]{2,1,0:T(4,128)S(1)}) custom-call(s32[8]{0:T(128)S(1)} %get-tuple-element.21.sb, bf16[2,1280,256]{2,1,0:T(8,128)(2,1)S(1)} %get-tuple-element.25.qx_ref, f32[2,1280,256]{2,1,0:T(8,128)S(1)} %visitor_1.1.acc_in, ...), custom_call_target="tpu_custom_call", output_to_operand_aliasing={{0}: (2, {})} | custom-call | flops 1677721600 | bytes 7000000 | tf_op jit(solution)/shard_map/visitor_2/pallas_call | solution.py:395
  31.6 1.2 %collective-permute-done.7.refs_2_.refs_16_ = bf16[2,320,128]{2,1,0:T(8,128)(2,1)S(1)} collective-permute-done((bf16[2,320,128]{2,1,0:T(8,128)(2,1)S(1)}, bf16[2,320,128]{2,1,0:T(8,128)(2,1)S(1)}, u32[]{:S(2)}, u32[]{:S(2)}) %collective-permute-start.7) | collective-permute-done | bytes 163872 | tf_op jit(solution)/shard_map/along_head/ppermute | solution.py:331
  32.8 0.0 collective-permute-start.11
  32.8 0.0 collective-permute-done.10.refs_1_.refs_15_
  32.8 1.4 %collective-permute-done.11.refs_3_.refs_17_ = bf16[2,320,128]{2,1,0:T(8,128)(2,1)S(1)} collective-permute-done((bf16[2,320,128]{2,1,0:T(8,128)(2,1)S(1)}, bf16[2,320,128]{2,1,0:T(8,128)(2,1)S(1)}, u32[]{:S(2)}, u32[]{:S(2)}) %collective-permute-start.11) | collective-permute-done | bytes 163872 | tf_op jit(solution)/shard_map/along_inner/ppermute | solution.py:335
  34.2 5.1 %last_visitor.1 = (bf16[2,320,512]{2,1,0:T(8,128)(2,1)}, f32[2,4,320]{2,1,0:T(4,128)}) custom-call(s32[8]{0:T(128)S(1)} %get-tuple-element.21.sb, bf16[2,1280,256]{2,1,0:T(8,128)(2,1)S(1)} %get-tuple-element.25.qx_ref, f32[2,1280,256]{2,1,0:T(8,128)S(1)} %get-tuple-element.37.acc_ref, f32[2,4,320]{2,1,0:T(4,128)S(1)} %get-tuple-element.38.top_ref, ...), custom_call_target="tpu_custom_call" | custom-call | flops 838860800 | bytes 7000000 | tf_op jit(solution)/shard_map/last_visitor/pallas_call | solution.py:433
Async XLA Ops:
  2.1 10.8 %collective-permute-start = (bf16[2,320,128]{2,1,0:T(8,128)(2,1)S(1)}, bf16[2,320,128]{2,1,0:T(8,128)(2,1)S(1)}, u32[]{:S(2)}, u32[]{:S(2)}) collective-permute-start(bf16[2,320,128]{2,1,0:T(8,128)(2,1)S(1)} %get-tuple-element.26), channel_id=1, source_target_pairs={{0,4},{4,0},{8,12},{12,8},{1,5},{5,1},{9,13},{13,9},{2,6},{6,2},{1... | collective-permute-start | bytes 491528 | tf_op jit(solution)/shard_map/along_seq/ppermute | solution.py:327
  5.2 11.6 %collective-permute-start.2 = (bf16[2,320,128]{2,1,0:T(8,128)(2,1)S(1)}, bf16[2,320,128]{2,1,0:T(8,128)(2,1)S(1)}, u32[]{:S(2)}, u32[]{:S(2)}) collective-permute-start(bf16[2,320,128]{2,1,0:T(8,128)(2,1)S(1)} %get-tuple-element.26), channel_id=1, source_target_pairs={{0,8},{4,12},{8,0},{12,4},{1,9},{5,13},{9,1},{13,5},{2,10},{6,14},... | collective-permute-start | bytes 491528 | tf_op jit(solution)/shard_map/along_seq/ppermute | solution.py:327
  12.9 5.4 %collective-permute-start.1 = (bf16[2,320,128]{2,1,0:T(8,128)(2,1)S(1)}, bf16[2,320,128]{2,1,0:T(8,128)(2,1)S(1)}, u32[]{:S(2)}, u32[]{:S(2)}) collective-permute-start(bf16[2,320,128]{2,1,0:T(8,128)(2,1)S(1)} %collective-permute-done.p0.refs_6_), channel_id=1, source_target_pairs={{0,2},{2,0},{1,3},{3,1},{4,6},{6,4},{5,7},{7,5},{8,10},{10,8},{9,1... | collective-permute-start | bytes 491528 | tf_op jit(solution)/shard_map/along_head/ppermute | solution.py:331
  14.5 5.8 %collective-permute-start.5 = (bf16[2,320,128]{2,1,0:T(8,128)(2,1)S(1)}, bf16[2,320,128]{2,1,0:T(8,128)(2,1)S(1)}, u32[]{:S(2)}, u32[]{:S(2)}) collective-permute-start(bf16[2,320,128]{2,1,0:T(8,128)(2,1)S(1)} %collective-permute-done.p0.refs_6_), channel_id=1, source_target_pairs={{0,1},{1,0},{2,3},{3,2},{4,5},{5,4},{6,7},{7,6},{8,9},{9,8},{10,11... | collective-permute-start | bytes 491528 | tf_op jit(solution)/shard_map/along_inner/ppermute | solution.py:335
  18.3 2.0 %collective-permute-start.6 = (bf16[2,320,128]{2,1,0:T(8,128)(2,1)S(1)}, bf16[2,320,128]{2,1,0:T(8,128)(2,1)S(1)}, u32[]{:S(2)}, u32[]{:S(2)}) collective-permute-start(bf16[2,320,128]{2,1,0:T(8,128)(2,1)S(1)} %collective-permute-done.1.p2.refs_8_), channel_id=1, source_target_pairs={{0,1},{1,0},{2,3},{3,2},{4,5},{5,4},{6,7},{7,6},{8,9},{9,8},{10,11... | collective-permute-start | bytes 491528 | tf_op jit(solution)/shard_map/along_inner/ppermute | solution.py:335
  18.3 6.6 %collective-permute-start.3 = (bf16[2,320,128]{2,1,0:T(8,128)(2,1)S(1)}, bf16[2,320,128]{2,1,0:T(8,128)(2,1)S(1)}, u32[]{:S(2)}, u32[]{:S(2)}) collective-permute-start(bf16[2,320,128]{2,1,0:T(8,128)(2,1)S(1)} %collective-permute-done.2.p0.refs_10_), channel_id=1, source_target_pairs={{0,2},{2,0},{1,3},{3,1},{4,6},{6,4},{5,7},{7,5},{8,10},{10,8},{9,1... | collective-permute-start | bytes 491528 | tf_op jit(solution)/shard_map/along_head/ppermute | solution.py:331
  19.8 6.3 %collective-permute-start.4 = (bf16[2,320,128]{2,1,0:T(8,128)(2,1)S(1)}, bf16[2,320,128]{2,1,0:T(8,128)(2,1)S(1)}, u32[]{:S(2)}, u32[]{:S(2)}) collective-permute-start(bf16[2,320,128]{2,1,0:T(8,128)(2,1)S(1)} %collective-permute-done.2.p0.refs_10_), channel_id=1, source_target_pairs={{0,4},{4,0},{8,12},{12,8},{1,5},{5,1},{9,13},{13,9},{2,6},{6,2},{1... | collective-permute-start | bytes 491528 | tf_op jit(solution)/shard_map/along_seq/ppermute | solution.py:327
  20.3 6.7 %collective-permute-start.8 = (bf16[2,320,128]{2,1,0:T(8,128)(2,1)S(1)}, bf16[2,320,128]{2,1,0:T(8,128)(2,1)S(1)}, u32[]{:S(2)}, u32[]{:S(2)}) collective-permute-start(bf16[2,320,128]{2,1,0:T(8,128)(2,1)S(1)} %collective-permute-done.2.p0.refs_10_), channel_id=1, source_target_pairs={{0,1},{1,0},{2,3},{3,2},{4,5},{5,4},{6,7},{7,6},{8,9},{9,8},{10,11... | collective-permute-start | bytes 491528 | tf_op jit(solution)/shard_map/along_inner/ppermute | solution.py:335
  26.2 1.4 %collective-permute-start.9 = (bf16[2,320,128]{2,1,0:T(8,128)(2,1)S(1)}, bf16[2,320,128]{2,1,0:T(8,128)(2,1)S(1)}, u32[]{:S(2)}, u32[]{:S(2)}) collective-permute-start(bf16[2,320,128]{2,1,0:T(8,128)(2,1)S(1)} %collective-permute-done.3.p2.refs_12_), channel_id=1, source_target_pairs={{0,1},{1,0},{2,3},{3,2},{4,5},{5,4},{6,7},{7,6},{8,9},{9,8},{10,11... | collective-permute-start | bytes 491528 | tf_op jit(solution)/shard_map/along_inner/ppermute | solution.py:335
  26.2 6.6 %collective-permute-start.7 = (bf16[2,320,128]{2,1,0:T(8,128)(2,1)S(1)}, bf16[2,320,128]{2,1,0:T(8,128)(2,1)S(1)}, u32[]{:S(2)}, u32[]{:S(2)}) collective-permute-start(bf16[2,320,128]{2,1,0:T(8,128)(2,1)S(1)} %collective-permute-done.4.refs_0_.refs_14_), channel_id=1, source_target_pairs={{0,2},{2,0},{1,3},{3,1},{4,6},{6,4},{5,7},{7,5},{8,10},{10,8},{9,1... | collective-permute-start | bytes 491528 | tf_op jit(solution)/shard_map/along_head/ppermute | solution.py:331
  26.7 6.1 %collective-permute-start.10 = (bf16[2,320,128]{2,1,0:T(8,128)(2,1)S(1)}, bf16[2,320,128]{2,1,0:T(8,128)(2,1)S(1)}, u32[]{:S(2)}, u32[]{:S(2)}) collective-permute-start(bf16[2,320,128]{2,1,0:T(8,128)(2,1)S(1)} %collective-permute-done.4.refs_0_.refs_14_), channel_id=1, source_target_pairs={{0,1},{1,0},{2,3},{3,2},{4,5},{5,4},{6,7},{7,6},{8,9},{9,8},{10,11... | collective-permute-start | bytes 491528 | tf_op jit(solution)/shard_map/along_inner/ppermute | solution.py:335
  32.8 1.4 %collective-permute-start.11 = (bf16[2,320,128]{2,1,0:T(8,128)(2,1)S(1)}, bf16[2,320,128]{2,1,0:T(8,128)(2,1)S(1)}, u32[]{:S(2)}, u32[]{:S(2)}) collective-permute-start(bf16[2,320,128]{2,1,0:T(8,128)(2,1)S(1)} %collective-permute-done.7.refs_2_.refs_16_), channel_id=1, source_target_pairs={{0,1},{1,0},{2,3},{3,2},{4,5},{5,4},{6,7},{7,6},{8,9},{9,8},{10,11... | collective-permute-start | bytes 491528 | tf_op jit(solution)/shard_map/along_inner/ppermute | solution.py:335

commit v2 on v0

--- a/solution.py
+++ b/solution.py
@@ -18,6 +18,10 @@
     return lax.dot_general(q, k, (((1,), (1,)), ((), ())), preferred_element_type=jnp.float32)
 
 
+def flat_dot(q, k_turned):
+    return jnp.dot(q, k_turned, preferred_element_type=jnp.float32)
+
+
 def value_dot(p, v):
     return jnp.dot(p, v, preferred_element_type=jnp.float32)
 
@@ -28,6 +32,10 @@
 
 def with_ones(x):
     return jnp.concatenate([x, jnp.ones_like(x)], axis=1)
+
+
+def over_ones(x):
+    return jnp.concatenate([x, jnp.ones_like(x)], axis=0)
 
 
 def is_power(count):
@@ -96,7 +104,7 @@
         finish(scaled_exp(coef, now), *chunk)
 
 
-def local_kernel(coef, rows, sb, q_ref, k_ref, v_ref, qx_ref, acc_ref):
+def local_kernel(coef, rows, sb, q_ref, k_ref, v_ref, qx_ref, acc_ref, turned):
     _, all_rows, width = q_ref.shape
     block_len = k_ref.shape[1]
     heads = all_rows // rows
@@ -104,8 +112,11 @@
     slots = {HI: hi, LO: 1 - hi}
     tiles = key_tiles(block_len)
 
-    def keys(slot, start, size):
-        return k_ref[slot, pl.ds(start, size)]
+    for order in (HI, LO):
+        turned[order] = jnp.transpose(k_ref[slots[order]])
+
+    def keys(order, start, size):
+        return turned[order, :, start : start + size]
 
     def values(slot, start, size):
         return with_ones(v_ref[slot, pl.ds(start, size)])
@@ -114,7 +125,7 @@
         row = lax.broadcasted_iota(jnp.int32, (rows, size), 0) + lax.axis_index("inner") * rows
         col = lax.broadcasted_iota(jnp.int32, (rows, size), 1) + start
         bias = jnp.where(col <= row, 0.0, NEG)
-        s = score_dot(q_ref[slots[order]], keys(slots[order], start, size))
+        s = flat_dot(q_ref[slots[order]], keys(order, start, size))
         return s + jnp.concatenate([bias] * heads, axis=0)
 
     def highest(scores):
@@ -142,7 +153,7 @@
     extend(LO, top)
 
     def score(start, size):
-        return score_dot(qx_ref[HI], with_ones(keys(slots[LO], start, size)))
+        return flat_dot(qx_ref[HI], over_ones(keys(LO, start, size)))
 
     def finish(p, start, size):
         acc_ref[HI] += value_dot(p, values(slots[LO], start, size))
@@ -151,28 +162,29 @@
     in_turn(coef, tiles, score, finish)
 
 
-def place_pieces(parts, own_half, k_buf, v_buf):
+def place_pieces(parts, k_buf, v_buf, turned):
     inner = lax.axis_index("inner")
+    own_half = lax.rem(lax.axis_index("head"), 2)
     for value, (own_buf, twin_buf) in enumerate([(k_buf, v_buf), (v_buf, k_buf)]):
 
         @pl.when(inner == value)
         def _():
-            for turn, pair in enumerate(parts):
+            for turn in range(2):
                 half = own_half if turn == 0 else 1 - own_half
-                for piece, buf in zip(pair, (own_buf, twin_buf)):
+                for piece, buf in zip(parts[2 * turn : 2 * turn + 2], (own_buf, twin_buf)):
                     size = piece.shape[1]
                     for slot in range(2):
-                        start = pl.multiple_of((slot * len(parts) + half) * size, size)
-                        buf[pl.ds(start, size)] = piece[slot]
+                        buf[pl.ds(pl.multiple_of((slot * 2 + half) * size, size), size)] = piece[slot]
+
+    turned[...] = jnp.transpose(k_buf[...])
 
 
 def visit(coef, distance, parts, sb, qx_ref, acc_ref, buffers, group, store):
     all_rows = qx_ref.shape[1]
     count = lax.axis_size("seq")
     me = lax.axis_index("seq")
-    k_buf, v_buf = buffers[:2] if len(parts) == 2 else buffers[2:]
-    own_half = lax.rem(lax.axis_index("head"), 2) if len(parts) == 2 else 0
-    place_pieces(parts, own_half, k_buf, v_buf)
+    k_buf, v_buf, turned = buffers
+    place_pieces(parts, k_buf, v_buf, turned)
     keys_here = k_buf.shape[0] // 2
 
     _, _, top_block = blocks_of(sb, me)
@@ -183,14 +195,19 @@
         tiles = key_tiles(key_count)
         totals = {}
 
-        def chosen(buf, start, size):
-            return with_ones(buf[pl.ds(first_key + start, size)])
+        def keys(start, size):
+            at = first_key + start
+            at = at if isinstance(at, int) else pl.multiple_of(at, 128)
+            return over_ones(turned[:, pl.ds(at, size)])
+
+        def values(start, size):
+            return with_ones(v_buf[pl.ds(first_key + start, size)])
 
         def score(order, row, start, size):
-            return score_dot(qx_ref[order, pl.ds(row, group)], chosen(k_buf, start, size))
+            return flat_dot(qx_ref[order, pl.ds(row, group)], keys(start, size))
 
         def finish(p, order, row, start, size):
-            part = value_dot(p, chosen(v_buf, start, size))
+            part = value_dot(p, values(start, size))
             before = acc_ref[order, pl.ds(row, group)] if start == 0 else totals[order, row]
             totals[order, row] = before + part
             if start == tiles[-1][0]:
@@ -215,18 +232,15 @@
 
 
 def middle_kernel(coef, visits, rows, sb, qx_ref, acc_in, *refs):
-    taken = []
-    for distance, pairs in visits:
-        taken.append((distance, [refs[2 * i : 2 * i + 2] for i in range(pairs)]))
-        refs = refs[2 * pairs :]
-    acc_ref, tops, buffers = refs[0], refs[1:-4], refs[-4:]
+    pieces, (acc_ref, *tops), buffers = refs[: 4 * len(visits)], refs[4 * len(visits) : -3], refs[-3:]
     _, all_rows, double = qx_ref.shape
 
     def store(order, row, value):
         if value is not None:
             acc_ref[order, pl.ds(row, all_rows)] = value
 
-    for distance, parts in taken:
+    for place, distance in enumerate(visits):
+        parts = pieces[4 * place : 4 * place + 4]
         visit(coef, distance, parts, sb, qx_ref, acc_ref, buffers, all_rows, store)
     for top_ref in tops:
         for order in (LO, HI):
@@ -237,12 +251,12 @@
 
 
 def last_kernel(coef, distances, sb, qx_ref, acc_ref, top_ref, *refs):
-    parts, every, rest = [refs[:2]], refs[2 : 4 * len(distances) + 4], refs[4 * len(distances) + 4 :]
+    parts, every, rest = refs[:4], refs[4 : 4 * len(distances) + 6], refs[4 * len(distances) + 6 :]
     out_hbm, lse_hbm, out_buf, lse_ref, *buffers, worst, run_top, run_acc, sem, out_sems = rest
     rows = out_buf.shape[1]
     all_rows = qx_ref.shape[1]
     heads = all_rows // rows
-    k_buf, v_buf = buffers[:2]
+    k_buf, v_buf, _ = buffers
     block_len, width = k_buf.shape[0] // 2, k_buf.shape[1]
     half_len = block_len // 2
     count = lax.axis_size("seq")
@@ -407,24 +421,25 @@
         out_specs=[whole] * 2,
         out_shape=[qx_shape, acc_shape],
         cost_estimate=cost(3, 6_000_000),
+        scratch_shapes=[pltpu.VMEM((2, width, block_len), key_rows.dtype)],
         compiler_params=params,
         name="local_part",
     )(sb_here, q_here, k_here, v_here)
     kv_buffers = [pltpu.VMEM((2 * block_len, width), jnp.bfloat16)] * 2
-    kv_buffers += [pltpu.VMEM((block_len, width), jnp.bfloat16)] * 2
+    kv_buffers += [pltpu.VMEM((width, 2 * block_len), jnp.bfloat16)]
 
     def attend(acc, visits, with_tops):
-        pieces = [part for _, pairs in visits for pair in pairs for part in pair]
+        pieces = [part[d] for d in visits for part in (arrived, beside, across, beside_across)]
         return pl.pallas_call(
-            functools.partial(middle_kernel, coef, [(distance, len(pairs)) for distance, pairs in visits], rows),
+            functools.partial(middle_kernel, coef, visits, rows),
             in_specs=[scalars] + [whole] * (2 + len(pieces)),
             out_specs=[whole] * (1 + with_tops),
             out_shape=[acc_shape] + [top_shape] * with_tops,
             scratch_shapes=kv_buffers,
             input_output_aliases={2: 0},
-            cost_estimate=cost(len(pieces) / 2, 7_000_000),
+            cost_estimate=cost(2 * len(visits), 7_000_000),
             compiler_params=params,
-            name=f"visitors_from_{visits[0][0]}",
+            name=f"visitors_from_{visits[0]}",
         )(sb_here, qx, acc, *pieces)
 
     def relay(distance):
@@ -437,39 +452,30 @@
             across[distance] = along_head(arrived[distance])
             beside[distance] = along_inner(arrived[distance])
 
-    def own_pair(distance):
-        return arrived[distance], beside[distance]
-
-    def far_pair(distance):
-        beside_across[distance] = along_inner(across[distance])
-        return across[distance], beside_across[distance]
-
     last = distances[-1]
+    groups = [distances[:2]] + [[d] for d in distances[2:-1]] if count > 3 else [[d] for d in distances[:-1]]
     first, acc = lax.optimization_barrier((dict(arrived), acc))
     arrived.update(first)
-    spread(1)
-    relay(3)
-    spread(2)
-    for distance in distances[:-1]:
-        ahead = distance + 2
-        tied = lax.optimization_barrier((across[distance], arrived.get(ahead), acc))
-        across[distance], arrived_ahead, acc = tied
-        if ahead in distances:
-            arrived[ahead] = arrived_ahead
-        visits = [(distance, [own_pair(distance), far_pair(distance)])]
-        if distance + 1 == last:
-            visits.append((last, [own_pair(last)]))
-        acc, *tops = attend(acc, visits, int(distance + 1 == last))
-        relay(ahead + 1)
+    tops = []
+    for distance in groups[0]:
+        spread(distance)
+    for visits in groups:
+        ahead = visits[-1] + 1
+        relay(ahead)
+        tied = lax.optimization_barrier(([across[d] for d in visits], arrived[ahead], acc))
+        sides, arrived[ahead], acc = tied
+        across.update(zip(visits, sides))
         spread(ahead)
+        for distance in visits:
+            beside_across[distance] = along_inner(across[distance])
+        acc, *tops = attend(acc, visits, int(ahead == last))
     across[last], acc = lax.optimization_barrier((across[last], acc))
-    far_pair(last)
-
-    pairs = [(arrived[d], beside[d], across[d], beside_across[d]) for d in distances]
-    flat = [part for pair in pairs for part in pair]
+    beside_across[last] = along_inner(across[last])
+
+    flat = [part[d] for d in distances for part in (arrived, beside, across, beside_across)]
     attended, log_total = pl.pallas_call(
         functools.partial(last_kernel, coef, distances),
-        in_specs=[scalars] + [whole] * 5 + [anywhere] * (2 + len(flat)),
+        in_specs=[scalars] + [whole] * 7 + [anywhere] * (2 + len(flat)),
         out_specs=[anywhere, anywhere],
         out_shape=[jax.ShapeDtypeStruct(query_rows.shape, query_rows.dtype), top_shape],
         scratch_shapes=[
@@ -487,7 +493,7 @@
         cost_estimate=cost(1, 7_000_000),
         compiler_params=params,
         name="last_visitor",
-    )(sb_here, qx, acc, *tops, *flat[-2:], in_hbm[1], in_hbm[2], *flat)
+    )(sb_here, qx, acc, *tops, *flat[-4:], in_hbm[1], in_hbm[2], *flat)
     return attended, log_total
 
 

time: 39.2 us -> 36.8 us (0.939)
  Pallas kernels: 17.6 us -> 16 us
  waiting for transfers between devices: 10.5 us -> 9.69 us
    pallas_call x2 -> x1, Pallas kernels: 8.15 us -> 5.69 us  [attend(): pl.pallas_call(functools.partial(middle_kernel, coef, visits, rows), in_s...]
    ppermute x3, starting transfers between devices: 7.11 us -> 6.13 us  [along_seq(): return lax.ppermute(block, 'seq', route)]
    ppermute x6, waiting for transfers between devices: 2.56 us -> 1.7 us  [along_inner(): return lax.ppermute(block, 'inner', [(0, 1), (1, 0)])]
    pallas_call x1, Pallas kernels: 3.38 us -> 4.18 us  [body(): pl.pallas_call(functools.partial(last_kernel, coef, distances), in_specs=...]
    ppermute x6, starting transfers between devices: 0.65 us -> 1.36 us  [along_inner(): return lax.ppermute(block, 'inner', [(0, 1), (1, 0)])]
  transfers between devices with their start and end apart: 12 -> 12, of which waited for: 9 -> 8; matrix products, arithmetic and copies ran while one was open for 0% -> 0% of each run, Pallas kernels for 32% -> 28%
where the time goes in v2:
time: 36.8 us; the launch traced here: 36.6 us
  Pallas kernels  16 us (43%)
  starting transfers between devices  10 us (27%)
  waiting for transfers between devices  9.69 us (26%)
  between operations  0.82 us (2%)
    ppermute x3, starting transfers between devices, along_seq(): return lax.ppermute(block, 'seq', route)  6.13 us
    pallas_call x1, Pallas kernels, attend(): pl.pallas_call(functools.partial(middle_kernel, coef, visits, rows), in_s...  5.69 us
    ppermute x3, waiting for transfers between devices, along_head(): lax.ppermute(block, 'head', [(i, i ^ 1) for i in range(lax.axis_size('hea...  4.75 us
    pallas_call x1, Pallas kernels, body(): pl.pallas_call(functools.partial(local_kernel, coef, rows), in_specs=[sca...  4.69 us
    pallas_call x1, Pallas kernels, body(): pl.pallas_call(functools.partial(last_kernel, coef, distances), in_specs=...  4.18 us
    ppermute x3, waiting for transfers between devices, along_seq(): return lax.ppermute(block, 'seq', route)  3.25 us
    ppermute x3, starting transfers between devices, along_head(): lax.ppermute(block, 'head', [(i, i ^ 1) for i in range(lax.axis_size('hea...  2.56 us
    ppermute x6, waiting for transfers between devices, along_inner(): return lax.ppermute(block, 'inner', [(0, 1), (1, 0)])  1.7 us
  transfers between devices with their start and end apart: 12, of which 8 were waited for; matrix products, arithmetic and copies ran while one was open for 0% of the time, Pallas kernels for 28%

profile of v2, /device:TPU:0, one launch (start us, length us, event | category | flops | bytes accessed | tf_op | source)
XLA Modules:
  0.0 36.6 jit_solution(13479256632461354731)
XLA Ops:
  0.6 1.5 %load.1 = (bf16[2,320,128]{2,1,0:T(8,128)(2,1)S(1)}, bf16[2,1280,128]{2,1,0:T(8,128)(2,1)S(1)}, bf16[2,640,128]{2,1,0:T(8,128)(2,1)S(1)}, bf16[2,640,128]{2,1,0:T(8,128)(2,1)S(1)}, s32[8]{0:T(128)S(1)}) custom-call(bf16[2,320,512]{2,1,0:T(8,128)(2,1)} %q_hbm.1, bf16[2,640,128]{2,1,0:T(8,128)(2,1)} %refs_4_.1, bf16[2,640,128]{2,1,0:T(8,128)(2,1)} %refs_5_.1, ...), custom_call_target="tpu_custom_call" | custom-call | bytes 3000000 | tf_op jit(solution)/shard_map/load/pallas_call | solution.py:402
  2.1 3.1 %collective-permute-start = (bf16[2,320,128]{2,1,0:T(8,128)(2,1)S(1)}, bf16[2,320,128]{2,1,0:T(8,128)(2,1)S(1)}, u32[]{:S(2)}, u32[]{:S(2)}) collective-permute-start(bf16[2,320,128]{2,1,0:T(8,128)(2,1)S(1)} %get-tuple-element.25), channel_id=1, source_target_pairs={{0,4},{4,0},{8,12},{12,8},{1,5},{5,1},{9,13},{13,9},{2,6},{6,2},{1... | collective-permute-start | bytes 491528 | tf_op jit(solution)/shard_map/along_seq/ppermute | solution.py:375
  5.2 2.6 %collective-permute-start.1 = (bf16[2,320,128]{2,1,0:T(8,128)(2,1)S(1)}, bf16[2,320,128]{2,1,0:T(8,128)(2,1)S(1)}, u32[]{:S(2)}, u32[]{:S(2)}) collective-permute-start(bf16[2,320,128]{2,1,0:T(8,128)(2,1)S(1)} %get-tuple-element.25), channel_id=1, source_target_pairs={{0,8},{4,12},{8,0},{12,4},{1,9},{5,13},{9,1},{13,5},{2,10},{6,14},... | collective-permute-start | bytes 491528 | tf_op jit(solution)/shard_map/along_seq/ppermute | solution.py:375
  7.8 4.7 %local_part.1 = (bf16[2,1280,256]{2,1,0:T(8,128)(2,1)S(1)}, f32[2,1280,256]{2,1,0:T(8,128)S(1)}) custom-call(s32[8]{0:T(128)S(1)} %get-tuple-element.20.sb, bf16[2,1280,128]{2,1,0:T(8,128)(2,1)S(1)} %get-tuple-element.21.q_ref, bf16[2,640,128]{2,1,0:T(8,128)(2,1)S(1)} %get-tuple-element.22.k_ref, bf16[2,640,128]{2,1,0:T(8,128)(2,1)S(1)} %get-tuple-element.23.v_ref), custom_call_target="tpu_custom_call" | custom-call | flops 2516582400 | bytes 6000000 | tf_op jit(solution)/shard_map/local_part/pallas_call | solution.py:418
  12.5 0.2 collective-permute-done.refs_0_.refs_6_
  12.7 2.7 %collective-permute-done.1.refs_4_.refs_10_ = bf16[2,320,128]{2,1,0:T(8,128)(2,1)S(1)} collective-permute-done((bf16[2,320,128]{2,1,0:T(8,128)(2,1)S(1)}, bf16[2,320,128]{2,1,0:T(8,128)(2,1)S(1)}, u32[]{:S(2)}, u32[]{:S(2)}) %collective-permute-start.1) | collective-permute-done | bytes 163872 | tf_op jit(solution)/shard_map/along_seq/ppermute | solution.py:375
  15.3 1.5 %collective-permute-start.3 = (bf16[2,320,128]{2,1,0:T(8,128)(2,1)S(1)}, bf16[2,320,128]{2,1,0:T(8,128)(2,1)S(1)}, u32[]{:S(2)}, u32[]{:S(2)}) collective-permute-start(bf16[2,320,128]{2,1,0:T(8,128)(2,1)S(1)} %collective-permute-done.1.refs_4_.refs_10_), channel_id=1, source_target_pairs={{0,2},{2,0},{1,3},{3,1},{4,6},{6,4},{5,7},{7,5},{8,10},{10,8},{9,1... | collective-permute-start | bytes 491528 | tf_op jit(solution)/shard_map/along_head/ppermute | solution.py:379
  16.8 0.4 %collective-permute-start.4 = (bf16[2,320,128]{2,1,0:T(8,128)(2,1)S(1)}, bf16[2,320,128]{2,1,0:T(8,128)(2,1)S(1)}, u32[]{:S(2)}, u32[]{:S(2)}) collective-permute-start(bf16[2,320,128]{2,1,0:T(8,128)(2,1)S(1)} %collective-permute-done.1.refs_4_.refs_10_), channel_id=1, source_target_pairs={{0,4},{4,0},{8,12},{12,8},{1,5},{5,1},{9,13},{13,9},{2,6},{6,2},{1... | collective-permute-start | bytes 491528 | tf_op jit(solution)/shard_map/along_seq/ppermute | solution.py:375
  17.3 0.5 %collective-permute-start.2 = (bf16[2,320,128]{2,1,0:T(8,128)(2,1)S(1)}, bf16[2,320,128]{2,1,0:T(8,128)(2,1)S(1)}, u32[]{:S(2)}, u32[]{:S(2)}) collective-permute-start(bf16[2,320,128]{2,1,0:T(8,128)(2,1)S(1)} %collective-permute-done.refs_0_.refs_6_), channel_id=1, source_target_pairs={{0,2},{2,0},{1,3},{3,1},{4,6},{6,4},{5,7},{7,5},{8,10},{10,8},{9,1... | collective-permute-start | bytes 491528 | tf_op jit(solution)/shard_map/along_head/ppermute | solution.py:379
  17.8 0.0 collective-permute-start.8
  17.8 0.5 %collective-permute-start.6 = (bf16[2,320,128]{2,1,0:T(8,128)(2,1)S(1)}, bf16[2,320,128]{2,1,0:T(8,128)(2,1)S(1)}, u32[]{:S(2)}, u32[]{:S(2)}) collective-permute-start(bf16[2,320,128]{2,1,0:T(8,128)(2,1)S(1)} %collective-permute-done.refs_0_.refs_6_), channel_id=1, source_target_pairs={{0,1},{1,0},{2,3},{3,2},{4,5},{5,4},{6,7},{7,6},{8,9},{9,8},{10,11... | collective-permute-start | bytes 491528 | tf_op jit(solution)/shard_map/along_inner/ppermute | solution.py:383
  18.3 3.4 %collective-permute-done.3.refs_6_.refs_12_ = bf16[2,320,128]{2,1,0:T(8,128)(2,1)S(1)} collective-permute-done((bf16[2,320,128]{2,1,0:T(8,128)(2,1)S(1)}, bf16[2,320,128]{2,1,0:T(8,128)(2,1)S(1)}, u32[]{:S(2)}, u32[]{:S(2)}) %collective-permute-start.3) | collective-permute-done | bytes 163872 | tf_op jit(solution)/shard_map/along_head/ppermute | solution.py:379
  21.7 0.4 %collective-permute-done.4.refs_0_.refs_14_ = bf16[2,320,128]{2,1,0:T(8,128)(2,1)S(1)} collective-permute-done((bf16[2,320,128]{2,1,0:T(8,128)(2,1)S(1)}, bf16[2,320,128]{2,1,0:T(8,128)(2,1)S(1)}, u32[]{:S(2)}, u32[]{:S(2)}) %collective-permute-start.4) | collective-permute-done | bytes 163872 | tf_op jit(solution)/shard_map/along_seq/ppermute | solution.py:375
  22.1 1.3 %collective-permute-done.2.refs_2_.refs_8_ = bf16[2,320,128]{2,1,0:T(8,128)(2,1)S(1)} collective-permute-done((bf16[2,320,128]{2,1,0:T(8,128)(2,1)S(1)}, bf16[2,320,128]{2,1,0:T(8,128)(2,1)S(1)}, u32[]{:S(2)}, u32[]{:S(2)}) %collective-permute-start.2) | collective-permute-done | bytes 163872 | tf_op jit(solution)/shard_map/along_head/ppermute | solution.py:379
  23.5 0.0 collective-permute-start.7
  23.5 0.5 %collective-permute-start.9 = (bf16[2,320,128]{2,1,0:T(8,128)(2,1)S(1)}, bf16[2,320,128]{2,1,0:T(8,128)(2,1)S(1)}, u32[]{:S(2)}, u32[]{:S(2)}) collective-permute-start(bf16[2,320,128]{2,1,0:T(8,128)(2,1)S(1)} %collective-permute-done.3.refs_6_.refs_12_), channel_id=1, source_target_pairs={{0,1},{1,0},{2,3},{3,2},{4,5},{5,4},{6,7},{7,6},{8,9},{9,8},{10,11... | collective-permute-start | bytes 491528 | tf_op jit(solution)/shard_map/along_inner/ppermute | solution.py:383
  24.0 0.5 %collective-permute-start.5 = (bf16[2,320,128]{2,1,0:T(8,128)(2,1)S(1)}, bf16[2,320,128]{2,1,0:T(8,128)(2,1)S(1)}, u32[]{:S(2)}, u32[]{:S(2)}) collective-permute-start(bf16[2,320,128]{2,1,0:T(8,128)(2,1)S(1)} %collective-permute-done.4.refs_0_.refs_14_), channel_id=1, source_target_pairs={{0,2},{2,0},{1,3},{3,1},{4,6},{6,4},{5,7},{7,5},{8,10},{10,8},{9,1... | collective-permute-start | bytes 491528 | tf_op jit(solution)/shard_map/along_head/ppermute | solution.py:379
  24.5 0.0 collective-permute-done.8.refs_5_.refs_11_
  24.5 0.0 collective-permute-start.10
  24.5 0.0 collective-permute-done.6.refs_1_.refs_7_
  24.5 0.3 collective-permute-done.7.refs_3_.refs_9_
  24.9 0.2 collective-permute-done.9.refs_7_.refs_13_
  25.1 5.7 %visitors_from_1.1 = (f32[2,1280,256]{2,1,0:T(8,128)S(1)}, f32[2,4,320]{2,1,0:T(4,128)S(1)}) custom-call(s32[8]{0:T(128)S(1)} %get-tuple-element.20.sb, bf16[2,1280,256]{2,1,0:T(8,128)(2,1)S(1)} %get-tuple-element.24.qx_ref, f32[2,1280,256]{2,1,0:T(8,128)S(1)} %get-tuple-element.31.acc_in, ...), custom_call_target="tpu_custom_call", output_to_operand_aliasing={{0}: (2, {})} | custom-call | flops 3355443200 | bytes 7000000 | tf_op jit(solution)/shard_map/visitors_from_1/pallas_call | solution.py:433
  30.8 0.0 collective-permute-done.5.refs_2_.refs_16_
  30.8 0.3 collective-permute-start.11
  31.1 0.0 collective-permute-done.10.refs_1_.refs_15_
  31.1 1.1 %collective-permute-done.11.refs_3_.refs_17_ = bf16[2,320,128]{2,1,0:T(8,128)(2,1)S(1)} collective-permute-done((bf16[2,320,128]{2,1,0:T(8,128)(2,1)S(1)}, bf16[2,320,128]{2,1,0:T(8,128)(2,1)S(1)}, u32[]{:S(2)}, u32[]{:S(2)}) %collective-permute-start.11) | collective-permute-done | bytes 163872 | tf_op jit(solution)/shard_map/along_inner/ppermute | solution.py:383
  32.3 4.2 %last_visitor.1 = (bf16[2,320,512]{2,1,0:T(8,128)(2,1)}, f32[2,4,320]{2,1,0:T(4,128)}) custom-call(s32[8]{0:T(128)S(1)} %get-tuple-element.20.sb, bf16[2,1280,256]{2,1,0:T(8,128)(2,1)S(1)} %get-tuple-element.24.qx_ref, f32[2,1280,256]{2,1,0:T(8,128)S(1)} %get-tuple-element.35.acc_ref, f32[2,4,320]{2,1,0:T(4,128)S(1)} %get-tuple-element.36.top_ref, ...), custom_call_target="tpu_custom_call" | custom-call | flops 838860800 | bytes 7000000 | tf_op jit(solution)/shard_map/last_visitor/pallas_call | solution.py:476
Async XLA Ops:
  2.1 10.5 %collective-permute-start = (bf16[2,320,128]{2,1,0:T(8,128)(2,1)S(1)}, bf16[2,320,128]{2,1,0:T(8,128)(2,1)S(1)}, u32[]{:S(2)}, u32[]{:S(2)}) collective-permute-start(bf16[2,320,128]{2,1,0:T(8,128)(2,1)S(1)} %get-tuple-element.25), channel_id=1, source_target_pairs={{0,4},{4,0},{8,12},{12,8},{1,5},{5,1},{9,13},{13,9},{2,6},{6,2},{1... | collective-permute-start | bytes 491528 | tf_op jit(solution)/shard_map/along_seq/ppermute | solution.py:375
  5.2 10.1 %collective-permute-start.1 = (bf16[2,320,128]{2,1,0:T(8,128)(2,1)S(1)}, bf16[2,320,128]{2,1,0:T(8,128)(2,1)S(1)}, u32[]{:S(2)}, u32[]{:S(2)}) collective-permute-start(bf16[2,320,128]{2,1,0:T(8,128)(2,1)S(1)} %get-tuple-element.25), channel_id=1, source_target_pairs={{0,8},{4,12},{8,0},{12,4},{1,9},{5,13},{9,1},{13,5},{2,10},{6,14},... | collective-permute-start | bytes 491528 | tf_op jit(solution)/shard_map/along_seq/ppermute | solution.py:375
  15.3 6.4 %collective-permute-start.3 = (bf16[2,320,128]{2,1,0:T(8,128)(2,1)S(1)}, bf16[2,320,128]{2,1,0:T(8,128)(2,1)S(1)}, u32[]{:S(2)}, u32[]{:S(2)}) collective-permute-start(bf16[2,320,128]{2,1,0:T(8,128)(2,1)S(1)} %collective-permute-done.1.refs_4_.refs_10_), channel_id=1, source_target_pairs={{0,2},{2,0},{1,3},{3,1},{4,6},{6,4},{5,7},{7,5},{8,10},{10,8},{9,1... | collective-permute-start | bytes 491528 | tf_op jit(solution)/shard_map/along_head/ppermute | solution.py:379
  16.8 5.3 %collective-permute-start.4 = (bf16[2,320,128]{2,1,0:T(8,128)(2,1)S(1)}, bf16[2,320,128]{2,1,0:T(8,128)(2,1)S(1)}, u32[]{:S(2)}, u32[]{:S(2)}) collective-permute-start(bf16[2,320,128]{2,1,0:T(8,128)(2,1)S(1)} %collective-permute-done.1.refs_4_.refs_10_), channel_id=1, source_target_pairs={{0,4},{4,0},{8,12},{12,8},{1,5},{5,1},{9,13},{13,9},{2,6},{6,2},{1... | collective-permute-start | bytes 491528 | tf_op jit(solution)/shard_map/along_seq/ppermute | solution.py:375
  17.3 6.2 %collective-permute-start.2 = (bf16[2,320,128]{2,1,0:T(8,128)(2,1)S(1)}, bf16[2,320,128]{2,1,0:T(8,128)(2,1)S(1)}, u32[]{:S(2)}, u32[]{:S(2)}) collective-permute-start(bf16[2,320,128]{2,1,0:T(8,128)(2,1)S(1)} %collective-permute-done.refs_0_.refs_6_), channel_id=1, source_target_pairs={{0,2},{2,0},{1,3},{3,1},{4,6},{6,4},{5,7},{7,5},{8,10},{10,8},{9,1... | collective-permute-start | bytes 491528 | tf_op jit(solution)/shard_map/along_head/ppermute | solution.py:379
  17.8 6.7 %collective-permute-start.8 = (bf16[2,320,128]{2,1,0:T(8,128)(2,1)S(1)}, bf16[2,320,128]{2,1,0:T(8,128)(2,1)S(1)}, u32[]{:S(2)}, u32[]{:S(2)}) collective-permute-start(bf16[2,320,128]{2,1,0:T(8,128)(2,1)S(1)} %collective-permute-done.1.refs_4_.refs_10_), channel_id=1, source_target_pairs={{0,1},{1,0},{2,3},{3,2},{4,5},{5,4},{6,7},{7,6},{8,9},{9,8},{10,11... | collective-permute-start | bytes 491528 | tf_op jit(solution)/shard_map/along_inner/ppermute | solution.py:383
  17.8 6.7 %collective-permute-start.6 = (bf16[2,320,128]{2,1,0:T(8,128)(2,1)S(1)}, bf16[2,320,128]{2,1,0:T(8,128)(2,1)S(1)}, u32[]{:S(2)}, u32[]{:S(2)}) collective-permute-start(bf16[2,320,128]{2,1,0:T(8,128)(2,1)S(1)} %collective-permute-done.refs_0_.refs_6_), channel_id=1, source_target_pairs={{0,1},{1,0},{2,3},{3,2},{4,5},{5,4},{6,7},{7,6},{8,9},{9,8},{10,11... | collective-permute-start | bytes 491528 | tf_op jit(solution)/shard_map/along_inner/ppermute | solution.py:383
  23.5 1.4 %collective-permute-start.7 = (bf16[2,320,128]{2,1,0:T(8,128)(2,1)S(1)}, bf16[2,320,128]{2,1,0:T(8,128)(2,1)S(1)}, u32[]{:S(2)}, u32[]{:S(2)}) collective-permute-start(bf16[2,320,128]{2,1,0:T(8,128)(2,1)S(1)} %collective-permute-done.2.refs_2_.refs_8_), channel_id=1, source_target_pairs={{0,1},{1,0},{2,3},{3,2},{4,5},{5,4},{6,7},{7,6},{8,9},{9,8},{10,11... | collective-permute-start | bytes 491528 | tf_op jit(solution)/shard_map/along_inner/ppermute | solution.py:383
  23.5 1.6 %collective-permute-start.9 = (bf16[2,320,128]{2,1,0:T(8,128)(2,1)S(1)}, bf16[2,320,128]{2,1,0:T(8,128)(2,1)S(1)}, u32[]{:S(2)}, u32[]{:S(2)}) collective-permute-start(bf16[2,320,128]{2,1,0:T(8,128)(2,1)S(1)} %collective-permute-done.3.refs_6_.refs_12_), channel_id=1, source_target_pairs={{0,1},{1,0},{2,3},{3,2},{4,5},{5,4},{6,7},{7,6},{8,9},{9,8},{10,11... | collective-permute-start | bytes 491528 | tf_op jit(solution)/shard_map/along_inner/ppermute | solution.py:383
  24.0 6.8 %collective-permute-start.5 = (bf16[2,320,128]{2,1,0:T(8,128)(2,1)S(1)}, bf16[2,320,128]{2,1,0:T(8,128)(2,1)S(1)}, u32[]{:S(2)}, u32[]{:S(2)}) collective-permute-start(bf16[2,320,128]{2,1,0:T(8,128)(2,1)S(1)} %collective-permute-done.4.refs_0_.refs_14_), channel_id=1, source_target_pairs={{0,2},{2,0},{1,3},{3,1},{4,6},{6,4},{5,7},{7,5},{8,10},{10,8},{9,1... | collective-permute-start | bytes 491528 | tf_op jit(solution)/shard_map/along_head/ppermute | solution.py:379
  24.5 6.6 %collective-permute-start.10 = (bf16[2,320,128]{2,1,0:T(8,128)(2,1)S(1)}, bf16[2,320,128]{2,1,0:T(8,128)(2,1)S(1)}, u32[]{:S(2)}, u32[]{:S(2)}) collective-permute-start(bf16[2,320,128]{2,1,0:T(8,128)(2,1)S(1)} %collective-permute-done.4.refs_0_.refs_14_), channel_id=1, source_target_pairs={{0,1},{1,0},{2,3},{3,2},{4,5},{5,4},{6,7},{7,6},{8,9},{9,8},{10,11... | collective-permute-start | bytes 491528 | tf_op jit(solution)/shard_map/along_inner/ppermute | solution.py:383
  30.8 1.5 %collective-permute-start.11 = (bf16[2,320,128]{2,1,0:T(8,128)(2,1)S(1)}, bf16[2,320,128]{2,1,0:T(8,128)(2,1)S(1)}, u32[]{:S(2)}, u32[]{:S(2)}) collective-permute-start(bf16[2,320,128]{2,1,0:T(8,128)(2,1)S(1)} %collective-permute-done.5.refs_2_.refs_16_), channel_id=1, source_target_pairs={{0,1},{1,0},{2,3},{3,2},{4,5},{5,4},{6,7},{7,6},{8,9},{9,8},{10,11... | collective-permute-start | bytes 491528 | tf_op jit(solution)/shard_map/along_inner/ppermute | solution.py:383

commit v3 on v2

--- a/solution.py
+++ b/solution.py
@@ -30,14 +30,6 @@
     return jnp.concatenate([x] * (width // x.shape[1]), axis=1)
 
 
-def with_ones(x):
-    return jnp.concatenate([x, jnp.ones_like(x)], axis=1)
-
-
-def over_ones(x):
-    return jnp.concatenate([x, jnp.ones_like(x)], axis=0)
-
-
 def is_power(count):
     return count & (count - 1) == 0
 
@@ -51,17 +43,6 @@
 def blocks_of(sb, seq_index):
     b0, b1 = sb[2 * seq_index], sb[2 * seq_index + 1]
     return jnp.where(b1 > b0, 1, 0), jnp.minimum(b0, b1), jnp.maximum(b0, b1)
-
-
-def minus_columns(top):
-    high = top.astype(jnp.bfloat16)
-    rest = top - high.astype(jnp.float32)
-    middle = rest.astype(jnp.bfloat16)
-    low = (rest - middle.astype(jnp.float32)).astype(jnp.bfloat16)
-    lane = lax.broadcasted_iota(jnp.int32, top.shape, 1)
-    high, middle, low = (x.astype(jnp.float32) for x in (high, middle, low))
-    picked = jnp.where(lane == 0, high, jnp.where(lane == 1, middle, jnp.where(lane == 2, low, 0.0)))
-    return (-picked).astype(jnp.bfloat16)
 
 
 def key_tiles(count):
@@ -91,20 +72,26 @@
         copy.wait()
 
 
-def scaled_exp(coef, s):
-    return jnp.exp2(s * coef).astype(jnp.bfloat16)
-
-
-def in_turn(coef, chunks, score, finish):
+def weights_of(coef, s, top):
+    p = jnp.exp2((s - widen(top, s.shape[1])) * coef)
+    sums = functools.reduce(jnp.add, [p[:, at : at + 128] for at in range(0, p.shape[1], 128)])
+    return p.astype(jnp.bfloat16), sums
+
+
+def with_sums(p, sums, v):
+    return jnp.concatenate([value_dot(p, v), sums], axis=1)
+
+
+def in_turn(chunks, score, finish):
     ready = score(*chunks[0])
     for place, chunk in enumerate(chunks):
         now = ready
         if place + 1 < len(chunks):
             ready = score(*chunks[place + 1])
-        finish(scaled_exp(coef, now), *chunk)
-
-
-def local_kernel(coef, rows, sb, q_ref, k_ref, v_ref, qx_ref, acc_ref, turned):
+        finish(now, *chunk)
+
+
+def local_kernel(coef, rows, sb, q_ref, k_ref, v_ref, top_ref, acc_ref, turned):
     _, all_rows, width = q_ref.shape
     block_len = k_ref.shape[1]
     heads = all_rows // rows
@@ -119,7 +106,7 @@
         return turned[order, :, start : start + size]
 
     def values(slot, start, size):
-        return with_ones(v_ref[slot, pl.ds(start, size)])
+        return v_ref[slot, pl.ds(start, size)]
 
     def masked(order, start, size):
         row = lax.broadcasted_iota(jnp.int32, (rows, size), 0) + lax.axis_index("inner") * rows
@@ -136,30 +123,26 @@
     def settle(order, scores, top):
         total = None
         for (start, size), s in zip(tiles, scores):
-            p = scaled_exp(coef, s - widen(top, size))
-            part = value_dot(p, values(slots[order], start, size))
+            part = with_sums(*weights_of(coef, s, top), values(slots[order], start, size))
             total = part if total is None else total + part
         acc_ref[order] = total
 
-    def extend(order, top):
-        qx_ref[order] = jnp.concatenate([q_ref[slots[order]], minus_columns(top)], axis=1)
-
     diag = [masked(HI, *tile) for tile in tiles]
     top = highest(diag)
-    extend(HI, top)
+    top_ref[HI] = top
     low = [masked(LO, *tile) for tile in tiles]
     settle(HI, diag, top)
     top = highest(low)
-    extend(LO, top)
+    top_ref[LO] = top
 
     def score(start, size):
-        return flat_dot(qx_ref[HI], over_ones(keys(LO, start, size)))
-
-    def finish(p, start, size):
-        acc_ref[HI] += value_dot(p, values(slots[LO], start, size))
+        return flat_dot(q_ref[slots[HI]], keys(LO, start, size))
+
+    def finish(s, start, size):
+        acc_ref[HI] += with_sums(*weights_of(coef, s, top_ref[HI]), values(slots[LO], start, size))
 
     settle(LO, low, top)
-    in_turn(coef, tiles, score, finish)
+    in_turn(tiles, score, finish)
 
 
 def place_pieces(parts, k_buf, v_buf, turned):
@@ -179,15 +162,16 @@
     turned[...] = jnp.transpose(k_buf[...])
 
 
-def visit(coef, distance, parts, sb, qx_ref, acc_ref, buffers, group, store):
-    all_rows = qx_ref.shape[1]
+def visit(coef, distance, parts, sb, q_ref, top_ref, acc_ref, buffers, group, store):
+    all_rows = q_ref.shape[1]
     count = lax.axis_size("seq")
     me = lax.axis_index("seq")
     k_buf, v_buf, turned = buffers
     place_pieces(parts, k_buf, v_buf, turned)
     keys_here = k_buf.shape[0] // 2
 
-    _, _, top_block = blocks_of(sb, me)
+    hi, _, top_block = blocks_of(sb, me)
+    slots = {HI: hi, LO: 1 - hi}
     other_hi, _, other_top = blocks_of(sb, source_of(me, distance, count))
     above = top_block > other_top
 
@@ -198,23 +182,24 @@
         def keys(start, size):
             at = first_key + start
             at = at if isinstance(at, int) else pl.multiple_of(at, 128)
-            return over_ones(turned[:, pl.ds(at, size)])
+            return turned[:, pl.ds(at, size)]
 
         def values(start, size):
-            return with_ones(v_buf[pl.ds(first_key + start, size)])
+            return v_buf[pl.ds(first_key + start, size)]
 
         def score(order, row, start, size):
-            return flat_dot(qx_ref[order, pl.ds(row, group)], keys(start, size))
-
-        def finish(p, order, row, start, size):
-            part = value_dot(p, values(start, size))
+            return flat_dot(q_ref[slots[order], pl.ds(row, group)], keys(start, size))
+
+        def finish(s, order, row, start, size):
+            top = top_ref[order, pl.ds(row, group)]
+            part = with_sums(*weights_of(coef, s, top), values(start, size))
             before = acc_ref[order, pl.ds(row, group)] if start == 0 else totals[order, row]
             totals[order, row] = before + part
             if start == tiles[-1][0]:
                 store(order, row, totals[order, row])
 
         chunks = [(order, row, *tile) for row in range(0, all_rows, group) for order in orders for tile in tiles]
-        in_turn(coef, chunks, score, finish)
+        in_turn(chunks, score, finish)
 
     @pl.when(above)
     def _():
@@ -231,9 +216,9 @@
     return jnp.transpose(x)[:1]
 
 
-def middle_kernel(coef, visits, rows, sb, qx_ref, acc_in, *refs):
-    pieces, (acc_ref, *tops), buffers = refs[: 4 * len(visits)], refs[4 * len(visits) : -3], refs[-3:]
-    _, all_rows, double = qx_ref.shape
+def middle_kernel(coef, visits, sb, q_ref, top_ref, acc_in, *refs):
+    pieces, acc_ref, buffers = refs[: 4 * len(visits)], refs[4 * len(visits)], refs[4 * len(visits) + 1 :]
+    all_rows = q_ref.shape[1]
 
     def store(order, row, value):
         if value is not None:
@@ -241,20 +226,14 @@
 
     for place, distance in enumerate(visits):
         parts = pieces[4 * place : 4 * place + 4]
-        visit(coef, distance, parts, sb, qx_ref, acc_ref, buffers, all_rows, store)
-    for top_ref in tops:
-        for order in (LO, HI):
-            for h in range(all_rows // rows):
-                columns = qx_ref[order, pl.ds(h * rows, rows), pl.ds(double // 2, double // 2)]
-                columns = jnp.transpose(columns.astype(jnp.float32))
-                top_ref[order, h : h + 1, :] = -(columns[0:1] + columns[1:2] + columns[2:3])
-
-
-def last_kernel(coef, distances, sb, qx_ref, acc_ref, top_ref, *refs):
+        visit(coef, distance, parts, sb, q_ref, top_ref, acc_ref, buffers, all_rows, store)
+
+
+def last_kernel(coef, distances, sb, q_ref, top_ref, acc_ref, *refs):
     parts, every, rest = refs[:4], refs[4 : 4 * len(distances) + 6], refs[4 * len(distances) + 6 :]
     out_hbm, lse_hbm, out_buf, lse_ref, *buffers, worst, run_top, run_acc, sem, out_sems = rest
     rows = out_buf.shape[1]
-    all_rows = qx_ref.shape[1]
+    all_rows = q_ref.shape[1]
     heads = all_rows // rows
     k_buf, v_buf, _ = buffers
     block_len, width = k_buf.shape[0] // 2, k_buf.shape[1]
@@ -270,11 +249,11 @@
         columns = pl.ds(h * width, width)
         return pltpu.make_async_copy(out_buf.at[:, :, columns], out_hbm.at[:, :, columns], out_sems.at[h])
 
-    def emit(order, h, value, top_row):
+    def emit(order, h, value, top):
         slot = hi if order == HI else 1 - hi
-        sums = value[:, width:]
+        sums = jnp.broadcast_to(jnp.sum(value[:, width:], axis=1, keepdims=True), (rows, width))
         out_buf[slot, :, h * width : (h + 1) * width] = (value[:, :width] / sums).astype(out_buf.dtype)
-        lse_ref[slot, h : h + 1, :] = top_row * (coef * math.log(2.0)) + jnp.log(first_row(sums))
+        lse_ref[slot, h : h + 1, :] = first_row(top * (coef * math.log(2.0)) + jnp.log(sums))
         return sums
 
     worst[...] = jnp.zeros_like(worst)
@@ -285,10 +264,10 @@
             value = acc_ref[order, pl.ds(row, group)]
         for at in range(0, group, rows):
             h = (row + at) // rows
-            sums = emit(order, h, value[at : at + rows], top_ref[order, h : h + 1, :])
+            sums = emit(order, h, value[at : at + rows], top_ref[order, pl.ds(row + at, rows)])
             worst[...] = jnp.maximum(worst[...], sums)
 
-    visit(coef, distances[-1], parts, sb, qx_ref, acc_ref, buffers, all_rows // 2 if heads > 1 else all_rows, store)
+    visit(coef, distances[-1], parts, sb, q_ref, top_ref, acc_ref, buffers, all_rows // 2 if heads > 1 else all_rows, store)
     for h in range(heads):
         out_copy(h).start()
     lse_copy.start()
@@ -312,7 +291,8 @@
 
                 @pl.when(shift + rows > 0)
                 def _():
-                    queries = qx_ref[order, pl.ds(pl.multiple_of(h * rows, rows), rows), pl.ds(0, width)]
+                    own_slot = jnp.where(order == HI, hi, 1 - hi)
+                    queries = q_ref[own_slot, pl.ds(pl.multiple_of(h * rows, rows), rows)]
                     at = pl.ds(pl.multiple_of(slot * block_len, block_len), block_len)
                     s = score_dot(queries, k_buf[at])
                     row = lax.broadcasted_iota(jnp.int32, s.shape, 0) + shift
@@ -323,7 +303,8 @@
                     p = jnp.where(allowed, jnp.exp2((s - widen(top, block_len)) * coef), 0.0)
                     run_top[order, h] = top
                     shrink = widen(jnp.exp2((before - top) * coef), 2 * width)
-                    fresh = value_dot(p.astype(jnp.bfloat16), with_ones(v_buf[at]))
+                    lanes = functools.reduce(jnp.add, [p[:, x : x + width] for x in range(0, block_len, width)])
+                    fresh = with_sums(p.astype(jnp.bfloat16), lanes, v_buf[at])
                     run_acc[order, h] = run_acc[order, h] * shrink + fresh
 
         run_top[...] = jnp.full_like(run_top, NEG)
@@ -350,7 +331,7 @@
             online(source_of(me, other, count))
         for h in range(heads):
             for order in (LO, HI):
-                emit(order, h, run_acc[order, h], first_row(run_top[order, h]))
+                emit(order, h, run_acc[order, h], run_top[order, h])
             out_copy(h).start()
             out_copy(h).wait()
         lse_copy.start()
@@ -386,7 +367,7 @@
     anywhere = pl.BlockSpec(memory_space=pl.ANY)
     scalars = pl.BlockSpec(memory_space=pltpu.SMEM)
     acc_shape = jax.ShapeDtypeStruct((2, all_rows, 2 * width), jnp.float32)
-    qx_shape = jax.ShapeDtypeStruct(acc_shape.shape, jnp.bfloat16)
+    tops_shape = jax.ShapeDtypeStruct((2, all_rows, width), jnp.float32)
     top_shape = jax.ShapeDtypeStruct((2, heads, rows), jnp.float32)
     params = pltpu.CompilerParams(vmem_limit_bytes=40 * 1024 * 1024)
     unit = rows * heads * block_len * width * 4
@@ -411,15 +392,15 @@
         name="load",
     )(*in_hbm)
     arrived, across, beside, beside_across = {}, {}, {}, {}
-    for distance in distances:
+    for distance in reversed(distances):
         if not is_power(count) or is_power(distance):
             arrived[distance] = along_seq(piece, distance)
 
-    qx, acc = pl.pallas_call(
+    tops, acc = pl.pallas_call(
         functools.partial(local_kernel, coef, rows),
         in_specs=[scalars] + [whole] * 3,
         out_specs=[whole] * 2,
-        out_shape=[qx_shape, acc_shape],
+        out_shape=[tops_shape, acc_shape],
         cost_estimate=cost(3, 6_000_000),
         scratch_shapes=[pltpu.VMEM((2, width, block_len), key_rows.dtype)],
         compiler_params=params,
@@ -428,19 +409,19 @@
     kv_buffers = [pltpu.VMEM((2 * block_len, width), jnp.bfloat16)] * 2
     kv_buffers += [pltpu.VMEM((width, 2 * block_len), jnp.bfloat16)]
 
-    def attend(acc, visits, with_tops):
+    def attend(acc, visits):
         pieces = [part[d] for d in visits for part in (arrived, beside, across, beside_across)]
         return pl.pallas_call(
-            functools.partial(middle_kernel, coef, visits, rows),
-            in_specs=[scalars] + [whole] * (2 + len(pieces)),
-            out_specs=[whole] * (1 + with_tops),
-            out_shape=[acc_shape] + [top_shape] * with_tops,
+            functools.partial(middle_kernel, coef, visits),
+            in_specs=[scalars] + [whole] * (3 + len(pieces)),
+            out_specs=whole,
+            out_shape=acc_shape,
             scratch_shapes=kv_buffers,
-            input_output_aliases={2: 0},
+            input_output_aliases={3: 0},
             cost_estimate=cost(2 * len(visits), 7_000_000),
             compiler_params=params,
             name=f"visitors_from_{visits[0]}",
-        )(sb_here, qx, acc, *pieces)
+        )(sb_here, q_here, tops, acc, *pieces)
 
     def relay(distance):
         if distance in distances and distance not in arrived:
@@ -454,9 +435,8 @@
 
     last = distances[-1]
     groups = [distances[:2]] + [[d] for d in distances[2:-1]] if count > 3 else [[d] for d in distances[:-1]]
-    first, acc = lax.optimization_barrier((dict(arrived), acc))
-    arrived.update(first)
-    tops = []
+    for distance in sorted(arrived, reverse=True):
+        arrived[distance], acc = lax.optimization_barrier((arrived[distance], acc))
     for distance in groups[0]:
         spread(distance)
     for visits in groups:
@@ -468,7 +448,7 @@
         spread(ahead)
         for distance in visits:
             beside_across[distance] = along_inner(across[distance])
-        acc, *tops = attend(acc, visits, int(ahead == last))
+        acc = attend(acc, visits)
     across[last], acc = lax.optimization_barrier((across[last], acc))
     beside_across[last] = along_inner(across[last])
 
@@ -493,7 +473,7 @@
         cost_estimate=cost(1, 7_000_000),
         compiler_params=params,
         name="last_visitor",
-    )(sb_here, qx, acc, *tops, *flat[-4:], in_hbm[1], in_hbm[2], *flat)
+    )(sb_here, q_here, tops, acc, *flat[-4:], in_hbm[1], in_hbm[2], *flat)
     return attended, log_total
 
 

time: 36.8 us -> 36.3 us (0.986)
  starting transfers between devices: 10 us -> 12 us
  waiting for transfers between devices: 9.69 us -> 7.71 us
    ppermute x3, waiting for transfers between devices: 3.25 us -> 2.09 us  [along_seq(): return lax.ppermute(block, 'seq', route)]
    ppermute x3, starting transfers between devices: 6.13 us -> 7.16 us  [along_seq(): return lax.ppermute(block, 'seq', route)]
    ppermute x3, starting transfers between devices: 2.56 us -> 3.27 us  [along_head(): lax.ppermute(block, 'head', [(i, i ^ 1) for i in range(lax.axis_size('hea...]
    ppermute x6, waiting for transfers between devices: 1.7 us -> 1.04 us  [along_inner(): return lax.ppermute(block, 'inner', [(0, 1), (1, 0)])]
  transfers between devices with their start and end apart: 12 -> 12, of which waited for: 8 -> 5; matrix products, arithmetic and copies ran while one was open for 0% -> 0% of each run, Pallas kernels for 28% -> 28%
where the time goes in v3:
time: 36.3 us
  Pallas kernels  15.7 us (43%)
  starting transfers between devices  12 us (33%)
  waiting for transfers between devices  7.71 us (21%)
  between operations  0.85 us (2%)
    ppermute x3, starting transfers between devices, along_seq(): return lax.ppermute(block, 'seq', route)  7.16 us
    pallas_call x1, Pallas kernels, attend(): pl.pallas_call(functools.partial(middle_kernel, coef, visits), in_specs=[...  5.65 us
    ppermute x3, waiting for transfers between devices, along_head(): lax.ppermute(block, 'head', [(i, i ^ 1) for i in range(lax.axis_size('hea...  4.58 us
    pallas_call x1, Pallas kernels, body(): pl.pallas_call(functools.partial(local_kernel, coef, rows), in_specs=[sca...  4.33 us
    pallas_call x1, Pallas kernels, body(): pl.pallas_call(functools.partial(last_kernel, coef, distances), in_specs=...  4.23 us
    ppermute x3, starting transfers between devices, along_head(): lax.ppermute(block, 'head', [(i, i ^ 1) for i in range(lax.axis_size('hea...  3.27 us
    ppermute x3, waiting for transfers between devices, along_seq(): return lax.ppermute(block, 'seq', route)  2.09 us
    ppermute x6, starting transfers between devices, along_inner(): return lax.ppermute(block, 'inner', [(0, 1), (1, 0)])  1.57 us
  transfers between devices with their start and end apart: 12, of which 5 were waited for; matrix products, arithmetic and copies ran while one was open for 0% of the time, Pallas kernels for 28%

profile of v3, /device:TPU:0, one launch (start us, length us, event | category | flops | bytes accessed | tf_op | source)
XLA Modules:
  0.0 36.3 jit_solution(10815366139350511475)
XLA Ops:
  0.6 1.5 %load.1 = (bf16[2,320,128]{2,1,0:T(8,128)(2,1)S(1)}, bf16[2,1280,128]{2,1,0:T(8,128)(2,1)S(1)}, bf16[2,640,128]{2,1,0:T(8,128)(2,1)S(1)}, bf16[2,640,128]{2,1,0:T(8,128)(2,1)S(1)}, s32[8]{0:T(128)S(1)}) custom-call(bf16[2,320,512]{2,1,0:T(8,128)(2,1)} %q_hbm.1, bf16[2,640,128]{2,1,0:T(8,128)(2,1)} %refs_4_.1, bf16[2,640,128]{2,1,0:T(8,128)(2,1)} %refs_5_.1, ...), custom_call_target="tpu_custom_call" | custom-call | bytes 3000000 | tf_op jit(solution)/shard_map/load/pallas_call | solution.py:383
  2.1 4.1 %collective-permute-start.1 = (bf16[2,320,128]{2,1,0:T(8,128)(2,1)S(1)}, bf16[2,320,128]{2,1,0:T(8,128)(2,1)S(1)}, u32[]{:S(2)}, u32[]{:S(2)}) collective-permute-start(bf16[2,320,128]{2,1,0:T(8,128)(2,1)S(1)} %get-tuple-element.24), channel_id=1, source_target_pairs={{0,8},{4,12},{8,0},{12,4},{1,9},{5,13},{9,1},{13,5},{2,10},{6,14},... | collective-permute-start | bytes 491528 | tf_op jit(solution)/shard_map/along_seq/ppermute | solution.py:356
  6.2 1.6 %collective-permute-start = (bf16[2,320,128]{2,1,0:T(8,128)(2,1)S(1)}, bf16[2,320,128]{2,1,0:T(8,128)(2,1)S(1)}, u32[]{:S(2)}, u32[]{:S(2)}) collective-permute-start(bf16[2,320,128]{2,1,0:T(8,128)(2,1)S(1)} %get-tuple-element.24), channel_id=1, source_target_pairs={{0,4},{4,0},{8,12},{12,8},{1,5},{5,1},{9,13},{13,9},{2,6},{6,2},{1... | collective-permute-start | bytes 491528 | tf_op jit(solution)/shard_map/along_seq/ppermute | solution.py:356
  7.8 4.3 %local_part.1 = (f32[2,1280,128]{2,1,0:T(8,128)S(1)}, f32[2,1280,256]{2,1,0:T(8,128)S(1)}) custom-call(s32[8]{0:T(128)S(1)} %get-tuple-element.19.sb, bf16[2,1280,128]{2,1,0:T(8,128)(2,1)S(1)} %get-tuple-element.20.q_ref, bf16[2,640,128]{2,1,0:T(8,128)(2,1)S(1)} %get-tuple-element.21.k_ref, bf16[2,640,128]{2,1,0:T(8,128)(2,1)S(1)} %get-tuple-element.22.v_ref), custom_call_target="tpu_custom_call" | custom-call | flops 2516582400 | bytes 6000000 | tf_op jit(solution)/shard_map/local_part/pallas_call | solution.py:399
  12.1 1.9 %collective-permute-done.1.refs_4_.refs_10_ = bf16[2,320,128]{2,1,0:T(8,128)(2,1)S(1)} collective-permute-done((bf16[2,320,128]{2,1,0:T(8,128)(2,1)S(1)}, bf16[2,320,128]{2,1,0:T(8,128)(2,1)S(1)}, u32[]{:S(2)}, u32[]{:S(2)}) %collective-permute-start.1) | collective-permute-done | bytes 163872 | tf_op jit(solution)/shard_map/along_seq/ppermute | solution.py:356
  14.0 0.2 collective-permute-done.refs_0_.refs_6_
  14.2 1.5 %collective-permute-start.2 = (bf16[2,320,128]{2,1,0:T(8,128)(2,1)S(1)}, bf16[2,320,128]{2,1,0:T(8,128)(2,1)S(1)}, u32[]{:S(2)}, u32[]{:S(2)}) collective-permute-start(bf16[2,320,128]{2,1,0:T(8,128)(2,1)S(1)} %collective-permute-done.refs_0_.refs_6_), channel_id=1, source_target_pairs={{0,2},{2,0},{1,3},{3,1},{4,6},{6,4},{5,7},{7,5},{8,10},{10,8},{9,1... | collective-permute-start | bytes 491528 | tf_op jit(solution)/shard_map/along_head/ppermute | solution.py:360
  15.8 0.5 %collective-permute-start.3 = (bf16[2,320,128]{2,1,0:T(8,128)(2,1)S(1)}, bf16[2,320,128]{2,1,0:T(8,128)(2,1)S(1)}, u32[]{:S(2)}, u32[]{:S(2)}) collective-permute-start(bf16[2,320,128]{2,1,0:T(8,128)(2,1)S(1)} %collective-permute-done.1.refs_4_.refs_10_), channel_id=1, source_target_pairs={{0,2},{2,0},{1,3},{3,1},{4,6},{6,4},{5,7},{7,5},{8,10},{10,8},{9,1... | collective-permute-start | bytes 491528 | tf_op jit(solution)/shard_map/along_head/ppermute | solution.py:360
  16.3 1.5 %collective-permute-start.4 = (bf16[2,320,128]{2,1,0:T(8,128)(2,1)S(1)}, bf16[2,320,128]{2,1,0:T(8,128)(2,1)S(1)}, u32[]{:S(2)}, u32[]{:S(2)}) collective-permute-start(bf16[2,320,128]{2,1,0:T(8,128)(2,1)S(1)} %collective-permute-done.1.refs_4_.refs_10_), channel_id=1, source_target_pairs={{0,4},{4,0},{8,12},{12,8},{1,5},{5,1},{9,13},{13,9},{2,6},{6,2},{1... | collective-permute-start | bytes 491528 | tf_op jit(solution)/shard_map/along_seq/ppermute | solution.py:356
  17.7 0.0 collective-permute-start.6
  17.7 0.5 %collective-permute-start.8 = (bf16[2,320,128]{2,1,0:T(8,128)(2,1)S(1)}, bf16[2,320,128]{2,1,0:T(8,128)(2,1)S(1)}, u32[]{:S(2)}, u32[]{:S(2)}) collective-permute-start(bf16[2,320,128]{2,1,0:T(8,128)(2,1)S(1)} %collective-permute-done.1.refs_4_.refs_10_), channel_id=1, source_target_pairs={{0,1},{1,0},{2,3},{3,2},{4,5},{5,4},{6,7},{7,6},{8,9},{9,8},{10,11... | collective-permute-start | bytes 491528 | tf_op jit(solution)/shard_map/along_inner/ppermute | solution.py:364
  18.3 2.8 %collective-permute-done.2.refs_2_.refs_8_ = bf16[2,320,128]{2,1,0:T(8,128)(2,1)S(1)} collective-permute-done((bf16[2,320,128]{2,1,0:T(8,128)(2,1)S(1)}, bf16[2,320,128]{2,1,0:T(8,128)(2,1)S(1)}, u32[]{:S(2)}, u32[]{:S(2)}) %collective-permute-start.2) | collective-permute-done | bytes 163872 | tf_op jit(solution)/shard_map/along_head/ppermute | solution.py:360
  21.1 1.8 %collective-permute-done.3.refs_6_.refs_12_ = bf16[2,320,128]{2,1,0:T(8,128)(2,1)S(1)} collective-permute-done((bf16[2,320,128]{2,1,0:T(8,128)(2,1)S(1)}, bf16[2,320,128]{2,1,0:T(8,128)(2,1)S(1)}, u32[]{:S(2)}, u32[]{:S(2)}) %collective-permute-start.3) | collective-permute-done | bytes 163872 | tf_op jit(solution)/shard_map/along_head/ppermute | solution.py:360
  22.8 0.0 collective-permute-done.4.refs_0_.refs_14_
  22.8 0.0 collective-permute-start.7
  22.8 0.5 %collective-permute-start.9 = (bf16[2,320,128]{2,1,0:T(8,128)(2,1)S(1)}, bf16[2,320,128]{2,1,0:T(8,128)(2,1)S(1)}, u32[]{:S(2)}, u32[]{:S(2)}) collective-permute-start(bf16[2,320,128]{2,1,0:T(8,128)(2,1)S(1)} %collective-permute-done.3.refs_6_.refs_12_), channel_id=1, source_target_pairs={{0,1},{1,0},{2,3},{3,2},{4,5},{5,4},{6,7},{7,6},{8,9},{9,8},{10,11... | collective-permute-start | bytes 491528 | tf_op jit(solution)/shard_map/along_inner/ppermute | solution.py:364
  23.3 1.2 %collective-permute-start.5 = (bf16[2,320,128]{2,1,0:T(8,128)(2,1)S(1)}, bf16[2,320,128]{2,1,0:T(8,128)(2,1)S(1)}, u32[]{:S(2)}, u32[]{:S(2)}) collective-permute-start(bf16[2,320,128]{2,1,0:T(8,128)(2,1)S(1)} %collective-permute-done.4.refs_0_.refs_14_), channel_id=1, source_target_pairs={{0,2},{2,0},{1,3},{3,1},{4,6},{6,4},{5,7},{7,5},{8,10},{10,8},{9,1... | collective-permute-start | bytes 491528 | tf_op jit(solution)/shard_map/along_head/ppermute | solution.py:360
  24.6 0.0 collective-permute-done.6.refs_1_.refs_7_
  24.6 0.0 collective-permute-start.10
  24.6 0.0 collective-permute-done.8.refs_5_.refs_11_
  24.6 0.0 collective-permute-done.7.refs_3_.refs_9_
  24.6 0.0 collective-permute-done.9.refs_7_.refs_13_
  24.6 5.7 %visitors_from_1.1.acc_ref = f32[2,1280,256]{2,1,0:T(8,128)S(1)} custom-call(s32[8]{0:T(128)S(1)} %get-tuple-element.19.sb, bf16[2,1280,128]{2,1,0:T(8,128)(2,1)S(1)} %get-tuple-element.20.q_ref, f32[2,1280,128]{2,1,0:T(8,128)S(1)} %get-tuple-element.23.top_ref, f32[2,1280,256]{2,1,0:T(8,128)S(1)} %get-tuple-element.31.acc_in, ...), custom_call_target="tpu_custom_call", output_to_operand_aliasing={{}: (3, {})} | custom-call | flops 3355443200 | bytes 7000000 | tf_op jit(solution)/shard_map/visitors_from_1/pallas_call | solution.py:414
  30.3 0.0 collective-permute-done.5.refs_2_.refs_16_
  30.3 0.5 %collective-permute-start.11 = (bf16[2,320,128]{2,1,0:T(8,128)(2,1)S(1)}, bf16[2,320,128]{2,1,0:T(8,128)(2,1)S(1)}, u32[]{:S(2)}, u32[]{:S(2)}) collective-permute-start(bf16[2,320,128]{2,1,0:T(8,128)(2,1)S(1)} %collective-permute-done.5.refs_2_.refs_16_), channel_id=1, source_target_pairs={{0,1},{1,0},{2,3},{3,2},{4,5},{5,4},{6,7},{7,6},{8,9},{9,8},{10,11... | collective-permute-start | bytes 491528 | tf_op jit(solution)/shard_map/along_inner/ppermute | solution.py:364
  30.8 0.0 collective-permute-done.10.refs_1_.refs_15_
  30.8 1.0 %collective-permute-done.11.refs_3_.refs_17_ = bf16[2,320,128]{2,1,0:T(8,128)(2,1)S(1)} collective-permute-done((bf16[2,320,128]{2,1,0:T(8,128)(2,1)S(1)}, bf16[2,320,128]{2,1,0:T(8,128)(2,1)S(1)}, u32[]{:S(2)}, u32[]{:S(2)}) %collective-permute-start.11) | collective-permute-done | bytes 163872 | tf_op jit(solution)/shard_map/along_inner/ppermute | solution.py:364
  31.9 4.2 %last_visitor.1 = (bf16[2,320,512]{2,1,0:T(8,128)(2,1)}, f32[2,4,320]{2,1,0:T(4,128)}) custom-call(s32[8]{0:T(128)S(1)} %get-tuple-element.19.sb, bf16[2,1280,128]{2,1,0:T(8,128)(2,1)S(1)} %get-tuple-element.20.q_ref, f32[2,1280,128]{2,1,0:T(8,128)S(1)} %get-tuple-element.23.top_ref, f32[2,1280,256]{2,1,0:T(8,128)S(1)} %visitors_from_1.1.acc_ref, ...), custom_call_target="tpu_custom_call" | custom-call | flops 838860800 | bytes 7000000 | tf_op jit(solution)/shard_map/last_visitor/pallas_call | solution.py:456
Async XLA Ops:
  2.1 11.9 %collective-permute-start.1 = (bf16[2,320,128]{2,1,0:T(8,128)(2,1)S(1)}, bf16[2,320,128]{2,1,0:T(8,128)(2,1)S(1)}, u32[]{:S(2)}, u32[]{:S(2)}) collective-permute-start(bf16[2,320,128]{2,1,0:T(8,128)(2,1)S(1)} %get-tuple-element.24), channel_id=1, source_target_pairs={{0,8},{4,12},{8,0},{12,4},{1,9},{5,13},{9,1},{13,5},{2,10},{6,14},... | collective-permute-start | bytes 491528 | tf_op jit(solution)/shard_map/along_seq/ppermute | solution.py:356
  6.2 8.0 %collective-permute-start = (bf16[2,320,128]{2,1,0:T(8,128)(2,1)S(1)}, bf16[2,320,128]{2,1,0:T(8,128)(2,1)S(1)}, u32[]{:S(2)}, u32[]{:S(2)}) collective-permute-start(bf16[2,320,128]{2,1,0:T(8,128)(2,1)S(1)} %get-tuple-element.24), channel_id=1, source_target_pairs={{0,4},{4,0},{8,12},{12,8},{1,5},{5,1},{9,13},{13,9},{2,6},{6,2},{1... | collective-permute-start | bytes 491528 | tf_op jit(solution)/shard_map/along_seq/ppermute | solution.py:356
  14.2 6.8 %collective-permute-start.2 = (bf16[2,320,128]{2,1,0:T(8,128)(2,1)S(1)}, bf16[2,320,128]{2,1,0:T(8,128)(2,1)S(1)}, u32[]{:S(2)}, u32[]{:S(2)}) collective-permute-start(bf16[2,320,128]{2,1,0:T(8,128)(2,1)S(1)} %collective-permute-done.refs_0_.refs_6_), channel_id=1, source_target_pairs={{0,2},{2,0},{1,3},{3,1},{4,6},{6,4},{5,7},{7,5},{8,10},{10,8},{9,1... | collective-permute-start | bytes 491528 | tf_op jit(solution)/shard_map/along_head/ppermute | solution.py:360
  15.8 7.1 %collective-permute-start.3 = (bf16[2,320,128]{2,1,0:T(8,128)(2,1)S(1)}, bf16[2,320,128]{2,1,0:T(8,128)(2,1)S(1)}, u32[]{:S(2)}, u32[]{:S(2)}) collective-permute-start(bf16[2,320,128]{2,1,0:T(8,128)(2,1)S(1)} %collective-permute-done.1.refs_4_.refs_10_), channel_id=1, source_target_pairs={{0,2},{2,0},{1,3},{3,1},{4,6},{6,4},{5,7},{7,5},{8,10},{10,8},{9,1... | collective-permute-start | bytes 491528 | tf_op jit(solution)/shard_map/along_head/ppermute | solution.py:360
  16.3 6.6 %collective-permute-start.4 = (bf16[2,320,128]{2,1,0:T(8,128)(2,1)S(1)}, bf16[2,320,128]{2,1,0:T(8,128)(2,1)S(1)}, u32[]{:S(2)}, u32[]{:S(2)}) collective-permute-start(bf16[2,320,128]{2,1,0:T(8,128)(2,1)S(1)} %collective-permute-done.1.refs_4_.refs_10_), channel_id=1, source_target_pairs={{0,4},{4,0},{8,12},{12,8},{1,5},{5,1},{9,13},{13,9},{2,6},{6,2},{1... | collective-permute-start | bytes 491528 | tf_op jit(solution)/shard_map/along_seq/ppermute | solution.py:356
  17.7 6.9 %collective-permute-start.6 = (bf16[2,320,128]{2,1,0:T(8,128)(2,1)S(1)}, bf16[2,320,128]{2,1,0:T(8,128)(2,1)S(1)}, u32[]{:S(2)}, u32[]{:S(2)}) collective-permute-start(bf16[2,320,128]{2,1,0:T(8,128)(2,1)S(1)} %collective-permute-done.refs_0_.refs_6_), channel_id=1, source_target_pairs={{0,1},{1,0},{2,3},{3,2},{4,5},{5,4},{6,7},{7,6},{8,9},{9,8},{10,11... | collective-permute-start | bytes 491528 | tf_op jit(solution)/shard_map/along_inner/ppermute | solution.py:364
  17.7 6.9 %collective-permute-start.8 = (bf16[2,320,128]{2,1,0:T(8,128)(2,1)S(1)}, bf16[2,320,128]{2,1,0:T(8,128)(2,1)S(1)}, u32[]{:S(2)}, u32[]{:S(2)}) collective-permute-start(bf16[2,320,128]{2,1,0:T(8,128)(2,1)S(1)} %collective-permute-done.1.refs_4_.refs_10_), channel_id=1, source_target_pairs={{0,1},{1,0},{2,3},{3,2},{4,5},{5,4},{6,7},{7,6},{8,9},{9,8},{10,11... | collective-permute-start | bytes 491528 | tf_op jit(solution)/shard_map/along_inner/ppermute | solution.py:364
  22.8 1.8 %collective-permute-start.7 = (bf16[2,320,128]{2,1,0:T(8,128)(2,1)S(1)}, bf16[2,320,128]{2,1,0:T(8,128)(2,1)S(1)}, u32[]{:S(2)}, u32[]{:S(2)}) collective-permute-start(bf16[2,320,128]{2,1,0:T(8,128)(2,1)S(1)} %collective-permute-done.2.refs_2_.refs_8_), channel_id=1, source_target_pairs={{0,1},{1,0},{2,3},{3,2},{4,5},{5,4},{6,7},{7,6},{8,9},{9,8},{10,11... | collective-permute-start | bytes 491528 | tf_op jit(solution)/shard_map/along_inner/ppermute | solution.py:364
  22.8 1.8 %collective-permute-start.9 = (bf16[2,320,128]{2,1,0:T(8,128)(2,1)S(1)}, bf16[2,320,128]{2,1,0:T(8,128)(2,1)S(1)}, u32[]{:S(2)}, u32[]{:S(2)}) collective-permute-start(bf16[2,320,128]{2,1,0:T(8,128)(2,1)S(1)} %collective-permute-done.3.refs_6_.refs_12_), channel_id=1, source_target_pairs={{0,1},{1,0},{2,3},{3,2},{4,5},{5,4},{6,7},{7,6},{8,9},{9,8},{10,11... | collective-permute-start | bytes 491528 | tf_op jit(solution)/shard_map/along_inner/ppermute | solution.py:364
  23.3 6.9 %collective-permute-start.5 = (bf16[2,320,128]{2,1,0:T(8,128)(2,1)S(1)}, bf16[2,320,128]{2,1,0:T(8,128)(2,1)S(1)}, u32[]{:S(2)}, u32[]{:S(2)}) collective-permute-start(bf16[2,320,128]{2,1,0:T(8,128)(2,1)S(1)} %collective-permute-done.4.refs_0_.refs_14_), channel_id=1, source_target_pairs={{0,2},{2,0},{1,3},{3,1},{4,6},{6,4},{5,7},{7,5},{8,10},{10,8},{9,1... | collective-permute-start | bytes 491528 | tf_op jit(solution)/shard_map/along_head/ppermute | solution.py:360
  24.6 6.3 %collective-permute-start.10 = (bf16[2,320,128]{2,1,0:T(8,128)(2,1)S(1)}, bf16[2,320,128]{2,1,0:T(8,128)(2,1)S(1)}, u32[]{:S(2)}, u32[]{:S(2)}) collective-permute-start(bf16[2,320,128]{2,1,0:T(8,128)(2,1)S(1)} %collective-permute-done.4.refs_0_.refs_14_), channel_id=1, source_target_pairs={{0,1},{1,0},{2,3},{3,2},{4,5},{5,4},{6,7},{7,6},{8,9},{9,8},{10,11... | collective-permute-start | bytes 491528 | tf_op jit(solution)/shard_map/along_inner/ppermute | solution.py:364
  30.3 1.6 %collective-permute-start.11 = (bf16[2,320,128]{2,1,0:T(8,128)(2,1)S(1)}, bf16[2,320,128]{2,1,0:T(8,128)(2,1)S(1)}, u32[]{:S(2)}, u32[]{:S(2)}) collective-permute-start(bf16[2,320,128]{2,1,0:T(8,128)(2,1)S(1)} %collective-permute-done.5.refs_2_.refs_16_), channel_id=1, source_target_pairs={{0,1},{1,0},{2,3},{3,2},{4,5},{5,4},{6,7},{7,6},{8,9},{9,8},{10,11... | collective-permute-start | bytes 491528 | tf_op jit(solution)/shard_map/along_inner/ppermute | solution.py:364

commit v4 on v3

--- a/solution.py
+++ b/solution.py
@@ -12,14 +12,11 @@
 SUM_LIMIT = 1e36
 LO, HI = 0, 1
 TILE = 256
+SUBLANES = 8
 
 
 def score_dot(q, k):
     return lax.dot_general(q, k, (((1,), (1,)), ((), ())), preferred_element_type=jnp.float32)
-
-
-def flat_dot(q, k_turned):
-    return jnp.dot(q, k_turned, preferred_element_type=jnp.float32)
 
 
 def value_dot(p, v):
@@ -73,9 +70,16 @@
 
 
 def weights_of(coef, s, top):
-    p = jnp.exp2((s - widen(top, s.shape[1])) * coef)
-    sums = functools.reduce(jnp.add, [p[:, at : at + 128] for at in range(0, p.shape[1], 128)])
-    return p.astype(jnp.bfloat16), sums
+    p = jnp.exp2((s - down(top, s.shape[0])) * coef)
+    return p.astype(jnp.bfloat16), folded(jnp.add, p)
+
+
+def down(x, height):
+    return jnp.concatenate([x] * (height // x.shape[0]), axis=0)
+
+
+def folded(combine, x):
+    return functools.reduce(combine, [x[at : at + SUBLANES] for at in range(0, x.shape[0], SUBLANES)])
 
 
 def with_sums(p, sums, v):
@@ -91,41 +95,42 @@
         finish(now, *chunk)
 
 
-def local_kernel(coef, rows, sb, q_ref, k_ref, v_ref, top_ref, acc_ref, turned):
+def local_kernel(coef, rows, sb, q_ref, k_ref, v_ref, turned_q, top_ref, sum_ref, acc_ref, turned_v):
     _, all_rows, width = q_ref.shape
     block_len = k_ref.shape[1]
-    heads = all_rows // rows
     hi, _, _ = blocks_of(sb, lax.axis_index("seq"))
     slots = {HI: hi, LO: 1 - hi}
     tiles = key_tiles(block_len)
-
     for order in (HI, LO):
-        turned[order] = jnp.transpose(k_ref[slots[order]])
+        turned_q[order] = jnp.transpose(q_ref[slots[order]])
+        turned_v[order] = jnp.transpose(v_ref[slots[order]])
 
     def keys(order, start, size):
-        return turned[order, :, start : start + size]
-
-    def values(slot, start, size):
-        return v_ref[slot, pl.ds(start, size)]
+        return k_ref[slots[order], pl.ds(start, size)]
+
+    def values(order, start, size):
+        return turned_v[order, :, start : start + size]
 
     def masked(order, start, size):
-        row = lax.broadcasted_iota(jnp.int32, (rows, size), 0) + lax.axis_index("inner") * rows
-        col = lax.broadcasted_iota(jnp.int32, (rows, size), 1) + start
-        bias = jnp.where(col <= row, 0.0, NEG)
-        s = flat_dot(q_ref[slots[order]], keys(order, start, size))
-        return s + jnp.concatenate([bias] * heads, axis=0)
+        lane = lax.broadcasted_iota(jnp.int32, (SUBLANES, all_rows), 1)
+        heads_below = sum((lane >= at).astype(jnp.int32) for at in range(rows, all_rows, rows))
+        row = lane - heads_below * rows + lax.axis_index("inner") * rows
+        key = lax.broadcasted_iota(jnp.int32, (size, all_rows), 0) + start
+        s = value_dot(keys(order, start, size), turned_q[order])
+        return jnp.where(key <= down(row, size), s, NEG)
 
     def highest(scores):
-        parts = [s[:, at : at + width] for s in scores for at in range(0, s.shape[1], width)]
-        top = functools.reduce(jnp.maximum, parts)
-        return jnp.broadcast_to(jnp.max(top, axis=1, keepdims=True), (all_rows, width))
+        top = functools.reduce(jnp.maximum, [folded(jnp.maximum, s) for s in scores])
+        return jnp.broadcast_to(jnp.max(top, axis=0, keepdims=True), top.shape)
 
     def settle(order, scores, top):
-        total = None
+        total, sums = None, None
         for (start, size), s in zip(tiles, scores):
-            part = with_sums(*weights_of(coef, s, top), values(slots[order], start, size))
-            total = part if total is None else total + part
+            p, more = weights_of(coef, s, top)
+            part = value_dot(values(order, start, size), p)
+            total, sums = (part, more) if total is None else (total + part, sums + more)
         acc_ref[order] = total
+        sum_ref[order] = sums
 
     diag = [masked(HI, *tile) for tile in tiles]
     top = highest(diag)
@@ -136,10 +141,12 @@
     top_ref[LO] = top
 
     def score(start, size):
-        return flat_dot(q_ref[slots[HI]], keys(LO, start, size))
+        return value_dot(keys(LO, start, size), turned_q[HI])
 
     def finish(s, start, size):
-        acc_ref[HI] += with_sums(*weights_of(coef, s, top_ref[HI]), values(slots[LO], start, size))
+        p, more = weights_of(coef, s, top_ref[HI])
+        acc_ref[HI] += value_dot(values(LO, start, size), p)
+        sum_ref[HI] += more
 
     settle(LO, low, top)
     in_turn(tiles, score, finish)
@@ -159,19 +166,17 @@
                     for slot in range(2):
                         buf[pl.ds(pl.multiple_of((slot * 2 + half) * size, size), size)] = piece[slot]
 
-    turned[...] = jnp.transpose(k_buf[...])
-
-
-def visit(coef, distance, parts, sb, q_ref, top_ref, acc_ref, buffers, group, store):
-    all_rows = q_ref.shape[1]
+    turned[...] = jnp.transpose(v_buf[...])
+
+
+def visit(coef, distance, parts, sb, turned_q, top_ref, sum_ref, acc_ref, buffers):
     count = lax.axis_size("seq")
     me = lax.axis_index("seq")
     k_buf, v_buf, turned = buffers
     place_pieces(parts, k_buf, v_buf, turned)
     keys_here = k_buf.shape[0] // 2
 
-    hi, _, top_block = blocks_of(sb, me)
-    slots = {HI: hi, LO: 1 - hi}
+    _, _, top_block = blocks_of(sb, me)
     other_hi, _, other_top = blocks_of(sb, source_of(me, distance, count))
     above = top_block > other_top
 
@@ -179,32 +184,25 @@
         tiles = key_tiles(key_count)
         totals = {}
 
-        def keys(start, size):
-            at = first_key + start
-            at = at if isinstance(at, int) else pl.multiple_of(at, 128)
-            return turned[:, pl.ds(at, size)]
-
-        def values(start, size):
-            return v_buf[pl.ds(first_key + start, size)]
-
-        def score(order, row, start, size):
-            return flat_dot(q_ref[slots[order], pl.ds(row, group)], keys(start, size))
-
-        def finish(s, order, row, start, size):
-            top = top_ref[order, pl.ds(row, group)]
-            part = with_sums(*weights_of(coef, s, top), values(start, size))
-            before = acc_ref[order, pl.ds(row, group)] if start == 0 else totals[order, row]
-            totals[order, row] = before + part
+        def at(start, size):
+            first = first_key + start
+            return pl.ds(first if isinstance(first, int) else pl.multiple_of(first, 128), size)
+
+        def score(order, start, size):
+            return value_dot(k_buf[at(start, size)], turned_q[order])
+
+        def finish(s, order, start, size):
+            p, sums = weights_of(coef, s, top_ref[order])
+            part = value_dot(turned[:, at(start, size)], p)
+            before = totals[order] if start else (acc_ref[order], sum_ref[order])
+            totals[order] = before[0] + part, before[1] + sums
             if start == tiles[-1][0]:
-                store(order, row, totals[order, row])
-
-        chunks = [(order, row, *tile) for row in range(0, all_rows, group) for order in orders for tile in tiles]
-        in_turn(chunks, score, finish)
+                acc_ref[order], sum_ref[order] = totals[order]
+
+        in_turn([(order, *tile) for order in orders for tile in tiles], score, finish)
 
     @pl.when(above)
     def _():
-        for row in range(0, all_rows, group):
-            store(LO, row, None)
         run((HI,), 0, 2 * keys_here)
 
     @pl.when(jnp.logical_not(above))
@@ -216,22 +214,15 @@
     return jnp.transpose(x)[:1]
 
 
-def middle_kernel(coef, visits, sb, q_ref, top_ref, acc_in, *refs):
-    pieces, acc_ref, buffers = refs[: 4 * len(visits)], refs[4 * len(visits)], refs[4 * len(visits) + 1 :]
-    all_rows = q_ref.shape[1]
-
-    def store(order, row, value):
-        if value is not None:
-            acc_ref[order, pl.ds(row, all_rows)] = value
-
+def middle_kernel(coef, visits, sb, turned_q, top_ref, sum_in, acc_in, *refs):
+    pieces, (sum_ref, acc_ref, *buffers) = refs[: 4 * len(visits)], refs[4 * len(visits) :]
     for place, distance in enumerate(visits):
-        parts = pieces[4 * place : 4 * place + 4]
-        visit(coef, distance, parts, sb, q_ref, top_ref, acc_ref, buffers, all_rows, store)
-
-
-def last_kernel(coef, distances, sb, q_ref, top_ref, acc_ref, *refs):
+        visit(coef, distance, pieces[4 * place : 4 * place + 4], sb, turned_q, top_ref, sum_ref, acc_ref, buffers)
+
+
+def last_kernel(coef, distances, sb, q_ref, turned_q, top_ref, sum_ref, acc_ref, *refs):
     parts, every, rest = refs[:4], refs[4 : 4 * len(distances) + 6], refs[4 * len(distances) + 6 :]
-    out_hbm, lse_hbm, out_buf, lse_ref, *buffers, worst, run_top, run_acc, sem, out_sems = rest
+    out_hbm, lse_hbm, out_buf, lse_ref, *buffers, run_top, run_acc, sem, out_sems = rest
     rows = out_buf.shape[1]
     all_rows = q_ref.shape[1]
     heads = all_rows // rows
@@ -254,20 +245,19 @@
         sums = jnp.broadcast_to(jnp.sum(value[:, width:], axis=1, keepdims=True), (rows, width))
         out_buf[slot, :, h * width : (h + 1) * width] = (value[:, :width] / sums).astype(out_buf.dtype)
         lse_ref[slot, h : h + 1, :] = first_row(top * (coef * math.log(2.0)) + jnp.log(sums))
-        return sums
-
-    worst[...] = jnp.zeros_like(worst)
-
-    def store(order, row, value):
-        group = all_rows // 2 if heads > 1 else all_rows
-        if value is None:
-            value = acc_ref[order, pl.ds(row, group)]
-        for at in range(0, group, rows):
-            h = (row + at) // rows
-            sums = emit(order, h, value[at : at + rows], top_ref[order, pl.ds(row + at, rows)])
-            worst[...] = jnp.maximum(worst[...], sums)
-
-    visit(coef, distances[-1], parts, sb, q_ref, top_ref, acc_ref, buffers, all_rows // 2 if heads > 1 else all_rows, store)
+
+    visit(coef, distances[-1], parts, sb, turned_q, top_ref, sum_ref, acc_ref, buffers)
+    worst = None
+    for order in (LO, HI):
+        slot = hi if order == HI else 1 - hi
+        sums = jnp.sum(sum_ref[order], axis=0, keepdims=True)
+        worst = sums if worst is None else jnp.maximum(worst, sums)
+        log_total = top_ref[order][:1] * (coef * math.log(2.0)) + jnp.log(sums)
+        settled = jnp.transpose(acc_ref[order] * (1.0 / sums)).astype(out_buf.dtype)
+        for h in range(heads):
+            mine = slice(h * rows, (h + 1) * rows)
+            lse_ref[slot, h : h + 1, :] = log_total[:, mine]
+            out_buf[slot, :, h * width : (h + 1) * width] = settled[mine]
     for h in range(heads):
         out_copy(h).start()
     lse_copy.start()
@@ -275,7 +265,7 @@
         out_copy(h).wait()
     lse_copy.wait()
 
-    @pl.when(jnp.logical_not(jnp.max(worst[...]) < SUM_LIMIT))
+    @pl.when(jnp.logical_not(jnp.max(worst) < SUM_LIMIT))
     def _():
         def fetch(src, dst):
             copy = pltpu.make_async_copy(src, dst, sem)
@@ -366,8 +356,9 @@
     whole = pl.BlockSpec(memory_space=pltpu.VMEM)
     anywhere = pl.BlockSpec(memory_space=pl.ANY)
     scalars = pl.BlockSpec(memory_space=pltpu.SMEM)
-    acc_shape = jax.ShapeDtypeStruct((2, all_rows, 2 * width), jnp.float32)
-    tops_shape = jax.ShapeDtypeStruct((2, all_rows, width), jnp.float32)
+    acc_shape = jax.ShapeDtypeStruct((2, width, all_rows), jnp.float32)
+    sum_shape = jax.ShapeDtypeStruct((2, SUBLANES, all_rows), jnp.float32)
+    turned_shape = jax.ShapeDtypeStruct(acc_shape.shape, query_rows.dtype)
     top_shape = jax.ShapeDtypeStruct((2, heads, rows), jnp.float32)
     params = pltpu.CompilerParams(vmem_limit_bytes=40 * 1024 * 1024)
     unit = rows * heads * block_len * width * 4
@@ -396,11 +387,11 @@
         if not is_power(count) or is_power(distance):
             arrived[distance] = along_seq(piece, distance)
 
-    tops, acc = pl.pallas_call(
+    turned, tops, sums, acc = pl.pallas_call(
         functools.partial(local_kernel, coef, rows),
         in_specs=[scalars] + [whole] * 3,
-        out_specs=[whole] * 2,
-        out_shape=[tops_shape, acc_shape],
+        out_specs=[whole] * 4,
+        out_shape=[turned_shape, sum_shape, sum_shape, acc_shape],
         cost_estimate=cost(3, 6_000_000),
         scratch_shapes=[pltpu.VMEM((2, width, block_len), key_rows.dtype)],
         compiler_params=params,
@@ -409,19 +400,19 @@
     kv_buffers = [pltpu.VMEM((2 * block_len, width), jnp.bfloat16)] * 2
     kv_buffers += [pltpu.VMEM((width, 2 * block_len), jnp.bfloat16)]
 
-    def attend(acc, visits):
+    def attend(sums, acc, visits):
         pieces = [part[d] for d in visits for part in (arrived, beside, across, beside_across)]
         return pl.pallas_call(
             functools.partial(middle_kernel, coef, visits),
-            in_specs=[scalars] + [whole] * (3 + len(pieces)),
-            out_specs=whole,
-            out_shape=acc_shape,
+            in_specs=[scalars] + [whole] * (4 + len(pieces)),
+            out_specs=[whole] * 2,
+            out_shape=[sum_shape, acc_shape],
             scratch_shapes=kv_buffers,
-            input_output_aliases={3: 0},
+            input_output_aliases={3: 0, 4: 1},
             cost_estimate=cost(2 * len(visits), 7_000_000),
             compiler_params=params,
             name=f"visitors_from_{visits[0]}",
-        )(sb_here, q_here, tops, acc, *pieces)
+        )(sb_here, turned, tops, sums, acc, *pieces)
 
     def relay(distance):
         if distance in distances and distance not in arrived:
@@ -448,14 +439,14 @@
         spread(ahead)
         for distance in visits:
             beside_across[distance] = along_inner(across[distance])
-        acc = attend(acc, visits)
+        sums, acc = attend(sums, acc, visits)
     across[last], acc = lax.optimization_barrier((across[last], acc))
     beside_across[last] = along_inner(across[last])
 
     flat = [part[d] for d in distances for part in (arrived, beside, across, beside_across)]
     attended, log_total = pl.pallas_call(
         functools.partial(last_kernel, coef, distances),
-        in_specs=[scalars] + [whole] * 7 + [anywhere] * (2 + len(flat)),
+        in_specs=[scalars] + [whole] * 9 + [anywhere] * (2 + len(flat)),
         out_specs=[anywhere, anywhere],
         out_shape=[jax.ShapeDtypeStruct(query_rows.shape, query_rows.dtype), top_shape],
         scratch_shapes=[
@@ -464,7 +455,6 @@
         ]
         + kv_buffers
         + [
-            pltpu.VMEM((rows, width), jnp.float32),
             pltpu.VMEM((2, heads, rows, width), jnp.float32),
             pltpu.VMEM((2, heads, rows, 2 * width), jnp.float32),
             pltpu.SemaphoreType.DMA,
@@ -473,7 +463,7 @@
         cost_estimate=cost(1, 7_000_000),
         compiler_params=params,
         name="last_visitor",
-    )(sb_here, q_here, tops, acc, *flat[-4:], in_hbm[1], in_hbm[2], *flat)
+    )(sb_here, q_here, turned, tops, sums, acc, *flat[-4:], in_hbm[1], in_hbm[2], *flat)
     return attended, log_total
 
 

time: 36.3 us -> 35.8 us (0.986)
  waiting for transfers between devices: 7.71 us -> 9.75 us
  Pallas kernels: 15.7 us -> 13.9 us
  starting transfers between devices: 12 us -> 11.2 us
    pallas_call x1, Pallas kernels: 5.65 us -> 4.33 us  [attend(): pl.pallas_call(functools.partial(middle_kernel, coef, visits), in_specs=[...]
    ppermute x3, waiting for transfers between devices: 4.58 us -> 5.84 us  [along_head(): lax.ppermute(block, 'head', [(i, i ^ 1) for i in range(lax.axis_size('hea...]
    ppermute x6, starting transfers between devices: 1.57 us -> 1.03 us  [along_inner(): return lax.ppermute(block, 'inner', [(0, 1), (1, 0)])]
    ppermute x6, waiting for transfers between devices: 1.04 us -> 1.49 us  [along_inner(): return lax.ppermute(block, 'inner', [(0, 1), (1, 0)])]
  transfers between devices with their start and end apart: 12 -> 12, of which waited for: 5 -> 8; matrix products, arithmetic and copies ran while one was open for 0% -> 0% of each run, Pallas kernels for 28% -> 24%
where the time goes in v4:
time: 35.8 us; the launch traced here: 35.7 us
  Pallas kernels  13.9 us (39%)
  starting transfers between devices  11.2 us (31%)
  waiting for transfers between devices  9.75 us (27%)
  between operations  0.82 us (2%)
    ppermute x3, starting transfers between devices, along_seq(): return lax.ppermute(block, 'seq', route)  7.1 us
    ppermute x3, waiting for transfers between devices, along_head(): lax.ppermute(block, 'head', [(i, i ^ 1) for i in range(lax.axis_size('hea...  5.84 us
    pallas_call x1, Pallas kernels, attend(): pl.pallas_call(functools.partial(middle_kernel, coef, visits), in_specs=[...  4.33 us
    pallas_call x1, Pallas kernels, body(): pl.pallas_call(functools.partial(local_kernel, coef, rows), in_specs=[sca...  4.12 us
    pallas_call x1, Pallas kernels, body(): pl.pallas_call(functools.partial(last_kernel, coef, distances), in_specs=...  4 us
    ppermute x3, starting transfers between devices, along_head(): lax.ppermute(block, 'head', [(i, i ^ 1) for i in range(lax.axis_size('hea...  3.11 us
    ppermute x3, waiting for transfers between devices, along_seq(): return lax.ppermute(block, 'seq', route)  2.43 us
    ppermute x6, waiting for transfers between devices, along_inner(): return lax.ppermute(block, 'inner', [(0, 1), (1, 0)])  1.49 us
  transfers between devices with their start and end apart: 12, of which 8 were waited for; matrix products, arithmetic and copies ran while one was open for 0% of the time, Pallas kernels for 24%

profile of v4, /device:TPU:0, one launch (start us, length us, event | category | flops | bytes accessed | tf_op | source)
XLA Modules:
  0.0 35.7 jit_solution(10274349536187290951)
XLA Ops:
  0.6 1.5 %load.1 = (bf16[2,320,128]{2,1,0:T(8,128)(2,1)S(1)}, bf16[2,1280,128]{2,1,0:T(8,128)(2,1)S(1)}, bf16[2,640,128]{2,1,0:T(8,128)(2,1)S(1)}, bf16[2,640,128]{2,1,0:T(8,128)(2,1)S(1)}, s32[8]{0:T(128)S(1)}) custom-call(bf16[2,320,512]{2,1,0:T(8,128)(2,1)} %q_hbm.1, bf16[2,640,128]{2,1,0:T(8,128)(2,1)} %refs_4_.1, bf16[2,640,128]{2,1,0:T(8,128)(2,1)} %refs_5_.1, ...), custom_call_target="tpu_custom_call" | custom-call | bytes 3000000 | tf_op jit(solution)/shard_map/load/pallas_call | solution.py:374
  2.1 4.1 %collective-permute-start.1 = (bf16[2,320,128]{2,1,0:T(8,128)(2,1)S(1)}, bf16[2,320,128]{2,1,0:T(8,128)(2,1)S(1)}, u32[]{:S(2)}, u32[]{:S(2)}) collective-permute-start(bf16[2,320,128]{2,1,0:T(8,128)(2,1)S(1)} %get-tuple-element.30), channel_id=1, source_target_pairs={{0,8},{4,12},{8,0},{12,4},{1,9},{5,13},{9,1},{13,5},{2,10},{6,14},... | collective-permute-start | bytes 491528 | tf_op jit(solution)/shard_map/along_seq/ppermute | solution.py:346
  6.2 1.6 %collective-permute-start = (bf16[2,320,128]{2,1,0:T(8,128)(2,1)S(1)}, bf16[2,320,128]{2,1,0:T(8,128)(2,1)S(1)}, u32[]{:S(2)}, u32[]{:S(2)}) collective-permute-start(bf16[2,320,128]{2,1,0:T(8,128)(2,1)S(1)} %get-tuple-element.30), channel_id=1, source_target_pairs={{0,4},{4,0},{8,12},{12,8},{1,5},{5,1},{9,13},{13,9},{2,6},{6,2},{1... | collective-permute-start | bytes 491528 | tf_op jit(solution)/shard_map/along_seq/ppermute | solution.py:346
  7.8 4.1 %local_part.1 = (bf16[2,128,1280]{2,1,0:T(8,128)(2,1)S(1)}, f32[2,8,1280]{2,1,0:T(8,128)S(1)}, f32[2,8,1280]{2,1,0:T(8,128)S(1)}, f32[2,128,1280]{2,1,0:T(8,128)S(1)}) custom-call(s32[8]{0:T(128)S(1)} %get-tuple-element.23.sb, bf16[2,1280,128]{2,1,0:T(8,128)(2,1)S(1)} %get-tuple-element.24.q_ref, bf16[2,640,128]{2,1,0:T(8,128)(2,1)S(1)} %get-tuple-element.25.k_ref, ...), custom_call_target="tpu_custom_call" | custom-call | flops 2516582400 | bytes 6000000 | tf_op jit(solution)/shard_map/local_part/pallas_call | solution.py:390
  11.9 2.1 %collective-permute-done.1.refs_4_.refs_10_ = bf16[2,320,128]{2,1,0:T(8,128)(2,1)S(1)} collective-permute-done((bf16[2,320,128]{2,1,0:T(8,128)(2,1)S(1)}, bf16[2,320,128]{2,1,0:T(8,128)(2,1)S(1)}, u32[]{:S(2)}, u32[]{:S(2)}) %collective-permute-start.1) | collective-permute-done | bytes 163872 | tf_op jit(solution)/shard_map/along_seq/ppermute | solution.py:346
  14.0 0.2 collective-permute-done.refs_0_.refs_6_
  14.2 1.6 %collective-permute-start.2 = (bf16[2,320,128]{2,1,0:T(8,128)(2,1)S(1)}, bf16[2,320,128]{2,1,0:T(8,128)(2,1)S(1)}, u32[]{:S(2)}, u32[]{:S(2)}) collective-permute-start(bf16[2,320,128]{2,1,0:T(8,128)(2,1)S(1)} %collective-permute-done.refs_0_.refs_6_), channel_id=1, source_target_pairs={{0,2},{2,0},{1,3},{3,1},{4,6},{6,4},{5,7},{7,5},{8,10},{10,8},{9,1... | collective-permute-start | bytes 491528 | tf_op jit(solution)/shard_map/along_head/ppermute | solution.py:350
  15.8 1.4 %collective-permute-start.4 = (bf16[2,320,128]{2,1,0:T(8,128)(2,1)S(1)}, bf16[2,320,128]{2,1,0:T(8,128)(2,1)S(1)}, u32[]{:S(2)}, u32[]{:S(2)}) collective-permute-start(bf16[2,320,128]{2,1,0:T(8,128)(2,1)S(1)} %collective-permute-done.1.refs_4_.refs_10_), channel_id=1, source_target_pairs={{0,4},{4,0},{8,12},{12,8},{1,5},{5,1},{9,13},{13,9},{2,6},{6,2},{1... | collective-permute-start | bytes 491528 | tf_op jit(solution)/shard_map/along_seq/ppermute | solution.py:346
  17.2 0.5 %collective-permute-start.3 = (bf16[2,320,128]{2,1,0:T(8,128)(2,1)S(1)}, bf16[2,320,128]{2,1,0:T(8,128)(2,1)S(1)}, u32[]{:S(2)}, u32[]{:S(2)}) collective-permute-start(bf16[2,320,128]{2,1,0:T(8,128)(2,1)S(1)} %collective-permute-done.1.refs_4_.refs_10_), channel_id=1, source_target_pairs={{0,2},{2,0},{1,3},{3,1},{4,6},{6,4},{5,7},{7,5},{8,10},{10,8},{9,1... | collective-permute-start | bytes 491528 | tf_op jit(solution)/shard_map/along_head/ppermute | solution.py:350
  17.7 0.0 collective-permute-start.5
  17.7 0.5 %collective-permute-start.7 = (bf16[2,320,128]{2,1,0:T(8,128)(2,1)S(1)}, bf16[2,320,128]{2,1,0:T(8,128)(2,1)S(1)}, u32[]{:S(2)}, u32[]{:S(2)}) collective-permute-start(bf16[2,320,128]{2,1,0:T(8,128)(2,1)S(1)} %collective-permute-done.1.refs_4_.refs_10_), channel_id=1, source_target_pairs={{0,1},{1,0},{2,3},{3,2},{4,5},{5,4},{6,7},{7,6},{8,9},{9,8},{10,11... | collective-permute-start | bytes 491528 | tf_op jit(solution)/shard_map/along_inner/ppermute | solution.py:354
  18.3 2.7 %collective-permute-done.2.refs_2_.refs_8_ = bf16[2,320,128]{2,1,0:T(8,128)(2,1)S(1)} collective-permute-done((bf16[2,320,128]{2,1,0:T(8,128)(2,1)S(1)}, bf16[2,320,128]{2,1,0:T(8,128)(2,1)S(1)}, u32[]{:S(2)}, u32[]{:S(2)}) %collective-permute-start.2) | collective-permute-done | bytes 163872 | tf_op jit(solution)/shard_map/along_head/ppermute | solution.py:350
  21.0 0.1 collective-permute-done.4.refs_0_.refs_14_
  21.1 2.0 %collective-permute-done.3.refs_6_.refs_12_ = bf16[2,320,128]{2,1,0:T(8,128)(2,1)S(1)} collective-permute-done((bf16[2,320,128]{2,1,0:T(8,128)(2,1)S(1)}, bf16[2,320,128]{2,1,0:T(8,128)(2,1)S(1)}, u32[]{:S(2)}, u32[]{:S(2)}) %collective-permute-start.3) | collective-permute-done | bytes 163872 | tf_op jit(solution)/shard_map/along_head/ppermute | solution.py:350
  23.1 0.0 collective-permute-start.6
  23.1 0.5 %collective-permute-start.8 = (bf16[2,320,128]{2,1,0:T(8,128)(2,1)S(1)}, bf16[2,320,128]{2,1,0:T(8,128)(2,1)S(1)}, u32[]{:S(2)}, u32[]{:S(2)}) collective-permute-start(bf16[2,320,128]{2,1,0:T(8,128)(2,1)S(1)} %collective-permute-done.3.refs_6_.refs_12_), channel_id=1, source_target_pairs={{0,1},{1,0},{2,3},{3,2},{4,5},{5,4},{6,7},{7,6},{8,9},{9,8},{10,11... | collective-permute-start | bytes 491528 | tf_op jit(solution)/shard_map/along_inner/ppermute | solution.py:354
  23.6 0.0 collective-permute-start.10
  23.6 0.0 collective-permute-done.5.refs_1_.refs_7_
  23.6 1.0 %collective-permute-start.9 = (bf16[2,320,128]{2,1,0:T(8,128)(2,1)S(1)}, bf16[2,320,128]{2,1,0:T(8,128)(2,1)S(1)}, u32[]{:S(2)}, u32[]{:S(2)}) collective-permute-start(bf16[2,320,128]{2,1,0:T(8,128)(2,1)S(1)} %collective-permute-done.4.refs_0_.refs_14_), channel_id=1, source_target_pairs={{0,2},{2,0},{1,3},{3,1},{4,6},{6,4},{5,7},{7,5},{8,10},{10,8},{9,1... | collective-permute-start | bytes 491528 | tf_op jit(solution)/shard_map/along_head/ppermute | solution.py:350
  24.6 0.0 collective-permute-done.7.refs_5_.refs_11_
  24.6 0.0 collective-permute-done.6.refs_3_.refs_9_
  24.6 0.1 collective-permute-done.8.refs_7_.refs_13_
  24.7 4.3 %visitors_from_1.1 = (f32[2,8,1280]{2,1,0:T(8,128)S(1)}, f32[2,128,1280]{2,1,0:T(8,128)S(1)}) custom-call(s32[8]{0:T(128)S(1)} %get-tuple-element.23.sb, bf16[2,128,1280]{2,1,0:T(8,128)(2,1)S(1)} %get-tuple-element.27.turned_q, f32[2,8,1280]{2,1,0:T(8,128)S(1)} %get-tuple-element.28.top_ref, ...), custom_call_target="tpu_custom_call", output_to_operand_aliasing={{0}: (3, {}), {1}: (4, {})} | custom-call | flops 3355443200 | bytes 7000000 | tf_op jit(solution)/shard_map/visitors_from_1/pallas_call | solution.py:405
  29.0 1.2 %collective-permute-done.9.refs_2_.refs_16_ = bf16[2,320,128]{2,1,0:T(8,128)(2,1)S(1)} collective-permute-done((bf16[2,320,128]{2,1,0:T(8,128)(2,1)S(1)}, bf16[2,320,128]{2,1,0:T(8,128)(2,1)S(1)}, u32[]{:S(2)}, u32[]{:S(2)}) %collective-permute-start.9) | collective-permute-done | bytes 163872 | tf_op jit(solution)/shard_map/along_head/ppermute | solution.py:350
  30.2 0.0 collective-permute-start.11
  30.2 0.0 collective-permute-done.10.refs_1_.refs_15_
  30.2 1.4 %collective-permute-done.11.refs_3_.refs_17_ = bf16[2,320,128]{2,1,0:T(8,128)(2,1)S(1)} collective-permute-done((bf16[2,320,128]{2,1,0:T(8,128)(2,1)S(1)}, bf16[2,320,128]{2,1,0:T(8,128)(2,1)S(1)}, u32[]{:S(2)}, u32[]{:S(2)}) %collective-permute-start.11) | collective-permute-done | bytes 163872 | tf_op jit(solution)/shard_map/along_inner/ppermute | solution.py:354
  31.6 4.0 %last_visitor.1 = (bf16[2,320,512]{2,1,0:T(8,128)(2,1)}, f32[2,4,320]{2,1,0:T(4,128)}) custom-call(s32[8]{0:T(128)S(1)} %get-tuple-element.23.sb, bf16[2,1280,128]{2,1,0:T(8,128)(2,1)S(1)} %get-tuple-element.24.q_ref, bf16[2,128,1280]{2,1,0:T(8,128)(2,1)S(1)} %get-tuple-element.27.turned_q, f32[2,8,1280]{2,1,0:T(8,128)S(1)} %get-tuple-element.28.top_ref, ...), custom_call_target="tpu_custom_call" | custom-call | flops 838860800 | bytes 7000000 | tf_op jit(solution)/shard_map/last_visitor/pallas_call | solution.py:447
Async XLA Ops:
  2.1 11.9 %collective-permute-start.1 = (bf16[2,320,128]{2,1,0:T(8,128)(2,1)S(1)}, bf16[2,320,128]{2,1,0:T(8,128)(2,1)S(1)}, u32[]{:S(2)}, u32[]{:S(2)}) collective-permute-start(bf16[2,320,128]{2,1,0:T(8,128)(2,1)S(1)} %get-tuple-element.30), channel_id=1, source_target_pairs={{0,8},{4,12},{8,0},{12,4},{1,9},{5,13},{9,1},{13,5},{2,10},{6,14},... | collective-permute-start | bytes 491528 | tf_op jit(solution)/shard_map/along_seq/ppermute | solution.py:346
  6.2 8.0 %collective-permute-start = (bf16[2,320,128]{2,1,0:T(8,128)(2,1)S(1)}, bf16[2,320,128]{2,1,0:T(8,128)(2,1)S(1)}, u32[]{:S(2)}, u32[]{:S(2)}) collective-permute-start(bf16[2,320,128]{2,1,0:T(8,128)(2,1)S(1)} %get-tuple-element.30), channel_id=1, source_target_pairs={{0,4},{4,0},{8,12},{12,8},{1,5},{5,1},{9,13},{13,9},{2,6},{6,2},{1... | collective-permute-start | bytes 491528 | tf_op jit(solution)/shard_map/along_seq/ppermute | solution.py:346
  14.2 6.7 %collective-permute-start.2 = (bf16[2,320,128]{2,1,0:T(8,128)(2,1)S(1)}, bf16[2,320,128]{2,1,0:T(8,128)(2,1)S(1)}, u32[]{:S(2)}, u32[]{:S(2)}) collective-permute-start(bf16[2,320,128]{2,1,0:T(8,128)(2,1)S(1)} %collective-permute-done.refs_0_.refs_6_), channel_id=1, source_target_pairs={{0,2},{2,0},{1,3},{3,1},{4,6},{6,4},{5,7},{7,5},{8,10},{10,8},{9,1... | collective-permute-start | bytes 491528 | tf_op jit(solution)/shard_map/along_head/ppermute | solution.py:350
  15.8 5.3 %collective-permute-start.4 = (bf16[2,320,128]{2,1,0:T(8,128)(2,1)S(1)}, bf16[2,320,128]{2,1,0:T(8,128)(2,1)S(1)}, u32[]{:S(2)}, u32[]{:S(2)}) collective-permute-start(bf16[2,320,128]{2,1,0:T(8,128)(2,1)S(1)} %collective-permute-done.1.refs_4_.refs_10_), channel_id=1, source_target_pairs={{0,4},{4,0},{8,12},{12,8},{1,5},{5,1},{9,13},{13,9},{2,6},{6,2},{1... | collective-permute-start | bytes 491528 | tf_op jit(solution)/shard_map/along_seq/ppermute | solution.py:346
  17.2 5.9 %collective-permute-start.3 = (bf16[2,320,128]{2,1,0:T(8,128)(2,1)S(1)}, bf16[2,320,128]{2,1,0:T(8,128)(2,1)S(1)}, u32[]{:S(2)}, u32[]{:S(2)}) collective-permute-start(bf16[2,320,128]{2,1,0:T(8,128)(2,1)S(1)} %collective-permute-done.1.refs_4_.refs_10_), channel_id=1, source_target_pairs={{0,2},{2,0},{1,3},{3,1},{4,6},{6,4},{5,7},{7,5},{8,10},{10,8},{9,1... | collective-permute-start | bytes 491528 | tf_op jit(solution)/shard_map/along_head/ppermute | solution.py:350
  17.7 5.8 %collective-permute-start.5 = (bf16[2,320,128]{2,1,0:T(8,128)(2,1)S(1)}, bf16[2,320,128]{2,1,0:T(8,128)(2,1)S(1)}, u32[]{:S(2)}, u32[]{:S(2)}) collective-permute-start(bf16[2,320,128]{2,1,0:T(8,128)(2,1)S(1)} %collective-permute-done.refs_0_.refs_6_), channel_id=1, source_target_pairs={{0,1},{1,0},{2,3},{3,2},{4,5},{5,4},{6,7},{7,6},{8,9},{9,8},{10,11... | collective-permute-start | bytes 491528 | tf_op jit(solution)/shard_map/along_inner/ppermute | solution.py:354
  17.7 6.9 %collective-permute-start.7 = (bf16[2,320,128]{2,1,0:T(8,128)(2,1)S(1)}, bf16[2,320,128]{2,1,0:T(8,128)(2,1)S(1)}, u32[]{:S(2)}, u32[]{:S(2)}) collective-permute-start(bf16[2,320,128]{2,1,0:T(8,128)(2,1)S(1)} %collective-permute-done.1.refs_4_.refs_10_), channel_id=1, source_target_pairs={{0,1},{1,0},{2,3},{3,2},{4,5},{5,4},{6,7},{7,6},{8,9},{9,8},{10,11... | collective-permute-start | bytes 491528 | tf_op jit(solution)/shard_map/along_inner/ppermute | solution.py:354
  23.1 1.5 %collective-permute-start.6 = (bf16[2,320,128]{2,1,0:T(8,128)(2,1)S(1)}, bf16[2,320,128]{2,1,0:T(8,128)(2,1)S(1)}, u32[]{:S(2)}, u32[]{:S(2)}) collective-permute-start(bf16[2,320,128]{2,1,0:T(8,128)(2,1)S(1)} %collective-permute-done.2.refs_2_.refs_8_), channel_id=1, source_target_pairs={{0,1},{1,0},{2,3},{3,2},{4,5},{5,4},{6,7},{7,6},{8,9},{9,8},{10,11... | collective-permute-start | bytes 491528 | tf_op jit(solution)/shard_map/along_inner/ppermute | solution.py:354
  23.1 1.6 %collective-permute-start.8 = (bf16[2,320,128]{2,1,0:T(8,128)(2,1)S(1)}, bf16[2,320,128]{2,1,0:T(8,128)(2,1)S(1)}, u32[]{:S(2)}, u32[]{:S(2)}) collective-permute-start(bf16[2,320,128]{2,1,0:T(8,128)(2,1)S(1)} %collective-permute-done.3.refs_6_.refs_12_), channel_id=1, source_target_pairs={{0,1},{1,0},{2,3},{3,2},{4,5},{5,4},{6,7},{7,6},{8,9},{9,8},{10,11... | collective-permute-start | bytes 491528 | tf_op jit(solution)/shard_map/along_inner/ppermute | solution.py:354
  23.6 6.6 %collective-permute-start.10 = (bf16[2,320,128]{2,1,0:T(8,128)(2,1)S(1)}, bf16[2,320,128]{2,1,0:T(8,128)(2,1)S(1)}, u32[]{:S(2)}, u32[]{:S(2)}) collective-permute-start(bf16[2,320,128]{2,1,0:T(8,128)(2,1)S(1)} %collective-permute-done.4.refs_0_.refs_14_), channel_id=1, source_target_pairs={{0,1},{1,0},{2,3},{3,2},{4,5},{5,4},{6,7},{7,6},{8,9},{9,8},{10,11... | collective-permute-start | bytes 491528 | tf_op jit(solution)/shard_map/along_inner/ppermute | solution.py:354
  23.6 6.6 %collective-permute-start.9 = (bf16[2,320,128]{2,1,0:T(8,128)(2,1)S(1)}, bf16[2,320,128]{2,1,0:T(8,128)(2,1)S(1)}, u32[]{:S(2)}, u32[]{:S(2)}) collective-permute-start(bf16[2,320,128]{2,1,0:T(8,128)(2,1)S(1)} %collective-permute-done.4.refs_0_.refs_14_), channel_id=1, source_target_pairs={{0,2},{2,0},{1,3},{3,1},{4,6},{6,4},{5,7},{7,5},{8,10},{10,8},{9,1... | collective-permute-start | bytes 491528 | tf_op jit(solution)/shard_map/along_head/ppermute | solution.py:350
  30.2 1.4 %collective-permute-start.11 = (bf16[2,320,128]{2,1,0:T(8,128)(2,1)S(1)}, bf16[2,320,128]{2,1,0:T(8,128)(2,1)S(1)}, u32[]{:S(2)}, u32[]{:S(2)}) collective-permute-start(bf16[2,320,128]{2,1,0:T(8,128)(2,1)S(1)} %collective-permute-done.9.refs_2_.refs_16_), channel_id=1, source_target_pairs={{0,1},{1,0},{2,3},{3,2},{4,5},{5,4},{6,7},{7,6},{8,9},{9,8},{10,11... | collective-permute-start | bytes 491528 | tf_op jit(solution)/shard_map/along_inner/ppermute | solution.py:354

commit v5 on v4

--- a/solution.py
+++ b/solution.py
@@ -46,27 +46,20 @@
     return [(start, min(TILE, count - start)) for start in range(0, count, TILE)]
 
 
-def load_kernel(q_hbm, k_hbm, v_hbm, sb_hbm, piece, q_out, k_out, v_out, sb_out, sems):
+def piece_kernel(k_hbm, v_hbm, sb_hbm, piece, sb_out, sems):
     half = piece.shape[1]
-    rows, width = q_hbm.shape[1], q_out.shape[2]
     inner = lax.axis_index("inner")
     mine = pl.ds(pl.multiple_of(lax.rem(lax.axis_index("head"), 2) * half, half), half)
+    sb_copy = pltpu.make_async_copy(sb_hbm, sb_out, sems.at[1])
     for value, src in enumerate((k_hbm, v_hbm)):
 
         @pl.when(inner == value)
         def _():
             pltpu.make_async_copy(src.at[:, mine], piece, sems.at[0]).start()
 
-    copies = [pltpu.make_async_copy(k_hbm.at[:, mine], piece, sems.at[0])]
-    pairs = [(k_hbm, k_out), (v_hbm, v_out), (sb_hbm, sb_out)]
-    for h in range(q_hbm.shape[2] // width):
-        pairs.append((q_hbm.at[:, :, pl.ds(h * width, width)], q_out.at[:, pl.ds(h * rows, rows)]))
-    for place, (src, dst) in enumerate(pairs):
-        copy = pltpu.make_async_copy(src, dst, sems.at[1 + place])
-        copy.start()
-        copies.append(copy)
-    for copy in copies:
-        copy.wait()
+    sb_copy.start()
+    pltpu.make_async_copy(k_hbm.at[:, mine], piece, sems.at[0]).wait()
+    sb_copy.wait()
 
 
 def weights_of(coef, s, top):
@@ -95,8 +88,18 @@
         finish(now, *chunk)
 
 
-def local_kernel(coef, rows, sb, q_ref, k_ref, v_ref, turned_q, top_ref, sum_ref, acc_ref, turned_v):
+def local_kernel(coef, rows, sb, q_hbm, k_hbm, v_hbm, turned_q, top_ref, sum_ref, acc_ref, q_ref, k_ref, v_ref, turned_v, sems):
     _, all_rows, width = q_ref.shape
+    copies = []
+    for h in range(all_rows // rows):
+        source, target = q_hbm.at[:, :, pl.ds(h * width, width)], q_ref.at[:, pl.ds(h * rows, rows)]
+        copies.append(pltpu.make_async_copy(source, target, sems.at[2 + h]))
+    copies.append(pltpu.make_async_copy(k_hbm, k_ref, sems.at[0]))
+    copies.append(pltpu.make_async_copy(v_hbm, v_ref, sems.at[1]))
+    for copy in copies:
+        copy.start()
+    for copy in copies:
+        copy.wait()
     block_len = k_ref.shape[1]
     hi, _, _ = blocks_of(sb, lax.axis_index("seq"))
     slots = {HI: hi, LO: 1 - hi}
@@ -152,82 +155,72 @@
     in_turn(tiles, score, finish)
 
 
-def place_pieces(parts, k_buf, v_buf, turned):
+def visit_chunks(distance, own, twin, sb, k_buf, v_buf, turned):
     inner = lax.axis_index("inner")
-    own_half = lax.rem(lax.axis_index("head"), 2)
     for value, (own_buf, twin_buf) in enumerate([(k_buf, v_buf), (v_buf, k_buf)]):
 
         @pl.when(inner == value)
         def _():
-            for turn in range(2):
-                half = own_half if turn == 0 else 1 - own_half
-                for piece, buf in zip(parts[2 * turn : 2 * turn + 2], (own_buf, twin_buf)):
-                    size = piece.shape[1]
-                    for slot in range(2):
-                        buf[pl.ds(pl.multiple_of((slot * 2 + half) * size, size), size)] = piece[slot]
-
-    turned[...] = jnp.transpose(v_buf[...])
-
-
-def visit(coef, distance, parts, sb, turned_q, top_ref, sum_ref, acc_ref, buffers):
-    count = lax.axis_size("seq")
+            own_buf[...] = own[...]
+            twin_buf[...] = twin[...]
+
+    for slot in range(2):
+        turned[slot] = jnp.transpose(v_buf[slot])
     me = lax.axis_index("seq")
-    k_buf, v_buf, turned = buffers
-    place_pieces(parts, k_buf, v_buf, turned)
-    keys_here = k_buf.shape[0] // 2
-
     _, _, top_block = blocks_of(sb, me)
-    other_hi, _, other_top = blocks_of(sb, source_of(me, distance, count))
+    other_hi, _, other_top = blocks_of(sb, source_of(me, distance, lax.axis_size("seq")))
     above = top_block > other_top
-
-    def run(orders, first_key, key_count):
-        tiles = key_tiles(key_count)
-        totals = {}
-
-        def at(start, size):
-            first = first_key + start
-            return pl.ds(first if isinstance(first, int) else pl.multiple_of(first, 128), size)
-
-        def score(order, start, size):
-            return value_dot(k_buf[at(start, size)], turned_q[order])
-
-        def finish(s, order, start, size):
-            p, sums = weights_of(coef, s, top_ref[order])
-            part = value_dot(turned[:, at(start, size)], p)
-            before = totals[order] if start else (acc_ref[order], sum_ref[order])
-            totals[order] = before[0] + part, before[1] + sums
-            if start == tiles[-1][0]:
-                acc_ref[order], sum_ref[order] = totals[order]
-
-        in_turn([(order, *tile) for order in orders for tile in tiles], score, finish)
-
-    @pl.when(above)
-    def _():
-        run((HI,), 0, 2 * keys_here)
-
-    @pl.when(jnp.logical_not(above))
-    def _():
-        run((HI, LO), pl.multiple_of((1 - other_hi) * keys_here, keys_here), keys_here)
+    first = (HI, jnp.where(above, 0, 1 - other_hi))
+    return first, (jnp.where(above, HI, LO), jnp.where(above, 1, 1 - other_hi))
+
+
+def attend(coef, visits, sb, turned_q, top_ref, sum_ref, acc_ref, buffers, done=None):
+    chunks, ends = [], []
+    laid_out = [visit_chunks(*visit, sb, *buffers[3 * i : 3 * i + 3]) for i, visit in enumerate(visits)]
+    for place, pairs in enumerate(laid_out):
+        k_buf, _, turned = buffers[3 * place : 3 * place + 3]
+        tiles = key_tiles(k_buf.shape[1])
+        for order, slot in pairs:
+            for tile in tiles:
+                chunks.append((len(ends), order, slot, k_buf, turned, *tile))
+            ends.append(tiles[-1][0])
+    totals = {}
+
+    def score(place, order, slot, k_buf, turned, start, size):
+        return value_dot(k_buf[slot, pl.ds(start, size)], turned_q[order])
+
+    def finish(s, place, order, slot, k_buf, turned, start, size):
+        p, sums = weights_of(coef, s, top_ref[order])
+        part = value_dot(turned[slot, :, pl.ds(start, size)], p)
+        if start:
+            part, sums = totals[place][0] + part, totals[place][1] + sums
+        totals[place] = part, sums
+        if start == ends[place]:
+            acc_ref[order] += part
+            sum_ref[order] += sums
+            if done is not None:
+                done(place, laid_out[-1][1][0])
+
+    in_turn(chunks, score, finish)
 
 
 def first_row(x):
     return jnp.transpose(x)[:1]
 
 
-def middle_kernel(coef, visits, sb, turned_q, top_ref, sum_in, acc_in, *refs):
-    pieces, (sum_ref, acc_ref, *buffers) = refs[: 4 * len(visits)], refs[4 * len(visits) :]
-    for place, distance in enumerate(visits):
-        visit(coef, distance, pieces[4 * place : 4 * place + 4], sb, turned_q, top_ref, sum_ref, acc_ref, buffers)
-
-
-def last_kernel(coef, distances, sb, q_ref, turned_q, top_ref, sum_ref, acc_ref, *refs):
-    parts, every, rest = refs[:4], refs[4 : 4 * len(distances) + 6], refs[4 * len(distances) + 6 :]
-    out_hbm, lse_hbm, out_buf, lse_ref, *buffers, run_top, run_acc, sem, out_sems = rest
-    rows = out_buf.shape[1]
-    all_rows = q_ref.shape[1]
-    heads = all_rows // rows
-    k_buf, v_buf, _ = buffers
-    block_len, width = k_buf.shape[0] // 2, k_buf.shape[1]
+def middle_kernel(coef, distances, sb, turned_q, top_ref, sum_in, acc_in, *refs):
+    count = len(distances)
+    visits = [(d, refs[2 * i], refs[2 * i + 1]) for i, d in enumerate(distances)]
+    sum_ref, acc_ref, *buffers = refs[2 * count :]
+    attend(coef, visits, sb, turned_q, top_ref, sum_ref, acc_ref, buffers)
+
+
+def last_kernel(coef, distances, sb, turned_q, top_ref, sum_ref, acc_ref, own, twin, *refs):
+    every, rest = refs[: 4 * len(distances) + 3], refs[4 * len(distances) + 3 :]
+    out_hbm, lse_hbm, out_buf, lse_ref, *buffers, worst, k_buf, v_buf, run_top, run_acc, sem, out_sems = rest
+    _, rows, feats = out_buf.shape
+    width = k_buf.shape[1]
+    block_len, heads = k_buf.shape[0] // 2, feats // width
     half_len = block_len // 2
     count = lax.axis_size("seq")
     me = lax.axis_index("seq")
@@ -236,9 +229,8 @@
     hi, lo_block, hi_block = blocks_of(sb, me)
     lse_copy = pltpu.make_async_copy(lse_ref, lse_hbm, sem)
 
-    def out_copy(h):
-        columns = pl.ds(h * width, width)
-        return pltpu.make_async_copy(out_buf.at[:, :, columns], out_hbm.at[:, :, columns], out_sems.at[h])
+    def out_copy(slot):
+        return pltpu.make_async_copy(out_buf.at[slot], out_hbm.at[slot], out_sems.at[slot])
 
     def emit(order, h, value, top):
         slot = hi if order == HI else 1 - hi
@@ -246,26 +238,26 @@
         out_buf[slot, :, h * width : (h + 1) * width] = (value[:, :width] / sums).astype(out_buf.dtype)
         lse_ref[slot, h : h + 1, :] = first_row(top * (coef * math.log(2.0)) + jnp.log(sums))
 
-    visit(coef, distances[-1], parts, sb, turned_q, top_ref, sum_ref, acc_ref, buffers)
-    worst = None
-    for order in (LO, HI):
-        slot = hi if order == HI else 1 - hi
+    def done(place, last_order):
+        order = 1 - last_order if place == 0 else last_order
+        slot = jnp.where(order == HI, hi, 1 - hi)
         sums = jnp.sum(sum_ref[order], axis=0, keepdims=True)
-        worst = sums if worst is None else jnp.maximum(worst, sums)
         log_total = top_ref[order][:1] * (coef * math.log(2.0)) + jnp.log(sums)
-        settled = jnp.transpose(acc_ref[order] * (1.0 / sums)).astype(out_buf.dtype)
+        settled = jnp.transpose((acc_ref[order] * (1.0 / sums)).astype(out_buf.dtype))
         for h in range(heads):
             mine = slice(h * rows, (h + 1) * rows)
             lse_ref[slot, h : h + 1, :] = log_total[:, mine]
             out_buf[slot, :, h * width : (h + 1) * width] = settled[mine]
-    for h in range(heads):
-        out_copy(h).start()
+        worst[place : place + 1] = sums
+        out_copy(slot).start()
+
+    attend(coef, [(distances[-1], own, twin)], sb, turned_q, top_ref, sum_ref, acc_ref, buffers, done)
     lse_copy.start()
-    for h in range(heads):
-        out_copy(h).wait()
+    for slot in range(2):
+        out_copy(slot).wait()
     lse_copy.wait()
 
-    @pl.when(jnp.logical_not(jnp.max(worst) < SUM_LIMIT))
+    @pl.when(jnp.logical_not(jnp.max(worst[...]) < SUM_LIMIT))
     def _():
         def fetch(src, dst):
             copy = pltpu.make_async_copy(src, dst, sem)
@@ -282,7 +274,7 @@
                 @pl.when(shift + rows > 0)
                 def _():
                     own_slot = jnp.where(order == HI, hi, 1 - hi)
-                    queries = q_ref[own_slot, pl.ds(pl.multiple_of(h * rows, rows), rows)]
+                    queries = out_buf[own_slot, :, pl.ds(pl.multiple_of(h * width, width), width)]
                     at = pl.ds(pl.multiple_of(slot * block_len, block_len), block_len)
                     s = score_dot(queries, k_buf[at])
                     row = lax.broadcasted_iota(jnp.int32, s.shape, 0) + shift
@@ -302,12 +294,13 @@
         def rows_of(slot, half):
             return pl.ds(pl.multiple_of((slot * 2 + half) * half_len, half_len), half_len)
 
+        fetch(every[2], out_buf)
         for slot in range(2):
             fetch(every[0].at[slot], k_buf.at[pl.ds(slot * block_len, block_len)])
             fetch(every[1].at[slot], v_buf.at[pl.ds(slot * block_len, block_len)])
         online(me)
         for place, other in enumerate(distances):
-            others = every[2 + 4 * place : 6 + 4 * place]
+            others = every[3 + 4 * place : 7 + 4 * place]
             for value, (own_buf, twin_buf) in enumerate([(k_buf, v_buf), (v_buf, k_buf)]):
 
                 @pl.when(inner == value)
@@ -322,10 +315,10 @@
         for h in range(heads):
             for order in (LO, HI):
                 emit(order, h, run_acc[order, h], run_top[order, h])
-            out_copy(h).start()
-            out_copy(h).wait()
-        lse_copy.start()
-        lse_copy.wait()
+        for copy in (lse_copy, out_copy(0), out_copy(1)):
+            copy.start()
+        for copy in (lse_copy, out_copy(0), out_copy(1)):
+            copy.wait()
 
 
 def body(query_rows, key_rows, value_rows, slot_block):
@@ -371,17 +364,16 @@
         pltpu.with_memory_space_constraint(x, pltpu.HBM) for x in (query_rows, key_rows, value_rows, slot_block)
     ]
     half_shape = jax.ShapeDtypeStruct((2, block_len // 2, width), key_rows.dtype)
-    piece, q_here, k_here, v_here, sb_here = pl.pallas_call(
-        load_kernel,
-        in_specs=[anywhere] * 4,
-        out_specs=[whole] * 5,
-        out_shape=[half_shape, jax.ShapeDtypeStruct((2, all_rows, width), query_rows.dtype)]
-        + [jax.ShapeDtypeStruct(x.shape, x.dtype) for x in in_hbm[1:]],
-        scratch_shapes=[pltpu.SemaphoreType.DMA((4 + heads,))],
-        cost_estimate=pl.CostEstimate(flops=0, bytes_accessed=3_000_000, transcendentals=0),
+    piece, sb_here = pl.pallas_call(
+        piece_kernel,
+        in_specs=[anywhere] * 3,
+        out_specs=[whole] * 2,
+        out_shape=[half_shape, jax.ShapeDtypeStruct(slot_block.shape, slot_block.dtype)],
+        scratch_shapes=[pltpu.SemaphoreType.DMA((2,))],
+        cost_estimate=pl.CostEstimate(flops=0, bytes_accessed=400_000, transcendentals=0),
         compiler_params=params,
-        name="load",
-    )(*in_hbm)
+        name="pick_piece",
+    )(*in_hbm[1:])
     arrived, across, beside, beside_across = {}, {}, {}, {}
     for distance in reversed(distances):
         if not is_power(count) or is_power(distance):
@@ -389,30 +381,44 @@
 
     turned, tops, sums, acc = pl.pallas_call(
         functools.partial(local_kernel, coef, rows),
-        in_specs=[scalars] + [whole] * 3,
+        in_specs=[scalars] + [anywhere] * 3,
         out_specs=[whole] * 4,
         out_shape=[turned_shape, sum_shape, sum_shape, acc_shape],
         cost_estimate=cost(3, 6_000_000),
-        scratch_shapes=[pltpu.VMEM((2, width, block_len), key_rows.dtype)],
+        scratch_shapes=[
+            pltpu.VMEM((2, all_rows, width), query_rows.dtype),
+            pltpu.VMEM(key_rows.shape, key_rows.dtype),
+            pltpu.VMEM(key_rows.shape, key_rows.dtype),
+            pltpu.VMEM((2, width, block_len), key_rows.dtype),
+            pltpu.SemaphoreType.DMA((2 + heads,)),
+        ],
         compiler_params=params,
         name="local_part",
-    )(sb_here, q_here, k_here, v_here)
-    kv_buffers = [pltpu.VMEM((2 * block_len, width), jnp.bfloat16)] * 2
-    kv_buffers += [pltpu.VMEM((width, 2 * block_len), jnp.bfloat16)]
-
-    def attend(sums, acc, visits):
-        pieces = [part[d] for d in visits for part in (arrived, beside, across, beside_across)]
+    )(sb_here, *in_hbm[:3])
+    half_buffers = [
+        pltpu.VMEM(half_shape.shape, half_shape.dtype),
+        pltpu.VMEM(half_shape.shape, half_shape.dtype),
+        pltpu.VMEM((2, width, block_len // 2), half_shape.dtype),
+    ]
+
+    def near_half(distance):
+        return distance, arrived[distance], beside[distance]
+
+    def far_half(distance):
+        return distance, across[distance], beside_across[distance]
+
+    def attended_with(sums, acc, visits):
         return pl.pallas_call(
-            functools.partial(middle_kernel, coef, visits),
-            in_specs=[scalars] + [whole] * (4 + len(pieces)),
+            functools.partial(middle_kernel, coef, [visit[0] for visit in visits]),
+            in_specs=[scalars] + [whole] * (4 + 2 * len(visits)),
             out_specs=[whole] * 2,
             out_shape=[sum_shape, acc_shape],
-            scratch_shapes=kv_buffers,
+            scratch_shapes=half_buffers * len(visits),
             input_output_aliases={3: 0, 4: 1},
-            cost_estimate=cost(2 * len(visits), 7_000_000),
+            cost_estimate=cost(len(visits), 4_000_000),
             compiler_params=params,
-            name=f"visitors_from_{visits[0]}",
-        )(sb_here, turned, tops, sums, acc, *pieces)
+            name="visits_of_" + "_".join(str(visit[0]) for visit in visits),
+        )(sb_here, turned, tops, sums, acc, *(part for visit in visits for part in visit[1:]))
 
     def relay(distance):
         if distance in distances and distance not in arrived:
@@ -425,45 +431,49 @@
             beside[distance] = along_inner(arrived[distance])
 
     last = distances[-1]
-    groups = [distances[:2]] + [[d] for d in distances[2:-1]] if count > 3 else [[d] for d in distances[:-1]]
     for distance in sorted(arrived, reverse=True):
         arrived[distance], acc = lax.optimization_barrier((arrived[distance], acc))
-    for distance in groups[0]:
+    waiting = distances[:2]
+    for distance in waiting:
         spread(distance)
-    for visits in groups:
-        ahead = visits[-1] + 1
+    relay(3)
+    sums, acc = attended_with(sums, acc, [near_half(d) for d in waiting])
+    for ahead in distances[2:]:
         relay(ahead)
-        tied = lax.optimization_barrier(([across[d] for d in visits], arrived[ahead], acc))
-        sides, arrived[ahead], acc = tied
-        across.update(zip(visits, sides))
+        arrived[ahead], acc = lax.optimization_barrier((arrived[ahead], acc))
         spread(ahead)
-        for distance in visits:
+        for distance in waiting:
+            across[distance], acc = lax.optimization_barrier((across[distance], acc))
             beside_across[distance] = along_inner(across[distance])
-        sums, acc = attend(sums, acc, visits)
+        sums, acc = attended_with(sums, acc, [far_half(d) for d in waiting] + [near_half(ahead)])
+        waiting = [ahead]
     across[last], acc = lax.optimization_barrier((across[last], acc))
     beside_across[last] = along_inner(across[last])
 
     flat = [part[d] for d in distances for part in (arrived, beside, across, beside_across)]
     attended, log_total = pl.pallas_call(
         functools.partial(last_kernel, coef, distances),
-        in_specs=[scalars] + [whole] * 9 + [anywhere] * (2 + len(flat)),
+        in_specs=[scalars] + [whole] * 6 + [anywhere] * (3 + len(flat)),
         out_specs=[anywhere, anywhere],
         out_shape=[jax.ShapeDtypeStruct(query_rows.shape, query_rows.dtype), top_shape],
         scratch_shapes=[
             pltpu.VMEM(query_rows.shape, query_rows.dtype),
             pltpu.VMEM(top_shape.shape, jnp.float32),
         ]
-        + kv_buffers
+        + half_buffers
         + [
+            pltpu.VMEM((2, all_rows), jnp.float32),
+            pltpu.VMEM((2 * block_len, width), key_rows.dtype),
+            pltpu.VMEM((2 * block_len, width), key_rows.dtype),
             pltpu.VMEM((2, heads, rows, width), jnp.float32),
             pltpu.VMEM((2, heads, rows, 2 * width), jnp.float32),
             pltpu.SemaphoreType.DMA,
-            pltpu.SemaphoreType.DMA((heads,)),
+            pltpu.SemaphoreType.DMA((2,)),
         ],
         cost_estimate=cost(1, 7_000_000),
         compiler_params=params,
         name="last_visitor",
-    )(sb_here, q_here, turned, tops, sums, acc, *flat[-4:], in_hbm[1], in_hbm[2], *flat)
+    )(sb_here, turned, tops, sums, acc, *far_half(last)[1:], in_hbm[1], in_hbm[2], in_hbm[0], *flat)
     return attended, log_total
 
 

time: 35.8 us -> 37.1 us (1.036)
  Pallas kernels: 13.9 us -> 16.4 us
  waiting for transfers between devices: 9.75 us -> 8.06 us
  starting transfers between devices: 11.2 us -> 11.7 us
    pallas_call x2 -> x3, Pallas kernels: 5.81 us -> 7.54 us  [the longest x2 6.59 us: attended_with(): pl.pallas_call(functools.partial(middle_kernel, coef, [visit[0] for visit...]
    ppermute x3, waiting for transfers between devices: 2.43 us -> 0.85 us  [along_seq(): return lax.ppermute(block, 'seq', route)]
    pallas_call x1, Pallas kernels: 4.12 us -> 5.57 us  [body(): pl.pallas_call(functools.partial(local_kernel, coef, rows), in_specs=[sca...]
    pallas_call x1, Pallas kernels: 4 us -> 3.24 us  [body(): pl.pallas_call(functools.partial(last_kernel, coef, distances), in_specs=...]
    ppermute x3, starting transfers between devices: 3.11 us -> 3.52 us  [along_head(): lax.ppermute(block, 'head', [(i, i ^ 1) for i in range(lax.axis_size('hea...]
  transfers between devices with their start and end apart: 12 -> 12, of which waited for: 8 -> 6; matrix products, arithmetic and copies ran while one was open for 0% -> 0% of each run, Pallas kernels for 24% -> 33%
where the time goes in v5:
time: 37.1 us; the launch traced here: 37 us
  Pallas kernels  16.4 us (44%)
  starting transfers between devices  11.7 us (32%)
  waiting for transfers between devices  8.06 us (22%)
  between operations  0.86 us (2%)
    ppermute x3, starting transfers between devices, along_seq(): return lax.ppermute(block, 'seq', route)  7.16 us
    pallas_call x2, Pallas kernels, attended_with(): pl.pallas_call(functools.partial(middle_kernel, coef, [visit[0] for visit...  6.59 us
    ppermute x3, waiting for transfers between devices, along_head(): lax.ppermute(block, 'head', [(i, i ^ 1) for i in range(lax.axis_size('hea...  5.8 us
    pallas_call x1, Pallas kernels, body(): pl.pallas_call(functools.partial(local_kernel, coef, rows), in_specs=[sca...  5.57 us
    ppermute x3, starting transfers between devices, along_head(): lax.ppermute(block, 'head', [(i, i ^ 1) for i in range(lax.axis_size('hea...  3.52 us
    pallas_call x1, Pallas kernels, body(): pl.pallas_call(functools.partial(last_kernel, coef, distances), in_specs=...  3.24 us
    ppermute x6, waiting for transfers between devices, along_inner(): return lax.ppermute(block, 'inner', [(0, 1), (1, 0)])  1.41 us
    ppermute x6, starting transfers between devices, along_inner(): return lax.ppermute(block, 'inner', [(0, 1), (1, 0)])  1.03 us
  transfers between devices with their start and end apart: 12, of which 6 were waited for; matrix products, arithmetic and copies ran while one was open for 0% of the time, Pallas kernels for 33%

profile of v5, /device:TPU:0, one launch (start us, length us, event | category | flops | bytes accessed | tf_op | source)
XLA Modules:
  0.0 37.0 jit_solution(17799978085186731996)
XLA Ops:
  0.6 1.0 %pick_piece.1 = (bf16[2,320,128]{2,1,0:T(8,128)(2,1)S(1)}, s32[8]{0:T(128)S(1)}) custom-call(bf16[2,640,128]{2,1,0:T(8,128)(2,1)} %refs_0_.1, bf16[2,640,128]{2,1,0:T(8,128)(2,1)} %refs_1_.1, s32[8]{0:T(128)} %sb_hbm.1), custom_call_target="tpu_custom_call" | custom-call | bytes 400000 | tf_op jit(solution)/shard_map/pick_piece/pallas_call | solution.py:367
  1.6 4.1 %collective-permute-start.1 = (bf16[2,320,128]{2,1,0:T(8,128)(2,1)S(1)}, bf16[2,320,128]{2,1,0:T(8,128)(2,1)S(1)}, u32[]{:S(2)}, u32[]{:S(2)}) collective-permute-start(bf16[2,320,128]{2,1,0:T(8,128)(2,1)S(1)} %get-tuple-element.28), channel_id=1, source_target_pairs={{0,8},{4,12},{8,0},{12,4},{1,9},{5,13},{9,1},{13,5},{2,10},{6,14},... | collective-permute-start | bytes 491528 | tf_op jit(solution)/shard_map/along_seq/ppermute | solution.py:339
  5.7 1.6 %collective-permute-start = (bf16[2,320,128]{2,1,0:T(8,128)(2,1)S(1)}, bf16[2,320,128]{2,1,0:T(8,128)(2,1)S(1)}, u32[]{:S(2)}, u32[]{:S(2)}) collective-permute-start(bf16[2,320,128]{2,1,0:T(8,128)(2,1)S(1)} %get-tuple-element.28), channel_id=1, source_target_pairs={{0,4},{4,0},{8,12},{12,8},{1,5},{5,1},{9,13},{13,9},{2,6},{6,2},{1... | collective-permute-start | bytes 491528 | tf_op jit(solution)/shard_map/along_seq/ppermute | solution.py:339
  7.3 5.6 %local_part.1 = (bf16[2,128,1280]{2,1,0:T(8,128)(2,1)S(1)}, f32[2,8,1280]{2,1,0:T(8,128)S(1)}, f32[2,8,1280]{2,1,0:T(8,128)S(1)}, f32[2,128,1280]{2,1,0:T(8,128)S(1)}) custom-call(s32[8]{0:T(128)S(1)} %get-tuple-element.24.sb, bf16[2,320,512]{2,1,0:T(8,128)(2,1)} %refs_2_.1, bf16[2,640,128]{2,1,0:T(8,128)(2,1)} %refs_0_.1, bf16[2,640,128]{2,1,0:T(8,128)(2,1)} %refs_1_.1), custom_call_target="tpu_custom_call" | custom-call | flops 2516582400 | bytes 6000000 | tf_op jit(solution)/shard_map/local_part/pallas_call | solution.py:382
  12.8 0.7 %collective-permute-done.1.refs_2_.refs_7_ = bf16[2,320,128]{2,1,0:T(8,128)(2,1)S(1)} collective-permute-done((bf16[2,320,128]{2,1,0:T(8,128)(2,1)S(1)}, bf16[2,320,128]{2,1,0:T(8,128)(2,1)S(1)}, u32[]{:S(2)}, u32[]{:S(2)}) %collective-permute-start.1) | collective-permute-done | bytes 163872 | tf_op jit(solution)/shard_map/along_seq/ppermute | solution.py:339
  13.5 0.2 collective-permute-done.refs_0_.refs_3_
  13.7 0.0 collective-permute-start.2
  13.7 0.5 %collective-permute-start.3 = (bf16[2,320,128]{2,1,0:T(8,128)(2,1)S(1)}, bf16[2,320,128]{2,1,0:T(8,128)(2,1)S(1)}, u32[]{:S(2)}, u32[]{:S(2)}) collective-permute-start(bf16[2,320,128]{2,1,0:T(8,128)(2,1)S(1)} %collective-permute-done.1.refs_2_.refs_7_), channel_id=1, source_target_pairs={{0,1},{1,0},{2,3},{3,2},{4,5},{5,4},{6,7},{7,6},{8,9},{9,8},{10,11... | collective-permute-start | bytes 491528 | tf_op jit(solution)/shard_map/along_inner/ppermute | solution.py:347
  14.2 1.5 %collective-permute-start.6 = (bf16[2,320,128]{2,1,0:T(8,128)(2,1)S(1)}, bf16[2,320,128]{2,1,0:T(8,128)(2,1)S(1)}, u32[]{:S(2)}, u32[]{:S(2)}) collective-permute-start(bf16[2,320,128]{2,1,0:T(8,128)(2,1)S(1)} %collective-permute-done.1.refs_2_.refs_7_), channel_id=1, source_target_pairs={{0,4},{4,0},{8,12},{12,8},{1,5},{5,1},{9,13},{13,9},{2,6},{6,2},{1... | collective-permute-start | bytes 491528 | tf_op jit(solution)/shard_map/along_seq/ppermute | solution.py:339
  15.7 1.5 %collective-permute-start.5 = (bf16[2,320,128]{2,1,0:T(8,128)(2,1)S(1)}, bf16[2,320,128]{2,1,0:T(8,128)(2,1)S(1)}, u32[]{:S(2)}, u32[]{:S(2)}) collective-permute-start(bf16[2,320,128]{2,1,0:T(8,128)(2,1)S(1)} %collective-permute-done.refs_0_.refs_3_), channel_id=1, source_target_pairs={{0,2},{2,0},{1,3},{3,1},{4,6},{6,4},{5,7},{7,5},{8,10},{10,8},{9,1... | collective-permute-start | bytes 491528 | tf_op jit(solution)/shard_map/along_head/ppermute | solution.py:343
  17.2 0.5 %collective-permute-start.4 = (bf16[2,320,128]{2,1,0:T(8,128)(2,1)S(1)}, bf16[2,320,128]{2,1,0:T(8,128)(2,1)S(1)}, u32[]{:S(2)}, u32[]{:S(2)}) collective-permute-start(bf16[2,320,128]{2,1,0:T(8,128)(2,1)S(1)} %collective-permute-done.1.refs_2_.refs_7_), channel_id=1, source_target_pairs={{0,2},{2,0},{1,3},{3,1},{4,6},{6,4},{5,7},{7,5},{8,10},{10,8},{9,1... | collective-permute-start | bytes 491528 | tf_op jit(solution)/shard_map/along_head/ppermute | solution.py:343
  17.7 0.0 collective-permute-done.2.refs_1_.refs_4_
  17.7 0.0 collective-permute-done.3.refs_3_.refs_8_
  17.7 2.8 %visits_of_1_2.1 = (f32[2,8,1280]{2,1,0:T(8,128)S(1)}, f32[2,128,1280]{2,1,0:T(8,128)S(1)}) custom-call(s32[8]{0:T(128)S(1)} %get-tuple-element.24.sb, bf16[2,128,1280]{2,1,0:T(8,128)(2,1)S(1)} %get-tuple-element.25.turned_q, f32[2,8,1280]{2,1,0:T(8,128)S(1)} %get-tuple-element.26.top_ref, ...), custom_call_target="tpu_custom_call", output_to_operand_aliasing={{0}: (3, {}), {1}: (4, {})} | custom-call | flops 1677721600 | bytes 4000000 | tf_op jit(solution)/shard_map/visits_of_1_2/pallas_call | solution.py:411
  20.5 0.0 collective-permute-done.6.refs_4_.refs_11_
  20.5 2.3 %collective-permute-done.5.refs_0_.refs_5_ = bf16[2,320,128]{2,1,0:T(8,128)(2,1)S(1)} collective-permute-done((bf16[2,320,128]{2,1,0:T(8,128)(2,1)S(1)}, bf16[2,320,128]{2,1,0:T(8,128)(2,1)S(1)}, u32[]{:S(2)}, u32[]{:S(2)}) %collective-permute-start.5) | collective-permute-done | bytes 163872 | tf_op jit(solution)/shard_map/along_head/ppermute | solution.py:343
  22.8 2.2 %collective-permute-done.4.refs_2_.refs_9_ = bf16[2,320,128]{2,1,0:T(8,128)(2,1)S(1)} collective-permute-done((bf16[2,320,128]{2,1,0:T(8,128)(2,1)S(1)}, bf16[2,320,128]{2,1,0:T(8,128)(2,1)S(1)}, u32[]{:S(2)}, u32[]{:S(2)}) %collective-permute-start.4) | collective-permute-done | bytes 163872 | tf_op jit(solution)/shard_map/along_head/ppermute | solution.py:343
  25.0 0.0 collective-permute-start.8
  25.0 0.5 %collective-permute-start.7 = (bf16[2,320,128]{2,1,0:T(8,128)(2,1)S(1)}, bf16[2,320,128]{2,1,0:T(8,128)(2,1)S(1)}, u32[]{:S(2)}, u32[]{:S(2)}) collective-permute-start(bf16[2,320,128]{2,1,0:T(8,128)(2,1)S(1)} %collective-permute-done.5.refs_0_.refs_5_), channel_id=1, source_target_pairs={{0,1},{1,0},{2,3},{3,2},{4,5},{5,4},{6,7},{7,6},{8,9},{9,8},{10,11... | collective-permute-start | bytes 491528 | tf_op jit(solution)/shard_map/along_inner/ppermute | solution.py:347
  25.5 0.0 collective-permute-start.9
  25.5 1.5 %collective-permute-start.10 = (bf16[2,320,128]{2,1,0:T(8,128)(2,1)S(1)}, bf16[2,320,128]{2,1,0:T(8,128)(2,1)S(1)}, u32[]{:S(2)}, u32[]{:S(2)}) collective-permute-start(bf16[2,320,128]{2,1,0:T(8,128)(2,1)S(1)} %collective-permute-done.6.refs_4_.refs_11_), channel_id=1, source_target_pairs={{0,2},{2,0},{1,3},{3,1},{4,6},{6,4},{5,7},{7,5},{8,10},{10,8},{9,1... | collective-permute-start | bytes 491528 | tf_op jit(solution)/shard_map/along_head/ppermute | solution.py:343
  27.0 0.0 collective-permute-done.8.refs_3_.refs_10_
  27.0 0.0 collective-permute-done.7.refs_1_.refs_6_
  27.0 0.0 collective-permute-done.9.refs_5_.refs_12_
  27.1 3.8 %visits_of_1_2_3.1 = (f32[2,8,1280]{2,1,0:T(8,128)S(1)}, f32[2,128,1280]{2,1,0:T(8,128)S(1)}) custom-call(s32[8]{0:T(128)S(1)} %get-tuple-element.24.sb, bf16[2,128,1280]{2,1,0:T(8,128)(2,1)S(1)} %get-tuple-element.25.turned_q, f32[2,8,1280]{2,1,0:T(8,128)S(1)} %get-tuple-element.26.top_ref, ...), custom_call_target="tpu_custom_call", output_to_operand_aliasing={{0}: (3, {}), {1}: (4, {})} | custom-call | flops 2516582400 | bytes 4000000 | tf_op jit(solution)/shard_map/visits_of_1_2_3/pallas_call | solution.py:411
  30.9 1.3 %collective-permute-done.10.own.refs_13_ = bf16[2,320,128]{2,1,0:T(8,128)(2,1)S(1)} collective-permute-done((bf16[2,320,128]{2,1,0:T(8,128)(2,1)S(1)}, bf16[2,320,128]{2,1,0:T(8,128)(2,1)S(1)}, u32[]{:S(2)}, u32[]{:S(2)}) %collective-permute-start.10) | collective-permute-done | bytes 163872 | tf_op jit(solution)/shard_map/along_head/ppermute | solution.py:343
  32.2 0.0 collective-permute-start.11
  32.2 1.4 %collective-permute-done.11.twin.refs_14_ = bf16[2,320,128]{2,1,0:T(8,128)(2,1)S(1)} collective-permute-done((bf16[2,320,128]{2,1,0:T(8,128)(2,1)S(1)}, bf16[2,320,128]{2,1,0:T(8,128)(2,1)S(1)}, u32[]{:S(2)}, u32[]{:S(2)}) %collective-permute-start.11) | collective-permute-done | bytes 163872 | tf_op jit(solution)/shard_map/along_inner/ppermute | solution.py:347
  33.6 3.2 %last_visitor.1 = (bf16[2,320,512]{2,1,0:T(8,128)(2,1)}, f32[2,4,320]{2,1,0:T(4,128)}) custom-call(s32[8]{0:T(128)S(1)} %get-tuple-element.24.sb, bf16[2,128,1280]{2,1,0:T(8,128)(2,1)S(1)} %get-tuple-element.25.turned_q, f32[2,8,1280]{2,1,0:T(8,128)S(1)} %get-tuple-element.26.top_ref, f32[2,8,1280]{2,1,0:T(8,128)S(1)} %get-tuple-element.42.sum_ref, ...), custom_call_target="tpu_custom_call" | custom-call | flops 838860800 | bytes 7000000 | tf_op jit(solution)/shard_map/last_visitor/pallas_call | solution.py:454
Async XLA Ops:
  1.6 11.9 %collective-permute-start.1 = (bf16[2,320,128]{2,1,0:T(8,128)(2,1)S(1)}, bf16[2,320,128]{2,1,0:T(8,128)(2,1)S(1)}, u32[]{:S(2)}, u32[]{:S(2)}) collective-permute-start(bf16[2,320,128]{2,1,0:T(8,128)(2,1)S(1)} %get-tuple-element.28), channel_id=1, source_target_pairs={{0,8},{4,12},{8,0},{12,4},{1,9},{5,13},{9,1},{13,5},{2,10},{6,14},... | collective-permute-start | bytes 491528 | tf_op jit(solution)/shard_map/along_seq/ppermute | solution.py:339
  5.7 8.0 %collective-permute-start = (bf16[2,320,128]{2,1,0:T(8,128)(2,1)S(1)}, bf16[2,320,128]{2,1,0:T(8,128)(2,1)S(1)}, u32[]{:S(2)}, u32[]{:S(2)}) collective-permute-start(bf16[2,320,128]{2,1,0:T(8,128)(2,1)S(1)} %get-tuple-element.28), channel_id=1, source_target_pairs={{0,4},{4,0},{8,12},{12,8},{1,5},{5,1},{9,13},{13,9},{2,6},{6,2},{1... | collective-permute-start | bytes 491528 | tf_op jit(solution)/shard_map/along_seq/ppermute | solution.py:339
  13.7 4.0 %collective-permute-start.2 = (bf16[2,320,128]{2,1,0:T(8,128)(2,1)S(1)}, bf16[2,320,128]{2,1,0:T(8,128)(2,1)S(1)}, u32[]{:S(2)}, u32[]{:S(2)}) collective-permute-start(bf16[2,320,128]{2,1,0:T(8,128)(2,1)S(1)} %collective-permute-done.refs_0_.refs_3_), channel_id=1, source_target_pairs={{0,1},{1,0},{2,3},{3,2},{4,5},{5,4},{6,7},{7,6},{8,9},{9,8},{10,11... | collective-permute-start | bytes 491528 | tf_op jit(solution)/shard_map/along_inner/ppermute | solution.py:347
  13.7 4.0 %collective-permute-start.3 = (bf16[2,320,128]{2,1,0:T(8,128)(2,1)S(1)}, bf16[2,320,128]{2,1,0:T(8,128)(2,1)S(1)}, u32[]{:S(2)}, u32[]{:S(2)}) collective-permute-start(bf16[2,320,128]{2,1,0:T(8,128)(2,1)S(1)} %collective-permute-done.1.refs_2_.refs_7_), channel_id=1, source_target_pairs={{0,1},{1,0},{2,3},{3,2},{4,5},{5,4},{6,7},{7,6},{8,9},{9,8},{10,11... | collective-permute-start | bytes 491528 | tf_op jit(solution)/shard_map/along_inner/ppermute | solution.py:347
  14.2 6.3 %collective-permute-start.6 = (bf16[2,320,128]{2,1,0:T(8,128)(2,1)S(1)}, bf16[2,320,128]{2,1,0:T(8,128)(2,1)S(1)}, u32[]{:S(2)}, u32[]{:S(2)}) collective-permute-start(bf16[2,320,128]{2,1,0:T(8,128)(2,1)S(1)} %collective-permute-done.1.refs_2_.refs_7_), channel_id=1, source_target_pairs={{0,4},{4,0},{8,12},{12,8},{1,5},{5,1},{9,13},{13,9},{2,6},{6,2},{1... | collective-permute-start | bytes 491528 | tf_op jit(solution)/shard_map/along_seq/ppermute | solution.py:339
  15.7 7.1 %collective-permute-start.5 = (bf16[2,320,128]{2,1,0:T(8,128)(2,1)S(1)}, bf16[2,320,128]{2,1,0:T(8,128)(2,1)S(1)}, u32[]{:S(2)}, u32[]{:S(2)}) collective-permute-start(bf16[2,320,128]{2,1,0:T(8,128)(2,1)S(1)} %collective-permute-done.refs_0_.refs_3_), channel_id=1, source_target_pairs={{0,2},{2,0},{1,3},{3,1},{4,6},{6,4},{5,7},{7,5},{8,10},{10,8},{9,1... | collective-permute-start | bytes 491528 | tf_op jit(solution)/shard_map/along_head/ppermute | solution.py:343
  17.2 7.8 %collective-permute-start.4 = (bf16[2,320,128]{2,1,0:T(8,128)(2,1)S(1)}, bf16[2,320,128]{2,1,0:T(8,128)(2,1)S(1)}, u32[]{:S(2)}, u32[]{:S(2)}) collective-permute-start(bf16[2,320,128]{2,1,0:T(8,128)(2,1)S(1)} %collective-permute-done.1.refs_2_.refs_7_), channel_id=1, source_target_pairs={{0,2},{2,0},{1,3},{3,1},{4,6},{6,4},{5,7},{7,5},{8,10},{10,8},{9,1... | collective-permute-start | bytes 491528 | tf_op jit(solution)/shard_map/along_head/ppermute | solution.py:343
  25.0 2.0 %collective-permute-start.8 = (bf16[2,320,128]{2,1,0:T(8,128)(2,1)S(1)}, bf16[2,320,128]{2,1,0:T(8,128)(2,1)S(1)}, u32[]{:S(2)}, u32[]{:S(2)}) collective-permute-start(bf16[2,320,128]{2,1,0:T(8,128)(2,1)S(1)} %collective-permute-done.4.refs_2_.refs_9_), channel_id=1, source_target_pairs={{0,1},{1,0},{2,3},{3,2},{4,5},{5,4},{6,7},{7,6},{8,9},{9,8},{10,11... | collective-permute-start | bytes 491528 | tf_op jit(solution)/shard_map/along_inner/ppermute | solution.py:347
  25.0 2.0 %collective-permute-start.7 = (bf16[2,320,128]{2,1,0:T(8,128)(2,1)S(1)}, bf16[2,320,128]{2,1,0:T(8,128)(2,1)S(1)}, u32[]{:S(2)}, u32[]{:S(2)}) collective-permute-start(bf16[2,320,128]{2,1,0:T(8,128)(2,1)S(1)} %collective-permute-done.5.refs_0_.refs_5_), channel_id=1, source_target_pairs={{0,1},{1,0},{2,3},{3,2},{4,5},{5,4},{6,7},{7,6},{8,9},{9,8},{10,11... | collective-permute-start | bytes 491528 | tf_op jit(solution)/shard_map/along_inner/ppermute | solution.py:347
  25.5 1.5 %collective-permute-start.9 = (bf16[2,320,128]{2,1,0:T(8,128)(2,1)S(1)}, bf16[2,320,128]{2,1,0:T(8,128)(2,1)S(1)}, u32[]{:S(2)}, u32[]{:S(2)}) collective-permute-start(bf16[2,320,128]{2,1,0:T(8,128)(2,1)S(1)} %collective-permute-done.6.refs_4_.refs_11_), channel_id=1, source_target_pairs={{0,1},{1,0},{2,3},{3,2},{4,5},{5,4},{6,7},{7,6},{8,9},{9,8},{10,11... | collective-permute-start | bytes 491528 | tf_op jit(solution)/shard_map/along_inner/ppermute | solution.py:347
  25.5 6.6 %collective-permute-start.10 = (bf16[2,320,128]{2,1,0:T(8,128)(2,1)S(1)}, bf16[2,320,128]{2,1,0:T(8,128)(2,1)S(1)}, u32[]{:S(2)}, u32[]{:S(2)}) collective-permute-start(bf16[2,320,128]{2,1,0:T(8,128)(2,1)S(1)} %collective-permute-done.6.refs_4_.refs_11_), channel_id=1, source_target_pairs={{0,2},{2,0},{1,3},{3,1},{4,6},{6,4},{5,7},{7,5},{8,10},{10,8},{9,1... | collective-permute-start | bytes 491528 | tf_op jit(solution)/shard_map/along_head/ppermute | solution.py:343
  32.2 1.4 %collective-permute-start.11 = (bf16[2,320,128]{2,1,0:T(8,128)(2,1)S(1)}, bf16[2,320,128]{2,1,0:T(8,128)(2,1)S(1)}, u32[]{:S(2)}, u32[]{:S(2)}) collective-permute-start(bf16[2,320,128]{2,1,0:T(8,128)(2,1)S(1)} %collective-permute-done.10.own.refs_13_), channel_id=1, source_target_pairs={{0,1},{1,0},{2,3},{3,2},{4,5},{5,4},{6,7},{7,6},{8,9},{9,8},{10,11... | collective-permute-start | bytes 491528 | tf_op jit(solution)/shard_map/along_inner/ppermute | solution.py:347

commit v6 on v5

--- a/solution.py
+++ b/solution.py
@@ -62,9 +62,23 @@
     sb_copy.wait()
 
 
-def weights_of(coef, s, top):
-    p = jnp.exp2((s - down(top, s.shape[0])) * coef)
+def weights_of(coef, s):
+    p = jnp.exp2(s * coef)
     return p.astype(jnp.bfloat16), folded(jnp.add, p)
+
+
+def with_ones(x):
+    return jnp.concatenate([x, jnp.ones_like(x)], axis=1)
+
+
+def minus_rows(top, height):
+    high = top.astype(jnp.bfloat16).astype(jnp.float32)
+    middle = (top - high).astype(jnp.bfloat16).astype(jnp.float32)
+    low = top - high - middle
+    row = lax.broadcasted_iota(jnp.int32, top.shape, 0)
+    picked = jnp.where(row == 0, high, jnp.where(row == 1, middle, jnp.where(row == 2, low, 0.0)))
+    zeros = jnp.zeros((height - top.shape[0], top.shape[1]), jnp.float32)
+    return jnp.concatenate([-picked, zeros], axis=0).astype(jnp.bfloat16)
 
 
 def down(x, height):
@@ -88,7 +102,7 @@
         finish(now, *chunk)
 
 
-def local_kernel(coef, rows, sb, q_hbm, k_hbm, v_hbm, turned_q, top_ref, sum_ref, acc_ref, q_ref, k_ref, v_ref, turned_v, sems):
+def diagonal_kernel(coef, rows, sb, q_hbm, k_hbm, v_hbm, turned_q, top_ref, sum_ref, acc_ref, k_ref, turned_v, q_ref, v_ref, sems):
     _, all_rows, width = q_ref.shape
     copies = []
     for h in range(all_rows // rows):
@@ -105,7 +119,7 @@
     slots = {HI: hi, LO: 1 - hi}
     tiles = key_tiles(block_len)
     for order in (HI, LO):
-        turned_q[order] = jnp.transpose(q_ref[slots[order]])
+        turned_q[order, pl.ds(0, width)] = jnp.transpose(q_ref[slots[order]])
         turned_v[order] = jnp.transpose(v_ref[slots[order]])
 
     def keys(order, start, size):
@@ -119,7 +133,7 @@
         heads_below = sum((lane >= at).astype(jnp.int32) for at in range(rows, all_rows, rows))
         row = lane - heads_below * rows + lax.axis_index("inner") * rows
         key = lax.broadcasted_iota(jnp.int32, (size, all_rows), 0) + start
-        s = value_dot(keys(order, start, size), turned_q[order])
+        s = value_dot(keys(order, start, size), turned_q[order, pl.ds(0, width)])
         return jnp.where(key <= down(row, size), s, NEG)
 
     def highest(scores):
@@ -129,30 +143,40 @@
     def settle(order, scores, top):
         total, sums = None, None
         for (start, size), s in zip(tiles, scores):
-            p, more = weights_of(coef, s, top)
+            p, more = weights_of(coef, s - down(top, size))
             part = value_dot(values(order, start, size), p)
             total, sums = (part, more) if total is None else (total + part, sums + more)
         acc_ref[order] = total
         sum_ref[order] = sums
 
+    def extend(order, scores):
+        top = highest(scores)
+        top_ref[order] = top
+        turned_q[order, pl.ds(width, width)] = minus_rows(top, width)
+        return top
+
     diag = [masked(HI, *tile) for tile in tiles]
-    top = highest(diag)
-    top_ref[HI] = top
+    top = extend(HI, diag)
     low = [masked(LO, *tile) for tile in tiles]
     settle(HI, diag, top)
-    top = highest(low)
-    top_ref[LO] = top
+    settle(LO, low, extend(LO, low))
+
+
+def past_kernel(coef, sb, turned_q, sum_in, acc_in, k_ref, turned_v, sum_ref, acc_ref):
+    hi, _, _ = blocks_of(sb, lax.axis_index("seq"))
+    tiles = key_tiles(k_ref.shape[1])
+    totals = []
 
     def score(start, size):
-        return value_dot(keys(LO, start, size), turned_q[HI])
+        return value_dot(with_ones(k_ref[1 - hi, pl.ds(start, size)]), turned_q[HI])
 
     def finish(s, start, size):
-        p, more = weights_of(coef, s, top_ref[HI])
-        acc_ref[HI] += value_dot(values(LO, start, size), p)
-        sum_ref[HI] += more
-
-    settle(LO, low, top)
+        p, sums = weights_of(coef, s)
+        totals.append((value_dot(turned_v[LO, :, pl.ds(start, size)], p), sums))
+
     in_turn(tiles, score, finish)
+    acc_ref[HI] += functools.reduce(jnp.add, [part for part, _ in totals])
+    sum_ref[HI] += functools.reduce(jnp.add, [sums for _, sums in totals])
 
 
 def visit_chunks(distance, own, twin, sb, k_buf, v_buf, turned):
@@ -174,7 +198,7 @@
     return first, (jnp.where(above, HI, LO), jnp.where(above, 1, 1 - other_hi))
 
 
-def attend(coef, visits, sb, turned_q, top_ref, sum_ref, acc_ref, buffers, done=None):
+def attend(coef, visits, sb, turned_q, sum_ref, acc_ref, buffers, done=None):
     chunks, ends = [], []
     laid_out = [visit_chunks(*visit, sb, *buffers[3 * i : 3 * i + 3]) for i, visit in enumerate(visits)]
     for place, pairs in enumerate(laid_out):
@@ -187,10 +211,10 @@
     totals = {}
 
     def score(place, order, slot, k_buf, turned, start, size):
-        return value_dot(k_buf[slot, pl.ds(start, size)], turned_q[order])
+        return value_dot(with_ones(k_buf[slot, pl.ds(start, size)]), turned_q[order])
 
     def finish(s, place, order, slot, k_buf, turned, start, size):
-        p, sums = weights_of(coef, s, top_ref[order])
+        p, sums = weights_of(coef, s)
         part = value_dot(turned[slot, :, pl.ds(start, size)], p)
         if start:
             part, sums = totals[place][0] + part, totals[place][1] + sums
@@ -208,11 +232,11 @@
     return jnp.transpose(x)[:1]
 
 
-def middle_kernel(coef, distances, sb, turned_q, top_ref, sum_in, acc_in, *refs):
+def middle_kernel(coef, distances, sb, turned_q, sum_in, acc_in, *refs):
     count = len(distances)
     visits = [(d, refs[2 * i], refs[2 * i + 1]) for i, d in enumerate(distances)]
     sum_ref, acc_ref, *buffers = refs[2 * count :]
-    attend(coef, visits, sb, turned_q, top_ref, sum_ref, acc_ref, buffers)
+    attend(coef, visits, sb, turned_q, sum_ref, acc_ref, buffers)
 
 
 def last_kernel(coef, distances, sb, turned_q, top_ref, sum_ref, acc_ref, own, twin, *refs):
@@ -251,13 +275,14 @@
         worst[place : place + 1] = sums
         out_copy(slot).start()
 
-    attend(coef, [(distances[-1], own, twin)], sb, turned_q, top_ref, sum_ref, acc_ref, buffers, done)
+    attend(coef, [(distances[-1], own, twin)], sb, turned_q, sum_ref, acc_ref, buffers, done)
+    fits = jnp.max(worst[...]) < SUM_LIMIT
     lse_copy.start()
     for slot in range(2):
         out_copy(slot).wait()
     lse_copy.wait()
 
-    @pl.when(jnp.logical_not(jnp.max(worst[...]) < SUM_LIMIT))
+    @pl.when(jnp.logical_not(fits))
     def _():
         def fetch(src, dst):
             copy = pltpu.make_async_copy(src, dst, sem)
@@ -351,7 +376,7 @@
     scalars = pl.BlockSpec(memory_space=pltpu.SMEM)
     acc_shape = jax.ShapeDtypeStruct((2, width, all_rows), jnp.float32)
     sum_shape = jax.ShapeDtypeStruct((2, SUBLANES, all_rows), jnp.float32)
-    turned_shape = jax.ShapeDtypeStruct(acc_shape.shape, query_rows.dtype)
+    turned_shape = jax.ShapeDtypeStruct((2, 2 * width, all_rows), query_rows.dtype)
     top_shape = jax.ShapeDtypeStruct((2, heads, rows), jnp.float32)
     params = pltpu.CompilerParams(vmem_limit_bytes=40 * 1024 * 1024)
     unit = rows * heads * block_len * width * 4
@@ -379,21 +404,21 @@
         if not is_power(count) or is_power(distance):
             arrived[distance] = along_seq(piece, distance)
 
-    turned, tops, sums, acc = pl.pallas_call(
-        functools.partial(local_kernel, coef, rows),
+    turned_kv = jax.ShapeDtypeStruct((2, width, block_len), key_rows.dtype)
+    turned, tops, sums, acc, k_here, v_turned = pl.pallas_call(
+        functools.partial(diagonal_kernel, coef, rows),
         in_specs=[scalars] + [anywhere] * 3,
-        out_specs=[whole] * 4,
-        out_shape=[turned_shape, sum_shape, sum_shape, acc_shape],
-        cost_estimate=cost(3, 6_000_000),
+        out_specs=[whole] * 6,
+        out_shape=[turned_shape, sum_shape, sum_shape, acc_shape]
+        + [jax.ShapeDtypeStruct(key_rows.shape, key_rows.dtype), turned_kv],
         scratch_shapes=[
             pltpu.VMEM((2, all_rows, width), query_rows.dtype),
             pltpu.VMEM(key_rows.shape, key_rows.dtype),
-            pltpu.VMEM(key_rows.shape, key_rows.dtype),
-            pltpu.VMEM((2, width, block_len), key_rows.dtype),
             pltpu.SemaphoreType.DMA((2 + heads,)),
         ],
+        cost_estimate=cost(2, 6_000_000),
         compiler_params=params,
-        name="local_part",
+        name="diagonal",
     )(sb_here, *in_hbm[:3])
     half_buffers = [
         pltpu.VMEM(half_shape.shape, half_shape.dtype),
@@ -410,15 +435,15 @@
     def attended_with(sums, acc, visits):
         return pl.pallas_call(
             functools.partial(middle_kernel, coef, [visit[0] for visit in visits]),
-            in_specs=[scalars] + [whole] * (4 + 2 * len(visits)),
+            in_specs=[scalars] + [whole] * (3 + 2 * len(visits)),
             out_specs=[whole] * 2,
             out_shape=[sum_shape, acc_shape],
             scratch_shapes=half_buffers * len(visits),
-            input_output_aliases={3: 0, 4: 1},
+            input_output_aliases={2: 0, 3: 1},
             cost_estimate=cost(len(visits), 4_000_000),
             compiler_params=params,
             name="visits_of_" + "_".join(str(visit[0]) for visit in visits),
-        )(sb_here, turned, tops, sums, acc, *(part for visit in visits for part in visit[1:]))
+        )(sb_here, turned, sums, acc, *(part for visit in visits for part in visit[1:]))
 
     def relay(distance):
         if distance in distances and distance not in arrived:
@@ -437,6 +462,16 @@
     for distance in waiting:
         spread(distance)
     relay(3)
+    sums, acc = pl.pallas_call(
+        functools.partial(past_kernel, coef),
+        in_specs=[scalars] + [whole] * 5,
+        out_specs=[whole] * 2,
+        out_shape=[sum_shape, acc_shape],
+        input_output_aliases={2: 0, 3: 1},
+        cost_estimate=cost(1, 4_000_000),
+        compiler_params=params,
+        name="past",
+    )(sb_here, turned, sums, acc, k_here, v_turned)
     sums, acc = attended_with(sums, acc, [near_half(d) for d in waiting])
     for ahead in distances[2:]:
         relay(ahead)

time: 37.1 us -> 35.6 us (0.960)
  waiting for transfers between devices: 8.06 us -> 5.59 us
  Pallas kernels: 16.4 us -> 17.2 us
    ppermute x3, waiting for transfers between devices: 5.8 us -> 2.74 us  [along_head(): lax.ppermute(block, 'head', [(i, i ^ 1) for i in range(lax.axis_size('hea...]
    pallas_call x1 -> x2, Pallas kernels: 5.57 us -> 6.48 us  [the longest x1 4.99 us: body(): pl.pallas_call(functools.partial(diagonal_kernel, coef, rows), in_specs=[...]
    ppermute x3, waiting for transfers between devices: 0.85 us -> 1.44 us  [along_seq(): return lax.ppermute(block, 'seq', route)]
  transfers between devices with their start and end apart: 12 -> 12, of which waited for: 6 -> 5; matrix products, arithmetic and copies ran while one was open for 0% -> 0% of each run, Pallas kernels for 33% -> 38%
where the time goes in v6:
time: 35.6 us; the launch traced here: 35.4 us
  Pallas kernels  17.2 us (48%)
  starting transfers between devices  11.8 us (33%)
  waiting for transfers between devices  5.59 us (16%)
  between operations  0.88 us (2%)
    ppermute x3, starting transfers between devices, along_seq(): return lax.ppermute(block, 'seq', route)  7.16 us
    pallas_call x2, Pallas kernels, attended_with(): pl.pallas_call(functools.partial(middle_kernel, coef, [visit[0] for visit...  6.88 us
    pallas_call x1, Pallas kernels, body(): pl.pallas_call(functools.partial(diagonal_kernel, coef, rows), in_specs=[...  4.99 us
    ppermute x3, starting transfers between devices, along_head(): lax.ppermute(block, 'head', [(i, i ^ 1) for i in range(lax.axis_size('hea...  3.57 us
    pallas_call x1, Pallas kernels, body(): pl.pallas_call(functools.partial(last_kernel, coef, distances), in_specs=...  2.88 us
    ppermute x3, waiting for transfers between devices, along_head(): lax.ppermute(block, 'head', [(i, i ^ 1) for i in range(lax.axis_size('hea...  2.74 us
    pallas_call x1, Pallas kernels, body(): pl.pallas_call(functools.partial(past_kernel, coef), in_specs=[scalars] +...  1.49 us
    ppermute x3, waiting for transfers between devices, along_seq(): return lax.ppermute(block, 'seq', route)  1.44 us
  transfers between devices with their start and end apart: 12, of which 5 were waited for; matrix products, arithmetic and copies ran while one was open for 0% of the time, Pallas kernels for 38%

profile of v6, /device:TPU:0, one launch (start us, length us, event | category | flops | bytes accessed | tf_op | source)
XLA Modules:
  0.0 35.4 jit_solution(17862478192280813041)
XLA Ops:
  0.6 1.0 %pick_piece.1 = (bf16[2,320,128]{2,1,0:T(8,128)(2,1)S(1)}, s32[8]{0:T(128)S(1)}) custom-call(bf16[2,640,128]{2,1,0:T(8,128)(2,1)} %refs_0_.1, bf16[2,640,128]{2,1,0:T(8,128)(2,1)} %refs_1_.1, s32[8]{0:T(128)} %sb_hbm.1), custom_call_target="tpu_custom_call" | custom-call | bytes 400000 | tf_op jit(solution)/shard_map/pick_piece/pallas_call | solution.py:392
  1.6 4.1 %collective-permute-start.1 = (bf16[2,320,128]{2,1,0:T(8,128)(2,1)S(1)}, bf16[2,320,128]{2,1,0:T(8,128)(2,1)S(1)}, u32[]{:S(2)}, u32[]{:S(2)}) collective-permute-start(bf16[2,320,128]{2,1,0:T(8,128)(2,1)S(1)} %get-tuple-element.32), channel_id=1, source_target_pairs={{0,8},{4,12},{8,0},{12,4},{1,9},{5,13},{9,1},{13,5},{2,10},{6,14},... | collective-permute-start | bytes 491528 | tf_op jit(solution)/shard_map/along_seq/ppermute | solution.py:364
  5.7 1.6 %collective-permute-start = (bf16[2,320,128]{2,1,0:T(8,128)(2,1)S(1)}, bf16[2,320,128]{2,1,0:T(8,128)(2,1)S(1)}, u32[]{:S(2)}, u32[]{:S(2)}) collective-permute-start(bf16[2,320,128]{2,1,0:T(8,128)(2,1)S(1)} %get-tuple-element.32), channel_id=1, source_target_pairs={{0,4},{4,0},{8,12},{12,8},{1,5},{5,1},{9,13},{13,9},{2,6},{6,2},{1... | collective-permute-start | bytes 491528 | tf_op jit(solution)/shard_map/along_seq/ppermute | solution.py:364
  7.3 5.0 %diagonal.1 = (bf16[2,256,1280]{2,1,0:T(8,128)(2,1)S(1)}, f32[2,8,1280]{2,1,0:T(8,128)S(1)}, f32[2,8,1280]{2,1,0:T(8,128)S(1)}, f32[2,128,1280]{2,1,0:T(8,128)S(...) custom-call(s32[8]{0:T(128)S(1)} %get-tuple-element.28.sb, bf16[2,320,512]{2,1,0:T(8,128)(2,1)} %refs_2_.1, ...), custom_call_target="tpu_custom_call" | custom-call | flops 1677721600 | bytes 6000000 | tf_op jit(solution)/shard_map/diagonal/pallas_call | solution.py:408
  12.3 1.2 %collective-permute-done.1.refs_2_.refs_7_ = bf16[2,320,128]{2,1,0:T(8,128)(2,1)S(1)} collective-permute-done((bf16[2,320,128]{2,1,0:T(8,128)(2,1)S(1)}, bf16[2,320,128]{2,1,0:T(8,128)(2,1)S(1)}, u32[]{:S(2)}, u32[]{:S(2)}) %collective-permute-start.1) | collective-permute-done | bytes 163872 | tf_op jit(solution)/shard_map/along_seq/ppermute | solution.py:364
  13.5 0.2 collective-permute-done.refs_0_.refs_3_
  13.7 0.0 collective-permute-start.2
  13.7 0.5 %collective-permute-start.3 = (bf16[2,320,128]{2,1,0:T(8,128)(2,1)S(1)}, bf16[2,320,128]{2,1,0:T(8,128)(2,1)S(1)}, u32[]{:S(2)}, u32[]{:S(2)}) collective-permute-start(bf16[2,320,128]{2,1,0:T(8,128)(2,1)S(1)} %collective-permute-done.1.refs_2_.refs_7_), channel_id=1, source_target_pairs={{0,1},{1,0},{2,3},{3,2},{4,5},{5,4},{6,7},{7,6},{8,9},{9,8},{10,11... | collective-permute-start | bytes 491528 | tf_op jit(solution)/shard_map/along_inner/ppermute | solution.py:372
  14.2 1.5 %collective-permute-start.4 = (bf16[2,320,128]{2,1,0:T(8,128)(2,1)S(1)}, bf16[2,320,128]{2,1,0:T(8,128)(2,1)S(1)}, u32[]{:S(2)}, u32[]{:S(2)}) collective-permute-start(bf16[2,320,128]{2,1,0:T(8,128)(2,1)S(1)} %collective-permute-done.1.refs_2_.refs_7_), channel_id=1, source_target_pairs={{0,2},{2,0},{1,3},{3,1},{4,6},{6,4},{5,7},{7,5},{8,10},{10,8},{9,1... | collective-permute-start | bytes 491528 | tf_op jit(solution)/shard_map/along_head/ppermute | solution.py:368
  15.8 0.5 %collective-permute-start.5 = (bf16[2,320,128]{2,1,0:T(8,128)(2,1)S(1)}, bf16[2,320,128]{2,1,0:T(8,128)(2,1)S(1)}, u32[]{:S(2)}, u32[]{:S(2)}) collective-permute-start(bf16[2,320,128]{2,1,0:T(8,128)(2,1)S(1)} %collective-permute-done.refs_0_.refs_3_), channel_id=1, source_target_pairs={{0,2},{2,0},{1,3},{3,1},{4,6},{6,4},{5,7},{7,5},{8,10},{10,8},{9,1... | collective-permute-start | bytes 491528 | tf_op jit(solution)/shard_map/along_head/ppermute | solution.py:368
  16.2 1.5 %collective-permute-start.6 = (bf16[2,320,128]{2,1,0:T(8,128)(2,1)S(1)}, bf16[2,320,128]{2,1,0:T(8,128)(2,1)S(1)}, u32[]{:S(2)}, u32[]{:S(2)}) collective-permute-start(bf16[2,320,128]{2,1,0:T(8,128)(2,1)S(1)} %collective-permute-done.1.refs_2_.refs_7_), channel_id=1, source_target_pairs={{0,4},{4,0},{8,12},{12,8},{1,5},{5,1},{9,13},{13,9},{2,6},{6,2},{1... | collective-permute-start | bytes 491528 | tf_op jit(solution)/shard_map/along_seq/ppermute | solution.py:364
  17.7 1.5 %past.1 = (f32[2,8,1280]{2,1,0:T(8,128)S(1)}, f32[2,128,1280]{2,1,0:T(8,128)S(1)}) custom-call(s32[8]{0:T(128)S(1)} %get-tuple-element.28.sb, bf16[2,256,1280]{2,1,0:T(8,128)(2,1)S(1)} %get-tuple-element.29.turned_q, f32[2,8,1280]{2,1,0:T(8,128)S(1)} %get-tuple-element.31.sum_in, ...), custom_call_target="tpu_custom_call", output_to_operand_aliasing={{0}: (2, {}), {1}: (3, {})} | custom-call | flops 838860800 | bytes 4000000 | tf_op jit(solution)/shard_map/past/pallas_call | solution.py:465
  19.2 0.0 collective-permute-done.2.refs_1_.refs_4_
  19.2 0.0 collective-permute-done.3.refs_3_.refs_8_
  19.2 2.9 %visits_of_1_2.1 = (f32[2,8,1280]{2,1,0:T(8,128)S(1)}, f32[2,128,1280]{2,1,0:T(8,128)S(1)}) custom-call(s32[8]{0:T(128)S(1)} %get-tuple-element.28.sb, bf16[2,256,1280]{2,1,0:T(8,128)(2,1)S(1)} %get-tuple-element.29.turned_q, f32[2,8,1280]{2,1,0:T(8,128)S(1)} %get-tuple-element.38.sum_in, ...), custom_call_target="tpu_custom_call", output_to_operand_aliasing={{0}: (2, {}), {1}: (3, {})} | custom-call | flops 1677721600 | bytes 4000000 | tf_op jit(solution)/shard_map/visits_of_1_2/pallas_call | solution.py:436
  22.1 0.0 collective-permute-done.6.refs_4_.refs_11_
  22.2 1.7 %collective-permute-done.5.refs_0_.refs_5_ = bf16[2,320,128]{2,1,0:T(8,128)(2,1)S(1)} collective-permute-done((bf16[2,320,128]{2,1,0:T(8,128)(2,1)S(1)}, bf16[2,320,128]{2,1,0:T(8,128)(2,1)S(1)}, u32[]{:S(2)}, u32[]{:S(2)}) %collective-permute-start.5) | collective-permute-done | bytes 163872 | tf_op jit(solution)/shard_map/along_head/ppermute | solution.py:368
  23.8 0.0 collective-permute-done.4.refs_2_.refs_9_
  23.8 0.0 collective-permute-start.7
  23.8 0.5 %collective-permute-start.8 = (bf16[2,320,128]{2,1,0:T(8,128)(2,1)S(1)}, bf16[2,320,128]{2,1,0:T(8,128)(2,1)S(1)}, u32[]{:S(2)}, u32[]{:S(2)}) collective-permute-start(bf16[2,320,128]{2,1,0:T(8,128)(2,1)S(1)} %collective-permute-done.4.refs_2_.refs_9_), channel_id=1, source_target_pairs={{0,1},{1,0},{2,3},{3,2},{4,5},{5,4},{6,7},{7,6},{8,9},{9,8},{10,11... | collective-permute-start | bytes 491528 | tf_op jit(solution)/shard_map/along_inner/ppermute | solution.py:372
  24.3 0.0 collective-permute-start.9
  24.3 1.5 %collective-permute-start.10 = (bf16[2,320,128]{2,1,0:T(8,128)(2,1)S(1)}, bf16[2,320,128]{2,1,0:T(8,128)(2,1)S(1)}, u32[]{:S(2)}, u32[]{:S(2)}) collective-permute-start(bf16[2,320,128]{2,1,0:T(8,128)(2,1)S(1)} %collective-permute-done.6.refs_4_.refs_11_), channel_id=1, source_target_pairs={{0,2},{2,0},{1,3},{3,1},{4,6},{6,4},{5,7},{7,5},{8,10},{10,8},{9,1... | collective-permute-start | bytes 491528 | tf_op jit(solution)/shard_map/along_head/ppermute | solution.py:368
  25.9 0.0 collective-permute-done.7.refs_1_.refs_6_
  25.9 0.0 collective-permute-done.8.refs_3_.refs_10_
  25.9 0.0 collective-permute-done.9.refs_5_.refs_12_
  25.9 4.0 %visits_of_1_2_3.1 = (f32[2,8,1280]{2,1,0:T(8,128)S(1)}, f32[2,128,1280]{2,1,0:T(8,128)S(1)}) custom-call(s32[8]{0:T(128)S(1)} %get-tuple-element.28.sb, bf16[2,256,1280]{2,1,0:T(8,128)(2,1)S(1)} %get-tuple-element.29.turned_q, f32[2,8,1280]{2,1,0:T(8,128)S(1)} %get-tuple-element.42.sum_in, ...), custom_call_target="tpu_custom_call", output_to_operand_aliasing={{0}: (2, {}), {1}: (3, {})} | custom-call | flops 2516582400 | bytes 4000000 | tf_op jit(solution)/shard_map/visits_of_1_2_3/pallas_call | solution.py:436
  29.9 1.1 %collective-permute-done.10.own.refs_13_ = bf16[2,320,128]{2,1,0:T(8,128)(2,1)S(1)} collective-permute-done((bf16[2,320,128]{2,1,0:T(8,128)(2,1)S(1)}, bf16[2,320,128]{2,1,0:T(8,128)(2,1)S(1)}, u32[]{:S(2)}, u32[]{:S(2)}) %collective-permute-start.10) | collective-permute-done | bytes 163872 | tf_op jit(solution)/shard_map/along_head/ppermute | solution.py:368
  31.0 0.0 collective-permute-start.11
  31.0 1.4 %collective-permute-done.11.twin.refs_14_ = bf16[2,320,128]{2,1,0:T(8,128)(2,1)S(1)} collective-permute-done((bf16[2,320,128]{2,1,0:T(8,128)(2,1)S(1)}, bf16[2,320,128]{2,1,0:T(8,128)(2,1)S(1)}, u32[]{:S(2)}, u32[]{:S(2)}) %collective-permute-start.11) | collective-permute-done | bytes 163872 | tf_op jit(solution)/shard_map/along_inner/ppermute | solution.py:372
  32.4 2.9 %last_visitor.1 = (bf16[2,320,512]{2,1,0:T(8,128)(2,1)}, f32[2,4,320]{2,1,0:T(4,128)}) custom-call(s32[8]{0:T(128)S(1)} %get-tuple-element.28.sb, bf16[2,256,1280]{2,1,0:T(8,128)(2,1)S(1)} %get-tuple-element.29.turned_q, f32[2,8,1280]{2,1,0:T(8,128)S(1)} %get-tuple-element.30.top_ref, f32[2,8,1280]{2,1,0:T(8,128)S(1)} %get-tuple-element.50.sum_ref, ...), custom_call_target="tpu_custom_call" | custom-call | flops 838860800 | bytes 7000000 | tf_op jit(solution)/shard_map/last_visitor/pallas_call | solution.py:489
Async XLA Ops:
  1.6 11.9 %collective-permute-start.1 = (bf16[2,320,128]{2,1,0:T(8,128)(2,1)S(1)}, bf16[2,320,128]{2,1,0:T(8,128)(2,1)S(1)}, u32[]{:S(2)}, u32[]{:S(2)}) collective-permute-start(bf16[2,320,128]{2,1,0:T(8,128)(2,1)S(1)} %get-tuple-element.32), channel_id=1, source_target_pairs={{0,8},{4,12},{8,0},{12,4},{1,9},{5,13},{9,1},{13,5},{2,10},{6,14},... | collective-permute-start | bytes 491528 | tf_op jit(solution)/shard_map/along_seq/ppermute | solution.py:364
  5.7 8.0 %collective-permute-start = (bf16[2,320,128]{2,1,0:T(8,128)(2,1)S(1)}, bf16[2,320,128]{2,1,0:T(8,128)(2,1)S(1)}, u32[]{:S(2)}, u32[]{:S(2)}) collective-permute-start(bf16[2,320,128]{2,1,0:T(8,128)(2,1)S(1)} %get-tuple-element.32), channel_id=1, source_target_pairs={{0,4},{4,0},{8,12},{12,8},{1,5},{5,1},{9,13},{13,9},{2,6},{6,2},{1... | collective-permute-start | bytes 491528 | tf_op jit(solution)/shard_map/along_seq/ppermute | solution.py:364
  13.7 5.5 %collective-permute-start.2 = (bf16[2,320,128]{2,1,0:T(8,128)(2,1)S(1)}, bf16[2,320,128]{2,1,0:T(8,128)(2,1)S(1)}, u32[]{:S(2)}, u32[]{:S(2)}) collective-permute-start(bf16[2,320,128]{2,1,0:T(8,128)(2,1)S(1)} %collective-permute-done.refs_0_.refs_3_), channel_id=1, source_target_pairs={{0,1},{1,0},{2,3},{3,2},{4,5},{5,4},{6,7},{7,6},{8,9},{9,8},{10,11... | collective-permute-start | bytes 491528 | tf_op jit(solution)/shard_map/along_inner/ppermute | solution.py:372
  13.7 5.5 %collective-permute-start.3 = (bf16[2,320,128]{2,1,0:T(8,128)(2,1)S(1)}, bf16[2,320,128]{2,1,0:T(8,128)(2,1)S(1)}, u32[]{:S(2)}, u32[]{:S(2)}) collective-permute-start(bf16[2,320,128]{2,1,0:T(8,128)(2,1)S(1)} %collective-permute-done.1.refs_2_.refs_7_), channel_id=1, source_target_pairs={{0,1},{1,0},{2,3},{3,2},{4,5},{5,4},{6,7},{7,6},{8,9},{9,8},{10,11... | collective-permute-start | bytes 491528 | tf_op jit(solution)/shard_map/along_inner/ppermute | solution.py:372
  14.2 9.6 %collective-permute-start.4 = (bf16[2,320,128]{2,1,0:T(8,128)(2,1)S(1)}, bf16[2,320,128]{2,1,0:T(8,128)(2,1)S(1)}, u32[]{:S(2)}, u32[]{:S(2)}) collective-permute-start(bf16[2,320,128]{2,1,0:T(8,128)(2,1)S(1)} %collective-permute-done.1.refs_2_.refs_7_), channel_id=1, source_target_pairs={{0,2},{2,0},{1,3},{3,1},{4,6},{6,4},{5,7},{7,5},{8,10},{10,8},{9,1... | collective-permute-start | bytes 491528 | tf_op jit(solution)/shard_map/along_head/ppermute | solution.py:368
  15.8 8.1 %collective-permute-start.5 = (bf16[2,320,128]{2,1,0:T(8,128)(2,1)S(1)}, bf16[2,320,128]{2,1,0:T(8,128)(2,1)S(1)}, u32[]{:S(2)}, u32[]{:S(2)}) collective-permute-start(bf16[2,320,128]{2,1,0:T(8,128)(2,1)S(1)} %collective-permute-done.refs_0_.refs_3_), channel_id=1, source_target_pairs={{0,2},{2,0},{1,3},{3,1},{4,6},{6,4},{5,7},{7,5},{8,10},{10,8},{9,1... | collective-permute-start | bytes 491528 | tf_op jit(solution)/shard_map/along_head/ppermute | solution.py:368
  16.2 5.9 %collective-permute-start.6 = (bf16[2,320,128]{2,1,0:T(8,128)(2,1)S(1)}, bf16[2,320,128]{2,1,0:T(8,128)(2,1)S(1)}, u32[]{:S(2)}, u32[]{:S(2)}) collective-permute-start(bf16[2,320,128]{2,1,0:T(8,128)(2,1)S(1)} %collective-permute-done.1.refs_2_.refs_7_), channel_id=1, source_target_pairs={{0,4},{4,0},{8,12},{12,8},{1,5},{5,1},{9,13},{13,9},{2,6},{6,2},{1... | collective-permute-start | bytes 491528 | tf_op jit(solution)/shard_map/along_seq/ppermute | solution.py:364
  23.8 2.1 %collective-permute-start.7 = (bf16[2,320,128]{2,1,0:T(8,128)(2,1)S(1)}, bf16[2,320,128]{2,1,0:T(8,128)(2,1)S(1)}, u32[]{:S(2)}, u32[]{:S(2)}) collective-permute-start(bf16[2,320,128]{2,1,0:T(8,128)(2,1)S(1)} %collective-permute-done.5.refs_0_.refs_5_), channel_id=1, source_target_pairs={{0,1},{1,0},{2,3},{3,2},{4,5},{5,4},{6,7},{7,6},{8,9},{9,8},{10,11... | collective-permute-start | bytes 491528 | tf_op jit(solution)/shard_map/along_inner/ppermute | solution.py:372
  23.8 2.1 %collective-permute-start.8 = (bf16[2,320,128]{2,1,0:T(8,128)(2,1)S(1)}, bf16[2,320,128]{2,1,0:T(8,128)(2,1)S(1)}, u32[]{:S(2)}, u32[]{:S(2)}) collective-permute-start(bf16[2,320,128]{2,1,0:T(8,128)(2,1)S(1)} %collective-permute-done.4.refs_2_.refs_9_), channel_id=1, source_target_pairs={{0,1},{1,0},{2,3},{3,2},{4,5},{5,4},{6,7},{7,6},{8,9},{9,8},{10,11... | collective-permute-start | bytes 491528 | tf_op jit(solution)/shard_map/along_inner/ppermute | solution.py:372
  24.3 1.6 %collective-permute-start.9 = (bf16[2,320,128]{2,1,0:T(8,128)(2,1)S(1)}, bf16[2,320,128]{2,1,0:T(8,128)(2,1)S(1)}, u32[]{:S(2)}, u32[]{:S(2)}) collective-permute-start(bf16[2,320,128]{2,1,0:T(8,128)(2,1)S(1)} %collective-permute-done.6.refs_4_.refs_11_), channel_id=1, source_target_pairs={{0,1},{1,0},{2,3},{3,2},{4,5},{5,4},{6,7},{7,6},{8,9},{9,8},{10,11... | collective-permute-start | bytes 491528 | tf_op jit(solution)/shard_map/along_inner/ppermute | solution.py:372
  24.3 6.6 %collective-permute-start.10 = (bf16[2,320,128]{2,1,0:T(8,128)(2,1)S(1)}, bf16[2,320,128]{2,1,0:T(8,128)(2,1)S(1)}, u32[]{:S(2)}, u32[]{:S(2)}) collective-permute-start(bf16[2,320,128]{2,1,0:T(8,128)(2,1)S(1)} %collective-permute-done.6.refs_4_.refs_11_), channel_id=1, source_target_pairs={{0,2},{2,0},{1,3},{3,1},{4,6},{6,4},{5,7},{7,5},{8,10},{10,8},{9,1... | collective-permute-start | bytes 491528 | tf_op jit(solution)/shard_map/along_head/ppermute | solution.py:368
  31.0 1.4 %collective-permute-start.11 = (bf16[2,320,128]{2,1,0:T(8,128)(2,1)S(1)}, bf16[2,320,128]{2,1,0:T(8,128)(2,1)S(1)}, u32[]{:S(2)}, u32[]{:S(2)}) collective-permute-start(bf16[2,320,128]{2,1,0:T(8,128)(2,1)S(1)} %collective-permute-done.10.own.refs_13_), channel_id=1, source_target_pairs={{0,1},{1,0},{2,3},{3,2},{4,5},{5,4},{6,7},{7,6},{8,9},{9,8},{10,11... | collective-permute-start | bytes 491528 | tf_op jit(solution)/shard_map/along_inner/ppermute | solution.py:372

commit v7 on v6

--- a/solution.py
+++ b/solution.py
@@ -223,7 +223,7 @@
             acc_ref[order] += part
             sum_ref[order] += sums
             if done is not None:
-                done(place, laid_out[-1][1][0])
+                done(place - len(ends), laid_out[-1][1][0])
 
     in_turn(chunks, score, finish)
 
@@ -239,7 +239,9 @@
     attend(coef, visits, sb, turned_q, sum_ref, acc_ref, buffers)
 
 
-def last_kernel(coef, distances, sb, turned_q, top_ref, sum_ref, acc_ref, own, twin, *refs):
+def last_kernel(coef, distances, final, sb, turned_q, top_ref, sum_ref, acc_ref, *refs):
+    visits = [(d, refs[2 * i], refs[2 * i + 1]) for i, d in enumerate(final)]
+    refs = refs[2 * len(final) :]
     every, rest = refs[: 4 * len(distances) + 3], refs[4 * len(distances) + 3 :]
     out_hbm, lse_hbm, out_buf, lse_ref, *buffers, worst, k_buf, v_buf, run_top, run_acc, sem, out_sems = rest
     _, rows, feats = out_buf.shape
@@ -263,7 +265,9 @@
         lse_ref[slot, h : h + 1, :] = first_row(top * (coef * math.log(2.0)) + jnp.log(sums))
 
     def done(place, last_order):
-        order = 1 - last_order if place == 0 else last_order
+        if place < -2:
+            return
+        order = 1 - last_order if place == -2 else last_order
         slot = jnp.where(order == HI, hi, 1 - hi)
         sums = jnp.sum(sum_ref[order], axis=0, keepdims=True)
         log_total = top_ref[order][:1] * (coef * math.log(2.0)) + jnp.log(sums)
@@ -272,10 +276,10 @@
             mine = slice(h * rows, (h + 1) * rows)
             lse_ref[slot, h : h + 1, :] = log_total[:, mine]
             out_buf[slot, :, h * width : (h + 1) * width] = settled[mine]
-        worst[place : place + 1] = sums
+        worst[place + 2 : place + 3] = sums
         out_copy(slot).start()
 
-    attend(coef, [(distances[-1], own, twin)], sb, turned_q, sum_ref, acc_ref, buffers, done)
+    attend(coef, visits, sb, turned_q, sum_ref, acc_ref, buffers, done)
     fits = jnp.max(worst[...]) < SUM_LIMIT
     lse_copy.start()
     for slot in range(2):
@@ -455,12 +459,18 @@
             across[distance] = along_head(arrived[distance])
             beside[distance] = along_inner(arrived[distance])
 
+    def settle(distance):
+        nonlocal acc
+        across[distance], acc = lax.optimization_barrier((across[distance], acc))
+        beside_across[distance] = along_inner(across[distance])
+
     last = distances[-1]
     for distance in sorted(arrived, reverse=True):
         arrived[distance], acc = lax.optimization_barrier((arrived[distance], acc))
     waiting = distances[:2]
     for distance in waiting:
-        spread(distance)
+        beside[distance] = along_inner(arrived[distance])
+    across[1] = along_head(arrived[1])
     relay(3)
     sums, acc = pl.pallas_call(
         functools.partial(past_kernel, coef),
@@ -472,30 +482,31 @@
         compiler_params=params,
         name="past",
     )(sb_here, turned, sums, acc, k_here, v_turned)
+    arrived[2], acc = lax.optimization_barrier((arrived[2], acc))
+    across[2] = along_head(arrived[2])
     sums, acc = attended_with(sums, acc, [near_half(d) for d in waiting])
     for ahead in distances[2:]:
         relay(ahead)
         arrived[ahead], acc = lax.optimization_barrier((arrived[ahead], acc))
         spread(ahead)
-        for distance in waiting:
-            across[distance], acc = lax.optimization_barrier((across[distance], acc))
-            beside_across[distance] = along_inner(across[distance])
-        sums, acc = attended_with(sums, acc, [far_half(d) for d in waiting] + [near_half(ahead)])
-        waiting = [ahead]
-    across[last], acc = lax.optimization_barrier((across[last], acc))
-    beside_across[last] = along_inner(across[last])
+        settle(ahead - 2)
+        across[ahead - 1], acc = lax.optimization_barrier((across[ahead - 1], acc))
+        sums, acc = attended_with(sums, acc, [far_half(ahead - 2), near_half(ahead)])
+    final = distances[-2:]
+    for distance in final:
+        settle(distance)
 
     flat = [part[d] for d in distances for part in (arrived, beside, across, beside_across)]
     attended, log_total = pl.pallas_call(
-        functools.partial(last_kernel, coef, distances),
-        in_specs=[scalars] + [whole] * 6 + [anywhere] * (3 + len(flat)),
+        functools.partial(last_kernel, coef, distances, final),
+        in_specs=[scalars] + [whole] * (4 + 2 * len(final)) + [anywhere] * (3 + len(flat)),
         out_specs=[anywhere, anywhere],
         out_shape=[jax.ShapeDtypeStruct(query_rows.shape, query_rows.dtype), top_shape],
         scratch_shapes=[
             pltpu.VMEM(query_rows.shape, query_rows.dtype),
             pltpu.VMEM(top_shape.shape, jnp.float32),
         ]
-        + half_buffers
+        + half_buffers * len(final)
         + [
             pltpu.VMEM((2, all_rows), jnp.float32),
             pltpu.VMEM((2 * block_len, width), key_rows.dtype),
@@ -508,7 +519,7 @@
         cost_estimate=cost(1, 7_000_000),
         compiler_params=params,
         name="last_visitor",
-    )(sb_here, turned, tops, sums, acc, *far_half(last)[1:], in_hbm[1], in_hbm[2], in_hbm[0], *flat)
+    )(sb_here, turned, tops, sums, acc, *(part for d in final for part in far_half(d)[1:]), in_hbm[1], in_hbm[2], in_hbm[0], *flat)
     return attended, log_total
 
 

time: 35.6 us -> 35 us (0.983)
  waiting for transfers between devices: 5.59 us -> 4.35 us
  starting transfers between devices: 11.8 us -> 12.3 us
    pallas_call x1, Pallas kernels: 2.88 us -> 4.01 us  [body(): pl.pallas_call(functools.partial(last_kernel, coef, distances, final), in...]
    pallas_call x2, Pallas kernels: 6.88 us -> 5.79 us  [attended_with(): pl.pallas_call(functools.partial(middle_kernel, coef, [visit[0] for visit...]
    ppermute x3, waiting for transfers between devices: 2.74 us -> 1.78 us  [along_head(): lax.ppermute(block, 'head', [(i, i ^ 1) for i in range(lax.axis_size('hea...]
    ppermute x6, starting transfers between devices: 1.03 us -> 1.59 us  [along_inner(): return lax.ppermute(block, 'inner', [(0, 1), (1, 0)])]
  transfers between devices with their start and end apart: 12 -> 12, of which waited for: 5 -> 5; matrix products, arithmetic and copies ran while one was open for 0% -> 0% of each run, Pallas kernels for 38% -> 35%
where the time goes in v7:
time: 35 us; the launch traced here: 34.8 us
  Pallas kernels  17.2 us (49%)
  starting transfers between devices  12.3 us (35%)
  waiting for transfers between devices  4.35 us (12%)
  between operations  0.88 us (3%)
    ppermute x3, starting transfers between devices, along_seq(): return lax.ppermute(block, 'seq', route)  7.11 us
    pallas_call x2, Pallas kernels, attended_with(): pl.pallas_call(functools.partial(middle_kernel, coef, [visit[0] for visit...  5.79 us
    pallas_call x1, Pallas kernels, body(): pl.pallas_call(functools.partial(diagonal_kernel, coef, rows), in_specs=[...  4.99 us
    pallas_call x1, Pallas kernels, body(): pl.pallas_call(functools.partial(last_kernel, coef, distances, final), in...  4.01 us
    ppermute x3, starting transfers between devices, along_head(): lax.ppermute(block, 'head', [(i, i ^ 1) for i in range(lax.axis_size('hea...  3.63 us
    ppermute x3, waiting for transfers between devices, along_head(): lax.ppermute(block, 'head', [(i, i ^ 1) for i in range(lax.axis_size('hea...  1.78 us
    ppermute x6, starting transfers between devices, along_inner(): return lax.ppermute(block, 'inner', [(0, 1), (1, 0)])  1.59 us
    pallas_call x1, Pallas kernels, body(): pl.pallas_call(functools.partial(past_kernel, coef), in_specs=[scalars] +...  1.49 us
  transfers between devices with their start and end apart: 12, of which 5 were waited for; matrix products, arithmetic and copies ran while one was open for 0% of the time, Pallas kernels for 35%

profile of v7, /device:TPU:0, one launch (start us, length us, event | category | flops | bytes accessed | tf_op | source)
XLA Modules:
  0.0 34.8 jit_solution(8312671147124863900)
XLA Ops:
  0.6 1.0 %pick_piece.1 = (bf16[2,320,128]{2,1,0:T(8,128)(2,1)S(1)}, s32[8]{0:T(128)S(1)}) custom-call(bf16[2,640,128]{2,1,0:T(8,128)(2,1)} %refs_4_.1, bf16[2,640,128]{2,1,0:T(8,128)(2,1)} %refs_5_.1, s32[8]{0:T(128)} %sb_hbm.1), custom_call_target="tpu_custom_call" | custom-call | bytes 400000 | tf_op jit(solution)/shard_map/pick_piece/pallas_call | solution.py:396
  1.6 4.1 %collective-permute-start.1 = (bf16[2,320,128]{2,1,0:T(8,128)(2,1)S(1)}, bf16[2,320,128]{2,1,0:T(8,128)(2,1)S(1)}, u32[]{:S(2)}, u32[]{:S(2)}) collective-permute-start(bf16[2,320,128]{2,1,0:T(8,128)(2,1)S(1)} %get-tuple-element.36), channel_id=1, source_target_pairs={{0,8},{4,12},{8,0},{12,4},{1,9},{5,13},{9,1},{13,5},{2,10},{6,14},... | collective-permute-start | bytes 491528 | tf_op jit(solution)/shard_map/along_seq/ppermute | solution.py:368
  5.7 1.6 %collective-permute-start = (bf16[2,320,128]{2,1,0:T(8,128)(2,1)S(1)}, bf16[2,320,128]{2,1,0:T(8,128)(2,1)S(1)}, u32[]{:S(2)}, u32[]{:S(2)}) collective-permute-start(bf16[2,320,128]{2,1,0:T(8,128)(2,1)S(1)} %get-tuple-element.36), channel_id=1, source_target_pairs={{0,4},{4,0},{8,12},{12,8},{1,5},{5,1},{9,13},{13,9},{2,6},{6,2},{1... | collective-permute-start | bytes 491528 | tf_op jit(solution)/shard_map/along_seq/ppermute | solution.py:368
  7.3 5.0 %diagonal.1 = (bf16[2,256,1280]{2,1,0:T(8,128)(2,1)S(1)}, f32[2,8,1280]{2,1,0:T(8,128)S(1)}, f32[2,8,1280]{2,1,0:T(8,128)S(1)}, f32[2,128,1280]{2,1,0:T(8,128)S(...) custom-call(s32[8]{0:T(128)S(1)} %get-tuple-element.32.sb, bf16[2,320,512]{2,1,0:T(8,128)(2,1)} %refs_6_.1, ...), custom_call_target="tpu_custom_call" | custom-call | flops 1677721600 | bytes 6000000 | tf_op jit(solution)/shard_map/diagonal/pallas_call | solution.py:412
  12.3 1.2 %collective-permute-done.1.refs_2_.refs_11_ = bf16[2,320,128]{2,1,0:T(8,128)(2,1)S(1)} collective-permute-done((bf16[2,320,128]{2,1,0:T(8,128)(2,1)S(1)}, bf16[2,320,128]{2,1,0:T(8,128)(2,1)S(1)}, u32[]{:S(2)}, u32[]{:S(2)}) %collective-permute-start.1) | collective-permute-done | bytes 163872 | tf_op jit(solution)/shard_map/along_seq/ppermute | solution.py:368
  13.5 0.2 collective-permute-done.refs_0_.refs_7_
  13.7 0.0 collective-permute-start.2
  13.7 0.5 %collective-permute-start.3 = (bf16[2,320,128]{2,1,0:T(8,128)(2,1)S(1)}, bf16[2,320,128]{2,1,0:T(8,128)(2,1)S(1)}, u32[]{:S(2)}, u32[]{:S(2)}) collective-permute-start(bf16[2,320,128]{2,1,0:T(8,128)(2,1)S(1)} %collective-permute-done.1.refs_2_.refs_11_), channel_id=1, source_target_pairs={{0,1},{1,0},{2,3},{3,2},{4,5},{5,4},{6,7},{7,6},{8,9},{9,8},{10,11... | collective-permute-start | bytes 491528 | tf_op jit(solution)/shard_map/along_inner/ppermute | solution.py:376
  14.2 1.5 %collective-permute-start.5 = (bf16[2,320,128]{2,1,0:T(8,128)(2,1)S(1)}, bf16[2,320,128]{2,1,0:T(8,128)(2,1)S(1)}, u32[]{:S(2)}, u32[]{:S(2)}) collective-permute-start(bf16[2,320,128]{2,1,0:T(8,128)(2,1)S(1)} %collective-permute-done.refs_0_.refs_7_), channel_id=1, source_target_pairs={{0,2},{2,0},{1,3},{3,1},{4,6},{6,4},{5,7},{7,5},{8,10},{10,8},{9,1... | collective-permute-start | bytes 491528 | tf_op jit(solution)/shard_map/along_head/ppermute | solution.py:372
  15.8 1.4 %collective-permute-start.6 = (bf16[2,320,128]{2,1,0:T(8,128)(2,1)S(1)}, bf16[2,320,128]{2,1,0:T(8,128)(2,1)S(1)}, u32[]{:S(2)}, u32[]{:S(2)}) collective-permute-start(bf16[2,320,128]{2,1,0:T(8,128)(2,1)S(1)} %collective-permute-done.1.refs_2_.refs_11_), channel_id=1, source_target_pairs={{0,4},{4,0},{8,12},{12,8},{1,5},{5,1},{9,13},{13,9},{2,6},{6,2},{1... | collective-permute-start | bytes 491528 | tf_op jit(solution)/shard_map/along_seq/ppermute | solution.py:368
  17.2 1.5 %past.1 = (f32[2,8,1280]{2,1,0:T(8,128)S(1)}, f32[2,128,1280]{2,1,0:T(8,128)S(1)}) custom-call(s32[8]{0:T(128)S(1)} %get-tuple-element.32.sb, bf16[2,256,1280]{2,1,0:T(8,128)(2,1)S(1)} %get-tuple-element.33.turned_q, f32[2,8,1280]{2,1,0:T(8,128)S(1)} %get-tuple-element.35.sum_in, ...), custom_call_target="tpu_custom_call", output_to_operand_aliasing={{0}: (2, {}), {1}: (3, {})} | custom-call | flops 838860800 | bytes 4000000 | tf_op jit(solution)/shard_map/past/pallas_call | solution.py:475
  18.7 0.6 %collective-permute-start.4 = (bf16[2,320,128]{2,1,0:T(8,128)(2,1)S(1)}, bf16[2,320,128]{2,1,0:T(8,128)(2,1)S(1)}, u32[]{:S(2)}, u32[]{:S(2)}) collective-permute-start(bf16[2,320,128]{2,1,0:T(8,128)(2,1)S(1)} %collective-permute-done.1.refs_2_.refs_11_), channel_id=1, source_target_pairs={{0,2},{2,0},{1,3},{3,1},{4,6},{6,4},{5,7},{7,5},{8,10},{10,8},{9,1... | collective-permute-start | bytes 491528 | tf_op jit(solution)/shard_map/along_head/ppermute | solution.py:372
  19.3 0.0 collective-permute-done.2.refs_1_.refs_8_
  19.3 0.0 collective-permute-done.3.refs_3_.refs_12_
  19.3 2.9 %visits_of_1_2.1 = (f32[2,8,1280]{2,1,0:T(8,128)S(1)}, f32[2,128,1280]{2,1,0:T(8,128)S(1)}) custom-call(s32[8]{0:T(128)S(1)} %get-tuple-element.32.sb, bf16[2,256,1280]{2,1,0:T(8,128)(2,1)S(1)} %get-tuple-element.33.turned_q, f32[2,8,1280]{2,1,0:T(8,128)S(1)} %get-tuple-element.42.sum_in, ...), custom_call_target="tpu_custom_call", output_to_operand_aliasing={{0}: (2, {}), {1}: (3, {})} | custom-call | flops 1677721600 | bytes 4000000 | tf_op jit(solution)/shard_map/visits_of_1_2/pallas_call | solution.py:440
  22.2 0.0 collective-permute-done.6.refs_2_.refs_15_
  22.2 0.0 collective-permute-done.5.refs_0_.refs_9_
  22.2 0.1 collective-permute-start.7
  22.3 0.5 %collective-permute-start.8 = (bf16[2,320,128]{2,1,0:T(8,128)(2,1)S(1)}, bf16[2,320,128]{2,1,0:T(8,128)(2,1)S(1)}, u32[]{:S(2)}, u32[]{:S(2)}) collective-permute-start(bf16[2,320,128]{2,1,0:T(8,128)(2,1)S(1)} %collective-permute-done.6.refs_2_.refs_15_), channel_id=1, source_target_pairs={{0,1},{1,0},{2,3},{3,2},{4,5},{5,4},{6,7},{7,6},{8,9},{9,8},{10,11... | collective-permute-start | bytes 491528 | tf_op jit(solution)/shard_map/along_inner/ppermute | solution.py:376
  22.8 1.5 %collective-permute-start.9 = (bf16[2,320,128]{2,1,0:T(8,128)(2,1)S(1)}, bf16[2,320,128]{2,1,0:T(8,128)(2,1)S(1)}, u32[]{:S(2)}, u32[]{:S(2)}) collective-permute-start(bf16[2,320,128]{2,1,0:T(8,128)(2,1)S(1)} %collective-permute-done.6.refs_2_.refs_15_), channel_id=1, source_target_pairs={{0,2},{2,0},{1,3},{3,1},{4,6},{6,4},{5,7},{7,5},{8,10},{10,8},{9,1... | collective-permute-start | bytes 491528 | tf_op jit(solution)/shard_map/along_head/ppermute | solution.py:372
  24.3 0.0 collective-permute-done.4.refs_0_.refs_13_
  24.3 0.0 collective-permute-done.7.refs_1_.refs_10_
  24.3 0.0 collective-permute-done.8.refs_3_.refs_16_
  24.3 2.9 %visits_of_1_3.1 = (f32[2,8,1280]{2,1,0:T(8,128)S(1)}, f32[2,128,1280]{2,1,0:T(8,128)S(1)}) custom-call(s32[8]{0:T(128)S(1)} %get-tuple-element.32.sb, bf16[2,256,1280]{2,1,0:T(8,128)(2,1)S(1)} %get-tuple-element.33.turned_q, f32[2,8,1280]{2,1,0:T(8,128)S(1)} %get-tuple-element.48.sum_in, ...), custom_call_target="tpu_custom_call", output_to_operand_aliasing={{0}: (2, {}), {1}: (3, {})} | custom-call | flops 1677721600 | bytes 4000000 | tf_op jit(solution)/shard_map/visits_of_1_3/pallas_call | solution.py:440
  27.2 1.8 %collective-permute-done.9.refs_2_.refs_17_ = bf16[2,320,128]{2,1,0:T(8,128)(2,1)S(1)} collective-permute-done((bf16[2,320,128]{2,1,0:T(8,128)(2,1)S(1)}, bf16[2,320,128]{2,1,0:T(8,128)(2,1)S(1)}, u32[]{:S(2)}, u32[]{:S(2)}) %collective-permute-start.9) | collective-permute-done | bytes 163872 | tf_op jit(solution)/shard_map/along_head/ppermute | solution.py:372
  29.0 0.0 collective-permute-start.10
  29.0 0.5 %collective-permute-start.11 = (bf16[2,320,128]{2,1,0:T(8,128)(2,1)S(1)}, bf16[2,320,128]{2,1,0:T(8,128)(2,1)S(1)}, u32[]{:S(2)}, u32[]{:S(2)}) collective-permute-start(bf16[2,320,128]{2,1,0:T(8,128)(2,1)S(1)} %collective-permute-done.9.refs_2_.refs_17_), channel_id=1, source_target_pairs={{0,1},{1,0},{2,3},{3,2},{4,5},{5,4},{6,7},{7,6},{8,9},{9,8},{10,11... | collective-permute-start | bytes 491528 | tf_op jit(solution)/shard_map/along_inner/ppermute | solution.py:376
  29.5 0.9 %collective-permute-done.10.refs_1_.refs_14_ = bf16[2,320,128]{2,1,0:T(8,128)(2,1)S(1)} collective-permute-done((bf16[2,320,128]{2,1,0:T(8,128)(2,1)S(1)}, bf16[2,320,128]{2,1,0:T(8,128)(2,1)S(1)}, u32[]{:S(2)}, u32[]{:S(2)}) %collective-permute-start.10) | collective-permute-done | bytes 163872 | tf_op jit(solution)/shard_map/along_inner/ppermute | solution.py:376
  30.4 0.2 collective-permute-done.11.refs_3_.refs_18_
  30.6 4.0 %last_visitor.1 = (bf16[2,320,512]{2,1,0:T(8,128)(2,1)}, f32[2,4,320]{2,1,0:T(4,128)}) custom-call(s32[8]{0:T(128)S(1)} %get-tuple-element.32.sb, bf16[2,256,1280]{2,1,0:T(8,128)(2,1)S(1)} %get-tuple-element.33.turned_q, f32[2,8,1280]{2,1,0:T(8,128)S(1)} %get-tuple-element.34.top_ref, f32[2,8,1280]{2,1,0:T(8,128)S(1)} %get-tuple-element.55.sum_ref, ...), custom_call_target="tpu_custom_call" | custom-call | flops 838860800 | bytes 7000000 | tf_op jit(solution)/shard_map/last_visitor/pallas_call | solution.py:500
Async XLA Ops:
  1.6 11.9 %collective-permute-start.1 = (bf16[2,320,128]{2,1,0:T(8,128)(2,1)S(1)}, bf16[2,320,128]{2,1,0:T(8,128)(2,1)S(1)}, u32[]{:S(2)}, u32[]{:S(2)}) collective-permute-start(bf16[2,320,128]{2,1,0:T(8,128)(2,1)S(1)} %get-tuple-element.36), channel_id=1, source_target_pairs={{0,8},{4,12},{8,0},{12,4},{1,9},{5,13},{9,1},{13,5},{2,10},{6,14},... | collective-permute-start | bytes 491528 | tf_op jit(solution)/shard_map/along_seq/ppermute | solution.py:368
  5.7 8.0 %collective-permute-start = (bf16[2,320,128]{2,1,0:T(8,128)(2,1)S(1)}, bf16[2,320,128]{2,1,0:T(8,128)(2,1)S(1)}, u32[]{:S(2)}, u32[]{:S(2)}) collective-permute-start(bf16[2,320,128]{2,1,0:T(8,128)(2,1)S(1)} %get-tuple-element.36), channel_id=1, source_target_pairs={{0,4},{4,0},{8,12},{12,8},{1,5},{5,1},{9,13},{13,9},{2,6},{6,2},{1... | collective-permute-start | bytes 491528 | tf_op jit(solution)/shard_map/along_seq/ppermute | solution.py:368
  13.7 5.6 %collective-permute-start.2 = (bf16[2,320,128]{2,1,0:T(8,128)(2,1)S(1)}, bf16[2,320,128]{2,1,0:T(8,128)(2,1)S(1)}, u32[]{:S(2)}, u32[]{:S(2)}) collective-permute-start(bf16[2,320,128]{2,1,0:T(8,128)(2,1)S(1)} %collective-permute-done.refs_0_.refs_7_), channel_id=1, source_target_pairs={{0,1},{1,0},{2,3},{3,2},{4,5},{5,4},{6,7},{7,6},{8,9},{9,8},{10,11... | collective-permute-start | bytes 491528 | tf_op jit(solution)/shard_map/along_inner/ppermute | solution.py:376
  13.7 5.6 %collective-permute-start.3 = (bf16[2,320,128]{2,1,0:T(8,128)(2,1)S(1)}, bf16[2,320,128]{2,1,0:T(8,128)(2,1)S(1)}, u32[]{:S(2)}, u32[]{:S(2)}) collective-permute-start(bf16[2,320,128]{2,1,0:T(8,128)(2,1)S(1)} %collective-permute-done.1.refs_2_.refs_11_), channel_id=1, source_target_pairs={{0,1},{1,0},{2,3},{3,2},{4,5},{5,4},{6,7},{7,6},{8,9},{9,8},{10,11... | collective-permute-start | bytes 491528 | tf_op jit(solution)/shard_map/along_inner/ppermute | solution.py:376
  14.2 8.0 %collective-permute-start.5 = (bf16[2,320,128]{2,1,0:T(8,128)(2,1)S(1)}, bf16[2,320,128]{2,1,0:T(8,128)(2,1)S(1)}, u32[]{:S(2)}, u32[]{:S(2)}) collective-permute-start(bf16[2,320,128]{2,1,0:T(8,128)(2,1)S(1)} %collective-permute-done.refs_0_.refs_7_), channel_id=1, source_target_pairs={{0,2},{2,0},{1,3},{3,1},{4,6},{6,4},{5,7},{7,5},{8,10},{10,8},{9,1... | collective-permute-start | bytes 491528 | tf_op jit(solution)/shard_map/along_head/ppermute | solution.py:372
  15.8 6.4 %collective-permute-start.6 = (bf16[2,320,128]{2,1,0:T(8,128)(2,1)S(1)}, bf16[2,320,128]{2,1,0:T(8,128)(2,1)S(1)}, u32[]{:S(2)}, u32[]{:S(2)}) collective-permute-start(bf16[2,320,128]{2,1,0:T(8,128)(2,1)S(1)} %collective-permute-done.1.refs_2_.refs_11_), channel_id=1, source_target_pairs={{0,4},{4,0},{8,12},{12,8},{1,5},{5,1},{9,13},{13,9},{2,6},{6,2},{1... | collective-permute-start | bytes 491528 | tf_op jit(solution)/shard_map/along_seq/ppermute | solution.py:368
  18.7 5.6 %collective-permute-start.4 = (bf16[2,320,128]{2,1,0:T(8,128)(2,1)S(1)}, bf16[2,320,128]{2,1,0:T(8,128)(2,1)S(1)}, u32[]{:S(2)}, u32[]{:S(2)}) collective-permute-start(bf16[2,320,128]{2,1,0:T(8,128)(2,1)S(1)} %collective-permute-done.1.refs_2_.refs_11_), channel_id=1, source_target_pairs={{0,2},{2,0},{1,3},{3,1},{4,6},{6,4},{5,7},{7,5},{8,10},{10,8},{9,1... | collective-permute-start | bytes 491528 | tf_op jit(solution)/shard_map/along_head/ppermute | solution.py:372
  22.2 2.1 %collective-permute-start.7 = (bf16[2,320,128]{2,1,0:T(8,128)(2,1)S(1)}, bf16[2,320,128]{2,1,0:T(8,128)(2,1)S(1)}, u32[]{:S(2)}, u32[]{:S(2)}) collective-permute-start(bf16[2,320,128]{2,1,0:T(8,128)(2,1)S(1)} %collective-permute-done.5.refs_0_.refs_9_), channel_id=1, source_target_pairs={{0,1},{1,0},{2,3},{3,2},{4,5},{5,4},{6,7},{7,6},{8,9},{9,8},{10,11... | collective-permute-start | bytes 491528 | tf_op jit(solution)/shard_map/along_inner/ppermute | solution.py:376
  22.3 2.0 %collective-permute-start.8 = (bf16[2,320,128]{2,1,0:T(8,128)(2,1)S(1)}, bf16[2,320,128]{2,1,0:T(8,128)(2,1)S(1)}, u32[]{:S(2)}, u32[]{:S(2)}) collective-permute-start(bf16[2,320,128]{2,1,0:T(8,128)(2,1)S(1)} %collective-permute-done.6.refs_2_.refs_15_), channel_id=1, source_target_pairs={{0,1},{1,0},{2,3},{3,2},{4,5},{5,4},{6,7},{7,6},{8,9},{9,8},{10,11... | collective-permute-start | bytes 491528 | tf_op jit(solution)/shard_map/along_inner/ppermute | solution.py:376
  22.8 6.2 %collective-permute-start.9 = (bf16[2,320,128]{2,1,0:T(8,128)(2,1)S(1)}, bf16[2,320,128]{2,1,0:T(8,128)(2,1)S(1)}, u32[]{:S(2)}, u32[]{:S(2)}) collective-permute-start(bf16[2,320,128]{2,1,0:T(8,128)(2,1)S(1)} %collective-permute-done.6.refs_2_.refs_15_), channel_id=1, source_target_pairs={{0,2},{2,0},{1,3},{3,1},{4,6},{6,4},{5,7},{7,5},{8,10},{10,8},{9,1... | collective-permute-start | bytes 491528 | tf_op jit(solution)/shard_map/along_head/ppermute | solution.py:372
  29.0 1.4 %collective-permute-start.10 = (bf16[2,320,128]{2,1,0:T(8,128)(2,1)S(1)}, bf16[2,320,128]{2,1,0:T(8,128)(2,1)S(1)}, u32[]{:S(2)}, u32[]{:S(2)}) collective-permute-start(bf16[2,320,128]{2,1,0:T(8,128)(2,1)S(1)} %collective-permute-done.4.refs_0_.refs_13_), channel_id=1, source_target_pairs={{0,1},{1,0},{2,3},{3,2},{4,5},{5,4},{6,7},{7,6},{8,9},{9,8},{10,11... | collective-permute-start | bytes 491528 | tf_op jit(solution)/shard_map/along_inner/ppermute | solution.py:376
  29.0 1.6 %collective-permute-start.11 = (bf16[2,320,128]{2,1,0:T(8,128)(2,1)S(1)}, bf16[2,320,128]{2,1,0:T(8,128)(2,1)S(1)}, u32[]{:S(2)}, u32[]{:S(2)}) collective-permute-start(bf16[2,320,128]{2,1,0:T(8,128)(2,1)S(1)} %collective-permute-done.9.refs_2_.refs_17_), channel_id=1, source_target_pairs={{0,1},{1,0},{2,3},{3,2},{4,5},{5,4},{6,7},{7,6},{8,9},{9,8},{10,11... | collective-permute-start | bytes 491528 | tf_op jit(solution)/shard_map/along_inner/ppermute | solution.py:376

commit v8 on v7

--- a/solution.py
+++ b/solution.py
@@ -102,7 +102,7 @@
         finish(now, *chunk)
 
 
-def diagonal_kernel(coef, rows, sb, q_hbm, k_hbm, v_hbm, turned_q, top_ref, sum_ref, acc_ref, k_ref, turned_v, q_ref, v_ref, sems):
+def local_kernel(coef, rows, sb, q_hbm, k_hbm, v_hbm, turned_q, top_ref, sum_ref, acc_ref, k_ref, turned_v, q_ref, v_ref, sems):
     _, all_rows, width = q_ref.shape
     copies = []
     for h in range(all_rows // rows):
@@ -159,24 +159,18 @@
     top = extend(HI, diag)
     low = [masked(LO, *tile) for tile in tiles]
     settle(HI, diag, top)
-    settle(LO, low, extend(LO, low))
-
-
-def past_kernel(coef, sb, turned_q, sum_in, acc_in, k_ref, turned_v, sum_ref, acc_ref):
-    hi, _, _ = blocks_of(sb, lax.axis_index("seq"))
-    tiles = key_tiles(k_ref.shape[1])
-    totals = []
+    low_top = extend(LO, low)
 
     def score(start, size):
-        return value_dot(with_ones(k_ref[1 - hi, pl.ds(start, size)]), turned_q[HI])
+        return value_dot(with_ones(keys(LO, start, size)), turned_q[HI])
 
     def finish(s, start, size):
         p, sums = weights_of(coef, s)
-        totals.append((value_dot(turned_v[LO, :, pl.ds(start, size)], p), sums))
-
+        acc_ref[HI] += value_dot(values(LO, start, size), p)
+        sum_ref[HI] += sums
+
+    settle(LO, low, low_top)
     in_turn(tiles, score, finish)
-    acc_ref[HI] += functools.reduce(jnp.add, [part for part, _ in totals])
-    sum_ref[HI] += functools.reduce(jnp.add, [sums for _, sums in totals])
 
 
 def visit_chunks(distance, own, twin, sb, k_buf, v_buf, turned):
@@ -408,21 +402,21 @@
         if not is_power(count) or is_power(distance):
             arrived[distance] = along_seq(piece, distance)
 
-    turned_kv = jax.ShapeDtypeStruct((2, width, block_len), key_rows.dtype)
-    turned, tops, sums, acc, k_here, v_turned = pl.pallas_call(
-        functools.partial(diagonal_kernel, coef, rows),
+    turned, tops, sums, acc = pl.pallas_call(
+        functools.partial(local_kernel, coef, rows),
         in_specs=[scalars] + [anywhere] * 3,
-        out_specs=[whole] * 6,
-        out_shape=[turned_shape, sum_shape, sum_shape, acc_shape]
-        + [jax.ShapeDtypeStruct(key_rows.shape, key_rows.dtype), turned_kv],
+        out_specs=[whole] * 4,
+        out_shape=[turned_shape, sum_shape, sum_shape, acc_shape],
         scratch_shapes=[
+            pltpu.VMEM(key_rows.shape, key_rows.dtype),
+            pltpu.VMEM((2, width, block_len), key_rows.dtype),
             pltpu.VMEM((2, all_rows, width), query_rows.dtype),
             pltpu.VMEM(key_rows.shape, key_rows.dtype),
             pltpu.SemaphoreType.DMA((2 + heads,)),
         ],
-        cost_estimate=cost(2, 6_000_000),
+        cost_estimate=cost(3, 6_000_000),
         compiler_params=params,
-        name="diagonal",
+        name="local_part",
     )(sb_here, *in_hbm[:3])
     half_buffers = [
         pltpu.VMEM(half_shape.shape, half_shape.dtype),
@@ -472,17 +466,6 @@
         beside[distance] = along_inner(arrived[distance])
     across[1] = along_head(arrived[1])
     relay(3)
-    sums, acc = pl.pallas_call(
-        functools.partial(past_kernel, coef),
-        in_specs=[scalars] + [whole] * 5,
-        out_specs=[whole] * 2,
-        out_shape=[sum_shape, acc_shape],
-        input_output_aliases={2: 0, 3: 1},
-        cost_estimate=cost(1, 4_000_000),
-        compiler_params=params,
-        name="past",
-    )(sb_here, turned, sums, acc, k_here, v_turned)
-    arrived[2], acc = lax.optimization_barrier((arrived[2], acc))
     across[2] = along_head(arrived[2])
     sums, acc = attended_with(sums, acc, [near_half(d) for d in waiting])
     for ahead in distances[2:]:
@@ -492,9 +475,11 @@
         settle(ahead - 2)
         across[ahead - 1], acc = lax.optimization_barrier((across[ahead - 1], acc))
         sums, acc = attended_with(sums, acc, [far_half(ahead - 2), near_half(ahead)])
-    final = distances[-2:]
-    for distance in final:
-        settle(distance)
+    across[last], acc = lax.optimization_barrier((across[last], acc))
+    for distance in distances[-2:]:
+        beside_across[distance] = along_inner(across[distance])
+    sums, acc = attended_with(sums, acc, [far_half(last - 1)])
+    final = [last]
 
     flat = [part[d] for d in distances for part in (arrived, beside, across, beside_across)]
     attended, log_total = pl.pallas_call(

time: 35 us -> 34.5 us (0.986)
  starting transfers between devices: 12.3 us -> 11.7 us
  waiting for transfers between devices: 4.35 us -> 4.71 us
    ppermute x3, waiting for transfers between devices: 1.78 us -> 3.85 us  [along_head(): lax.ppermute(block, 'head', [(i, i ^ 1) for i in range(lax.axis_size('hea...]
    pallas_call x2 -> x3, Pallas kernels: 5.79 us -> 7.6 us  [attended_with(): pl.pallas_call(functools.partial(middle_kernel, coef, [visit[0] for visit...]
    ppermute x6, waiting for transfers between devices: 1.13 us -> 0.02 us  [along_inner(): return lax.ppermute(block, 'inner', [(0, 1), (1, 0)])]
    pallas_call x1, Pallas kernels: 4.01 us -> 2.91 us  [body(): pl.pallas_call(functools.partial(last_kernel, coef, distances, final), in...]
    pallas_call x2 -> x1, Pallas kernels: 6.48 us -> 5.58 us  [body(): pl.pallas_call(functools.partial(local_kernel, coef, rows), in_specs=[sca...]
    ppermute x3, waiting for transfers between devices: 1.44 us -> 0.84 us  [along_seq(): return lax.ppermute(block, 'seq', route)]
    ppermute x6, starting transfers between devices: 1.59 us -> 1.03 us  [along_inner(): return lax.ppermute(block, 'inner', [(0, 1), (1, 0)])]
  transfers between devices with their start and end apart: 12 -> 12, of which waited for: 5 -> 5; matrix products, arithmetic and copies ran while one was open for 0% -> 0% of each run, Pallas kernels for 35% -> 38%
where the time goes in v8:
time: 34.5 us; the launch traced here: 34.3 us
  Pallas kernels  17 us (49%)
  starting transfers between devices  11.7 us (34%)
  waiting for transfers between devices  4.71 us (14%)
  between operations  0.88 us (3%)
    pallas_call x3, Pallas kernels, attended_with(): pl.pallas_call(functools.partial(middle_kernel, coef, [visit[0] for visit...  7.6 us
    ppermute x3, starting transfers between devices, along_seq(): return lax.ppermute(block, 'seq', route)  7.16 us
    pallas_call x1, Pallas kernels, body(): pl.pallas_call(functools.partial(local_kernel, coef, rows), in_specs=[sca...  5.58 us
    ppermute x3, waiting for transfers between devices, along_head(): lax.ppermute(block, 'head', [(i, i ^ 1) for i in range(lax.axis_size('hea...  3.85 us
    ppermute x3, starting transfers between devices, along_head(): lax.ppermute(block, 'head', [(i, i ^ 1) for i in range(lax.axis_size('hea...  3.52 us
    pallas_call x1, Pallas kernels, body(): pl.pallas_call(functools.partial(last_kernel, coef, distances, final), in...  2.91 us
    ppermute x6, starting transfers between devices, along_inner(): return lax.ppermute(block, 'inner', [(0, 1), (1, 0)])  1.03 us
    pallas_call x1, Pallas kernels, body(): pl.pallas_call(piece_kernel, in_specs=[anywhere] * 3, out_specs=[whole] *...  0.95 us
  transfers between devices with their start and end apart: 12, of which 5 were waited for; matrix products, arithmetic and copies ran while one was open for 0% of the time, Pallas kernels for 38%

profile of v8, /device:TPU:0, one launch (start us, length us, event | category | flops | bytes accessed | tf_op | source)
XLA Modules:
  0.0 34.3 jit_solution(10476709530577372032)
XLA Ops:
  0.6 1.0 %pick_piece.1 = (bf16[2,320,128]{2,1,0:T(8,128)(2,1)S(1)}, s32[8]{0:T(128)S(1)}) custom-call(bf16[2,640,128]{2,1,0:T(8,128)(2,1)} %refs_2_.1, bf16[2,640,128]{2,1,0:T(8,128)(2,1)} %refs_3_.1, s32[8]{0:T(128)} %sb_hbm.1), custom_call_target="tpu_custom_call" | custom-call | bytes 400000 | tf_op jit(solution)/shard_map/pick_piece/pallas_call | solution.py:390
  1.6 4.1 %collective-permute-start.1 = (bf16[2,320,128]{2,1,0:T(8,128)(2,1)S(1)}, bf16[2,320,128]{2,1,0:T(8,128)(2,1)S(1)}, u32[]{:S(2)}, u32[]{:S(2)}) collective-permute-start(bf16[2,320,128]{2,1,0:T(8,128)(2,1)S(1)} %get-tuple-element.30), channel_id=1, source_target_pairs={{0,8},{4,12},{8,0},{12,4},{1,9},{5,13},{9,1},{13,5},{2,10},{6,14},... | collective-permute-start | bytes 491528 | tf_op jit(solution)/shard_map/along_seq/ppermute | solution.py:362
  5.7 1.6 %collective-permute-start = (bf16[2,320,128]{2,1,0:T(8,128)(2,1)S(1)}, bf16[2,320,128]{2,1,0:T(8,128)(2,1)S(1)}, u32[]{:S(2)}, u32[]{:S(2)}) collective-permute-start(bf16[2,320,128]{2,1,0:T(8,128)(2,1)S(1)} %get-tuple-element.30), channel_id=1, source_target_pairs={{0,4},{4,0},{8,12},{12,8},{1,5},{5,1},{9,13},{13,9},{2,6},{6,2},{1... | collective-permute-start | bytes 491528 | tf_op jit(solution)/shard_map/along_seq/ppermute | solution.py:362
  7.3 5.6 %local_part.1 = (bf16[2,256,1280]{2,1,0:T(8,128)(2,1)S(1)}, f32[2,8,1280]{2,1,0:T(8,128)S(1)}, f32[2,8,1280]{2,1,0:T(8,128)S(1)}, f32[2,128,1280]{2,1,0:T(8,128)S(1)}) custom-call(s32[8]{0:T(128)S(1)} %get-tuple-element.26.sb, bf16[2,320,512]{2,1,0:T(8,128)(2,1)} %refs_4_.1, bf16[2,640,128]{2,1,0:T(8,128)(2,1)} %refs_2_.1, bf16[2,640,128]{2,1,0:T(8,128)(2,1)} %refs_3_.1), custom_call_target="tpu_custom_call" | custom-call | flops 2516582400 | bytes 6000000 | tf_op jit(solution)/shard_map/local_part/pallas_call | solution.py:405
  12.9 0.7 %collective-permute-done.1.refs_2_.refs_9_ = bf16[2,320,128]{2,1,0:T(8,128)(2,1)S(1)} collective-permute-done((bf16[2,320,128]{2,1,0:T(8,128)(2,1)S(1)}, bf16[2,320,128]{2,1,0:T(8,128)(2,1)S(1)}, u32[]{:S(2)}, u32[]{:S(2)}) %collective-permute-start.1) | collective-permute-done | bytes 163872 | tf_op jit(solution)/shard_map/along_seq/ppermute | solution.py:362
  13.5 0.2 collective-permute-done.refs_0_.refs_5_
  13.7 0.0 collective-permute-start.2
  13.7 0.5 %collective-permute-start.3 = (bf16[2,320,128]{2,1,0:T(8,128)(2,1)S(1)}, bf16[2,320,128]{2,1,0:T(8,128)(2,1)S(1)}, u32[]{:S(2)}, u32[]{:S(2)}) collective-permute-start(bf16[2,320,128]{2,1,0:T(8,128)(2,1)S(1)} %collective-permute-done.1.refs_2_.refs_9_), channel_id=1, source_target_pairs={{0,1},{1,0},{2,3},{3,2},{4,5},{5,4},{6,7},{7,6},{8,9},{9,8},{10,11... | collective-permute-start | bytes 491528 | tf_op jit(solution)/shard_map/along_inner/ppermute | solution.py:370
  14.2 1.5 %collective-permute-start.6 = (bf16[2,320,128]{2,1,0:T(8,128)(2,1)S(1)}, bf16[2,320,128]{2,1,0:T(8,128)(2,1)S(1)}, u32[]{:S(2)}, u32[]{:S(2)}) collective-permute-start(bf16[2,320,128]{2,1,0:T(8,128)(2,1)S(1)} %collective-permute-done.1.refs_2_.refs_9_), channel_id=1, source_target_pairs={{0,4},{4,0},{8,12},{12,8},{1,5},{5,1},{9,13},{13,9},{2,6},{6,2},{1... | collective-permute-start | bytes 491528 | tf_op jit(solution)/shard_map/along_seq/ppermute | solution.py:362
  15.7 1.5 %collective-permute-start.5 = (bf16[2,320,128]{2,1,0:T(8,128)(2,1)S(1)}, bf16[2,320,128]{2,1,0:T(8,128)(2,1)S(1)}, u32[]{:S(2)}, u32[]{:S(2)}) collective-permute-start(bf16[2,320,128]{2,1,0:T(8,128)(2,1)S(1)} %collective-permute-done.refs_0_.refs_5_), channel_id=1, source_target_pairs={{0,2},{2,0},{1,3},{3,1},{4,6},{6,4},{5,7},{7,5},{8,10},{10,8},{9,1... | collective-permute-start | bytes 491528 | tf_op jit(solution)/shard_map/along_head/ppermute | solution.py:366
  17.2 0.5 %collective-permute-start.4 = (bf16[2,320,128]{2,1,0:T(8,128)(2,1)S(1)}, bf16[2,320,128]{2,1,0:T(8,128)(2,1)S(1)}, u32[]{:S(2)}, u32[]{:S(2)}) collective-permute-start(bf16[2,320,128]{2,1,0:T(8,128)(2,1)S(1)} %collective-permute-done.1.refs_2_.refs_9_), channel_id=1, source_target_pairs={{0,2},{2,0},{1,3},{3,1},{4,6},{6,4},{5,7},{7,5},{8,10},{10,8},{9,1... | collective-permute-start | bytes 491528 | tf_op jit(solution)/shard_map/along_head/ppermute | solution.py:366
  17.7 0.0 collective-permute-done.2.refs_1_.refs_6_
  17.7 0.0 collective-permute-done.3.refs_3_.refs_10_
  17.7 2.9 %visits_of_1_2.1 = (f32[2,8,1280]{2,1,0:T(8,128)S(1)}, f32[2,128,1280]{2,1,0:T(8,128)S(1)}) custom-call(s32[8]{0:T(128)S(1)} %get-tuple-element.26.sb, bf16[2,256,1280]{2,1,0:T(8,128)(2,1)S(1)} %get-tuple-element.27.turned_q, f32[2,8,1280]{2,1,0:T(8,128)S(1)} %get-tuple-element.29.sum_in, ...), custom_call_target="tpu_custom_call", output_to_operand_aliasing={{0}: (2, {}), {1}: (3, {})} | custom-call | flops 1677721600 | bytes 4000000 | tf_op jit(solution)/shard_map/visits_of_1_2/pallas_call | solution.py:434
  20.6 0.0 collective-permute-done.6.refs_2_.refs_13_
  20.6 2.2 %collective-permute-done.5.refs_0_.refs_7_ = bf16[2,320,128]{2,1,0:T(8,128)(2,1)S(1)} collective-permute-done((bf16[2,320,128]{2,1,0:T(8,128)(2,1)S(1)}, bf16[2,320,128]{2,1,0:T(8,128)(2,1)S(1)}, u32[]{:S(2)}, u32[]{:S(2)}) %collective-permute-start.5) | collective-permute-done | bytes 163872 | tf_op jit(solution)/shard_map/along_head/ppermute | solution.py:366
  22.8 0.0 collective-permute-start.7
  22.8 0.5 %collective-permute-start.8 = (bf16[2,320,128]{2,1,0:T(8,128)(2,1)S(1)}, bf16[2,320,128]{2,1,0:T(8,128)(2,1)S(1)}, u32[]{:S(2)}, u32[]{:S(2)}) collective-permute-start(bf16[2,320,128]{2,1,0:T(8,128)(2,1)S(1)} %collective-permute-done.6.refs_2_.refs_13_), channel_id=1, source_target_pairs={{0,1},{1,0},{2,3},{3,2},{4,5},{5,4},{6,7},{7,6},{8,9},{9,8},{10,11... | collective-permute-start | bytes 491528 | tf_op jit(solution)/shard_map/along_inner/ppermute | solution.py:370
  23.3 1.5 %collective-permute-start.9 = (bf16[2,320,128]{2,1,0:T(8,128)(2,1)S(1)}, bf16[2,320,128]{2,1,0:T(8,128)(2,1)S(1)}, u32[]{:S(2)}, u32[]{:S(2)}) collective-permute-start(bf16[2,320,128]{2,1,0:T(8,128)(2,1)S(1)} %collective-permute-done.6.refs_2_.refs_13_), channel_id=1, source_target_pairs={{0,2},{2,0},{1,3},{3,1},{4,6},{6,4},{5,7},{7,5},{8,10},{10,8},{9,1... | collective-permute-start | bytes 491528 | tf_op jit(solution)/shard_map/along_head/ppermute | solution.py:366
  24.8 0.2 collective-permute-done.4.refs_0_.refs_11_
  25.0 0.0 collective-permute-start.10
  25.0 0.0 collective-permute-done.7.refs_1_.refs_8_
  25.0 0.0 collective-permute-done.8.refs_3_.refs_14_
  25.0 2.9 %visits_of_1_3.1 = (f32[2,8,1280]{2,1,0:T(8,128)S(1)}, f32[2,128,1280]{2,1,0:T(8,128)S(1)}) custom-call(s32[8]{0:T(128)S(1)} %get-tuple-element.26.sb, bf16[2,256,1280]{2,1,0:T(8,128)(2,1)S(1)} %get-tuple-element.27.turned_q, f32[2,8,1280]{2,1,0:T(8,128)S(1)} %get-tuple-element.36.sum_in, ...), custom_call_target="tpu_custom_call", output_to_operand_aliasing={{0}: (2, {}), {1}: (3, {})} | custom-call | flops 1677721600 | bytes 4000000 | tf_op jit(solution)/shard_map/visits_of_1_3/pallas_call | solution.py:434
  28.0 1.5 %collective-permute-done.9.refs_0_.refs_15_ = bf16[2,320,128]{2,1,0:T(8,128)(2,1)S(1)} collective-permute-done((bf16[2,320,128]{2,1,0:T(8,128)(2,1)S(1)}, bf16[2,320,128]{2,1,0:T(8,128)(2,1)S(1)}, u32[]{:S(2)}, u32[]{:S(2)}) %collective-permute-start.9) | collective-permute-done | bytes 163872 | tf_op jit(solution)/shard_map/along_head/ppermute | solution.py:366
  29.4 0.0 collective-permute-start.11
  29.4 0.0 collective-permute-done.10.refs_1_.refs_12_
  29.4 1.8 %visits_of_2.1 = (f32[2,8,1280]{2,1,0:T(8,128)S(1)}, f32[2,128,1280]{2,1,0:T(8,128)S(1)}) custom-call(s32[8]{0:T(128)S(1)} %get-tuple-element.26.sb, bf16[2,256,1280]{2,1,0:T(8,128)(2,1)S(1)} %get-tuple-element.27.turned_q, f32[2,8,1280]{2,1,0:T(8,128)S(1)} %get-tuple-element.43.sum_in, ...), custom_call_target="tpu_custom_call", output_to_operand_aliasing={{0}: (2, {}), {1}: (3, {})} | custom-call | flops 838860800 | bytes 4000000 | tf_op jit(solution)/shard_map/visits_of_2/pallas_call | solution.py:434
  31.2 0.0 collective-permute-done.11.refs_1_.refs_16_
  31.2 2.9 %last_visitor.1 = (bf16[2,320,512]{2,1,0:T(8,128)(2,1)}, f32[2,4,320]{2,1,0:T(4,128)}) custom-call(s32[8]{0:T(128)S(1)} %get-tuple-element.26.sb, bf16[2,256,1280]{2,1,0:T(8,128)(2,1)S(1)} %get-tuple-element.27.turned_q, f32[2,8,1280]{2,1,0:T(8,128)S(1)} %get-tuple-element.28.top_ref, f32[2,8,1280]{2,1,0:T(8,128)S(1)} %get-tuple-element.47.sum_ref, ...), custom_call_target="tpu_custom_call" | custom-call | flops 838860800 | bytes 7000000 | tf_op jit(solution)/shard_map/last_visitor/pallas_call | solution.py:485
Async XLA Ops:
  1.6 11.9 %collective-permute-start.1 = (bf16[2,320,128]{2,1,0:T(8,128)(2,1)S(1)}, bf16[2,320,128]{2,1,0:T(8,128)(2,1)S(1)}, u32[]{:S(2)}, u32[]{:S(2)}) collective-permute-start(bf16[2,320,128]{2,1,0:T(8,128)(2,1)S(1)} %get-tuple-element.30), channel_id=1, source_target_pairs={{0,8},{4,12},{8,0},{12,4},{1,9},{5,13},{9,1},{13,5},{2,10},{6,14},... | collective-permute-start | bytes 491528 | tf_op jit(solution)/shard_map/along_seq/ppermute | solution.py:362
  5.7 8.0 %collective-permute-start = (bf16[2,320,128]{2,1,0:T(8,128)(2,1)S(1)}, bf16[2,320,128]{2,1,0:T(8,128)(2,1)S(1)}, u32[]{:S(2)}, u32[]{:S(2)}) collective-permute-start(bf16[2,320,128]{2,1,0:T(8,128)(2,1)S(1)} %get-tuple-element.30), channel_id=1, source_target_pairs={{0,4},{4,0},{8,12},{12,8},{1,5},{5,1},{9,13},{13,9},{2,6},{6,2},{1... | collective-permute-start | bytes 491528 | tf_op jit(solution)/shard_map/along_seq/ppermute | solution.py:362
  13.7 4.0 %collective-permute-start.2 = (bf16[2,320,128]{2,1,0:T(8,128)(2,1)S(1)}, bf16[2,320,128]{2,1,0:T(8,128)(2,1)S(1)}, u32[]{:S(2)}, u32[]{:S(2)}) collective-permute-start(bf16[2,320,128]{2,1,0:T(8,128)(2,1)S(1)} %collective-permute-done.refs_0_.refs_5_), channel_id=1, source_target_pairs={{0,1},{1,0},{2,3},{3,2},{4,5},{5,4},{6,7},{7,6},{8,9},{9,8},{10,11... | collective-permute-start | bytes 491528 | tf_op jit(solution)/shard_map/along_inner/ppermute | solution.py:370
  13.7 4.0 %collective-permute-start.3 = (bf16[2,320,128]{2,1,0:T(8,128)(2,1)S(1)}, bf16[2,320,128]{2,1,0:T(8,128)(2,1)S(1)}, u32[]{:S(2)}, u32[]{:S(2)}) collective-permute-start(bf16[2,320,128]{2,1,0:T(8,128)(2,1)S(1)} %collective-permute-done.1.refs_2_.refs_9_), channel_id=1, source_target_pairs={{0,1},{1,0},{2,3},{3,2},{4,5},{5,4},{6,7},{7,6},{8,9},{9,8},{10,11... | collective-permute-start | bytes 491528 | tf_op jit(solution)/shard_map/along_inner/ppermute | solution.py:370
  14.2 6.4 %collective-permute-start.6 = (bf16[2,320,128]{2,1,0:T(8,128)(2,1)S(1)}, bf16[2,320,128]{2,1,0:T(8,128)(2,1)S(1)}, u32[]{:S(2)}, u32[]{:S(2)}) collective-permute-start(bf16[2,320,128]{2,1,0:T(8,128)(2,1)S(1)} %collective-permute-done.1.refs_2_.refs_9_), channel_id=1, source_target_pairs={{0,4},{4,0},{8,12},{12,8},{1,5},{5,1},{9,13},{13,9},{2,6},{6,2},{1... | collective-permute-start | bytes 491528 | tf_op jit(solution)/shard_map/along_seq/ppermute | solution.py:362
  15.7 7.1 %collective-permute-start.5 = (bf16[2,320,128]{2,1,0:T(8,128)(2,1)S(1)}, bf16[2,320,128]{2,1,0:T(8,128)(2,1)S(1)}, u32[]{:S(2)}, u32[]{:S(2)}) collective-permute-start(bf16[2,320,128]{2,1,0:T(8,128)(2,1)S(1)} %collective-permute-done.refs_0_.refs_5_), channel_id=1, source_target_pairs={{0,2},{2,0},{1,3},{3,1},{4,6},{6,4},{5,7},{7,5},{8,10},{10,8},{9,1... | collective-permute-start | bytes 491528 | tf_op jit(solution)/shard_map/along_head/ppermute | solution.py:366
  17.2 7.8 %collective-permute-start.4 = (bf16[2,320,128]{2,1,0:T(8,128)(2,1)S(1)}, bf16[2,320,128]{2,1,0:T(8,128)(2,1)S(1)}, u32[]{:S(2)}, u32[]{:S(2)}) collective-permute-start(bf16[2,320,128]{2,1,0:T(8,128)(2,1)S(1)} %collective-permute-done.1.refs_2_.refs_9_), channel_id=1, source_target_pairs={{0,2},{2,0},{1,3},{3,1},{4,6},{6,4},{5,7},{7,5},{8,10},{10,8},{9,1... | collective-permute-start | bytes 491528 | tf_op jit(solution)/shard_map/along_head/ppermute | solution.py:366
  22.8 2.2 %collective-permute-start.7 = (bf16[2,320,128]{2,1,0:T(8,128)(2,1)S(1)}, bf16[2,320,128]{2,1,0:T(8,128)(2,1)S(1)}, u32[]{:S(2)}, u32[]{:S(2)}) collective-permute-start(bf16[2,320,128]{2,1,0:T(8,128)(2,1)S(1)} %collective-permute-done.5.refs_0_.refs_7_), channel_id=1, source_target_pairs={{0,1},{1,0},{2,3},{3,2},{4,5},{5,4},{6,7},{7,6},{8,9},{9,8},{10,11... | collective-permute-start | bytes 491528 | tf_op jit(solution)/shard_map/along_inner/ppermute | solution.py:370
  22.8 2.2 %collective-permute-start.8 = (bf16[2,320,128]{2,1,0:T(8,128)(2,1)S(1)}, bf16[2,320,128]{2,1,0:T(8,128)(2,1)S(1)}, u32[]{:S(2)}, u32[]{:S(2)}) collective-permute-start(bf16[2,320,128]{2,1,0:T(8,128)(2,1)S(1)} %collective-permute-done.6.refs_2_.refs_13_), channel_id=1, source_target_pairs={{0,1},{1,0},{2,3},{3,2},{4,5},{5,4},{6,7},{7,6},{8,9},{9,8},{10,11... | collective-permute-start | bytes 491528 | tf_op jit(solution)/shard_map/along_inner/ppermute | solution.py:370
  23.3 6.1 %collective-permute-start.9 = (bf16[2,320,128]{2,1,0:T(8,128)(2,1)S(1)}, bf16[2,320,128]{2,1,0:T(8,128)(2,1)S(1)}, u32[]{:S(2)}, u32[]{:S(2)}) collective-permute-start(bf16[2,320,128]{2,1,0:T(8,128)(2,1)S(1)} %collective-permute-done.6.refs_2_.refs_13_), channel_id=1, source_target_pairs={{0,2},{2,0},{1,3},{3,1},{4,6},{6,4},{5,7},{7,5},{8,10},{10,8},{9,1... | collective-permute-start | bytes 491528 | tf_op jit(solution)/shard_map/along_head/ppermute | solution.py:366
  25.0 4.4 %collective-permute-start.10 = (bf16[2,320,128]{2,1,0:T(8,128)(2,1)S(1)}, bf16[2,320,128]{2,1,0:T(8,128)(2,1)S(1)}, u32[]{:S(2)}, u32[]{:S(2)}) collective-permute-start(bf16[2,320,128]{2,1,0:T(8,128)(2,1)S(1)} %collective-permute-done.4.refs_0_.refs_11_), channel_id=1, source_target_pairs={{0,1},{1,0},{2,3},{3,2},{4,5},{5,4},{6,7},{7,6},{8,9},{9,8},{10,11... | collective-permute-start | bytes 491528 | tf_op jit(solution)/shard_map/along_inner/ppermute | solution.py:370
  29.4 1.8 %collective-permute-start.11 = (bf16[2,320,128]{2,1,0:T(8,128)(2,1)S(1)}, bf16[2,320,128]{2,1,0:T(8,128)(2,1)S(1)}, u32[]{:S(2)}, u32[]{:S(2)}) collective-permute-start(bf16[2,320,128]{2,1,0:T(8,128)(2,1)S(1)} %collective-permute-done.9.refs_0_.refs_15_), channel_id=1, source_target_pairs={{0,1},{1,0},{2,3},{3,2},{4,5},{5,4},{6,7},{7,6},{8,9},{9,8},{10,11... | collective-permute-start | bytes 491528 | tf_op jit(solution)/shard_map/along_inner/ppermute | solution.py:370

commit v9 on v8

--- a/solution.py
+++ b/solution.py
@@ -46,19 +46,29 @@
     return [(start, min(TILE, count - start)) for start in range(0, count, TILE)]
 
 
-def piece_kernel(k_hbm, v_hbm, sb_hbm, piece, sb_out, sems):
+def piece_kernel(k_hbm, v_hbm, sb_hbm, piece, far_piece, sb_out, sems):
     half = piece.shape[1]
     inner = lax.axis_index("inner")
-    mine = pl.ds(pl.multiple_of(lax.rem(lax.axis_index("head"), 2) * half, half), half)
-    sb_copy = pltpu.make_async_copy(sb_hbm, sb_out, sems.at[1])
+    own_half = lax.rem(lax.axis_index("head"), 2)
+
+    def copies(src):
+        found = []
+        for place, (part, target) in enumerate([(own_half, piece), (1 - own_half, far_piece)]):
+            rows = pl.ds(pl.multiple_of(part * half, half), half)
+            found.append(pltpu.make_async_copy(src.at[:, rows], target, sems.at[place]))
+        return found
+
     for value, src in enumerate((k_hbm, v_hbm)):
 
         @pl.when(inner == value)
         def _():
-            pltpu.make_async_copy(src.at[:, mine], piece, sems.at[0]).start()
-
+            for copy in copies(src):
+                copy.start()
+
+    sb_copy = pltpu.make_async_copy(sb_hbm, sb_out, sems.at[2])
     sb_copy.start()
-    pltpu.make_async_copy(k_hbm.at[:, mine], piece, sems.at[0]).wait()
+    for copy in copies(k_hbm):
+        copy.wait()
     sb_copy.wait()
 
 
@@ -387,12 +397,12 @@
         pltpu.with_memory_space_constraint(x, pltpu.HBM) for x in (query_rows, key_rows, value_rows, slot_block)
     ]
     half_shape = jax.ShapeDtypeStruct((2, block_len // 2, width), key_rows.dtype)
-    piece, sb_here = pl.pallas_call(
+    piece, far_piece, sb_here = pl.pallas_call(
         piece_kernel,
         in_specs=[anywhere] * 3,
-        out_specs=[whole] * 2,
-        out_shape=[half_shape, jax.ShapeDtypeStruct(slot_block.shape, slot_block.dtype)],
-        scratch_shapes=[pltpu.SemaphoreType.DMA((2,))],
+        out_specs=[whole] * 3,
+        out_shape=[half_shape, half_shape, jax.ShapeDtypeStruct(slot_block.shape, slot_block.dtype)],
+        scratch_shapes=[pltpu.SemaphoreType.DMA((3,))],
         cost_estimate=pl.CostEstimate(flops=0, bytes_accessed=400_000, transcendentals=0),
         compiler_params=params,
         name="pick_piece",
@@ -459,26 +469,33 @@
         beside_across[distance] = along_inner(across[distance])
 
     last = distances[-1]
-    for distance in sorted(arrived, reverse=True):
+    ready = sorted(arrived, reverse=True)
+    *first, acc = lax.optimization_barrier((*(arrived[d] for d in ready), acc))
+    arrived.update(zip(ready, first))
+
+    def meet(distance):
+        nonlocal acc
         arrived[distance], acc = lax.optimization_barrier((arrived[distance], acc))
-    waiting = distances[:2]
-    for distance in waiting:
-        beside[distance] = along_inner(arrived[distance])
-    across[1] = along_head(arrived[1])
+
     relay(3)
     across[2] = along_head(arrived[2])
-    sums, acc = attended_with(sums, acc, [near_half(d) for d in waiting])
+    for distance in (1, 2):
+        beside[distance] = along_inner(arrived[distance])
+    sums, acc = attended_with(sums, acc, [near_half(1), near_half(2)])
     for ahead in distances[2:]:
         relay(ahead)
-        arrived[ahead], acc = lax.optimization_barrier((arrived[ahead], acc))
+        meet(ahead)
         spread(ahead)
-        settle(ahead - 2)
-        across[ahead - 1], acc = lax.optimization_barrier((across[ahead - 1], acc))
-        sums, acc = attended_with(sums, acc, [far_half(ahead - 2), near_half(ahead)])
-    across[last], acc = lax.optimization_barrier((across[last], acc))
-    for distance in distances[-2:]:
+        if ahead == 3:
+            far_piece, acc = lax.optimization_barrier((far_piece, acc))
+            across[1] = along_seq(far_piece, 1)
+        settle(ahead - 1)
+        sums, acc = attended_with(sums, acc, [far_half(ahead - 1), near_half(ahead)])
+    tied = (across[last], across[1], acc)
+    across[last], across[1], acc = lax.optimization_barrier(tied)
+    for distance in (1, last):
         beside_across[distance] = along_inner(across[distance])
-    sums, acc = attended_with(sums, acc, [far_half(last - 1)])
+    sums, acc = attended_with(sums, acc, [far_half(1)])
     final = [last]
 
     flat = [part[d] for d in distances for part in (arrived, beside, across, beside_across)]

time: 34.5 us -> 35.9 us (1.041)
  waiting for transfers between devices: 4.71 us -> 5.48 us
  starting transfers between devices: 11.7 us -> 12.3 us
    ppermute x3 -> x2, waiting for transfers between devices: 3.85 us -> 2.32 us  [along_head(): lax.ppermute(block, 'head', [(i, i ^ 1) for i in range(lax.axis_size('hea...]
    ppermute x3 -> x4, waiting for transfers between devices: 0.84 us -> 2.26 us  [along_seq(): return lax.ppermute(block, 'seq', route)]
    ppermute x6, waiting for transfers between devices: 0.02 us -> 0.9 us  [along_inner(): return lax.ppermute(block, 'inner', [(0, 1), (1, 0)])]
    ppermute x3 -> x4, starting transfers between devices: 7.16 us -> 7.75 us  [along_seq(): return lax.ppermute(block, 'seq', route)]
    ppermute x3 -> x2, starting transfers between devices: 3.52 us -> 2.98 us  [along_head(): lax.ppermute(block, 'head', [(i, i ^ 1) for i in range(lax.axis_size('hea...]
    ppermute x6, starting transfers between devices: 1.03 us -> 1.53 us  [along_inner(): return lax.ppermute(block, 'inner', [(0, 1), (1, 0)])]
  transfers between devices with their start and end apart: 12 -> 12, of which waited for: 5 -> 7; matrix products, arithmetic and copies ran while one was open for 0% -> 0% of each run, Pallas kernels for 38% -> 37%
where the time goes in v9:
time: 35.9 us; the launch traced here: 35.7 us
  Pallas kernels  17.1 us (48%)
  starting transfers between devices  12.3 us (34%)
  waiting for transfers between devices  5.48 us (15%)
  between operations  0.87 us (2%)
    ppermute x4, starting transfers between devices, along_seq(): return lax.ppermute(block, 'seq', route)  7.75 us
    pallas_call x3, Pallas kernels, attended_with(): pl.pallas_call(functools.partial(middle_kernel, coef, [visit[0] for visit...  7.6 us
    pallas_call x1, Pallas kernels, body(): pl.pallas_call(functools.partial(local_kernel, coef, rows), in_specs=[sca...  5.58 us
    ppermute x2, starting transfers between devices, along_head(): lax.ppermute(block, 'head', [(i, i ^ 1) for i in range(lax.axis_size('hea...  2.98 us
    pallas_call x1, Pallas kernels, body(): pl.pallas_call(functools.partial(last_kernel, coef, distances, final), in...  2.91 us
    ppermute x2, waiting for transfers between devices, along_head(): lax.ppermute(block, 'head', [(i, i ^ 1) for i in range(lax.axis_size('hea...  2.32 us
    ppermute x4, waiting for transfers between devices, along_seq(): return lax.ppermute(block, 'seq', route)  2.26 us
    ppermute x6, starting transfers between devices, along_inner(): return lax.ppermute(block, 'inner', [(0, 1), (1, 0)])  1.53 us
  transfers between devices with their start and end apart: 12, of which 7 were waited for; matrix products, arithmetic and copies ran while one was open for 0% of the time, Pallas kernels for 37%

profile of v9, /device:TPU:0, one launch (start us, length us, event | category | flops | bytes accessed | tf_op | source)
XLA Modules:
  0.0 35.7 jit_solution(5503799796636780837)
XLA Ops:
  0.6 1.0 %pick_piece.1 = (bf16[2,320,128]{2,1,0:T(8,128)(2,1)S(1)}, bf16[2,320,128]{2,1,0:T(8,128)(2,1)S(1)}, s32[8]{0:T(128)S(1)}) custom-call(bf16[2,640,128]{2,1,0:T(8,128)(2,1)} %refs_2_.1, bf16[2,640,128]{2,1,0:T(8,128)(2,1)} %refs_3_.1, s32[8]{0:T(128)} %sb_hbm.1), custom_call_target="tpu_custom_call" | custom-call | bytes 400000 | tf_op jit(solution)/shard_map/pick_piece/pallas_call | solution.py:400
  1.7 4.1 %collective-permute-start = (bf16[2,320,128]{2,1,0:T(8,128)(2,1)S(1)}, bf16[2,320,128]{2,1,0:T(8,128)(2,1)S(1)}, u32[]{:S(2)}, u32[]{:S(2)}) collective-permute-start(bf16[2,320,128]{2,1,0:T(8,128)(2,1)S(1)} %get-tuple-element.31), channel_id=1, source_target_pairs={{0,8},{4,12},{8,0},{12,4},{1,9},{5,13},{9,1},{13,5},{2,10},{6,14},... | collective-permute-start | bytes 491528 | tf_op jit(solution)/shard_map/along_seq/ppermute | solution.py:372
  5.8 1.6 %collective-permute-start.1 = (bf16[2,320,128]{2,1,0:T(8,128)(2,1)S(1)}, bf16[2,320,128]{2,1,0:T(8,128)(2,1)S(1)}, u32[]{:S(2)}, u32[]{:S(2)}) collective-permute-start(bf16[2,320,128]{2,1,0:T(8,128)(2,1)S(1)} %get-tuple-element.31), channel_id=1, source_target_pairs={{0,4},{4,0},{8,12},{12,8},{1,5},{5,1},{9,13},{13,9},{2,6},{6,2},{1... | collective-permute-start | bytes 491528 | tf_op jit(solution)/shard_map/along_seq/ppermute | solution.py:372
  7.4 5.6 %local_part.1 = (bf16[2,256,1280]{2,1,0:T(8,128)(2,1)S(1)}, f32[2,8,1280]{2,1,0:T(8,128)S(1)}, f32[2,8,1280]{2,1,0:T(8,128)S(1)}, f32[2,128,1280]{2,1,0:T(8,128)S(1)}) custom-call(s32[8]{0:T(128)S(1)} %get-tuple-element.27.sb, bf16[2,320,512]{2,1,0:T(8,128)(2,1)} %refs_4_.1, bf16[2,640,128]{2,1,0:T(8,128)(2,1)} %refs_2_.1, bf16[2,640,128]{2,1,0:T(8,128)(2,1)} %refs_3_.1), custom_call_target="tpu_custom_call" | custom-call | flops 2516582400 | bytes 6000000 | tf_op jit(solution)/shard_map/local_part/pallas_call | solution.py:415
  12.9 0.6 %collective-permute-done.refs_2_.refs_9_ = bf16[2,320,128]{2,1,0:T(8,128)(2,1)S(1)} collective-permute-done((bf16[2,320,128]{2,1,0:T(8,128)(2,1)S(1)}, bf16[2,320,128]{2,1,0:T(8,128)(2,1)S(1)}, u32[]{:S(2)}, u32[]{:S(2)}) %collective-permute-start) | collective-permute-done | bytes 163872 | tf_op jit(solution)/shard_map/along_seq/ppermute | solution.py:372
  13.6 0.2 collective-permute-done.1.refs_0_.refs_5_
  13.8 0.0 collective-permute-start.2
  13.8 0.5 %collective-permute-start.3 = (bf16[2,320,128]{2,1,0:T(8,128)(2,1)S(1)}, bf16[2,320,128]{2,1,0:T(8,128)(2,1)S(1)}, u32[]{:S(2)}, u32[]{:S(2)}) collective-permute-start(bf16[2,320,128]{2,1,0:T(8,128)(2,1)S(1)} %collective-permute-done.refs_2_.refs_9_), channel_id=1, source_target_pairs={{0,1},{1,0},{2,3},{3,2},{4,5},{5,4},{6,7},{7,6},{8,9},{9,8},{10,11... | collective-permute-start | bytes 491528 | tf_op jit(solution)/shard_map/along_inner/ppermute | solution.py:380
  14.3 1.5 %collective-permute-start.5 = (bf16[2,320,128]{2,1,0:T(8,128)(2,1)S(1)}, bf16[2,320,128]{2,1,0:T(8,128)(2,1)S(1)}, u32[]{:S(2)}, u32[]{:S(2)}) collective-permute-start(bf16[2,320,128]{2,1,0:T(8,128)(2,1)S(1)} %collective-permute-done.refs_2_.refs_9_), channel_id=1, source_target_pairs={{0,4},{4,0},{8,12},{12,8},{1,5},{5,1},{9,13},{13,9},{2,6},{6,2},{1... | collective-permute-start | bytes 491528 | tf_op jit(solution)/shard_map/along_seq/ppermute | solution.py:372
  15.8 1.5 %collective-permute-start.4 = (bf16[2,320,128]{2,1,0:T(8,128)(2,1)S(1)}, bf16[2,320,128]{2,1,0:T(8,128)(2,1)S(1)}, u32[]{:S(2)}, u32[]{:S(2)}) collective-permute-start(bf16[2,320,128]{2,1,0:T(8,128)(2,1)S(1)} %collective-permute-done.refs_2_.refs_9_), channel_id=1, source_target_pairs={{0,2},{2,0},{1,3},{3,1},{4,6},{6,4},{5,7},{7,5},{8,10},{10,8},{9,1... | collective-permute-start | bytes 491528 | tf_op jit(solution)/shard_map/along_head/ppermute | solution.py:376
  17.3 0.0 collective-permute-done.2.refs_1_.refs_6_
  17.3 0.0 collective-permute-done.3.refs_3_.refs_10_
  17.3 2.9 %visits_of_1_2.1 = (f32[2,8,1280]{2,1,0:T(8,128)S(1)}, f32[2,128,1280]{2,1,0:T(8,128)S(1)}) custom-call(s32[8]{0:T(128)S(1)} %get-tuple-element.27.sb, bf16[2,256,1280]{2,1,0:T(8,128)(2,1)S(1)} %get-tuple-element.28.turned_q, f32[2,8,1280]{2,1,0:T(8,128)S(1)} %get-tuple-element.30.sum_in, ...), custom_call_target="tpu_custom_call", output_to_operand_aliasing={{0}: (2, {}), {1}: (3, {})} | custom-call | flops 1677721600 | bytes 4000000 | tf_op jit(solution)/shard_map/visits_of_1_2/pallas_call | solution.py:444
  20.2 0.2 collective-permute-done.5.refs_2_.refs_13_
  20.4 1.2 %collective-permute-done.4.refs_0_.refs_11_ = bf16[2,320,128]{2,1,0:T(8,128)(2,1)S(1)} collective-permute-done((bf16[2,320,128]{2,1,0:T(8,128)(2,1)S(1)}, bf16[2,320,128]{2,1,0:T(8,128)(2,1)S(1)}, u32[]{:S(2)}, u32[]{:S(2)}) %collective-permute-start.4) | collective-permute-done | bytes 163872 | tf_op jit(solution)/shard_map/along_head/ppermute | solution.py:376
  21.6 0.0 collective-permute-start.6
  21.6 0.5 %collective-permute-start.7 = (bf16[2,320,128]{2,1,0:T(8,128)(2,1)S(1)}, bf16[2,320,128]{2,1,0:T(8,128)(2,1)S(1)}, u32[]{:S(2)}, u32[]{:S(2)}) collective-permute-start(bf16[2,320,128]{2,1,0:T(8,128)(2,1)S(1)} %collective-permute-done.5.refs_2_.refs_13_), channel_id=1, source_target_pairs={{0,1},{1,0},{2,3},{3,2},{4,5},{5,4},{6,7},{7,6},{8,9},{9,8},{10,11... | collective-permute-start | bytes 491528 | tf_op jit(solution)/shard_map/along_inner/ppermute | solution.py:380
  22.1 1.5 %collective-permute-start.8 = (bf16[2,320,128]{2,1,0:T(8,128)(2,1)S(1)}, bf16[2,320,128]{2,1,0:T(8,128)(2,1)S(1)}, u32[]{:S(2)}, u32[]{:S(2)}) collective-permute-start(bf16[2,320,128]{2,1,0:T(8,128)(2,1)S(1)} %collective-permute-done.5.refs_2_.refs_13_), channel_id=1, source_target_pairs={{0,2},{2,0},{1,3},{3,1},{4,6},{6,4},{5,7},{7,5},{8,10},{10,8},{9,1... | collective-permute-start | bytes 491528 | tf_op jit(solution)/shard_map/along_head/ppermute | solution.py:376
  23.6 0.6 %collective-permute-start.9 = (bf16[2,320,128]{2,1,0:T(8,128)(2,1)S(1)}, bf16[2,320,128]{2,1,0:T(8,128)(2,1)S(1)}, u32[]{:S(2)}, u32[]{:S(2)}) collective-permute-start(bf16[2,320,128]{2,1,0:T(8,128)(2,1)S(1)} %get-tuple-element.45), channel_id=1, source_target_pairs={{0,4},{4,0},{8,12},{12,8},{1,5},{5,1},{9,13},{13,9},{2,6},{6,2},{1... | collective-permute-start | bytes 491528 | tf_op jit(solution)/shard_map/along_seq/ppermute | solution.py:372
  24.2 0.0 collective-permute-done.6.refs_1_.refs_12_
  24.2 0.0 collective-permute-done.7.refs_3_.refs_14_
  24.2 2.9 %visits_of_2_3.1 = (f32[2,8,1280]{2,1,0:T(8,128)S(1)}, f32[2,128,1280]{2,1,0:T(8,128)S(1)}) custom-call(s32[8]{0:T(128)S(1)} %get-tuple-element.27.sb, bf16[2,256,1280]{2,1,0:T(8,128)(2,1)S(1)} %get-tuple-element.28.turned_q, f32[2,8,1280]{2,1,0:T(8,128)S(1)} %get-tuple-element.36.sum_in, ...), custom_call_target="tpu_custom_call", output_to_operand_aliasing={{0}: (2, {}), {1}: (3, {})} | custom-call | flops 1677721600 | bytes 4000000 | tf_op jit(solution)/shard_map/visits_of_2_3/pallas_call | solution.py:444
  27.1 1.1 %collective-permute-done.8.refs_0_.refs_15_ = bf16[2,320,128]{2,1,0:T(8,128)(2,1)S(1)} collective-permute-done((bf16[2,320,128]{2,1,0:T(8,128)(2,1)S(1)}, bf16[2,320,128]{2,1,0:T(8,128)(2,1)S(1)}, u32[]{:S(2)}, u32[]{:S(2)}) %collective-permute-start.8) | collective-permute-done | bytes 163872 | tf_op jit(solution)/shard_map/along_head/ppermute | solution.py:376
  28.2 1.2 %collective-permute-done.9.refs_0_.refs_7_ = bf16[2,320,128]{2,1,0:T(8,128)(2,1)S(1)} collective-permute-done((bf16[2,320,128]{2,1,0:T(8,128)(2,1)S(1)}, bf16[2,320,128]{2,1,0:T(8,128)(2,1)S(1)}, u32[]{:S(2)}, u32[]{:S(2)}) %collective-permute-start.9) | collective-permute-done | bytes 163872 | tf_op jit(solution)/shard_map/along_seq/ppermute | solution.py:372
  29.4 0.0 collective-permute-start.10
  29.4 0.5 %collective-permute-start.11 = (bf16[2,320,128]{2,1,0:T(8,128)(2,1)S(1)}, bf16[2,320,128]{2,1,0:T(8,128)(2,1)S(1)}, u32[]{:S(2)}, u32[]{:S(2)}) collective-permute-start(bf16[2,320,128]{2,1,0:T(8,128)(2,1)S(1)} %collective-permute-done.8.refs_0_.refs_15_), channel_id=1, source_target_pairs={{0,1},{1,0},{2,3},{3,2},{4,5},{5,4},{6,7},{7,6},{8,9},{9,8},{10,11... | collective-permute-start | bytes 491528 | tf_op jit(solution)/shard_map/along_inner/ppermute | solution.py:380
  30.0 0.9 %collective-permute-done.10.refs_1_.refs_8_ = bf16[2,320,128]{2,1,0:T(8,128)(2,1)S(1)} collective-permute-done((bf16[2,320,128]{2,1,0:T(8,128)(2,1)S(1)}, bf16[2,320,128]{2,1,0:T(8,128)(2,1)S(1)}, u32[]{:S(2)}, u32[]{:S(2)}) %collective-permute-start.10) | collective-permute-done | bytes 163872 | tf_op jit(solution)/shard_map/along_inner/ppermute | solution.py:380
  30.8 1.8 %visits_of_1.1 = (f32[2,8,1280]{2,1,0:T(8,128)S(1)}, f32[2,128,1280]{2,1,0:T(8,128)S(1)}) custom-call(s32[8]{0:T(128)S(1)} %get-tuple-element.27.sb, bf16[2,256,1280]{2,1,0:T(8,128)(2,1)S(1)} %get-tuple-element.28.turned_q, f32[2,8,1280]{2,1,0:T(8,128)S(1)} %get-tuple-element.44.sum_in, ...), custom_call_target="tpu_custom_call", output_to_operand_aliasing={{0}: (2, {}), {1}: (3, {})} | custom-call | flops 838860800 | bytes 4000000 | tf_op jit(solution)/shard_map/visits_of_1/pallas_call | solution.py:444
  32.6 0.0 collective-permute-done.11.refs_1_.refs_16_
  32.7 2.9 %last_visitor.1 = (bf16[2,320,512]{2,1,0:T(8,128)(2,1)}, f32[2,4,320]{2,1,0:T(4,128)}) custom-call(s32[8]{0:T(128)S(1)} %get-tuple-element.27.sb, bf16[2,256,1280]{2,1,0:T(8,128)(2,1)S(1)} %get-tuple-element.28.turned_q, f32[2,8,1280]{2,1,0:T(8,128)S(1)} %get-tuple-element.29.top_ref, f32[2,8,1280]{2,1,0:T(8,128)S(1)} %get-tuple-element.49.sum_ref, ...), custom_call_target="tpu_custom_call" | custom-call | flops 838860800 | bytes 7000000 | tf_op jit(solution)/shard_map/last_visitor/pallas_call | solution.py:502
Async XLA Ops:
  1.7 11.9 %collective-permute-start = (bf16[2,320,128]{2,1,0:T(8,128)(2,1)S(1)}, bf16[2,320,128]{2,1,0:T(8,128)(2,1)S(1)}, u32[]{:S(2)}, u32[]{:S(2)}) collective-permute-start(bf16[2,320,128]{2,1,0:T(8,128)(2,1)S(1)} %get-tuple-element.31), channel_id=1, source_target_pairs={{0,8},{4,12},{8,0},{12,4},{1,9},{5,13},{9,1},{13,5},{2,10},{6,14},... | collective-permute-start | bytes 491528 | tf_op jit(solution)/shard_map/along_seq/ppermute | solution.py:372
  5.8 8.0 %collective-permute-start.1 = (bf16[2,320,128]{2,1,0:T(8,128)(2,1)S(1)}, bf16[2,320,128]{2,1,0:T(8,128)(2,1)S(1)}, u32[]{:S(2)}, u32[]{:S(2)}) collective-permute-start(bf16[2,320,128]{2,1,0:T(8,128)(2,1)S(1)} %get-tuple-element.31), channel_id=1, source_target_pairs={{0,4},{4,0},{8,12},{12,8},{1,5},{5,1},{9,13},{13,9},{2,6},{6,2},{1... | collective-permute-start | bytes 491528 | tf_op jit(solution)/shard_map/along_seq/ppermute | solution.py:372
  13.8 3.5 %collective-permute-start.2 = (bf16[2,320,128]{2,1,0:T(8,128)(2,1)S(1)}, bf16[2,320,128]{2,1,0:T(8,128)(2,1)S(1)}, u32[]{:S(2)}, u32[]{:S(2)}) collective-permute-start(bf16[2,320,128]{2,1,0:T(8,128)(2,1)S(1)} %collective-permute-done.1.refs_0_.refs_5_), channel_id=1, source_target_pairs={{0,1},{1,0},{2,3},{3,2},{4,5},{5,4},{6,7},{7,6},{8,9},{9,8},{10,11... | collective-permute-start | bytes 491528 | tf_op jit(solution)/shard_map/along_inner/ppermute | solution.py:380
  13.8 3.5 %collective-permute-start.3 = (bf16[2,320,128]{2,1,0:T(8,128)(2,1)S(1)}, bf16[2,320,128]{2,1,0:T(8,128)(2,1)S(1)}, u32[]{:S(2)}, u32[]{:S(2)}) collective-permute-start(bf16[2,320,128]{2,1,0:T(8,128)(2,1)S(1)} %collective-permute-done.refs_2_.refs_9_), channel_id=1, source_target_pairs={{0,1},{1,0},{2,3},{3,2},{4,5},{5,4},{6,7},{7,6},{8,9},{9,8},{10,11... | collective-permute-start | bytes 491528 | tf_op jit(solution)/shard_map/along_inner/ppermute | solution.py:380
  14.3 6.1 %collective-permute-start.5 = (bf16[2,320,128]{2,1,0:T(8,128)(2,1)S(1)}, bf16[2,320,128]{2,1,0:T(8,128)(2,1)S(1)}, u32[]{:S(2)}, u32[]{:S(2)}) collective-permute-start(bf16[2,320,128]{2,1,0:T(8,128)(2,1)S(1)} %collective-permute-done.refs_2_.refs_9_), channel_id=1, source_target_pairs={{0,4},{4,0},{8,12},{12,8},{1,5},{5,1},{9,13},{13,9},{2,6},{6,2},{1... | collective-permute-start | bytes 491528 | tf_op jit(solution)/shard_map/along_seq/ppermute | solution.py:372
  15.8 5.8 %collective-permute-start.4 = (bf16[2,320,128]{2,1,0:T(8,128)(2,1)S(1)}, bf16[2,320,128]{2,1,0:T(8,128)(2,1)S(1)}, u32[]{:S(2)}, u32[]{:S(2)}) collective-permute-start(bf16[2,320,128]{2,1,0:T(8,128)(2,1)S(1)} %collective-permute-done.refs_2_.refs_9_), channel_id=1, source_target_pairs={{0,2},{2,0},{1,3},{3,1},{4,6},{6,4},{5,7},{7,5},{8,10},{10,8},{9,1... | collective-permute-start | bytes 491528 | tf_op jit(solution)/shard_map/along_head/ppermute | solution.py:376
  21.6 2.6 %collective-permute-start.6 = (bf16[2,320,128]{2,1,0:T(8,128)(2,1)S(1)}, bf16[2,320,128]{2,1,0:T(8,128)(2,1)S(1)}, u32[]{:S(2)}, u32[]{:S(2)}) collective-permute-start(bf16[2,320,128]{2,1,0:T(8,128)(2,1)S(1)} %collective-permute-done.4.refs_0_.refs_11_), channel_id=1, source_target_pairs={{0,1},{1,0},{2,3},{3,2},{4,5},{5,4},{6,7},{7,6},{8,9},{9,8},{10,11... | collective-permute-start | bytes 491528 | tf_op jit(solution)/shard_map/along_inner/ppermute | solution.py:380
  21.6 2.6 %collective-permute-start.7 = (bf16[2,320,128]{2,1,0:T(8,128)(2,1)S(1)}, bf16[2,320,128]{2,1,0:T(8,128)(2,1)S(1)}, u32[]{:S(2)}, u32[]{:S(2)}) collective-permute-start(bf16[2,320,128]{2,1,0:T(8,128)(2,1)S(1)} %collective-permute-done.5.refs_2_.refs_13_), channel_id=1, source_target_pairs={{0,1},{1,0},{2,3},{3,2},{4,5},{5,4},{6,7},{7,6},{8,9},{9,8},{10,11... | collective-permute-start | bytes 491528 | tf_op jit(solution)/shard_map/along_inner/ppermute | solution.py:380
  22.1 6.1 %collective-permute-start.8 = (bf16[2,320,128]{2,1,0:T(8,128)(2,1)S(1)}, bf16[2,320,128]{2,1,0:T(8,128)(2,1)S(1)}, u32[]{:S(2)}, u32[]{:S(2)}) collective-permute-start(bf16[2,320,128]{2,1,0:T(8,128)(2,1)S(1)} %collective-permute-done.5.refs_2_.refs_13_), channel_id=1, source_target_pairs={{0,2},{2,0},{1,3},{3,1},{4,6},{6,4},{5,7},{7,5},{8,10},{10,8},{9,1... | collective-permute-start | bytes 491528 | tf_op jit(solution)/shard_map/along_head/ppermute | solution.py:376
  23.6 5.8 %collective-permute-start.9 = (bf16[2,320,128]{2,1,0:T(8,128)(2,1)S(1)}, bf16[2,320,128]{2,1,0:T(8,128)(2,1)S(1)}, u32[]{:S(2)}, u32[]{:S(2)}) collective-permute-start(bf16[2,320,128]{2,1,0:T(8,128)(2,1)S(1)} %get-tuple-element.45), channel_id=1, source_target_pairs={{0,4},{4,0},{8,12},{12,8},{1,5},{5,1},{9,13},{13,9},{2,6},{6,2},{1... | collective-permute-start | bytes 491528 | tf_op jit(solution)/shard_map/along_seq/ppermute | solution.py:372
  29.4 1.4 %collective-permute-start.10 = (bf16[2,320,128]{2,1,0:T(8,128)(2,1)S(1)}, bf16[2,320,128]{2,1,0:T(8,128)(2,1)S(1)}, u32[]{:S(2)}, u32[]{:S(2)}) collective-permute-start(bf16[2,320,128]{2,1,0:T(8,128)(2,1)S(1)} %collective-permute-done.9.refs_0_.refs_7_), channel_id=1, source_target_pairs={{0,1},{1,0},{2,3},{3,2},{4,5},{5,4},{6,7},{7,6},{8,9},{9,8},{10,11... | collective-permute-start | bytes 491528 | tf_op jit(solution)/shard_map/along_inner/ppermute | solution.py:380
  29.4 3.2 %collective-permute-start.11 = (bf16[2,320,128]{2,1,0:T(8,128)(2,1)S(1)}, bf16[2,320,128]{2,1,0:T(8,128)(2,1)S(1)}, u32[]{:S(2)}, u32[]{:S(2)}) collective-permute-start(bf16[2,320,128]{2,1,0:T(8,128)(2,1)S(1)} %collective-permute-done.8.refs_0_.refs_15_), channel_id=1, source_target_pairs={{0,1},{1,0},{2,3},{3,2},{4,5},{5,4},{6,7},{7,6},{8,9},{9,8},{10,11... | collective-permute-start | bytes 491528 | tf_op jit(solution)/shard_map/along_inner/ppermute | solution.py:380

commit v10 on v8

--- a/solution.py
+++ b/solution.py
@@ -102,7 +102,7 @@
         finish(now, *chunk)
 
 
-def local_kernel(coef, rows, sb, q_hbm, k_hbm, v_hbm, turned_q, top_ref, sum_ref, acc_ref, k_ref, turned_v, q_ref, v_ref, sems):
+def local_kernel(coef, rows, sb, q_hbm, k_hbm, v_hbm, turned_q, top_ref, sum_ref, acc_ref, notes, k_ref, turned_v, q_ref, v_ref, sems):
     _, all_rows, width = q_ref.shape
     copies = []
     for h in range(all_rows // rows):
@@ -118,6 +118,10 @@
     hi, _, _ = blocks_of(sb, lax.axis_index("seq"))
     slots = {HI: hi, LO: 1 - hi}
     tiles = key_tiles(block_len)
+    me, count = lax.axis_index("seq"), lax.axis_size("seq")
+    notes[0] = jnp.full(notes.shape[1:], hi, jnp.int32).astype(jnp.float32)
+    for distance in range(1, count):
+        notes[distance] = jnp.full(notes.shape[1:], visit_code(sb, me, distance, count), jnp.int32).astype(jnp.float32)
     for order in (HI, LO):
         turned_q[order, pl.ds(0, width)] = jnp.transpose(q_ref[slots[order]])
         turned_v[order] = jnp.transpose(v_ref[slots[order]])
@@ -173,7 +177,20 @@
     in_turn(tiles, score, finish)
 
 
-def visit_chunks(distance, own, twin, sb, k_buf, v_buf, turned):
+def visit_code(sb, me, distance, count):
+    _, _, top_block = blocks_of(sb, me)
+    other_hi, _, other_top = blocks_of(sb, source_of(me, distance, count))
+    above = top_block > other_top
+    other_lo = 1 - other_hi
+    return other_lo + 2 * jnp.where(above, other_hi, other_lo) + 4 * jnp.where(above, HI, LO)
+
+
+def noted(notes, place):
+    return jnp.max(notes[place]).astype(jnp.int32)
+
+
+def visit_chunks(distance, own, twin, notes, k_buf, v_buf, turned):
+    code = noted(notes, distance)
     inner = lax.axis_index("inner")
     for value, (own_buf, twin_buf) in enumerate([(k_buf, v_buf), (v_buf, k_buf)]):
 
@@ -184,17 +201,12 @@
 
     for slot in range(2):
         turned[slot] = jnp.transpose(v_buf[slot])
-    me = lax.axis_index("seq")
-    _, _, top_block = blocks_of(sb, me)
-    other_hi, _, other_top = blocks_of(sb, source_of(me, distance, lax.axis_size("seq")))
-    above = top_block > other_top
-    first = (HI, jnp.where(above, 0, 1 - other_hi))
-    return first, (jnp.where(above, HI, LO), jnp.where(above, 1, 1 - other_hi))
-
-
-def attend(coef, visits, sb, turned_q, sum_ref, acc_ref, buffers, done=None):
+    return (HI, code & 1), (code >> 2, (code >> 1) & 1)
+
+
+def attend(coef, visits, notes, turned_q, sum_ref, acc_ref, buffers, done=None):
     chunks, ends = [], []
-    laid_out = [visit_chunks(*visit, sb, *buffers[3 * i : 3 * i + 3]) for i, visit in enumerate(visits)]
+    laid_out = [visit_chunks(*visit, notes, *buffers[3 * i : 3 * i + 3]) for i, visit in enumerate(visits)]
     for place, pairs in enumerate(laid_out):
         k_buf, _, turned = buffers[3 * place : 3 * place + 3]
         tiles = key_tiles(k_buf.shape[1])
@@ -226,18 +238,18 @@
     return jnp.transpose(x)[:1]
 
 
-def middle_kernel(coef, distances, sb, turned_q, sum_in, acc_in, *refs):
+def middle_kernel(coef, distances, notes, turned_q, sum_in, acc_in, *refs):
     count = len(distances)
     visits = [(d, refs[2 * i], refs[2 * i + 1]) for i, d in enumerate(distances)]
     sum_ref, acc_ref, *buffers = refs[2 * count :]
-    attend(coef, visits, sb, turned_q, sum_ref, acc_ref, buffers)
-
-
-def last_kernel(coef, distances, final, sb, turned_q, top_ref, sum_ref, acc_ref, *refs):
+    attend(coef, visits, notes, turned_q, sum_ref, acc_ref, buffers)
+
+
+def last_kernel(coef, distances, final, sb_ref, notes, turned_q, top_ref, sum_ref, acc_ref, *refs):
     visits = [(d, refs[2 * i], refs[2 * i + 1]) for i, d in enumerate(final)]
     refs = refs[2 * len(final) :]
     every, rest = refs[: 4 * len(distances) + 3], refs[4 * len(distances) + 3 :]
-    out_hbm, lse_hbm, out_buf, lse_ref, *buffers, worst, k_buf, v_buf, run_top, run_acc, sem, out_sems = rest
+    out_hbm, lse_hbm, out_buf, lse_ref, *buffers, worst, k_buf, v_buf, run_top, run_acc, sb, sem, out_sems = rest
     _, rows, feats = out_buf.shape
     width = k_buf.shape[1]
     block_len, heads = k_buf.shape[0] // 2, feats // width
@@ -246,7 +258,7 @@
     me = lax.axis_index("seq")
     own_half = lax.rem(lax.axis_index("head"), 2)
     inner = lax.axis_index("inner")
-    hi, lo_block, hi_block = blocks_of(sb, me)
+    hi = noted(notes, 0)
     lse_copy = pltpu.make_async_copy(lse_ref, lse_hbm, sem)
 
     def out_copy(slot):
@@ -273,7 +285,7 @@
         worst[place + 2 : place + 3] = sums
         out_copy(slot).start()
 
-    attend(coef, visits, sb, turned_q, sum_ref, acc_ref, buffers, done)
+    attend(coef, visits, notes, turned_q, sum_ref, acc_ref, buffers, done)
     fits = jnp.max(worst[...]) < SUM_LIMIT
     lse_copy.start()
     for slot in range(2):
@@ -286,6 +298,9 @@
             copy = pltpu.make_async_copy(src, dst, sem)
             copy.start()
             copy.wait()
+
+        fetch(sb_ref, sb)
+        _, lo_block, hi_block = blocks_of(sb, me)
 
         def online(source):
             @pl.loop(0, 4 * heads)
@@ -402,11 +417,12 @@
         if not is_power(count) or is_power(distance):
             arrived[distance] = along_seq(piece, distance)
 
-    turned, tops, sums, acc = pl.pallas_call(
+    notes_shape = jax.ShapeDtypeStruct((count, SUBLANES, 128), jnp.float32)
+    turned, tops, sums, acc, notes = pl.pallas_call(
         functools.partial(local_kernel, coef, rows),
         in_specs=[scalars] + [anywhere] * 3,
-        out_specs=[whole] * 4,
-        out_shape=[turned_shape, sum_shape, sum_shape, acc_shape],
+        out_specs=[whole] * 5,
+        out_shape=[turned_shape, sum_shape, sum_shape, acc_shape, notes_shape],
         scratch_shapes=[
             pltpu.VMEM(key_rows.shape, key_rows.dtype),
             pltpu.VMEM((2, width, block_len), key_rows.dtype),
@@ -433,7 +449,7 @@
     def attended_with(sums, acc, visits):
         return pl.pallas_call(
             functools.partial(middle_kernel, coef, [visit[0] for visit in visits]),
-            in_specs=[scalars] + [whole] * (3 + 2 * len(visits)),
+            in_specs=[whole] * (4 + 2 * len(visits)),
             out_specs=[whole] * 2,
             out_shape=[sum_shape, acc_shape],
             scratch_shapes=half_buffers * len(visits),
@@ -441,7 +457,7 @@
             cost_estimate=cost(len(visits), 4_000_000),
             compiler_params=params,
             name="visits_of_" + "_".join(str(visit[0]) for visit in visits),
-        )(sb_here, turned, sums, acc, *(part for visit in visits for part in visit[1:]))
+        )(notes, turned, sums, acc, *(part for visit in visits for part in visit[1:]))
 
     def relay(distance):
         if distance in distances and distance not in arrived:
@@ -470,9 +486,9 @@
     sums, acc = attended_with(sums, acc, [near_half(d) for d in waiting])
     for ahead in distances[2:]:
         relay(ahead)
+        settle(ahead - 2)
         arrived[ahead], acc = lax.optimization_barrier((arrived[ahead], acc))
         spread(ahead)
-        settle(ahead - 2)
         across[ahead - 1], acc = lax.optimization_barrier((across[ahead - 1], acc))
         sums, acc = attended_with(sums, acc, [far_half(ahead - 2), near_half(ahead)])
     across[last], acc = lax.optimization_barrier((across[last], acc))
@@ -484,7 +500,7 @@
     flat = [part[d] for d in distances for part in (arrived, beside, across, beside_across)]
     attended, log_total = pl.pallas_call(
         functools.partial(last_kernel, coef, distances, final),
-        in_specs=[scalars] + [whole] * (4 + 2 * len(final)) + [anywhere] * (3 + len(flat)),
+        in_specs=[anywhere] + [whole] * (5 + 2 * len(final)) + [anywhere] * (3 + len(flat)),
         out_specs=[anywhere, anywhere],
         out_shape=[jax.ShapeDtypeStruct(query_rows.shape, query_rows.dtype), top_shape],
         scratch_shapes=[
@@ -498,13 +514,14 @@
             pltpu.VMEM((2 * block_len, width), key_rows.dtype),
             pltpu.VMEM((2, heads, rows, width), jnp.float32),
             pltpu.VMEM((2, heads, rows, 2 * width), jnp.float32),
+            pltpu.SMEM(slot_block.shape, slot_block.dtype),
             pltpu.SemaphoreType.DMA,
             pltpu.SemaphoreType.DMA((2,)),
         ],
         cost_estimate=cost(1, 7_000_000),
         compiler_params=params,
         name="last_visitor",
-    )(sb_here, turned, tops, sums, acc, *(part for d in final for part in far_half(d)[1:]), in_hbm[1], in_hbm[2], in_hbm[0], *flat)
+    )(sb_here, notes, turned, tops, sums, acc, *(part for d in final for part in far_half(d)[1:]), in_hbm[1], in_hbm[2], in_hbm[0], *flat)
     return attended, log_total
 
 

time: 34.5 us -> 32.2 us (0.933)
  Pallas kernels: 17 us -> 15.1 us
    pallas_call x3, Pallas kernels: 7.6 us -> 6.32 us  [attended_with(): pl.pallas_call(functools.partial(middle_kernel, coef, [visit[0] for visit...]
    pallas_call x1, Pallas kernels: 2.91 us -> 2.22 us  [body(): pl.pallas_call(functools.partial(last_kernel, coef, distances, final), in...]
    ppermute x3, waiting for transfers between devices: 3.85 us -> 3.42 us  [along_head(): lax.ppermute(block, 'head', [(i, i ^ 1) for i in range(lax.axis_size('hea...]
  transfers between devices with their start and end apart: 12 -> 12, of which waited for: 5 -> 6; matrix products, arithmetic and copies ran while one was open for 0% -> 0% of each run, Pallas kernels for 38% -> 37%
where the time goes in v10:
time: 32.2 us; the launch traced here: 32 us
  Pallas kernels  15.1 us (47%)
  starting transfers between devices  11.5 us (36%)
  waiting for transfers between devices  4.6 us (14%)
  between operations  0.86 us (3%)
    ppermute x3, starting transfers between devices, along_seq(): return lax.ppermute(block, 'seq', route)  7.11 us
    pallas_call x3, Pallas kernels, attended_with(): pl.pallas_call(functools.partial(middle_kernel, coef, [visit[0] for visit...  6.32 us
    pallas_call x1, Pallas kernels, body(): pl.pallas_call(functools.partial(local_kernel, coef, rows), in_specs=[sca...  5.59 us
    ppermute x3, waiting for transfers between devices, along_head(): lax.ppermute(block, 'head', [(i, i ^ 1) for i in range(lax.axis_size('hea...  3.42 us
    ppermute x3, starting transfers between devices, along_head(): lax.ppermute(block, 'head', [(i, i ^ 1) for i in range(lax.axis_size('hea...  3.32 us
    pallas_call x1, Pallas kernels, body(): pl.pallas_call(functools.partial(last_kernel, coef, distances, final), in...  2.22 us
    ppermute x3, waiting for transfers between devices, along_seq(): return lax.ppermute(block, 'seq', route)  1.14 us
    ppermute x6, starting transfers between devices, along_inner(): return lax.ppermute(block, 'inner', [(0, 1), (1, 0)])  1.03 us
  transfers between devices with their start and end apart: 12, of which 6 were waited for; matrix products, arithmetic and copies ran while one was open for 0% of the time, Pallas kernels for 37%

profile of v10, /device:TPU:0, one launch (start us, length us, event | category | flops | bytes accessed | tf_op | source)
XLA Modules:
  0.0 32.0 jit_solution(2751859982711083728)
XLA Ops:
  0.6 1.0 %pick_piece.1 = (bf16[2,320,128]{2,1,0:T(8,128)(2,1)S(1)}, s32[8]{0:T(128)S(1)}) custom-call(bf16[2,640,128]{2,1,0:T(8,128)(2,1)} %refs_2_.1, bf16[2,640,128]{2,1,0:T(8,128)(2,1)} %refs_3_.1, s32[8]{0:T(128)} %sb_hbm.1), custom_call_target="tpu_custom_call" | custom-call | bytes 400000 | tf_op jit(solution)/shard_map/pick_piece/pallas_call | solution.py:405
  1.6 4.1 %collective-permute-start.1 = (bf16[2,320,128]{2,1,0:T(8,128)(2,1)S(1)}, bf16[2,320,128]{2,1,0:T(8,128)(2,1)S(1)}, u32[]{:S(2)}, u32[]{:S(2)}) collective-permute-start(bf16[2,320,128]{2,1,0:T(8,128)(2,1)S(1)} %get-tuple-element.32), channel_id=1, source_target_pairs={{0,8},{4,12},{8,0},{12,4},{1,9},{5,13},{9,1},{13,5},{2,10},{6,14},... | collective-permute-start | bytes 491528 | tf_op jit(solution)/shard_map/along_seq/ppermute | solution.py:377
  5.7 1.6 %collective-permute-start = (bf16[2,320,128]{2,1,0:T(8,128)(2,1)S(1)}, bf16[2,320,128]{2,1,0:T(8,128)(2,1)S(1)}, u32[]{:S(2)}, u32[]{:S(2)}) collective-permute-start(bf16[2,320,128]{2,1,0:T(8,128)(2,1)S(1)} %get-tuple-element.32), channel_id=1, source_target_pairs={{0,4},{4,0},{8,12},{12,8},{1,5},{5,1},{9,13},{13,9},{2,6},{6,2},{1... | collective-permute-start | bytes 491528 | tf_op jit(solution)/shard_map/along_seq/ppermute | solution.py:377
  7.3 5.6 %local_part.1 = (bf16[2,256,1280]{2,1,0:T(8,128)(2,1)S(1)}, f32[2,8,1280]{2,1,0:T(8,128)S(1)}, f32[2,8,1280]{2,1,0:T(8,128)S(1)}, f32[2,128,1280]{2,1,0:T(8,128)S(1)}, f32[4,8,128]{2,1,0:T(8,128)S(1)}) custom-call(s32[8]{0:T(128)S(1)} %get-tuple-element.27.sb.sb_ref, bf16[2,320,512]{2,1,0:T(8,128)(2,1)} %refs_4_.1, bf16[2,640,128]{2,1,0:T(8,128)(2,1)} %refs_2_.1, ...), custom_call_target="tpu_custom_call" | custom-call | flops 2516582400 | bytes 6000000 | tf_op jit(solution)/shard_map/local_part/pallas_call | solution.py:421
  12.9 0.6 %collective-permute-done.1.refs_2_.refs_9_ = bf16[2,320,128]{2,1,0:T(8,128)(2,1)S(1)} collective-permute-done((bf16[2,320,128]{2,1,0:T(8,128)(2,1)S(1)}, bf16[2,320,128]{2,1,0:T(8,128)(2,1)S(1)}, u32[]{:S(2)}, u32[]{:S(2)}) %collective-permute-start.1) | collective-permute-done | bytes 163872 | tf_op jit(solution)/shard_map/along_seq/ppermute | solution.py:377
  13.5 0.2 collective-permute-done.refs_0_.refs_5_
  13.7 0.0 collective-permute-start.2
  13.7 0.5 %collective-permute-start.3 = (bf16[2,320,128]{2,1,0:T(8,128)(2,1)S(1)}, bf16[2,320,128]{2,1,0:T(8,128)(2,1)S(1)}, u32[]{:S(2)}, u32[]{:S(2)}) collective-permute-start(bf16[2,320,128]{2,1,0:T(8,128)(2,1)S(1)} %collective-permute-done.1.refs_2_.refs_9_), channel_id=1, source_target_pairs={{0,1},{1,0},{2,3},{3,2},{4,5},{5,4},{6,7},{7,6},{8,9},{9,8},{10,11... | collective-permute-start | bytes 491528 | tf_op jit(solution)/shard_map/along_inner/ppermute | solution.py:385
  14.2 1.5 %collective-permute-start.6 = (bf16[2,320,128]{2,1,0:T(8,128)(2,1)S(1)}, bf16[2,320,128]{2,1,0:T(8,128)(2,1)S(1)}, u32[]{:S(2)}, u32[]{:S(2)}) collective-permute-start(bf16[2,320,128]{2,1,0:T(8,128)(2,1)S(1)} %collective-permute-done.refs_0_.refs_5_), channel_id=1, source_target_pairs={{0,2},{2,0},{1,3},{3,1},{4,6},{6,4},{5,7},{7,5},{8,10},{10,8},{9,1... | collective-permute-start | bytes 491528 | tf_op jit(solution)/shard_map/along_head/ppermute | solution.py:381
  15.8 1.4 %collective-permute-start.5 = (bf16[2,320,128]{2,1,0:T(8,128)(2,1)S(1)}, bf16[2,320,128]{2,1,0:T(8,128)(2,1)S(1)}, u32[]{:S(2)}, u32[]{:S(2)}) collective-permute-start(bf16[2,320,128]{2,1,0:T(8,128)(2,1)S(1)} %collective-permute-done.1.refs_2_.refs_9_), channel_id=1, source_target_pairs={{0,4},{4,0},{8,12},{12,8},{1,5},{5,1},{9,13},{13,9},{2,6},{6,2},{1... | collective-permute-start | bytes 491528 | tf_op jit(solution)/shard_map/along_seq/ppermute | solution.py:377
  17.2 0.5 %collective-permute-start.4 = (bf16[2,320,128]{2,1,0:T(8,128)(2,1)S(1)}, bf16[2,320,128]{2,1,0:T(8,128)(2,1)S(1)}, u32[]{:S(2)}, u32[]{:S(2)}) collective-permute-start(bf16[2,320,128]{2,1,0:T(8,128)(2,1)S(1)} %collective-permute-done.1.refs_2_.refs_9_), channel_id=1, source_target_pairs={{0,2},{2,0},{1,3},{3,1},{4,6},{6,4},{5,7},{7,5},{8,10},{10,8},{9,1... | collective-permute-start | bytes 491528 | tf_op jit(solution)/shard_map/along_head/ppermute | solution.py:381
  17.7 0.0 collective-permute-done.2.refs_1_.refs_6_
  17.7 0.0 collective-permute-done.3.refs_3_.refs_10_
  17.7 2.5 %visits_of_1_2.1 = (f32[2,8,1280]{2,1,0:T(8,128)S(1)}, f32[2,128,1280]{2,1,0:T(8,128)S(1)}) custom-call(f32[4,8,128]{2,1,0:T(8,128)S(1)} %get-tuple-element.28.notes, bf16[2,256,1280]{2,1,0:T(8,128)(2,1)S(1)} %get-tuple-element.29.turned_q, f32[2,8,1280]{2,1,0:T(8,128)S(1)} %get-tuple-element.31.sum_in, ...), custom_call_target="tpu_custom_call", output_to_operand_aliasing={{0}: (2, {}), {1}: (3, {})} | custom-call | flops 1677721600 | bytes 4000000 | tf_op jit(solution)/shard_map/visits_of_1_2/pallas_call | solution.py:450
  20.2 1.1 %collective-permute-done.6.refs_0_.refs_7_ = bf16[2,320,128]{2,1,0:T(8,128)(2,1)S(1)} collective-permute-done((bf16[2,320,128]{2,1,0:T(8,128)(2,1)S(1)}, bf16[2,320,128]{2,1,0:T(8,128)(2,1)S(1)}, u32[]{:S(2)}, u32[]{:S(2)}) %collective-permute-start.6) | collective-permute-done | bytes 163872 | tf_op jit(solution)/shard_map/along_head/ppermute | solution.py:381
  21.3 0.3 collective-permute-done.5.refs_2_.refs_13_
  21.6 0.0 collective-permute-start.8
  21.6 0.5 %collective-permute-start.7 = (bf16[2,320,128]{2,1,0:T(8,128)(2,1)S(1)}, bf16[2,320,128]{2,1,0:T(8,128)(2,1)S(1)}, u32[]{:S(2)}, u32[]{:S(2)}) collective-permute-start(bf16[2,320,128]{2,1,0:T(8,128)(2,1)S(1)} %collective-permute-done.6.refs_0_.refs_7_), channel_id=1, source_target_pairs={{0,1},{1,0},{2,3},{3,2},{4,5},{5,4},{6,7},{7,6},{8,9},{9,8},{10,11... | collective-permute-start | bytes 491528 | tf_op jit(solution)/shard_map/along_inner/ppermute | solution.py:385
  22.1 1.2 %collective-permute-start.9 = (bf16[2,320,128]{2,1,0:T(8,128)(2,1)S(1)}, bf16[2,320,128]{2,1,0:T(8,128)(2,1)S(1)}, u32[]{:S(2)}, u32[]{:S(2)}) collective-permute-start(bf16[2,320,128]{2,1,0:T(8,128)(2,1)S(1)} %collective-permute-done.5.refs_2_.refs_13_), channel_id=1, source_target_pairs={{0,2},{2,0},{1,3},{3,1},{4,6},{6,4},{5,7},{7,5},{8,10},{10,8},{9,1... | collective-permute-start | bytes 491528 | tf_op jit(solution)/shard_map/along_head/ppermute | solution.py:381
  23.3 0.5 %collective-permute-done.4.refs_0_.refs_11_ = bf16[2,320,128]{2,1,0:T(8,128)(2,1)S(1)} collective-permute-done((bf16[2,320,128]{2,1,0:T(8,128)(2,1)S(1)}, bf16[2,320,128]{2,1,0:T(8,128)(2,1)S(1)}, u32[]{:S(2)}, u32[]{:S(2)}) %collective-permute-start.4) | collective-permute-done | bytes 163872 | tf_op jit(solution)/shard_map/along_head/ppermute | solution.py:381
  23.8 0.0 collective-permute-start.10
  23.8 0.0 collective-permute-done.8.refs_3_.refs_14_
  23.8 0.0 collective-permute-done.7.refs_1_.refs_8_
  23.8 2.5 %visits_of_1_3.1 = (f32[2,8,1280]{2,1,0:T(8,128)S(1)}, f32[2,128,1280]{2,1,0:T(8,128)S(1)}) custom-call(f32[4,8,128]{2,1,0:T(8,128)S(1)} %get-tuple-element.28.notes, bf16[2,256,1280]{2,1,0:T(8,128)(2,1)S(1)} %get-tuple-element.29.turned_q, f32[2,8,1280]{2,1,0:T(8,128)S(1)} %get-tuple-element.38.sum_in, ...), custom_call_target="tpu_custom_call", output_to_operand_aliasing={{0}: (2, {}), {1}: (3, {})} | custom-call | flops 1677721600 | bytes 4000000 | tf_op jit(solution)/shard_map/visits_of_1_3/pallas_call | solution.py:450
  26.3 1.9 %collective-permute-done.9.refs_0_.refs_15_ = bf16[2,320,128]{2,1,0:T(8,128)(2,1)S(1)} collective-permute-done((bf16[2,320,128]{2,1,0:T(8,128)(2,1)S(1)}, bf16[2,320,128]{2,1,0:T(8,128)(2,1)S(1)}, u32[]{:S(2)}, u32[]{:S(2)}) %collective-permute-start.9) | collective-permute-done | bytes 163872 | tf_op jit(solution)/shard_map/along_head/ppermute | solution.py:381
  28.2 0.0 collective-permute-start.11
  28.2 0.0 collective-permute-done.10.refs_1_.refs_12_
  28.2 1.4 %visits_of_2.1 = (f32[2,8,1280]{2,1,0:T(8,128)S(1)}, f32[2,128,1280]{2,1,0:T(8,128)S(1)}) custom-call(f32[4,8,128]{2,1,0:T(8,128)S(1)} %get-tuple-element.28.notes, bf16[2,256,1280]{2,1,0:T(8,128)(2,1)S(1)} %get-tuple-element.29.turned_q, f32[2,8,1280]{2,1,0:T(8,128)S(1)} %get-tuple-element.45.sum_in, ...), custom_call_target="tpu_custom_call", output_to_operand_aliasing={{0}: (2, {}), {1}: (3, {})} | custom-call | flops 838860800 | bytes 4000000 | tf_op jit(solution)/shard_map/visits_of_2/pallas_call | solution.py:450
  29.6 0.0 collective-permute-done.11.refs_1_.refs_16_
  29.6 2.2 %last_visitor.1 = (bf16[2,320,512]{2,1,0:T(8,128)(2,1)}, f32[2,4,320]{2,1,0:T(4,128)}) custom-call(s32[8]{0:T(128)S(1)} %get-tuple-element.27.sb.sb_ref, f32[4,8,128]{2,1,0:T(8,128)S(1)} %get-tuple-element.28.notes, bf16[2,256,1280]{2,1,0:T(8,128)(2,1)S(1)} %get-tuple-element.29.turned_q, f32[2,8,1280]{2,1,0:T(8,128)S(1)} %get-tuple-element.30.top_ref, ...), custom_call_target="tpu_custom_call" | custom-call | flops 838860800 | bytes 7000000 | tf_op jit(solution)/shard_map/last_visitor/pallas_call | solution.py:501
Async XLA Ops:
  1.6 11.9 %collective-permute-start.1 = (bf16[2,320,128]{2,1,0:T(8,128)(2,1)S(1)}, bf16[2,320,128]{2,1,0:T(8,128)(2,1)S(1)}, u32[]{:S(2)}, u32[]{:S(2)}) collective-permute-start(bf16[2,320,128]{2,1,0:T(8,128)(2,1)S(1)} %get-tuple-element.32), channel_id=1, source_target_pairs={{0,8},{4,12},{8,0},{12,4},{1,9},{5,13},{9,1},{13,5},{2,10},{6,14},... | collective-permute-start | bytes 491528 | tf_op jit(solution)/shard_map/along_seq/ppermute | solution.py:377
  5.7 8.0 %collective-permute-start = (bf16[2,320,128]{2,1,0:T(8,128)(2,1)S(1)}, bf16[2,320,128]{2,1,0:T(8,128)(2,1)S(1)}, u32[]{:S(2)}, u32[]{:S(2)}) collective-permute-start(bf16[2,320,128]{2,1,0:T(8,128)(2,1)S(1)} %get-tuple-element.32), channel_id=1, source_target_pairs={{0,4},{4,0},{8,12},{12,8},{1,5},{5,1},{9,13},{13,9},{2,6},{6,2},{1... | collective-permute-start | bytes 491528 | tf_op jit(solution)/shard_map/along_seq/ppermute | solution.py:377
  13.7 4.0 %collective-permute-start.2 = (bf16[2,320,128]{2,1,0:T(8,128)(2,1)S(1)}, bf16[2,320,128]{2,1,0:T(8,128)(2,1)S(1)}, u32[]{:S(2)}, u32[]{:S(2)}) collective-permute-start(bf16[2,320,128]{2,1,0:T(8,128)(2,1)S(1)} %collective-permute-done.refs_0_.refs_5_), channel_id=1, source_target_pairs={{0,1},{1,0},{2,3},{3,2},{4,5},{5,4},{6,7},{7,6},{8,9},{9,8},{10,11... | collective-permute-start | bytes 491528 | tf_op jit(solution)/shard_map/along_inner/ppermute | solution.py:385
  13.7 4.0 %collective-permute-start.3 = (bf16[2,320,128]{2,1,0:T(8,128)(2,1)S(1)}, bf16[2,320,128]{2,1,0:T(8,128)(2,1)S(1)}, u32[]{:S(2)}, u32[]{:S(2)}) collective-permute-start(bf16[2,320,128]{2,1,0:T(8,128)(2,1)S(1)} %collective-permute-done.1.refs_2_.refs_9_), channel_id=1, source_target_pairs={{0,1},{1,0},{2,3},{3,2},{4,5},{5,4},{6,7},{7,6},{8,9},{9,8},{10,11... | collective-permute-start | bytes 491528 | tf_op jit(solution)/shard_map/along_inner/ppermute | solution.py:385
  14.2 7.1 %collective-permute-start.6 = (bf16[2,320,128]{2,1,0:T(8,128)(2,1)S(1)}, bf16[2,320,128]{2,1,0:T(8,128)(2,1)S(1)}, u32[]{:S(2)}, u32[]{:S(2)}) collective-permute-start(bf16[2,320,128]{2,1,0:T(8,128)(2,1)S(1)} %collective-permute-done.refs_0_.refs_5_), channel_id=1, source_target_pairs={{0,2},{2,0},{1,3},{3,1},{4,6},{6,4},{5,7},{7,5},{8,10},{10,8},{9,1... | collective-permute-start | bytes 491528 | tf_op jit(solution)/shard_map/along_head/ppermute | solution.py:381
  15.8 5.8 %collective-permute-start.5 = (bf16[2,320,128]{2,1,0:T(8,128)(2,1)S(1)}, bf16[2,320,128]{2,1,0:T(8,128)(2,1)S(1)}, u32[]{:S(2)}, u32[]{:S(2)}) collective-permute-start(bf16[2,320,128]{2,1,0:T(8,128)(2,1)S(1)} %collective-permute-done.1.refs_2_.refs_9_), channel_id=1, source_target_pairs={{0,4},{4,0},{8,12},{12,8},{1,5},{5,1},{9,13},{13,9},{2,6},{6,2},{1... | collective-permute-start | bytes 491528 | tf_op jit(solution)/shard_map/along_seq/ppermute | solution.py:377
  17.2 6.6 %collective-permute-start.4 = (bf16[2,320,128]{2,1,0:T(8,128)(2,1)S(1)}, bf16[2,320,128]{2,1,0:T(8,128)(2,1)S(1)}, u32[]{:S(2)}, u32[]{:S(2)}) collective-permute-start(bf16[2,320,128]{2,1,0:T(8,128)(2,1)S(1)} %collective-permute-done.1.refs_2_.refs_9_), channel_id=1, source_target_pairs={{0,2},{2,0},{1,3},{3,1},{4,6},{6,4},{5,7},{7,5},{8,10},{10,8},{9,1... | collective-permute-start | bytes 491528 | tf_op jit(solution)/shard_map/along_head/ppermute | solution.py:381
  21.6 2.3 %collective-permute-start.8 = (bf16[2,320,128]{2,1,0:T(8,128)(2,1)S(1)}, bf16[2,320,128]{2,1,0:T(8,128)(2,1)S(1)}, u32[]{:S(2)}, u32[]{:S(2)}) collective-permute-start(bf16[2,320,128]{2,1,0:T(8,128)(2,1)S(1)} %collective-permute-done.5.refs_2_.refs_13_), channel_id=1, source_target_pairs={{0,1},{1,0},{2,3},{3,2},{4,5},{5,4},{6,7},{7,6},{8,9},{9,8},{10,11... | collective-permute-start | bytes 491528 | tf_op jit(solution)/shard_map/along_inner/ppermute | solution.py:385
  21.6 2.3 %collective-permute-start.7 = (bf16[2,320,128]{2,1,0:T(8,128)(2,1)S(1)}, bf16[2,320,128]{2,1,0:T(8,128)(2,1)S(1)}, u32[]{:S(2)}, u32[]{:S(2)}) collective-permute-start(bf16[2,320,128]{2,1,0:T(8,128)(2,1)S(1)} %collective-permute-done.6.refs_0_.refs_7_), channel_id=1, source_target_pairs={{0,1},{1,0},{2,3},{3,2},{4,5},{5,4},{6,7},{7,6},{8,9},{9,8},{10,11... | collective-permute-start | bytes 491528 | tf_op jit(solution)/shard_map/along_inner/ppermute | solution.py:385
  22.1 6.1 %collective-permute-start.9 = (bf16[2,320,128]{2,1,0:T(8,128)(2,1)S(1)}, bf16[2,320,128]{2,1,0:T(8,128)(2,1)S(1)}, u32[]{:S(2)}, u32[]{:S(2)}) collective-permute-start(bf16[2,320,128]{2,1,0:T(8,128)(2,1)S(1)} %collective-permute-done.5.refs_2_.refs_13_), channel_id=1, source_target_pairs={{0,2},{2,0},{1,3},{3,1},{4,6},{6,4},{5,7},{7,5},{8,10},{10,8},{9,1... | collective-permute-start | bytes 491528 | tf_op jit(solution)/shard_map/along_head/ppermute | solution.py:381
  23.8 4.4 %collective-permute-start.10 = (bf16[2,320,128]{2,1,0:T(8,128)(2,1)S(1)}, bf16[2,320,128]{2,1,0:T(8,128)(2,1)S(1)}, u32[]{:S(2)}, u32[]{:S(2)}) collective-permute-start(bf16[2,320,128]{2,1,0:T(8,128)(2,1)S(1)} %collective-permute-done.4.refs_0_.refs_11_), channel_id=1, source_target_pairs={{0,1},{1,0},{2,3},{3,2},{4,5},{5,4},{6,7},{7,6},{8,9},{9,8},{10,11... | collective-permute-start | bytes 491528 | tf_op jit(solution)/shard_map/along_inner/ppermute | solution.py:385
  28.2 1.4 %collective-permute-start.11 = (bf16[2,320,128]{2,1,0:T(8,128)(2,1)S(1)}, bf16[2,320,128]{2,1,0:T(8,128)(2,1)S(1)}, u32[]{:S(2)}, u32[]{:S(2)}) collective-permute-start(bf16[2,320,128]{2,1,0:T(8,128)(2,1)S(1)} %collective-permute-done.9.refs_0_.refs_15_), channel_id=1, source_target_pairs={{0,1},{1,0},{2,3},{3,2},{4,5},{5,4},{6,7},{7,6},{8,9},{9,8},{10,11... | collective-permute-start | bytes 491528 | tf_op jit(solution)/shard_map/along_inner/ppermute | solution.py:385

commit v11 on v10

--- a/solution.py
+++ b/solution.py
@@ -46,20 +46,17 @@
     return [(start, min(TILE, count - start)) for start in range(0, count, TILE)]
 
 
-def piece_kernel(k_hbm, v_hbm, sb_hbm, piece, sb_out, sems):
+def piece_kernel(k_hbm, v_hbm, piece, sem):
     half = piece.shape[1]
     inner = lax.axis_index("inner")
     mine = pl.ds(pl.multiple_of(lax.rem(lax.axis_index("head"), 2) * half, half), half)
-    sb_copy = pltpu.make_async_copy(sb_hbm, sb_out, sems.at[1])
     for value, src in enumerate((k_hbm, v_hbm)):
 
         @pl.when(inner == value)
         def _():
-            pltpu.make_async_copy(src.at[:, mine], piece, sems.at[0]).start()
-
-    sb_copy.start()
-    pltpu.make_async_copy(k_hbm.at[:, mine], piece, sems.at[0]).wait()
-    sb_copy.wait()
+            pltpu.make_async_copy(src.at[:, mine], piece, sem).start()
+
+    pltpu.make_async_copy(k_hbm.at[:, mine], piece, sem).wait()
 
 
 def weights_of(coef, s):
@@ -211,10 +208,10 @@
         k_buf, _, turned = buffers[3 * place : 3 * place + 3]
         tiles = key_tiles(k_buf.shape[1])
         for order, slot in pairs:
-            for tile in tiles:
+            for tile in tiles if ends else tiles[::-1]:
                 chunks.append((len(ends), order, slot, k_buf, turned, *tile))
-            ends.append(tiles[-1][0])
-    totals = {}
+            ends.append(len(chunks) - 1)
+    totals, seen = {}, []
 
     def score(place, order, slot, k_buf, turned, start, size):
         return value_dot(with_ones(k_buf[slot, pl.ds(start, size)]), turned_q[order])
@@ -222,10 +219,11 @@
     def finish(s, place, order, slot, k_buf, turned, start, size):
         p, sums = weights_of(coef, s)
         part = value_dot(turned[slot, :, pl.ds(start, size)], p)
-        if start:
+        if place in totals:
             part, sums = totals[place][0] + part, totals[place][1] + sums
         totals[place] = part, sums
-        if start == ends[place]:
+        seen.append(place)
+        if len(seen) - 1 == ends[place]:
             acc_ref[order] += part
             sum_ref[order] += sums
             if done is not None:
@@ -402,16 +400,16 @@
         pltpu.with_memory_space_constraint(x, pltpu.HBM) for x in (query_rows, key_rows, value_rows, slot_block)
     ]
     half_shape = jax.ShapeDtypeStruct((2, block_len // 2, width), key_rows.dtype)
-    piece, sb_here = pl.pallas_call(
+    piece = pl.pallas_call(
         piece_kernel,
-        in_specs=[anywhere] * 3,
-        out_specs=[whole] * 2,
-        out_shape=[half_shape, jax.ShapeDtypeStruct(slot_block.shape, slot_block.dtype)],
-        scratch_shapes=[pltpu.SemaphoreType.DMA((2,))],
+        in_specs=[anywhere] * 2,
+        out_specs=whole,
+        out_shape=half_shape,
+        scratch_shapes=[pltpu.SemaphoreType.DMA],
         cost_estimate=pl.CostEstimate(flops=0, bytes_accessed=400_000, transcendentals=0),
         compiler_params=params,
         name="pick_piece",
-    )(*in_hbm[1:])
+    )(*in_hbm[1:3])
     arrived, across, beside, beside_across = {}, {}, {}, {}
     for distance in reversed(distances):
         if not is_power(count) or is_power(distance):
@@ -433,7 +431,7 @@
         cost_estimate=cost(3, 6_000_000),
         compiler_params=params,
         name="local_part",
-    )(sb_here, *in_hbm[:3])
+    )(in_hbm[3], *in_hbm[:3])
     half_buffers = [
         pltpu.VMEM(half_shape.shape, half_shape.dtype),
         pltpu.VMEM(half_shape.shape, half_shape.dtype),
@@ -475,14 +473,14 @@
         beside_across[distance] = along_inner(across[distance])
 
     last = distances[-1]
-    for distance in sorted(arrived, reverse=True):
-        arrived[distance], acc = lax.optimization_barrier((arrived[distance], acc))
+    arrived[2], acc = lax.optimization_barrier((arrived[2], acc))
+    relay(3)
+    arrived[1], arrived[2], acc = lax.optimization_barrier((arrived[1], arrived[2], acc))
     waiting = distances[:2]
+    across[1] = along_head(arrived[1])
+    across[2] = along_head(arrived[2])
     for distance in waiting:
         beside[distance] = along_inner(arrived[distance])
-    across[1] = along_head(arrived[1])
-    relay(3)
-    across[2] = along_head(arrived[2])
     sums, acc = attended_with(sums, acc, [near_half(d) for d in waiting])
     for ahead in distances[2:]:
         relay(ahead)
@@ -521,7 +519,7 @@
         cost_estimate=cost(1, 7_000_000),
         compiler_params=params,
         name="last_visitor",
-    )(sb_here, notes, turned, tops, sums, acc, *(part for d in final for part in far_half(d)[1:]), in_hbm[1], in_hbm[2], in_hbm[0], *flat)
+    )(in_hbm[3], notes, turned, tops, sums, acc, *(part for d in final for part in far_half(d)[1:]), in_hbm[1], in_hbm[2], in_hbm[0], *flat)
     return attended, log_total
 
 

time: 32.2 us -> 32.1 us (level)
  transfers between devices with their start and end apart: 12 -> 12, of which waited for: 6 -> 7; matrix products, arithmetic and copies ran while one was open for 0% -> 0% of each run, Pallas kernels for 37% -> 37%
where the time goes in v11:
time: 32.1 us; the launch traced here: 31.9 us
  Pallas kernels  14.9 us (46%)
  starting transfers between devices  11.5 us (36%)
  waiting for transfers between devices  4.65 us (14%)
  between operations  0.86 us (3%)
    ppermute x3, starting transfers between devices, along_seq(): return lax.ppermute(block, 'seq', route)  7.11 us
    pallas_call x3, Pallas kernels, attended_with(): pl.pallas_call(functools.partial(middle_kernel, coef, [visit[0] for visit...  6.15 us
    pallas_call x1, Pallas kernels, body(): pl.pallas_call(functools.partial(local_kernel, coef, rows), in_specs=[sca...  5.69 us
    ppermute x3, starting transfers between devices, along_head(): lax.ppermute(block, 'head', [(i, i ^ 1) for i in range(lax.axis_size('hea...  3.62 us
    ppermute x3, waiting for transfers between devices, along_head(): lax.ppermute(block, 'head', [(i, i ^ 1) for i in range(lax.axis_size('hea...  3.55 us
    pallas_call x1, Pallas kernels, body(): pl.pallas_call(functools.partial(last_kernel, coef, distances, final), in...  2.16 us
    ppermute x3, waiting for transfers between devices, along_seq(): return lax.ppermute(block, 'seq', route)  1.03 us
    pallas_call x1, Pallas kernels, body(): pl.pallas_call(piece_kernel, in_specs=[anywhere] * 2, out_specs=whole, ou...  0.94 us
  transfers between devices with their start and end apart: 12, of which 7 were waited for; matrix products, arithmetic and copies ran while one was open for 0% of the time, Pallas kernels for 37%

profile of v11, /device:TPU:0, one launch (start us, length us, event | category | flops | bytes accessed | tf_op | source)
XLA Modules:
  0.0 31.9 jit_solution(2131261289607978402)
XLA Ops:
  0.6 0.9 %pick_piece.1 = bf16[2,320,128]{2,1,0:T(8,128)(2,1)S(1)} custom-call(bf16[2,640,128]{2,1,0:T(8,128)(2,1)} %refs_2_.1, bf16[2,640,128]{2,1,0:T(8,128)(2,1)} %refs_3_.1), custom_call_target="tpu_custom_call" | custom-call | bytes 400000 | tf_op jit(solution)/shard_map/pick_piece/pallas_call | solution.py:403
  1.6 4.1 %collective-permute-start.1 = (bf16[2,320,128]{2,1,0:T(8,128)(2,1)S(1)}, bf16[2,320,128]{2,1,0:T(8,128)(2,1)S(1)}, u32[]{:S(2)}, u32[]{:S(2)}) collective-permute-start(bf16[2,320,128]{2,1,0:T(8,128)(2,1)S(1)} %pick_piece.1), channel_id=1, source_target_pairs={{0,8},{4,12},{8,0},{12,4},{1,9},{5,13},{9,1},{13,5},{2,10},{6,14},... | collective-permute-start | bytes 491528 | tf_op jit(solution)/shard_map/along_seq/ppermute | solution.py:375
  5.7 1.6 %collective-permute-start = (bf16[2,320,128]{2,1,0:T(8,128)(2,1)S(1)}, bf16[2,320,128]{2,1,0:T(8,128)(2,1)S(1)}, u32[]{:S(2)}, u32[]{:S(2)}) collective-permute-start(bf16[2,320,128]{2,1,0:T(8,128)(2,1)S(1)} %pick_piece.1), channel_id=1, source_target_pairs={{0,4},{4,0},{8,12},{12,8},{1,5},{5,1},{9,13},{13,9},{2,6},{6,2},{1... | collective-permute-start | bytes 491528 | tf_op jit(solution)/shard_map/along_seq/ppermute | solution.py:375
  7.3 5.7 %local_part.1 = (bf16[2,256,1280]{2,1,0:T(8,128)(2,1)S(1)}, f32[2,8,1280]{2,1,0:T(8,128)S(1)}, f32[2,8,1280]{2,1,0:T(8,128)S(1)}, f32[2,128,1280]{2,1,0:T(8,128)S(1)}, f32[4,8,128]{2,1,0:T(8,128)S(1)}) custom-call(s32[8]{0:T(128)} %sb_ref.1, bf16[2,320,512]{2,1,0:T(8,128)(2,1)} %refs_4_.1, bf16[2,640,128]{2,1,0:T(8,128)(2,1)} %refs_2_.1, ...), custom_call_target="tpu_custom_call" | custom-call | flops 2516582400 | bytes 6000000 | tf_op jit(solution)/shard_map/local_part/pallas_call | solution.py:419
  13.0 0.5 %collective-permute-done.1.refs_2_.refs_9_ = bf16[2,320,128]{2,1,0:T(8,128)(2,1)S(1)} collective-permute-done((bf16[2,320,128]{2,1,0:T(8,128)(2,1)S(1)}, bf16[2,320,128]{2,1,0:T(8,128)(2,1)S(1)}, u32[]{:S(2)}, u32[]{:S(2)}) %collective-permute-start.1) | collective-permute-done | bytes 163872 | tf_op jit(solution)/shard_map/along_seq/ppermute | solution.py:375
  13.5 0.2 collective-permute-done.refs_0_.refs_5_
  13.7 0.0 collective-permute-start.2
  13.7 0.5 %collective-permute-start.3 = (bf16[2,320,128]{2,1,0:T(8,128)(2,1)S(1)}, bf16[2,320,128]{2,1,0:T(8,128)(2,1)S(1)}, u32[]{:S(2)}, u32[]{:S(2)}) collective-permute-start(bf16[2,320,128]{2,1,0:T(8,128)(2,1)S(1)} %collective-permute-done.1.refs_2_.refs_9_), channel_id=1, source_target_pairs={{0,1},{1,0},{2,3},{3,2},{4,5},{5,4},{6,7},{7,6},{8,9},{9,8},{10,11... | collective-permute-start | bytes 491528 | tf_op jit(solution)/shard_map/along_inner/ppermute | solution.py:383
  14.2 1.5 %collective-permute-start.6 = (bf16[2,320,128]{2,1,0:T(8,128)(2,1)S(1)}, bf16[2,320,128]{2,1,0:T(8,128)(2,1)S(1)}, u32[]{:S(2)}, u32[]{:S(2)}) collective-permute-start(bf16[2,320,128]{2,1,0:T(8,128)(2,1)S(1)} %collective-permute-done.refs_0_.refs_5_), channel_id=1, source_target_pairs={{0,2},{2,0},{1,3},{3,1},{4,6},{6,4},{5,7},{7,5},{8,10},{10,8},{9,1... | collective-permute-start | bytes 491528 | tf_op jit(solution)/shard_map/along_head/ppermute | solution.py:379
  15.7 1.4 %collective-permute-start.5 = (bf16[2,320,128]{2,1,0:T(8,128)(2,1)S(1)}, bf16[2,320,128]{2,1,0:T(8,128)(2,1)S(1)}, u32[]{:S(2)}, u32[]{:S(2)}) collective-permute-start(bf16[2,320,128]{2,1,0:T(8,128)(2,1)S(1)} %collective-permute-done.1.refs_2_.refs_9_), channel_id=1, source_target_pairs={{0,4},{4,0},{8,12},{12,8},{1,5},{5,1},{9,13},{13,9},{2,6},{6,2},{1... | collective-permute-start | bytes 491528 | tf_op jit(solution)/shard_map/along_seq/ppermute | solution.py:375
  17.2 0.5 %collective-permute-start.4 = (bf16[2,320,128]{2,1,0:T(8,128)(2,1)S(1)}, bf16[2,320,128]{2,1,0:T(8,128)(2,1)S(1)}, u32[]{:S(2)}, u32[]{:S(2)}) collective-permute-start(bf16[2,320,128]{2,1,0:T(8,128)(2,1)S(1)} %collective-permute-done.1.refs_2_.refs_9_), channel_id=1, source_target_pairs={{0,2},{2,0},{1,3},{3,1},{4,6},{6,4},{5,7},{7,5},{8,10},{10,8},{9,1... | collective-permute-start | bytes 491528 | tf_op jit(solution)/shard_map/along_head/ppermute | solution.py:379
  17.7 0.0 collective-permute-done.2.refs_1_.refs_6_
  17.7 0.0 collective-permute-done.3.refs_3_.refs_10_
  17.7 2.4 %visits_of_1_2.1 = (f32[2,8,1280]{2,1,0:T(8,128)S(1)}, f32[2,128,1280]{2,1,0:T(8,128)S(1)}) custom-call(f32[4,8,128]{2,1,0:T(8,128)S(1)} %get-tuple-element.26.notes, bf16[2,256,1280]{2,1,0:T(8,128)(2,1)S(1)} %get-tuple-element.27.turned_q, f32[2,8,1280]{2,1,0:T(8,128)S(1)} %get-tuple-element.29.sum_in, ...), custom_call_target="tpu_custom_call", output_to_operand_aliasing={{0}: (2, {}), {1}: (3, {})} | custom-call | flops 1677721600 | bytes 4000000 | tf_op jit(solution)/shard_map/visits_of_1_2/pallas_call | solution.py:448
  20.1 1.1 %collective-permute-done.6.refs_0_.refs_7_ = bf16[2,320,128]{2,1,0:T(8,128)(2,1)S(1)} collective-permute-done((bf16[2,320,128]{2,1,0:T(8,128)(2,1)S(1)}, bf16[2,320,128]{2,1,0:T(8,128)(2,1)S(1)}, u32[]{:S(2)}, u32[]{:S(2)}) %collective-permute-start.6) | collective-permute-done | bytes 163872 | tf_op jit(solution)/shard_map/along_head/ppermute | solution.py:379
  21.3 0.0 collective-permute-start.7
  21.3 0.3 collective-permute-done.5.refs_2_.refs_13_
  21.6 0.2 collective-permute-start.8
  21.8 1.5 %collective-permute-start.9 = (bf16[2,320,128]{2,1,0:T(8,128)(2,1)S(1)}, bf16[2,320,128]{2,1,0:T(8,128)(2,1)S(1)}, u32[]{:S(2)}, u32[]{:S(2)}) collective-permute-start(bf16[2,320,128]{2,1,0:T(8,128)(2,1)S(1)} %collective-permute-done.5.refs_2_.refs_13_), channel_id=1, source_target_pairs={{0,2},{2,0},{1,3},{3,1},{4,6},{6,4},{5,7},{7,5},{8,10},{10,8},{9,1... | collective-permute-start | bytes 491528 | tf_op jit(solution)/shard_map/along_head/ppermute | solution.py:379
  23.3 0.5 %collective-permute-done.4.refs_0_.refs_11_ = bf16[2,320,128]{2,1,0:T(8,128)(2,1)S(1)} collective-permute-done((bf16[2,320,128]{2,1,0:T(8,128)(2,1)S(1)}, bf16[2,320,128]{2,1,0:T(8,128)(2,1)S(1)}, u32[]{:S(2)}, u32[]{:S(2)}) %collective-permute-start.4) | collective-permute-done | bytes 163872 | tf_op jit(solution)/shard_map/along_head/ppermute | solution.py:379
  23.8 0.0 collective-permute-start.10
  23.8 0.0 collective-permute-done.7.refs_1_.refs_8_
  23.8 0.0 collective-permute-done.8.refs_3_.refs_14_
  23.8 2.4 %visits_of_1_3.1 = (f32[2,8,1280]{2,1,0:T(8,128)S(1)}, f32[2,128,1280]{2,1,0:T(8,128)S(1)}) custom-call(f32[4,8,128]{2,1,0:T(8,128)S(1)} %get-tuple-element.26.notes, bf16[2,256,1280]{2,1,0:T(8,128)(2,1)S(1)} %get-tuple-element.27.turned_q, f32[2,8,1280]{2,1,0:T(8,128)S(1)} %get-tuple-element.36.sum_in, ...), custom_call_target="tpu_custom_call", output_to_operand_aliasing={{0}: (2, {}), {1}: (3, {})} | custom-call | flops 1677721600 | bytes 4000000 | tf_op jit(solution)/shard_map/visits_of_1_3/pallas_call | solution.py:448
  26.3 1.9 %collective-permute-done.9.refs_0_.refs_15_ = bf16[2,320,128]{2,1,0:T(8,128)(2,1)S(1)} collective-permute-done((bf16[2,320,128]{2,1,0:T(8,128)(2,1)S(1)}, bf16[2,320,128]{2,1,0:T(8,128)(2,1)S(1)}, u32[]{:S(2)}, u32[]{:S(2)}) %collective-permute-start.9) | collective-permute-done | bytes 163872 | tf_op jit(solution)/shard_map/along_head/ppermute | solution.py:379
  28.2 0.0 collective-permute-start.11
  28.2 0.0 collective-permute-done.10.refs_1_.refs_12_
  28.2 1.3 %visits_of_2.1 = (f32[2,8,1280]{2,1,0:T(8,128)S(1)}, f32[2,128,1280]{2,1,0:T(8,128)S(1)}) custom-call(f32[4,8,128]{2,1,0:T(8,128)S(1)} %get-tuple-element.26.notes, bf16[2,256,1280]{2,1,0:T(8,128)(2,1)S(1)} %get-tuple-element.27.turned_q, f32[2,8,1280]{2,1,0:T(8,128)S(1)} %get-tuple-element.43.sum_in, ...), custom_call_target="tpu_custom_call", output_to_operand_aliasing={{0}: (2, {}), {1}: (3, {})} | custom-call | flops 838860800 | bytes 4000000 | tf_op jit(solution)/shard_map/visits_of_2/pallas_call | solution.py:448
  29.5 0.1 collective-permute-done.11.refs_1_.refs_16_
  29.6 2.2 %last_visitor.1 = (bf16[2,320,512]{2,1,0:T(8,128)(2,1)}, f32[2,4,320]{2,1,0:T(4,128)}) custom-call(s32[8]{0:T(128)} %sb_ref.1, f32[4,8,128]{2,1,0:T(8,128)S(1)} %get-tuple-element.26.notes, bf16[2,256,1280]{2,1,0:T(8,128)(2,1)S(1)} %get-tuple-element.27.turned_q, f32[2,8,1280]{2,1,0:T(8,128)S(1)} %get-tuple-element.28.top_ref, ...), custom_call_target="tpu_custom_call" | custom-call | flops 838860800 | bytes 7000000 | tf_op jit(solution)/shard_map/last_visitor/pallas_call | solution.py:499
Async XLA Ops:
  1.6 11.9 %collective-permute-start.1 = (bf16[2,320,128]{2,1,0:T(8,128)(2,1)S(1)}, bf16[2,320,128]{2,1,0:T(8,128)(2,1)S(1)}, u32[]{:S(2)}, u32[]{:S(2)}) collective-permute-start(bf16[2,320,128]{2,1,0:T(8,128)(2,1)S(1)} %pick_piece.1), channel_id=1, source_target_pairs={{0,8},{4,12},{8,0},{12,4},{1,9},{5,13},{9,1},{13,5},{2,10},{6,14},... | collective-permute-start | bytes 491528 | tf_op jit(solution)/shard_map/along_seq/ppermute | solution.py:375
  5.7 8.0 %collective-permute-start = (bf16[2,320,128]{2,1,0:T(8,128)(2,1)S(1)}, bf16[2,320,128]{2,1,0:T(8,128)(2,1)S(1)}, u32[]{:S(2)}, u32[]{:S(2)}) collective-permute-start(bf16[2,320,128]{2,1,0:T(8,128)(2,1)S(1)} %pick_piece.1), channel_id=1, source_target_pairs={{0,4},{4,0},{8,12},{12,8},{1,5},{5,1},{9,13},{13,9},{2,6},{6,2},{1... | collective-permute-start | bytes 491528 | tf_op jit(solution)/shard_map/along_seq/ppermute | solution.py:375
  13.7 4.0 %collective-permute-start.2 = (bf16[2,320,128]{2,1,0:T(8,128)(2,1)S(1)}, bf16[2,320,128]{2,1,0:T(8,128)(2,1)S(1)}, u32[]{:S(2)}, u32[]{:S(2)}) collective-permute-start(bf16[2,320,128]{2,1,0:T(8,128)(2,1)S(1)} %collective-permute-done.refs_0_.refs_5_), channel_id=1, source_target_pairs={{0,1},{1,0},{2,3},{3,2},{4,5},{5,4},{6,7},{7,6},{8,9},{9,8},{10,11... | collective-permute-start | bytes 491528 | tf_op jit(solution)/shard_map/along_inner/ppermute | solution.py:383
  13.7 4.0 %collective-permute-start.3 = (bf16[2,320,128]{2,1,0:T(8,128)(2,1)S(1)}, bf16[2,320,128]{2,1,0:T(8,128)(2,1)S(1)}, u32[]{:S(2)}, u32[]{:S(2)}) collective-permute-start(bf16[2,320,128]{2,1,0:T(8,128)(2,1)S(1)} %collective-permute-done.1.refs_2_.refs_9_), channel_id=1, source_target_pairs={{0,1},{1,0},{2,3},{3,2},{4,5},{5,4},{6,7},{7,6},{8,9},{9,8},{10,11... | collective-permute-start | bytes 491528 | tf_op jit(solution)/shard_map/along_inner/ppermute | solution.py:383
  14.2 7.1 %collective-permute-start.6 = (bf16[2,320,128]{2,1,0:T(8,128)(2,1)S(1)}, bf16[2,320,128]{2,1,0:T(8,128)(2,1)S(1)}, u32[]{:S(2)}, u32[]{:S(2)}) collective-permute-start(bf16[2,320,128]{2,1,0:T(8,128)(2,1)S(1)} %collective-permute-done.refs_0_.refs_5_), channel_id=1, source_target_pairs={{0,2},{2,0},{1,3},{3,1},{4,6},{6,4},{5,7},{7,5},{8,10},{10,8},{9,1... | collective-permute-start | bytes 491528 | tf_op jit(solution)/shard_map/along_head/ppermute | solution.py:379
  15.7 5.8 %collective-permute-start.5 = (bf16[2,320,128]{2,1,0:T(8,128)(2,1)S(1)}, bf16[2,320,128]{2,1,0:T(8,128)(2,1)S(1)}, u32[]{:S(2)}, u32[]{:S(2)}) collective-permute-start(bf16[2,320,128]{2,1,0:T(8,128)(2,1)S(1)} %collective-permute-done.1.refs_2_.refs_9_), channel_id=1, source_target_pairs={{0,4},{4,0},{8,12},{12,8},{1,5},{5,1},{9,13},{13,9},{2,6},{6,2},{1... | collective-permute-start | bytes 491528 | tf_op jit(solution)/shard_map/along_seq/ppermute | solution.py:375
  17.2 6.6 %collective-permute-start.4 = (bf16[2,320,128]{2,1,0:T(8,128)(2,1)S(1)}, bf16[2,320,128]{2,1,0:T(8,128)(2,1)S(1)}, u32[]{:S(2)}, u32[]{:S(2)}) collective-permute-start(bf16[2,320,128]{2,1,0:T(8,128)(2,1)S(1)} %collective-permute-done.1.refs_2_.refs_9_), channel_id=1, source_target_pairs={{0,2},{2,0},{1,3},{3,1},{4,6},{6,4},{5,7},{7,5},{8,10},{10,8},{9,1... | collective-permute-start | bytes 491528 | tf_op jit(solution)/shard_map/along_head/ppermute | solution.py:379
  21.3 2.6 %collective-permute-start.7 = (bf16[2,320,128]{2,1,0:T(8,128)(2,1)S(1)}, bf16[2,320,128]{2,1,0:T(8,128)(2,1)S(1)}, u32[]{:S(2)}, u32[]{:S(2)}) collective-permute-start(bf16[2,320,128]{2,1,0:T(8,128)(2,1)S(1)} %collective-permute-done.6.refs_0_.refs_7_), channel_id=1, source_target_pairs={{0,1},{1,0},{2,3},{3,2},{4,5},{5,4},{6,7},{7,6},{8,9},{9,8},{10,11... | collective-permute-start | bytes 491528 | tf_op jit(solution)/shard_map/along_inner/ppermute | solution.py:383
  21.6 2.3 %collective-permute-start.8 = (bf16[2,320,128]{2,1,0:T(8,128)(2,1)S(1)}, bf16[2,320,128]{2,1,0:T(8,128)(2,1)S(1)}, u32[]{:S(2)}, u32[]{:S(2)}) collective-permute-start(bf16[2,320,128]{2,1,0:T(8,128)(2,1)S(1)} %collective-permute-done.5.refs_2_.refs_13_), channel_id=1, source_target_pairs={{0,1},{1,0},{2,3},{3,2},{4,5},{5,4},{6,7},{7,6},{8,9},{9,8},{10,11... | collective-permute-start | bytes 491528 | tf_op jit(solution)/shard_map/along_inner/ppermute | solution.py:383
  21.8 6.4 %collective-permute-start.9 = (bf16[2,320,128]{2,1,0:T(8,128)(2,1)S(1)}, bf16[2,320,128]{2,1,0:T(8,128)(2,1)S(1)}, u32[]{:S(2)}, u32[]{:S(2)}) collective-permute-start(bf16[2,320,128]{2,1,0:T(8,128)(2,1)S(1)} %collective-permute-done.5.refs_2_.refs_13_), channel_id=1, source_target_pairs={{0,2},{2,0},{1,3},{3,1},{4,6},{6,4},{5,7},{7,5},{8,10},{10,8},{9,1... | collective-permute-start | bytes 491528 | tf_op jit(solution)/shard_map/along_head/ppermute | solution.py:379
  23.8 4.4 %collective-permute-start.10 = (bf16[2,320,128]{2,1,0:T(8,128)(2,1)S(1)}, bf16[2,320,128]{2,1,0:T(8,128)(2,1)S(1)}, u32[]{:S(2)}, u32[]{:S(2)}) collective-permute-start(bf16[2,320,128]{2,1,0:T(8,128)(2,1)S(1)} %collective-permute-done.4.refs_0_.refs_11_), channel_id=1, source_target_pairs={{0,1},{1,0},{2,3},{3,2},{4,5},{5,4},{6,7},{7,6},{8,9},{9,8},{10,11... | collective-permute-start | bytes 491528 | tf_op jit(solution)/shard_map/along_inner/ppermute | solution.py:383
  28.2 1.4 %collective-permute-start.11 = (bf16[2,320,128]{2,1,0:T(8,128)(2,1)S(1)}, bf16[2,320,128]{2,1,0:T(8,128)(2,1)S(1)}, u32[]{:S(2)}, u32[]{:S(2)}) collective-permute-start(bf16[2,320,128]{2,1,0:T(8,128)(2,1)S(1)} %collective-permute-done.9.refs_0_.refs_15_), channel_id=1, source_target_pairs={{0,1},{1,0},{2,3},{3,2},{4,5},{5,4},{6,7},{7,6},{8,9},{9,8},{10,11... | collective-permute-start | bytes 491528 | tf_op jit(solution)/shard_map/along_inner/ppermute | solution.py:383

commit v12 on v11

--- a/solution.py
+++ b/solution.py
@@ -46,17 +46,27 @@
     return [(start, min(TILE, count - start)) for start in range(0, count, TILE)]
 
 
-def piece_kernel(k_hbm, v_hbm, piece, sem):
+def piece_kernel(k_hbm, v_hbm, piece, far_piece, sems):
     half = piece.shape[1]
     inner = lax.axis_index("inner")
-    mine = pl.ds(pl.multiple_of(lax.rem(lax.axis_index("head"), 2) * half, half), half)
+    own_half = lax.rem(lax.axis_index("head"), 2)
+
+    def copies(src):
+        found = []
+        for place, (part, target) in enumerate([(own_half, piece), (1 - own_half, far_piece)]):
+            rows = pl.ds(pl.multiple_of(part * half, half), half)
+            found.append(pltpu.make_async_copy(src.at[:, rows], target, sems.at[place]))
+        return found
+
     for value, src in enumerate((k_hbm, v_hbm)):
 
         @pl.when(inner == value)
         def _():
-            pltpu.make_async_copy(src.at[:, mine], piece, sem).start()
-
-    pltpu.make_async_copy(k_hbm.at[:, mine], piece, sem).wait()
+            for copy in copies(src):
+                copy.start()
+
+    for copy in copies(k_hbm):
+        copy.wait()
 
 
 def weights_of(coef, s):
@@ -400,12 +410,12 @@
         pltpu.with_memory_space_constraint(x, pltpu.HBM) for x in (query_rows, key_rows, value_rows, slot_block)
     ]
     half_shape = jax.ShapeDtypeStruct((2, block_len // 2, width), key_rows.dtype)
-    piece = pl.pallas_call(
+    piece, far_piece = pl.pallas_call(
         piece_kernel,
         in_specs=[anywhere] * 2,
-        out_specs=whole,
-        out_shape=half_shape,
-        scratch_shapes=[pltpu.SemaphoreType.DMA],
+        out_specs=[whole] * 2,
+        out_shape=[half_shape] * 2,
+        scratch_shapes=[pltpu.SemaphoreType.DMA((2,))],
         cost_estimate=pl.CostEstimate(flops=0, bytes_accessed=400_000, transcendentals=0),
         compiler_params=params,
         name="pick_piece",
@@ -473,27 +483,32 @@
         beside_across[distance] = along_inner(across[distance])
 
     last = distances[-1]
-    arrived[2], acc = lax.optimization_barrier((arrived[2], acc))
+    ready = sorted(arrived, reverse=True)
+    *first, acc = lax.optimization_barrier((*(arrived[d] for d in ready), acc))
+    arrived.update(zip(ready, first))
+
+    def meet(distance):
+        nonlocal acc
+        arrived[distance], acc = lax.optimization_barrier((arrived[distance], acc))
+
     relay(3)
-    arrived[1], arrived[2], acc = lax.optimization_barrier((arrived[1], arrived[2], acc))
-    waiting = distances[:2]
-    across[1] = along_head(arrived[1])
     across[2] = along_head(arrived[2])
-    for distance in waiting:
+    for distance in (1, 2):
         beside[distance] = along_inner(arrived[distance])
-    sums, acc = attended_with(sums, acc, [near_half(d) for d in waiting])
+    sums, acc = attended_with(sums, acc, [near_half(1), near_half(2)])
     for ahead in distances[2:]:
         relay(ahead)
-        settle(ahead - 2)
-        arrived[ahead], acc = lax.optimization_barrier((arrived[ahead], acc))
+        meet(ahead)
         spread(ahead)
-        across[ahead - 1], acc = lax.optimization_barrier((across[ahead - 1], acc))
-        sums, acc = attended_with(sums, acc, [far_half(ahead - 2), near_half(ahead)])
-    across[last], acc = lax.optimization_barrier((across[last], acc))
-    for distance in distances[-2:]:
+        if ahead == 3:
+            far_piece, acc = lax.optimization_barrier((far_piece, acc))
+            across[1] = along_seq(far_piece, 1)
+        settle(ahead - 1)
+        sums, acc = attended_with(sums, acc, [far_half(ahead - 1), near_half(ahead)])
+    final = [1, last]
+    across[last], across[1], acc = lax.optimization_barrier((across[last], across[1], acc))
+    for distance in final:
         beside_across[distance] = along_inner(across[distance])
-    sums, acc = attended_with(sums, acc, [far_half(last - 1)])
-    final = [last]
 
     flat = [part[d] for d in distances for part in (arrived, beside, across, beside_across)]
     attended, log_total = pl.pallas_call(

time: 32.1 us -> 34.6 us (1.078)
  waiting for transfers between devices: 4.65 us -> 6.56 us
  starting transfers between devices: 11.5 us -> 12.3 us
    ppermute x3 -> x4, waiting for transfers between devices: 1.03 us -> 2.66 us  [along_seq(): return lax.ppermute(block, 'seq', route)]
    pallas_call x3 -> x2, Pallas kernels: 6.15 us -> 4.87 us  [attended_with(): pl.pallas_call(functools.partial(middle_kernel, coef, [visit[0] for visit...]
    pallas_call x1, Pallas kernels: 2.16 us -> 3.22 us  [body(): pl.pallas_call(functools.partial(last_kernel, coef, distances, final), in...]
    ppermute x6, waiting for transfers between devices: 0.08 us -> 1.13 us  [along_inner(): return lax.ppermute(block, 'inner', [(0, 1), (1, 0)])]
    ppermute x6, starting transfers between devices: 0.73 us -> 1.53 us  [along_inner(): return lax.ppermute(block, 'inner', [(0, 1), (1, 0)])]
    ppermute x3 -> x2, waiting for transfers between devices: 3.55 us -> 2.77 us  [along_head(): lax.ppermute(block, 'head', [(i, i ^ 1) for i in range(lax.axis_size('hea...]
    ppermute x3 -> x4, starting transfers between devices: 7.11 us -> 7.75 us  [along_seq(): return lax.ppermute(block, 'seq', route)]
    ppermute x3 -> x2, starting transfers between devices: 3.62 us -> 2.98 us  [along_head(): lax.ppermute(block, 'head', [(i, i ^ 1) for i in range(lax.axis_size('hea...]
  transfers between devices with their start and end apart: 12 -> 12, of which waited for: 7 -> 8; matrix products, arithmetic and copies ran while one was open for 0% -> 0% of each run, Pallas kernels for 37% -> 31%
where the time goes in v12:
time: 34.6 us; the launch traced here: 34.5 us
  Pallas kernels  14.8 us (43%)
  starting transfers between devices  12.3 us (36%)
  waiting for transfers between devices  6.56 us (19%)
  between operations  0.85 us (2%)
    ppermute x4, starting transfers between devices, along_seq(): return lax.ppermute(block, 'seq', route)  7.75 us
    pallas_call x1, Pallas kernels, body(): pl.pallas_call(functools.partial(local_kernel, coef, rows), in_specs=[sca...  5.67 us
    pallas_call x2, Pallas kernels, attended_with(): pl.pallas_call(functools.partial(middle_kernel, coef, [visit[0] for visit...  4.87 us
    pallas_call x1, Pallas kernels, body(): pl.pallas_call(functools.partial(last_kernel, coef, distances, final), in...  3.22 us
    ppermute x2, starting transfers between devices, along_head(): lax.ppermute(block, 'head', [(i, i ^ 1) for i in range(lax.axis_size('hea...  2.98 us
    ppermute x2, waiting for transfers between devices, along_head(): lax.ppermute(block, 'head', [(i, i ^ 1) for i in range(lax.axis_size('hea...  2.77 us
    ppermute x4, waiting for transfers between devices, along_seq(): return lax.ppermute(block, 'seq', route)  2.66 us
    ppermute x6, starting transfers between devices, along_inner(): return lax.ppermute(block, 'inner', [(0, 1), (1, 0)])  1.53 us
  transfers between devices with their start and end apart: 12, of which 8 were waited for; matrix products, arithmetic and copies ran while one was open for 0% of the time, Pallas kernels for 31%

profile of v12, /device:TPU:0, one launch (start us, length us, event | category | flops | bytes accessed | tf_op | source)
XLA Modules:
  0.0 34.5 jit_solution(9201552901033446832)
XLA Ops:
  0.6 1.0 %pick_piece.1 = (bf16[2,320,128]{2,1,0:T(8,128)(2,1)S(1)}, bf16[2,320,128]{2,1,0:T(8,128)(2,1)S(1)}) custom-call(bf16[2,640,128]{2,1,0:T(8,128)(2,1)} %refs_4_.1, bf16[2,640,128]{2,1,0:T(8,128)(2,1)} %refs_5_.1), custom_call_target="tpu_custom_call" | custom-call | bytes 400000 | tf_op jit(solution)/shard_map/pick_piece/pallas_call | solution.py:413
  1.7 4.1 %collective-permute-start = (bf16[2,320,128]{2,1,0:T(8,128)(2,1)S(1)}, bf16[2,320,128]{2,1,0:T(8,128)(2,1)S(1)}, u32[]{:S(2)}, u32[]{:S(2)}) collective-permute-start(bf16[2,320,128]{2,1,0:T(8,128)(2,1)S(1)} %get-tuple-element.29), channel_id=1, source_target_pairs={{0,8},{4,12},{8,0},{12,4},{1,9},{5,13},{9,1},{13,5},{2,10},{6,14},... | collective-permute-start | bytes 491528 | tf_op jit(solution)/shard_map/along_seq/ppermute | solution.py:385
  5.8 1.6 %collective-permute-start.1 = (bf16[2,320,128]{2,1,0:T(8,128)(2,1)S(1)}, bf16[2,320,128]{2,1,0:T(8,128)(2,1)S(1)}, u32[]{:S(2)}, u32[]{:S(2)}) collective-permute-start(bf16[2,320,128]{2,1,0:T(8,128)(2,1)S(1)} %get-tuple-element.29), channel_id=1, source_target_pairs={{0,4},{4,0},{8,12},{12,8},{1,5},{5,1},{9,13},{13,9},{2,6},{6,2},{1... | collective-permute-start | bytes 491528 | tf_op jit(solution)/shard_map/along_seq/ppermute | solution.py:385
  7.3 5.7 %local_part.1 = (bf16[2,256,1280]{2,1,0:T(8,128)(2,1)S(1)}, f32[2,8,1280]{2,1,0:T(8,128)S(1)}, f32[2,8,1280]{2,1,0:T(8,128)S(1)}, f32[2,128,1280]{2,1,0:T(8,128)S(1)}, f32[4,8,128]{2,1,0:T(8,128)S(1)}) custom-call(s32[8]{0:T(128)} %sb_ref.1, bf16[2,320,512]{2,1,0:T(8,128)(2,1)} %refs_6_.1, bf16[2,640,128]{2,1,0:T(8,128)(2,1)} %refs_4_.1, ...), custom_call_target="tpu_custom_call" | custom-call | flops 2516582400 | bytes 6000000 | tf_op jit(solution)/shard_map/local_part/pallas_call | solution.py:429
  13.0 0.6 %collective-permute-done.refs_2_.refs_11_ = bf16[2,320,128]{2,1,0:T(8,128)(2,1)S(1)} collective-permute-done((bf16[2,320,128]{2,1,0:T(8,128)(2,1)S(1)}, bf16[2,320,128]{2,1,0:T(8,128)(2,1)S(1)}, u32[]{:S(2)}, u32[]{:S(2)}) %collective-permute-start) | collective-permute-done | bytes 163872 | tf_op jit(solution)/shard_map/along_seq/ppermute | solution.py:385
  13.6 0.2 collective-permute-done.1.refs_0_.refs_7_
  13.8 0.0 collective-permute-start.2
  13.8 0.5 %collective-permute-start.3 = (bf16[2,320,128]{2,1,0:T(8,128)(2,1)S(1)}, bf16[2,320,128]{2,1,0:T(8,128)(2,1)S(1)}, u32[]{:S(2)}, u32[]{:S(2)}) collective-permute-start(bf16[2,320,128]{2,1,0:T(8,128)(2,1)S(1)} %collective-permute-done.refs_2_.refs_11_), channel_id=1, source_target_pairs={{0,1},{1,0},{2,3},{3,2},{4,5},{5,4},{6,7},{7,6},{8,9},{9,8},{10,11... | collective-permute-start | bytes 491528 | tf_op jit(solution)/shard_map/along_inner/ppermute | solution.py:393
  14.3 1.5 %collective-permute-start.5 = (bf16[2,320,128]{2,1,0:T(8,128)(2,1)S(1)}, bf16[2,320,128]{2,1,0:T(8,128)(2,1)S(1)}, u32[]{:S(2)}, u32[]{:S(2)}) collective-permute-start(bf16[2,320,128]{2,1,0:T(8,128)(2,1)S(1)} %collective-permute-done.refs_2_.refs_11_), channel_id=1, source_target_pairs={{0,4},{4,0},{8,12},{12,8},{1,5},{5,1},{9,13},{13,9},{2,6},{6,2},{1... | collective-permute-start | bytes 491528 | tf_op jit(solution)/shard_map/along_seq/ppermute | solution.py:385
  15.8 1.5 %collective-permute-start.4 = (bf16[2,320,128]{2,1,0:T(8,128)(2,1)S(1)}, bf16[2,320,128]{2,1,0:T(8,128)(2,1)S(1)}, u32[]{:S(2)}, u32[]{:S(2)}) collective-permute-start(bf16[2,320,128]{2,1,0:T(8,128)(2,1)S(1)} %collective-permute-done.refs_2_.refs_11_), channel_id=1, source_target_pairs={{0,2},{2,0},{1,3},{3,1},{4,6},{6,4},{5,7},{7,5},{8,10},{10,8},{9,1... | collective-permute-start | bytes 491528 | tf_op jit(solution)/shard_map/along_head/ppermute | solution.py:389
  17.3 0.0 collective-permute-done.2.refs_1_.refs_8_
  17.3 0.0 collective-permute-done.3.refs_3_.refs_12_
  17.3 2.4 %visits_of_1_2.1 = (f32[2,8,1280]{2,1,0:T(8,128)S(1)}, f32[2,128,1280]{2,1,0:T(8,128)S(1)}) custom-call(f32[4,8,128]{2,1,0:T(8,128)S(1)} %get-tuple-element.25.notes, bf16[2,256,1280]{2,1,0:T(8,128)(2,1)S(1)} %get-tuple-element.26.turned_q, f32[2,8,1280]{2,1,0:T(8,128)S(1)} %get-tuple-element.28.sum_in, ...), custom_call_target="tpu_custom_call", output_to_operand_aliasing={{0}: (2, {}), {1}: (3, {})} | custom-call | flops 1677721600 | bytes 4000000 | tf_op jit(solution)/shard_map/visits_of_1_2/pallas_call | solution.py:458
  19.7 0.7 %collective-permute-done.5.refs_2_.refs_15_ = bf16[2,320,128]{2,1,0:T(8,128)(2,1)S(1)} collective-permute-done((bf16[2,320,128]{2,1,0:T(8,128)(2,1)S(1)}, bf16[2,320,128]{2,1,0:T(8,128)(2,1)S(1)}, u32[]{:S(2)}, u32[]{:S(2)}) %collective-permute-start.5) | collective-permute-done | bytes 163872 | tf_op jit(solution)/shard_map/along_seq/ppermute | solution.py:385
  20.4 1.2 %collective-permute-done.4.refs_0_.refs_13_ = bf16[2,320,128]{2,1,0:T(8,128)(2,1)S(1)} collective-permute-done((bf16[2,320,128]{2,1,0:T(8,128)(2,1)S(1)}, bf16[2,320,128]{2,1,0:T(8,128)(2,1)S(1)}, u32[]{:S(2)}, u32[]{:S(2)}) %collective-permute-start.4) | collective-permute-done | bytes 163872 | tf_op jit(solution)/shard_map/along_head/ppermute | solution.py:389
  21.6 0.0 collective-permute-start.6
  21.6 0.5 %collective-permute-start.7 = (bf16[2,320,128]{2,1,0:T(8,128)(2,1)S(1)}, bf16[2,320,128]{2,1,0:T(8,128)(2,1)S(1)}, u32[]{:S(2)}, u32[]{:S(2)}) collective-permute-start(bf16[2,320,128]{2,1,0:T(8,128)(2,1)S(1)} %collective-permute-done.5.refs_2_.refs_15_), channel_id=1, source_target_pairs={{0,1},{1,0},{2,3},{3,2},{4,5},{5,4},{6,7},{7,6},{8,9},{9,8},{10,11... | collective-permute-start | bytes 491528 | tf_op jit(solution)/shard_map/along_inner/ppermute | solution.py:393
  22.1 1.5 %collective-permute-start.8 = (bf16[2,320,128]{2,1,0:T(8,128)(2,1)S(1)}, bf16[2,320,128]{2,1,0:T(8,128)(2,1)S(1)}, u32[]{:S(2)}, u32[]{:S(2)}) collective-permute-start(bf16[2,320,128]{2,1,0:T(8,128)(2,1)S(1)} %collective-permute-done.5.refs_2_.refs_15_), channel_id=1, source_target_pairs={{0,2},{2,0},{1,3},{3,1},{4,6},{6,4},{5,7},{7,5},{8,10},{10,8},{9,1... | collective-permute-start | bytes 491528 | tf_op jit(solution)/shard_map/along_head/ppermute | solution.py:389
  23.6 0.6 %collective-permute-start.9 = (bf16[2,320,128]{2,1,0:T(8,128)(2,1)S(1)}, bf16[2,320,128]{2,1,0:T(8,128)(2,1)S(1)}, u32[]{:S(2)}, u32[]{:S(2)}) collective-permute-start(bf16[2,320,128]{2,1,0:T(8,128)(2,1)S(1)} %get-tuple-element.43), channel_id=1, source_target_pairs={{0,4},{4,0},{8,12},{12,8},{1,5},{5,1},{9,13},{13,9},{2,6},{6,2},{1... | collective-permute-start | bytes 491528 | tf_op jit(solution)/shard_map/along_seq/ppermute | solution.py:385
  24.2 0.0 collective-permute-done.6.refs_1_.refs_14_
  24.2 0.0 collective-permute-done.7.refs_3_.refs_16_
  24.2 2.4 %visits_of_2_3.1 = (f32[2,8,1280]{2,1,0:T(8,128)S(1)}, f32[2,128,1280]{2,1,0:T(8,128)S(1)}) custom-call(f32[4,8,128]{2,1,0:T(8,128)S(1)} %get-tuple-element.25.notes, bf16[2,256,1280]{2,1,0:T(8,128)(2,1)S(1)} %get-tuple-element.26.turned_q, f32[2,8,1280]{2,1,0:T(8,128)S(1)} %get-tuple-element.34.sum_in, ...), custom_call_target="tpu_custom_call", output_to_operand_aliasing={{0}: (2, {}), {1}: (3, {})} | custom-call | flops 1677721600 | bytes 4000000 | tf_op jit(solution)/shard_map/visits_of_2_3/pallas_call | solution.py:458
  26.7 1.6 %collective-permute-done.8.refs_2_.refs_17_ = bf16[2,320,128]{2,1,0:T(8,128)(2,1)S(1)} collective-permute-done((bf16[2,320,128]{2,1,0:T(8,128)(2,1)S(1)}, bf16[2,320,128]{2,1,0:T(8,128)(2,1)S(1)}, u32[]{:S(2)}, u32[]{:S(2)}) %collective-permute-start.8) | collective-permute-done | bytes 163872 | tf_op jit(solution)/shard_map/along_head/ppermute | solution.py:389
  28.2 1.2 %collective-permute-done.9.refs_0_.refs_9_ = bf16[2,320,128]{2,1,0:T(8,128)(2,1)S(1)} collective-permute-done((bf16[2,320,128]{2,1,0:T(8,128)(2,1)S(1)}, bf16[2,320,128]{2,1,0:T(8,128)(2,1)S(1)}, u32[]{:S(2)}, u32[]{:S(2)}) %collective-permute-start.9) | collective-permute-done | bytes 163872 | tf_op jit(solution)/shard_map/along_seq/ppermute | solution.py:385
  29.4 0.0 collective-permute-start.10
  29.4 0.5 %collective-permute-start.11 = (bf16[2,320,128]{2,1,0:T(8,128)(2,1)S(1)}, bf16[2,320,128]{2,1,0:T(8,128)(2,1)S(1)}, u32[]{:S(2)}, u32[]{:S(2)}) collective-permute-start(bf16[2,320,128]{2,1,0:T(8,128)(2,1)S(1)} %collective-permute-done.8.refs_2_.refs_17_), channel_id=1, source_target_pairs={{0,1},{1,0},{2,3},{3,2},{4,5},{5,4},{6,7},{7,6},{8,9},{9,8},{10,11... | collective-permute-start | bytes 491528 | tf_op jit(solution)/shard_map/along_inner/ppermute | solution.py:393
  29.9 0.9 %collective-permute-done.10.refs_1_.refs_10_ = bf16[2,320,128]{2,1,0:T(8,128)(2,1)S(1)} collective-permute-done((bf16[2,320,128]{2,1,0:T(8,128)(2,1)S(1)}, bf16[2,320,128]{2,1,0:T(8,128)(2,1)S(1)}, u32[]{:S(2)}, u32[]{:S(2)}) %collective-permute-start.10) | collective-permute-done | bytes 163872 | tf_op jit(solution)/shard_map/along_inner/ppermute | solution.py:393
  30.8 0.2 collective-permute-done.11.refs_3_.refs_18_
  31.1 3.2 %last_visitor.1 = (bf16[2,320,512]{2,1,0:T(8,128)(2,1)}, f32[2,4,320]{2,1,0:T(4,128)}) custom-call(s32[8]{0:T(128)} %sb_ref.1, f32[4,8,128]{2,1,0:T(8,128)S(1)} %get-tuple-element.25.notes, bf16[2,256,1280]{2,1,0:T(8,128)(2,1)S(1)} %get-tuple-element.26.turned_q, f32[2,8,1280]{2,1,0:T(8,128)S(1)} %get-tuple-element.27.top_ref, ...), custom_call_target="tpu_custom_call" | custom-call | flops 838860800 | bytes 7000000 | tf_op jit(solution)/shard_map/last_visitor/pallas_call | solution.py:514
Async XLA Ops:
  1.7 11.9 %collective-permute-start = (bf16[2,320,128]{2,1,0:T(8,128)(2,1)S(1)}, bf16[2,320,128]{2,1,0:T(8,128)(2,1)S(1)}, u32[]{:S(2)}, u32[]{:S(2)}) collective-permute-start(bf16[2,320,128]{2,1,0:T(8,128)(2,1)S(1)} %get-tuple-element.29), channel_id=1, source_target_pairs={{0,8},{4,12},{8,0},{12,4},{1,9},{5,13},{9,1},{13,5},{2,10},{6,14},... | collective-permute-start | bytes 491528 | tf_op jit(solution)/shard_map/along_seq/ppermute | solution.py:385
  5.8 8.0 %collective-permute-start.1 = (bf16[2,320,128]{2,1,0:T(8,128)(2,1)S(1)}, bf16[2,320,128]{2,1,0:T(8,128)(2,1)S(1)}, u32[]{:S(2)}, u32[]{:S(2)}) collective-permute-start(bf16[2,320,128]{2,1,0:T(8,128)(2,1)S(1)} %get-tuple-element.29), channel_id=1, source_target_pairs={{0,4},{4,0},{8,12},{12,8},{1,5},{5,1},{9,13},{13,9},{2,6},{6,2},{1... | collective-permute-start | bytes 491528 | tf_op jit(solution)/shard_map/along_seq/ppermute | solution.py:385
  13.8 3.5 %collective-permute-start.2 = (bf16[2,320,128]{2,1,0:T(8,128)(2,1)S(1)}, bf16[2,320,128]{2,1,0:T(8,128)(2,1)S(1)}, u32[]{:S(2)}, u32[]{:S(2)}) collective-permute-start(bf16[2,320,128]{2,1,0:T(8,128)(2,1)S(1)} %collective-permute-done.1.refs_0_.refs_7_), channel_id=1, source_target_pairs={{0,1},{1,0},{2,3},{3,2},{4,5},{5,4},{6,7},{7,6},{8,9},{9,8},{10,11... | collective-permute-start | bytes 491528 | tf_op jit(solution)/shard_map/along_inner/ppermute | solution.py:393
  13.8 3.5 %collective-permute-start.3 = (bf16[2,320,128]{2,1,0:T(8,128)(2,1)S(1)}, bf16[2,320,128]{2,1,0:T(8,128)(2,1)S(1)}, u32[]{:S(2)}, u32[]{:S(2)}) collective-permute-start(bf16[2,320,128]{2,1,0:T(8,128)(2,1)S(1)} %collective-permute-done.refs_2_.refs_11_), channel_id=1, source_target_pairs={{0,1},{1,0},{2,3},{3,2},{4,5},{5,4},{6,7},{7,6},{8,9},{9,8},{10,11... | collective-permute-start | bytes 491528 | tf_op jit(solution)/shard_map/along_inner/ppermute | solution.py:393
  14.3 6.1 %collective-permute-start.5 = (bf16[2,320,128]{2,1,0:T(8,128)(2,1)S(1)}, bf16[2,320,128]{2,1,0:T(8,128)(2,1)S(1)}, u32[]{:S(2)}, u32[]{:S(2)}) collective-permute-start(bf16[2,320,128]{2,1,0:T(8,128)(2,1)S(1)} %collective-permute-done.refs_2_.refs_11_), channel_id=1, source_target_pairs={{0,4},{4,0},{8,12},{12,8},{1,5},{5,1},{9,13},{13,9},{2,6},{6,2},{1... | collective-permute-start | bytes 491528 | tf_op jit(solution)/shard_map/along_seq/ppermute | solution.py:385
  15.8 5.8 %collective-permute-start.4 = (bf16[2,320,128]{2,1,0:T(8,128)(2,1)S(1)}, bf16[2,320,128]{2,1,0:T(8,128)(2,1)S(1)}, u32[]{:S(2)}, u32[]{:S(2)}) collective-permute-start(bf16[2,320,128]{2,1,0:T(8,128)(2,1)S(1)} %collective-permute-done.refs_2_.refs_11_), channel_id=1, source_target_pairs={{0,2},{2,0},{1,3},{3,1},{4,6},{6,4},{5,7},{7,5},{8,10},{10,8},{9,1... | collective-permute-start | bytes 491528 | tf_op jit(solution)/shard_map/along_head/ppermute | solution.py:389
  21.6 2.6 %collective-permute-start.6 = (bf16[2,320,128]{2,1,0:T(8,128)(2,1)S(1)}, bf16[2,320,128]{2,1,0:T(8,128)(2,1)S(1)}, u32[]{:S(2)}, u32[]{:S(2)}) collective-permute-start(bf16[2,320,128]{2,1,0:T(8,128)(2,1)S(1)} %collective-permute-done.4.refs_0_.refs_13_), channel_id=1, source_target_pairs={{0,1},{1,0},{2,3},{3,2},{4,5},{5,4},{6,7},{7,6},{8,9},{9,8},{10,11... | collective-permute-start | bytes 491528 | tf_op jit(solution)/shard_map/along_inner/ppermute | solution.py:393
  21.6 2.6 %collective-permute-start.7 = (bf16[2,320,128]{2,1,0:T(8,128)(2,1)S(1)}, bf16[2,320,128]{2,1,0:T(8,128)(2,1)S(1)}, u32[]{:S(2)}, u32[]{:S(2)}) collective-permute-start(bf16[2,320,128]{2,1,0:T(8,128)(2,1)S(1)} %collective-permute-done.5.refs_2_.refs_15_), channel_id=1, source_target_pairs={{0,1},{1,0},{2,3},{3,2},{4,5},{5,4},{6,7},{7,6},{8,9},{9,8},{10,11... | collective-permute-start | bytes 491528 | tf_op jit(solution)/shard_map/along_inner/ppermute | solution.py:393
  22.1 6.1 %collective-permute-start.8 = (bf16[2,320,128]{2,1,0:T(8,128)(2,1)S(1)}, bf16[2,320,128]{2,1,0:T(8,128)(2,1)S(1)}, u32[]{:S(2)}, u32[]{:S(2)}) collective-permute-start(bf16[2,320,128]{2,1,0:T(8,128)(2,1)S(1)} %collective-permute-done.5.refs_2_.refs_15_), channel_id=1, source_target_pairs={{0,2},{2,0},{1,3},{3,1},{4,6},{6,4},{5,7},{7,5},{8,10},{10,8},{9,1... | collective-permute-start | bytes 491528 | tf_op jit(solution)/shard_map/along_head/ppermute | solution.py:389
  23.6 5.8 %collective-permute-start.9 = (bf16[2,320,128]{2,1,0:T(8,128)(2,1)S(1)}, bf16[2,320,128]{2,1,0:T(8,128)(2,1)S(1)}, u32[]{:S(2)}, u32[]{:S(2)}) collective-permute-start(bf16[2,320,128]{2,1,0:T(8,128)(2,1)S(1)} %get-tuple-element.43), channel_id=1, source_target_pairs={{0,4},{4,0},{8,12},{12,8},{1,5},{5,1},{9,13},{13,9},{2,6},{6,2},{1... | collective-permute-start | bytes 491528 | tf_op jit(solution)/shard_map/along_seq/ppermute | solution.py:385
  29.4 1.4 %collective-permute-start.10 = (bf16[2,320,128]{2,1,0:T(8,128)(2,1)S(1)}, bf16[2,320,128]{2,1,0:T(8,128)(2,1)S(1)}, u32[]{:S(2)}, u32[]{:S(2)}) collective-permute-start(bf16[2,320,128]{2,1,0:T(8,128)(2,1)S(1)} %collective-permute-done.9.refs_0_.refs_9_), channel_id=1, source_target_pairs={{0,1},{1,0},{2,3},{3,2},{4,5},{5,4},{6,7},{7,6},{8,9},{9,8},{10,11... | collective-permute-start | bytes 491528 | tf_op jit(solution)/shard_map/along_inner/ppermute | solution.py:393
  29.4 1.6 %collective-permute-start.11 = (bf16[2,320,128]{2,1,0:T(8,128)(2,1)S(1)}, bf16[2,320,128]{2,1,0:T(8,128)(2,1)S(1)}, u32[]{:S(2)}, u32[]{:S(2)}) collective-permute-start(bf16[2,320,128]{2,1,0:T(8,128)(2,1)S(1)} %collective-permute-done.8.refs_2_.refs_17_), channel_id=1, source_target_pairs={{0,1},{1,0},{2,3},{3,2},{4,5},{5,4},{6,7},{7,6},{8,9},{9,8},{10,11... | collective-permute-start | bytes 491528 | tf_op jit(solution)/shard_map/along_inner/ppermute | solution.py:393

commit v13 on v10

--- a/solution.py
+++ b/solution.py
@@ -207,29 +207,35 @@
 def attend(coef, visits, notes, turned_q, sum_ref, acc_ref, buffers, done=None):
     chunks, ends = [], []
     laid_out = [visit_chunks(*visit, notes, *buffers[3 * i : 3 * i + 3]) for i, visit in enumerate(visits)]
+    all_rows = turned_q.shape[2]
+    split = -(-all_rows // (2 * TILE)) * TILE
     for place, pairs in enumerate(laid_out):
         k_buf, _, turned = buffers[3 * place : 3 * place + 3]
         tiles = key_tiles(k_buf.shape[1])
-        for order, slot in pairs:
-            for tile in tiles:
-                chunks.append((len(ends), order, slot, k_buf, turned, *tile))
-            ends.append(tiles[-1][0])
+        for turn, (order, slot) in enumerate(pairs):
+            groups = [(0, all_rows)]
+            if done is not None and (place, turn) == (len(laid_out) - 1, 1) and all_rows >= 4 * TILE:
+                groups = [(0, split), (split, all_rows - split)]
+            for group in groups:
+                for tile in tiles:
+                    chunks.append((len(ends), turn, order, slot, k_buf, turned, *group, *tile))
+                ends.append(tiles[-1][0])
     totals = {}
 
-    def score(place, order, slot, k_buf, turned, start, size):
-        return value_dot(with_ones(k_buf[slot, pl.ds(start, size)]), turned_q[order])
-
-    def finish(s, place, order, slot, k_buf, turned, start, size):
+    def score(place, turn, order, slot, k_buf, turned, lane, lanes, start, size):
+        return value_dot(with_ones(k_buf[slot, pl.ds(start, size)]), turned_q[order, :, pl.ds(lane, lanes)])
+
+    def finish(s, place, turn, order, slot, k_buf, turned, lane, lanes, start, size):
         p, sums = weights_of(coef, s)
         part = value_dot(turned[slot, :, pl.ds(start, size)], p)
         if start:
             part, sums = totals[place][0] + part, totals[place][1] + sums
         totals[place] = part, sums
         if start == ends[place]:
-            acc_ref[order] += part
-            sum_ref[order] += sums
+            acc_ref[order, :, pl.ds(lane, lanes)] += part
+            sum_ref[order, :, pl.ds(lane, lanes)] += sums
             if done is not None:
-                done(place - len(ends), laid_out[-1][1][0])
+                done(turn, laid_out[-1][1][0], lane + lanes)
 
     in_turn(chunks, score, finish)
 
@@ -270,26 +276,32 @@
         out_buf[slot, :, h * width : (h + 1) * width] = (value[:, :width] / sums).astype(out_buf.dtype)
         lse_ref[slot, h : h + 1, :] = first_row(top * (coef * math.log(2.0)) + jnp.log(sums))
 
-    def done(place, last_order):
-        if place < -2:
-            return
-        order = 1 - last_order if place == -2 else last_order
+    written, started = [0, 0], []
+
+    def done(turn, last_order, covered):
+        order = 1 - last_order if turn == 0 else last_order
+        first, written[turn] = written[turn], covered // rows
+        count_here = written[turn] - first
+        lanes, columns = pl.ds(first * rows, count_here * rows), pl.ds(first * width, count_here * width)
         slot = jnp.where(order == HI, hi, 1 - hi)
-        sums = jnp.sum(sum_ref[order], axis=0, keepdims=True)
-        log_total = top_ref[order][:1] * (coef * math.log(2.0)) + jnp.log(sums)
-        settled = jnp.transpose((acc_ref[order] * (1.0 / sums)).astype(out_buf.dtype))
-        for h in range(heads):
+        sums = jnp.sum(sum_ref[order, :, lanes], axis=0, keepdims=True)
+        log_total = top_ref[order, :, lanes][:1] * (coef * math.log(2.0)) + jnp.log(sums)
+        settled = jnp.transpose((acc_ref[order, :, lanes] * (1.0 / sums)).astype(out_buf.dtype))
+        for h in range(count_here):
             mine = slice(h * rows, (h + 1) * rows)
-            lse_ref[slot, h : h + 1, :] = log_total[:, mine]
-            out_buf[slot, :, h * width : (h + 1) * width] = settled[mine]
-        worst[place + 2 : place + 3] = sums
-        out_copy(slot).start()
+            lse_ref[slot, first + h : first + h + 1, :] = log_total[:, mine]
+            out_buf[slot, :, (first + h) * width : (first + h + 1) * width] = settled[mine]
+        worst[turn : turn + 1, lanes] = sums
+        target = out_hbm.at[slot, :, columns]
+        copy = pltpu.make_async_copy(out_buf.at[slot, :, columns], target, out_sems.at[len(started)])
+        copy.start()
+        started.append(copy)
 
     attend(coef, visits, notes, turned_q, sum_ref, acc_ref, buffers, done)
     fits = jnp.max(worst[...]) < SUM_LIMIT
     lse_copy.start()
-    for slot in range(2):
-        out_copy(slot).wait()
+    for copy in started:
+        copy.wait()
     lse_copy.wait()
 
     @pl.when(jnp.logical_not(fits))
@@ -516,7 +528,7 @@
             pltpu.VMEM((2, heads, rows, 2 * width), jnp.float32),
             pltpu.SMEM(slot_block.shape, slot_block.dtype),
             pltpu.SemaphoreType.DMA,
-            pltpu.SemaphoreType.DMA((2,)),
+            pltpu.SemaphoreType.DMA((3,)),
         ],
         cost_estimate=cost(1, 7_000_000),
         compiler_params=params,

time: 32.2 us -> 32.2 us (level)
  no operation moved by 1% of the time
where the time goes in v13:
time: 32.2 us; the launch traced here: 32 us
  Pallas kernels  15.1 us (47%)
  starting transfers between devices  11.5 us (36%)
  waiting for transfers between devices  4.59 us (14%)
  between operations  0.86 us (3%)
    ppermute x3, starting transfers between devices, along_seq(): return lax.ppermute(block, 'seq', route)  7.11 us
    pallas_call x3, Pallas kernels, attended_with(): pl.pallas_call(functools.partial(middle_kernel, coef, [visit[0] for visit...  6.33 us
    pallas_call x1, Pallas kernels, body(): pl.pallas_call(functools.partial(local_kernel, coef, rows), in_specs=[sca...  5.59 us
    ppermute x3, waiting for transfers between devices, along_head(): lax.ppermute(block, 'head', [(i, i ^ 1) for i in range(lax.axis_size('hea...  3.41 us
    ppermute x3, starting transfers between devices, along_head(): lax.ppermute(block, 'head', [(i, i ^ 1) for i in range(lax.axis_size('hea...  3.32 us
    pallas_call x1, Pallas kernels, body(): pl.pallas_call(functools.partial(last_kernel, coef, distances, final), in...  2.21 us
    ppermute x3, waiting for transfers between devices, along_seq(): return lax.ppermute(block, 'seq', route)  1.14 us
    ppermute x6, starting transfers between devices, along_inner(): return lax.ppermute(block, 'inner', [(0, 1), (1, 0)])  1.03 us
  transfers between devices with their start and end apart: 12, of which 6 were waited for; matrix products, arithmetic and copies ran while one was open for 0% of the time, Pallas kernels for 37%

profile of v13, /device:TPU:0, one launch (start us, length us, event | category | flops | bytes accessed | tf_op | source)
XLA Modules:
  0.0 32.0 jit_solution(3658149674707292300)
XLA Ops:
  0.6 1.0 %pick_piece.1 = (bf16[2,320,128]{2,1,0:T(8,128)(2,1)S(1)}, s32[8]{0:T(128)S(1)}) custom-call(bf16[2,640,128]{2,1,0:T(8,128)(2,1)} %refs_2_.1, bf16[2,640,128]{2,1,0:T(8,128)(2,1)} %refs_3_.1, s32[8]{0:T(128)} %sb_hbm.1), custom_call_target="tpu_custom_call" | custom-call | bytes 400000 | tf_op jit(solution)/shard_map/pick_piece/pallas_call | solution.py:417
  1.6 4.1 %collective-permute-start.1 = (bf16[2,320,128]{2,1,0:T(8,128)(2,1)S(1)}, bf16[2,320,128]{2,1,0:T(8,128)(2,1)S(1)}, u32[]{:S(2)}, u32[]{:S(2)}) collective-permute-start(bf16[2,320,128]{2,1,0:T(8,128)(2,1)S(1)} %get-tuple-element.32), channel_id=1, source_target_pairs={{0,8},{4,12},{8,0},{12,4},{1,9},{5,13},{9,1},{13,5},{2,10},{6,14},... | collective-permute-start | bytes 491528 | tf_op jit(solution)/shard_map/along_seq/ppermute | solution.py:389
  5.7 1.6 %collective-permute-start = (bf16[2,320,128]{2,1,0:T(8,128)(2,1)S(1)}, bf16[2,320,128]{2,1,0:T(8,128)(2,1)S(1)}, u32[]{:S(2)}, u32[]{:S(2)}) collective-permute-start(bf16[2,320,128]{2,1,0:T(8,128)(2,1)S(1)} %get-tuple-element.32), channel_id=1, source_target_pairs={{0,4},{4,0},{8,12},{12,8},{1,5},{5,1},{9,13},{13,9},{2,6},{6,2},{1... | collective-permute-start | bytes 491528 | tf_op jit(solution)/shard_map/along_seq/ppermute | solution.py:389
  7.3 5.6 %local_part.1 = (bf16[2,256,1280]{2,1,0:T(8,128)(2,1)S(1)}, f32[2,8,1280]{2,1,0:T(8,128)S(1)}, f32[2,8,1280]{2,1,0:T(8,128)S(1)}, f32[2,128,1280]{2,1,0:T(8,128)S(1)}, f32[4,8,128]{2,1,0:T(8,128)S(1)}) custom-call(s32[8]{0:T(128)S(1)} %get-tuple-element.27.sb.sb_ref, bf16[2,320,512]{2,1,0:T(8,128)(2,1)} %refs_4_.1, bf16[2,640,128]{2,1,0:T(8,128)(2,1)} %refs_2_.1, ...), custom_call_target="tpu_custom_call" | custom-call | flops 2516582400 | bytes 6000000 | tf_op jit(solution)/shard_map/local_part/pallas_call | solution.py:433
  12.9 0.6 %collective-permute-done.1.refs_2_.refs_9_ = bf16[2,320,128]{2,1,0:T(8,128)(2,1)S(1)} collective-permute-done((bf16[2,320,128]{2,1,0:T(8,128)(2,1)S(1)}, bf16[2,320,128]{2,1,0:T(8,128)(2,1)S(1)}, u32[]{:S(2)}, u32[]{:S(2)}) %collective-permute-start.1) | collective-permute-done | bytes 163872 | tf_op jit(solution)/shard_map/along_seq/ppermute | solution.py:389
  13.5 0.2 collective-permute-done.refs_0_.refs_5_
  13.7 0.0 collective-permute-start.2
  13.7 0.5 %collective-permute-start.3 = (bf16[2,320,128]{2,1,0:T(8,128)(2,1)S(1)}, bf16[2,320,128]{2,1,0:T(8,128)(2,1)S(1)}, u32[]{:S(2)}, u32[]{:S(2)}) collective-permute-start(bf16[2,320,128]{2,1,0:T(8,128)(2,1)S(1)} %collective-permute-done.1.refs_2_.refs_9_), channel_id=1, source_target_pairs={{0,1},{1,0},{2,3},{3,2},{4,5},{5,4},{6,7},{7,6},{8,9},{9,8},{10,11... | collective-permute-start | bytes 491528 | tf_op jit(solution)/shard_map/along_inner/ppermute | solution.py:397
  14.2 1.5 %collective-permute-start.6 = (bf16[2,320,128]{2,1,0:T(8,128)(2,1)S(1)}, bf16[2,320,128]{2,1,0:T(8,128)(2,1)S(1)}, u32[]{:S(2)}, u32[]{:S(2)}) collective-permute-start(bf16[2,320,128]{2,1,0:T(8,128)(2,1)S(1)} %collective-permute-done.refs_0_.refs_5_), channel_id=1, source_target_pairs={{0,2},{2,0},{1,3},{3,1},{4,6},{6,4},{5,7},{7,5},{8,10},{10,8},{9,1... | collective-permute-start | bytes 491528 | tf_op jit(solution)/shard_map/along_head/ppermute | solution.py:393
  15.8 1.4 %collective-permute-start.5 = (bf16[2,320,128]{2,1,0:T(8,128)(2,1)S(1)}, bf16[2,320,128]{2,1,0:T(8,128)(2,1)S(1)}, u32[]{:S(2)}, u32[]{:S(2)}) collective-permute-start(bf16[2,320,128]{2,1,0:T(8,128)(2,1)S(1)} %collective-permute-done.1.refs_2_.refs_9_), channel_id=1, source_target_pairs={{0,4},{4,0},{8,12},{12,8},{1,5},{5,1},{9,13},{13,9},{2,6},{6,2},{1... | collective-permute-start | bytes 491528 | tf_op jit(solution)/shard_map/along_seq/ppermute | solution.py:389
  17.2 0.5 %collective-permute-start.4 = (bf16[2,320,128]{2,1,0:T(8,128)(2,1)S(1)}, bf16[2,320,128]{2,1,0:T(8,128)(2,1)S(1)}, u32[]{:S(2)}, u32[]{:S(2)}) collective-permute-start(bf16[2,320,128]{2,1,0:T(8,128)(2,1)S(1)} %collective-permute-done.1.refs_2_.refs_9_), channel_id=1, source_target_pairs={{0,2},{2,0},{1,3},{3,1},{4,6},{6,4},{5,7},{7,5},{8,10},{10,8},{9,1... | collective-permute-start | bytes 491528 | tf_op jit(solution)/shard_map/along_head/ppermute | solution.py:393
  17.7 0.0 collective-permute-done.2.refs_1_.refs_6_
  17.7 0.0 collective-permute-done.3.refs_3_.refs_10_
  17.7 2.5 %visits_of_1_2.1 = (f32[2,8,1280]{2,1,0:T(8,128)S(1)}, f32[2,128,1280]{2,1,0:T(8,128)S(1)}) custom-call(f32[4,8,128]{2,1,0:T(8,128)S(1)} %get-tuple-element.28.notes, bf16[2,256,1280]{2,1,0:T(8,128)(2,1)S(1)} %get-tuple-element.29.turned_q, f32[2,8,1280]{2,1,0:T(8,128)S(1)} %get-tuple-element.31.sum_in, ...), custom_call_target="tpu_custom_call", output_to_operand_aliasing={{0}: (2, {}), {1}: (3, {})} | custom-call | flops 1677721600 | bytes 4000000 | tf_op jit(solution)/shard_map/visits_of_1_2/pallas_call | solution.py:462
  20.2 1.1 %collective-permute-done.6.refs_0_.refs_7_ = bf16[2,320,128]{2,1,0:T(8,128)(2,1)S(1)} collective-permute-done((bf16[2,320,128]{2,1,0:T(8,128)(2,1)S(1)}, bf16[2,320,128]{2,1,0:T(8,128)(2,1)S(1)}, u32[]{:S(2)}, u32[]{:S(2)}) %collective-permute-start.6) | collective-permute-done | bytes 163872 | tf_op jit(solution)/shard_map/along_head/ppermute | solution.py:393
  21.3 0.3 collective-permute-done.5.refs_2_.refs_13_
  21.6 0.0 collective-permute-start.8
  21.6 0.5 %collective-permute-start.7 = (bf16[2,320,128]{2,1,0:T(8,128)(2,1)S(1)}, bf16[2,320,128]{2,1,0:T(8,128)(2,1)S(1)}, u32[]{:S(2)}, u32[]{:S(2)}) collective-permute-start(bf16[2,320,128]{2,1,0:T(8,128)(2,1)S(1)} %collective-permute-done.6.refs_0_.refs_7_), channel_id=1, source_target_pairs={{0,1},{1,0},{2,3},{3,2},{4,5},{5,4},{6,7},{7,6},{8,9},{9,8},{10,11... | collective-permute-start | bytes 491528 | tf_op jit(solution)/shard_map/along_inner/ppermute | solution.py:397
  22.1 1.2 %collective-permute-start.9 = (bf16[2,320,128]{2,1,0:T(8,128)(2,1)S(1)}, bf16[2,320,128]{2,1,0:T(8,128)(2,1)S(1)}, u32[]{:S(2)}, u32[]{:S(2)}) collective-permute-start(bf16[2,320,128]{2,1,0:T(8,128)(2,1)S(1)} %collective-permute-done.5.refs_2_.refs_13_), channel_id=1, source_target_pairs={{0,2},{2,0},{1,3},{3,1},{4,6},{6,4},{5,7},{7,5},{8,10},{10,8},{9,1... | collective-permute-start | bytes 491528 | tf_op jit(solution)/shard_map/along_head/ppermute | solution.py:393
  23.3 0.5 %collective-permute-done.4.refs_0_.refs_11_ = bf16[2,320,128]{2,1,0:T(8,128)(2,1)S(1)} collective-permute-done((bf16[2,320,128]{2,1,0:T(8,128)(2,1)S(1)}, bf16[2,320,128]{2,1,0:T(8,128)(2,1)S(1)}, u32[]{:S(2)}, u32[]{:S(2)}) %collective-permute-start.4) | collective-permute-done | bytes 163872 | tf_op jit(solution)/shard_map/along_head/ppermute | solution.py:393
  23.8 0.0 collective-permute-start.10
  23.8 0.0 collective-permute-done.8.refs_3_.refs_14_
  23.8 0.0 collective-permute-done.7.refs_1_.refs_8_
  23.8 2.5 %visits_of_1_3.1 = (f32[2,8,1280]{2,1,0:T(8,128)S(1)}, f32[2,128,1280]{2,1,0:T(8,128)S(1)}) custom-call(f32[4,8,128]{2,1,0:T(8,128)S(1)} %get-tuple-element.28.notes, bf16[2,256,1280]{2,1,0:T(8,128)(2,1)S(1)} %get-tuple-element.29.turned_q, f32[2,8,1280]{2,1,0:T(8,128)S(1)} %get-tuple-element.38.sum_in, ...), custom_call_target="tpu_custom_call", output_to_operand_aliasing={{0}: (2, {}), {1}: (3, {})} | custom-call | flops 1677721600 | bytes 4000000 | tf_op jit(solution)/shard_map/visits_of_1_3/pallas_call | solution.py:462
  26.3 1.9 %collective-permute-done.9.refs_0_.refs_15_ = bf16[2,320,128]{2,1,0:T(8,128)(2,1)S(1)} collective-permute-done((bf16[2,320,128]{2,1,0:T(8,128)(2,1)S(1)}, bf16[2,320,128]{2,1,0:T(8,128)(2,1)S(1)}, u32[]{:S(2)}, u32[]{:S(2)}) %collective-permute-start.9) | collective-permute-done | bytes 163872 | tf_op jit(solution)/shard_map/along_head/ppermute | solution.py:393
  28.2 0.0 collective-permute-start.11
  28.2 0.0 collective-permute-done.10.refs_1_.refs_12_
  28.2 1.4 %visits_of_2.1 = (f32[2,8,1280]{2,1,0:T(8,128)S(1)}, f32[2,128,1280]{2,1,0:T(8,128)S(1)}) custom-call(f32[4,8,128]{2,1,0:T(8,128)S(1)} %get-tuple-element.28.notes, bf16[2,256,1280]{2,1,0:T(8,128)(2,1)S(1)} %get-tuple-element.29.turned_q, f32[2,8,1280]{2,1,0:T(8,128)S(1)} %get-tuple-element.45.sum_in, ...), custom_call_target="tpu_custom_call", output_to_operand_aliasing={{0}: (2, {}), {1}: (3, {})} | custom-call | flops 838860800 | bytes 4000000 | tf_op jit(solution)/shard_map/visits_of_2/pallas_call | solution.py:462
  29.6 0.0 collective-permute-done.11.refs_1_.refs_16_
  29.6 2.2 %last_visitor.1 = (bf16[2,320,512]{2,1,0:T(8,128)(2,1)}, f32[2,4,320]{2,1,0:T(4,128)}) custom-call(s32[8]{0:T(128)S(1)} %get-tuple-element.27.sb.sb_ref, f32[4,8,128]{2,1,0:T(8,128)S(1)} %get-tuple-element.28.notes, bf16[2,256,1280]{2,1,0:T(8,128)(2,1)S(1)} %get-tuple-element.29.turned_q, f32[2,8,1280]{2,1,0:T(8,128)S(1)} %get-tuple-element.30.top_ref, ...), custom_call_target="tpu_custom_call" | custom-call | flops 838860800 | bytes 7000000 | tf_op jit(solution)/shard_map/last_visitor/pallas_call | solution.py:513
Async XLA Ops:
  1.6 11.9 %collective-permute-start.1 = (bf16[2,320,128]{2,1,0:T(8,128)(2,1)S(1)}, bf16[2,320,128]{2,1,0:T(8,128)(2,1)S(1)}, u32[]{:S(2)}, u32[]{:S(2)}) collective-permute-start(bf16[2,320,128]{2,1,0:T(8,128)(2,1)S(1)} %get-tuple-element.32), channel_id=1, source_target_pairs={{0,8},{4,12},{8,0},{12,4},{1,9},{5,13},{9,1},{13,5},{2,10},{6,14},... | collective-permute-start | bytes 491528 | tf_op jit(solution)/shard_map/along_seq/ppermute | solution.py:389
  5.7 8.0 %collective-permute-start = (bf16[2,320,128]{2,1,0:T(8,128)(2,1)S(1)}, bf16[2,320,128]{2,1,0:T(8,128)(2,1)S(1)}, u32[]{:S(2)}, u32[]{:S(2)}) collective-permute-start(bf16[2,320,128]{2,1,0:T(8,128)(2,1)S(1)} %get-tuple-element.32), channel_id=1, source_target_pairs={{0,4},{4,0},{8,12},{12,8},{1,5},{5,1},{9,13},{13,9},{2,6},{6,2},{1... | collective-permute-start | bytes 491528 | tf_op jit(solution)/shard_map/along_seq/ppermute | solution.py:389
  13.7 4.0 %collective-permute-start.2 = (bf16[2,320,128]{2,1,0:T(8,128)(2,1)S(1)}, bf16[2,320,128]{2,1,0:T(8,128)(2,1)S(1)}, u32[]{:S(2)}, u32[]{:S(2)}) collective-permute-start(bf16[2,320,128]{2,1,0:T(8,128)(2,1)S(1)} %collective-permute-done.refs_0_.refs_5_), channel_id=1, source_target_pairs={{0,1},{1,0},{2,3},{3,2},{4,5},{5,4},{6,7},{7,6},{8,9},{9,8},{10,11... | collective-permute-start | bytes 491528 | tf_op jit(solution)/shard_map/along_inner/ppermute | solution.py:397
  13.7 4.0 %collective-permute-start.3 = (bf16[2,320,128]{2,1,0:T(8,128)(2,1)S(1)}, bf16[2,320,128]{2,1,0:T(8,128)(2,1)S(1)}, u32[]{:S(2)}, u32[]{:S(2)}) collective-permute-start(bf16[2,320,128]{2,1,0:T(8,128)(2,1)S(1)} %collective-permute-done.1.refs_2_.refs_9_), channel_id=1, source_target_pairs={{0,1},{1,0},{2,3},{3,2},{4,5},{5,4},{6,7},{7,6},{8,9},{9,8},{10,11... | collective-permute-start | bytes 491528 | tf_op jit(solution)/shard_map/along_inner/ppermute | solution.py:397
  14.2 7.1 %collective-permute-start.6 = (bf16[2,320,128]{2,1,0:T(8,128)(2,1)S(1)}, bf16[2,320,128]{2,1,0:T(8,128)(2,1)S(1)}, u32[]{:S(2)}, u32[]{:S(2)}) collective-permute-start(bf16[2,320,128]{2,1,0:T(8,128)(2,1)S(1)} %collective-permute-done.refs_0_.refs_5_), channel_id=1, source_target_pairs={{0,2},{2,0},{1,3},{3,1},{4,6},{6,4},{5,7},{7,5},{8,10},{10,8},{9,1... | collective-permute-start | bytes 491528 | tf_op jit(solution)/shard_map/along_head/ppermute | solution.py:393
  15.8 5.8 %collective-permute-start.5 = (bf16[2,320,128]{2,1,0:T(8,128)(2,1)S(1)}, bf16[2,320,128]{2,1,0:T(8,128)(2,1)S(1)}, u32[]{:S(2)}, u32[]{:S(2)}) collective-permute-start(bf16[2,320,128]{2,1,0:T(8,128)(2,1)S(1)} %collective-permute-done.1.refs_2_.refs_9_), channel_id=1, source_target_pairs={{0,4},{4,0},{8,12},{12,8},{1,5},{5,1},{9,13},{13,9},{2,6},{6,2},{1... | collective-permute-start | bytes 491528 | tf_op jit(solution)/shard_map/along_seq/ppermute | solution.py:389
  17.2 6.6 %collective-permute-start.4 = (bf16[2,320,128]{2,1,0:T(8,128)(2,1)S(1)}, bf16[2,320,128]{2,1,0:T(8,128)(2,1)S(1)}, u32[]{:S(2)}, u32[]{:S(2)}) collective-permute-start(bf16[2,320,128]{2,1,0:T(8,128)(2,1)S(1)} %collective-permute-done.1.refs_2_.refs_9_), channel_id=1, source_target_pairs={{0,2},{2,0},{1,3},{3,1},{4,6},{6,4},{5,7},{7,5},{8,10},{10,8},{9,1... | collective-permute-start | bytes 491528 | tf_op jit(solution)/shard_map/along_head/ppermute | solution.py:393
  21.6 2.3 %collective-permute-start.8 = (bf16[2,320,128]{2,1,0:T(8,128)(2,1)S(1)}, bf16[2,320,128]{2,1,0:T(8,128)(2,1)S(1)}, u32[]{:S(2)}, u32[]{:S(2)}) collective-permute-start(bf16[2,320,128]{2,1,0:T(8,128)(2,1)S(1)} %collective-permute-done.5.refs_2_.refs_13_), channel_id=1, source_target_pairs={{0,1},{1,0},{2,3},{3,2},{4,5},{5,4},{6,7},{7,6},{8,9},{9,8},{10,11... | collective-permute-start | bytes 491528 | tf_op jit(solution)/shard_map/along_inner/ppermute | solution.py:397
  21.6 2.3 %collective-permute-start.7 = (bf16[2,320,128]{2,1,0:T(8,128)(2,1)S(1)}, bf16[2,320,128]{2,1,0:T(8,128)(2,1)S(1)}, u32[]{:S(2)}, u32[]{:S(2)}) collective-permute-start(bf16[2,320,128]{2,1,0:T(8,128)(2,1)S(1)} %collective-permute-done.6.refs_0_.refs_7_), channel_id=1, source_target_pairs={{0,1},{1,0},{2,3},{3,2},{4,5},{5,4},{6,7},{7,6},{8,9},{9,8},{10,11... | collective-permute-start | bytes 491528 | tf_op jit(solution)/shard_map/along_inner/ppermute | solution.py:397
  22.1 6.1 %collective-permute-start.9 = (bf16[2,320,128]{2,1,0:T(8,128)(2,1)S(1)}, bf16[2,320,128]{2,1,0:T(8,128)(2,1)S(1)}, u32[]{:S(2)}, u32[]{:S(2)}) collective-permute-start(bf16[2,320,128]{2,1,0:T(8,128)(2,1)S(1)} %collective-permute-done.5.refs_2_.refs_13_), channel_id=1, source_target_pairs={{0,2},{2,0},{1,3},{3,1},{4,6},{6,4},{5,7},{7,5},{8,10},{10,8},{9,1... | collective-permute-start | bytes 491528 | tf_op jit(solution)/shard_map/along_head/ppermute | solution.py:393
  23.8 4.4 %collective-permute-start.10 = (bf16[2,320,128]{2,1,0:T(8,128)(2,1)S(1)}, bf16[2,320,128]{2,1,0:T(8,128)(2,1)S(1)}, u32[]{:S(2)}, u32[]{:S(2)}) collective-permute-start(bf16[2,320,128]{2,1,0:T(8,128)(2,1)S(1)} %collective-permute-done.4.refs_0_.refs_11_), channel_id=1, source_target_pairs={{0,1},{1,0},{2,3},{3,2},{4,5},{5,4},{6,7},{7,6},{8,9},{9,8},{10,11... | collective-permute-start | bytes 491528 | tf_op jit(solution)/shard_map/along_inner/ppermute | solution.py:397
  28.2 1.4 %collective-permute-start.11 = (bf16[2,320,128]{2,1,0:T(8,128)(2,1)S(1)}, bf16[2,320,128]{2,1,0:T(8,128)(2,1)S(1)}, u32[]{:S(2)}, u32[]{:S(2)}) collective-permute-start(bf16[2,320,128]{2,1,0:T(8,128)(2,1)S(1)} %collective-permute-done.9.refs_0_.refs_15_), channel_id=1, source_target_pairs={{0,1},{1,0},{2,3},{3,2},{4,5},{5,4},{6,7},{7,6},{8,9},{9,8},{10,11... | collective-permute-start | bytes 491528 | tf_op jit(solution)/shard_map/along_inner/ppermute | solution.py:397

commit v14 on v10

--- a/solution.py
+++ b/solution.py
@@ -209,7 +209,7 @@
     laid_out = [visit_chunks(*visit, notes, *buffers[3 * i : 3 * i + 3]) for i, visit in enumerate(visits)]
     for place, pairs in enumerate(laid_out):
         k_buf, _, turned = buffers[3 * place : 3 * place + 3]
-        tiles = key_tiles(k_buf.shape[1])
+        tiles = [(0, k_buf.shape[1])]
         for order, slot in pairs:
             for tile in tiles:
                 chunks.append((len(ends), order, slot, k_buf, turned, *tile))

time: 32.2 us -> 32 us (level)
  Pallas kernels: 15.1 us -> 13.8 us
  waiting for transfers between devices: 4.6 us -> 5.7 us
    pallas_call x3, Pallas kernels: 6.32 us -> 5.21 us  [attended_with(): pl.pallas_call(functools.partial(middle_kernel, coef, [visit[0] for visit...]
    ppermute x3, waiting for transfers between devices: 3.42 us -> 4.26 us  [along_head(): lax.ppermute(block, 'head', [(i, i ^ 1) for i in range(lax.axis_size('hea...]
  transfers between devices with their start and end apart: 12 -> 12, of which waited for: 6 -> 7; matrix products, arithmetic and copies ran while one was open for 0% -> 0% of each run, Pallas kernels for 37% -> 34%
where the time goes in v14:
time: 32 us; the launch traced here: 31.9 us
  Pallas kernels  13.8 us (43%)
  starting transfers between devices  11.5 us (36%)
  waiting for transfers between devices  5.7 us (18%)
  between operations  0.86 us (3%)
    ppermute x3, starting transfers between devices, along_seq(): return lax.ppermute(block, 'seq', route)  7.11 us
    pallas_call x1, Pallas kernels, body(): pl.pallas_call(functools.partial(local_kernel, coef, rows), in_specs=[sca...  5.59 us
    pallas_call x3, Pallas kernels, attended_with(): pl.pallas_call(functools.partial(middle_kernel, coef, [visit[0] for visit...  5.21 us
    ppermute x3, waiting for transfers between devices, along_head(): lax.ppermute(block, 'head', [(i, i ^ 1) for i in range(lax.axis_size('hea...  4.26 us
    ppermute x3, starting transfers between devices, along_head(): lax.ppermute(block, 'head', [(i, i ^ 1) for i in range(lax.axis_size('hea...  3.32 us
    pallas_call x1, Pallas kernels, body(): pl.pallas_call(functools.partial(last_kernel, coef, distances, final), in...  2.08 us
    ppermute x3, waiting for transfers between devices, along_seq(): return lax.ppermute(block, 'seq', route)  1.14 us
    ppermute x6, starting transfers between devices, along_inner(): return lax.ppermute(block, 'inner', [(0, 1), (1, 0)])  1.03 us
  transfers between devices with their start and end apart: 12, of which 7 were waited for; matrix products, arithmetic and copies ran while one was open for 0% of the time, Pallas kernels for 34%

profile of v14, /device:TPU:0, one launch (start us, length us, event | category | flops | bytes accessed | tf_op | source)
XLA Modules:
  0.0 31.9 jit_solution(1229115522034078335)
XLA Ops:
  0.6 1.0 %pick_piece.1 = (bf16[2,320,128]{2,1,0:T(8,128)(2,1)S(1)}, s32[8]{0:T(128)S(1)}) custom-call(bf16[2,640,128]{2,1,0:T(8,128)(2,1)} %refs_2_.1, bf16[2,640,128]{2,1,0:T(8,128)(2,1)} %refs_3_.1, s32[8]{0:T(128)} %sb_hbm.1), custom_call_target="tpu_custom_call" | custom-call | bytes 400000 | tf_op jit(solution)/shard_map/pick_piece/pallas_call | solution.py:405
  1.6 4.1 %collective-permute-start.1 = (bf16[2,320,128]{2,1,0:T(8,128)(2,1)S(1)}, bf16[2,320,128]{2,1,0:T(8,128)(2,1)S(1)}, u32[]{:S(2)}, u32[]{:S(2)}) collective-permute-start(bf16[2,320,128]{2,1,0:T(8,128)(2,1)S(1)} %get-tuple-element.32), channel_id=1, source_target_pairs={{0,8},{4,12},{8,0},{12,4},{1,9},{5,13},{9,1},{13,5},{2,10},{6,14},... | collective-permute-start | bytes 491528 | tf_op jit(solution)/shard_map/along_seq/ppermute | solution.py:377
  5.7 1.6 %collective-permute-start = (bf16[2,320,128]{2,1,0:T(8,128)(2,1)S(1)}, bf16[2,320,128]{2,1,0:T(8,128)(2,1)S(1)}, u32[]{:S(2)}, u32[]{:S(2)}) collective-permute-start(bf16[2,320,128]{2,1,0:T(8,128)(2,1)S(1)} %get-tuple-element.32), channel_id=1, source_target_pairs={{0,4},{4,0},{8,12},{12,8},{1,5},{5,1},{9,13},{13,9},{2,6},{6,2},{1... | collective-permute-start | bytes 491528 | tf_op jit(solution)/shard_map/along_seq/ppermute | solution.py:377
  7.3 5.6 %local_part.1 = (bf16[2,256,1280]{2,1,0:T(8,128)(2,1)S(1)}, f32[2,8,1280]{2,1,0:T(8,128)S(1)}, f32[2,8,1280]{2,1,0:T(8,128)S(1)}, f32[2,128,1280]{2,1,0:T(8,128)S(1)}, f32[4,8,128]{2,1,0:T(8,128)S(1)}) custom-call(s32[8]{0:T(128)S(1)} %get-tuple-element.27.sb.sb_ref, bf16[2,320,512]{2,1,0:T(8,128)(2,1)} %refs_4_.1, bf16[2,640,128]{2,1,0:T(8,128)(2,1)} %refs_2_.1, ...), custom_call_target="tpu_custom_call" | custom-call | flops 2516582400 | bytes 6000000 | tf_op jit(solution)/shard_map/local_part/pallas_call | solution.py:421
  12.9 0.6 %collective-permute-done.1.refs_2_.refs_9_ = bf16[2,320,128]{2,1,0:T(8,128)(2,1)S(1)} collective-permute-done((bf16[2,320,128]{2,1,0:T(8,128)(2,1)S(1)}, bf16[2,320,128]{2,1,0:T(8,128)(2,1)S(1)}, u32[]{:S(2)}, u32[]{:S(2)}) %collective-permute-start.1) | collective-permute-done | bytes 163872 | tf_op jit(solution)/shard_map/along_seq/ppermute | solution.py:377
  13.5 0.2 collective-permute-done.refs_0_.refs_5_
  13.7 0.0 collective-permute-start.2
  13.7 0.5 %collective-permute-start.3 = (bf16[2,320,128]{2,1,0:T(8,128)(2,1)S(1)}, bf16[2,320,128]{2,1,0:T(8,128)(2,1)S(1)}, u32[]{:S(2)}, u32[]{:S(2)}) collective-permute-start(bf16[2,320,128]{2,1,0:T(8,128)(2,1)S(1)} %collective-permute-done.1.refs_2_.refs_9_), channel_id=1, source_target_pairs={{0,1},{1,0},{2,3},{3,2},{4,5},{5,4},{6,7},{7,6},{8,9},{9,8},{10,11... | collective-permute-start | bytes 491528 | tf_op jit(solution)/shard_map/along_inner/ppermute | solution.py:385
  14.2 1.5 %collective-permute-start.6 = (bf16[2,320,128]{2,1,0:T(8,128)(2,1)S(1)}, bf16[2,320,128]{2,1,0:T(8,128)(2,1)S(1)}, u32[]{:S(2)}, u32[]{:S(2)}) collective-permute-start(bf16[2,320,128]{2,1,0:T(8,128)(2,1)S(1)} %collective-permute-done.refs_0_.refs_5_), channel_id=1, source_target_pairs={{0,2},{2,0},{1,3},{3,1},{4,6},{6,4},{5,7},{7,5},{8,10},{10,8},{9,1... | collective-permute-start | bytes 491528 | tf_op jit(solution)/shard_map/along_head/ppermute | solution.py:381
  15.8 1.4 %collective-permute-start.5 = (bf16[2,320,128]{2,1,0:T(8,128)(2,1)S(1)}, bf16[2,320,128]{2,1,0:T(8,128)(2,1)S(1)}, u32[]{:S(2)}, u32[]{:S(2)}) collective-permute-start(bf16[2,320,128]{2,1,0:T(8,128)(2,1)S(1)} %collective-permute-done.1.refs_2_.refs_9_), channel_id=1, source_target_pairs={{0,4},{4,0},{8,12},{12,8},{1,5},{5,1},{9,13},{13,9},{2,6},{6,2},{1... | collective-permute-start | bytes 491528 | tf_op jit(solution)/shard_map/along_seq/ppermute | solution.py:377
  17.2 0.5 %collective-permute-start.4 = (bf16[2,320,128]{2,1,0:T(8,128)(2,1)S(1)}, bf16[2,320,128]{2,1,0:T(8,128)(2,1)S(1)}, u32[]{:S(2)}, u32[]{:S(2)}) collective-permute-start(bf16[2,320,128]{2,1,0:T(8,128)(2,1)S(1)} %collective-permute-done.1.refs_2_.refs_9_), channel_id=1, source_target_pairs={{0,2},{2,0},{1,3},{3,1},{4,6},{6,4},{5,7},{7,5},{8,10},{10,8},{9,1... | collective-permute-start | bytes 491528 | tf_op jit(solution)/shard_map/along_head/ppermute | solution.py:381
  17.7 0.0 collective-permute-done.2.refs_1_.refs_6_
  17.7 0.0 collective-permute-done.3.refs_3_.refs_10_
  17.7 2.1 %visits_of_1_2.1 = (f32[2,8,1280]{2,1,0:T(8,128)S(1)}, f32[2,128,1280]{2,1,0:T(8,128)S(1)}) custom-call(f32[4,8,128]{2,1,0:T(8,128)S(1)} %get-tuple-element.28.notes, bf16[2,256,1280]{2,1,0:T(8,128)(2,1)S(1)} %get-tuple-element.29.turned_q, f32[2,8,1280]{2,1,0:T(8,128)S(1)} %get-tuple-element.31.sum_in, ...), custom_call_target="tpu_custom_call", output_to_operand_aliasing={{0}: (2, {}), {1}: (3, {})} | custom-call | flops 1677721600 | bytes 4000000 | tf_op jit(solution)/shard_map/visits_of_1_2/pallas_call | solution.py:450
  19.8 1.5 %collective-permute-done.6.refs_0_.refs_7_ = bf16[2,320,128]{2,1,0:T(8,128)(2,1)S(1)} collective-permute-done((bf16[2,320,128]{2,1,0:T(8,128)(2,1)S(1)}, bf16[2,320,128]{2,1,0:T(8,128)(2,1)S(1)}, u32[]{:S(2)}, u32[]{:S(2)}) %collective-permute-start.6) | collective-permute-done | bytes 163872 | tf_op jit(solution)/shard_map/along_head/ppermute | solution.py:381
  21.3 0.3 collective-permute-done.5.refs_2_.refs_13_
  21.6 0.0 collective-permute-start.8
  21.6 0.5 %collective-permute-start.7 = (bf16[2,320,128]{2,1,0:T(8,128)(2,1)S(1)}, bf16[2,320,128]{2,1,0:T(8,128)(2,1)S(1)}, u32[]{:S(2)}, u32[]{:S(2)}) collective-permute-start(bf16[2,320,128]{2,1,0:T(8,128)(2,1)S(1)} %collective-permute-done.6.refs_0_.refs_7_), channel_id=1, source_target_pairs={{0,1},{1,0},{2,3},{3,2},{4,5},{5,4},{6,7},{7,6},{8,9},{9,8},{10,11... | collective-permute-start | bytes 491528 | tf_op jit(solution)/shard_map/along_inner/ppermute | solution.py:385
  22.1 1.2 %collective-permute-start.9 = (bf16[2,320,128]{2,1,0:T(8,128)(2,1)S(1)}, bf16[2,320,128]{2,1,0:T(8,128)(2,1)S(1)}, u32[]{:S(2)}, u32[]{:S(2)}) collective-permute-start(bf16[2,320,128]{2,1,0:T(8,128)(2,1)S(1)} %collective-permute-done.5.refs_2_.refs_13_), channel_id=1, source_target_pairs={{0,2},{2,0},{1,3},{3,1},{4,6},{6,4},{5,7},{7,5},{8,10},{10,8},{9,1... | collective-permute-start | bytes 491528 | tf_op jit(solution)/shard_map/along_head/ppermute | solution.py:381
  23.3 0.5 %collective-permute-done.4.refs_0_.refs_11_ = bf16[2,320,128]{2,1,0:T(8,128)(2,1)S(1)} collective-permute-done((bf16[2,320,128]{2,1,0:T(8,128)(2,1)S(1)}, bf16[2,320,128]{2,1,0:T(8,128)(2,1)S(1)}, u32[]{:S(2)}, u32[]{:S(2)}) %collective-permute-start.4) | collective-permute-done | bytes 163872 | tf_op jit(solution)/shard_map/along_head/ppermute | solution.py:381
  23.8 0.0 collective-permute-start.10
  23.8 0.0 collective-permute-done.8.refs_3_.refs_14_
  23.8 0.0 collective-permute-done.7.refs_1_.refs_8_
  23.8 2.1 %visits_of_1_3.1 = (f32[2,8,1280]{2,1,0:T(8,128)S(1)}, f32[2,128,1280]{2,1,0:T(8,128)S(1)}) custom-call(f32[4,8,128]{2,1,0:T(8,128)S(1)} %get-tuple-element.28.notes, bf16[2,256,1280]{2,1,0:T(8,128)(2,1)S(1)} %get-tuple-element.29.turned_q, f32[2,8,1280]{2,1,0:T(8,128)S(1)} %get-tuple-element.38.sum_in, ...), custom_call_target="tpu_custom_call", output_to_operand_aliasing={{0}: (2, {}), {1}: (3, {})} | custom-call | flops 1677721600 | bytes 4000000 | tf_op jit(solution)/shard_map/visits_of_1_3/pallas_call | solution.py:450
  25.9 2.3 %collective-permute-done.9.refs_0_.refs_15_ = bf16[2,320,128]{2,1,0:T(8,128)(2,1)S(1)} collective-permute-done((bf16[2,320,128]{2,1,0:T(8,128)(2,1)S(1)}, bf16[2,320,128]{2,1,0:T(8,128)(2,1)S(1)}, u32[]{:S(2)}, u32[]{:S(2)}) %collective-permute-start.9) | collective-permute-done | bytes 163872 | tf_op jit(solution)/shard_map/along_head/ppermute | solution.py:381
  28.2 0.0 collective-permute-start.11
  28.2 0.0 collective-permute-done.10.refs_1_.refs_12_
  28.2 1.1 %visits_of_2.1 = (f32[2,8,1280]{2,1,0:T(8,128)S(1)}, f32[2,128,1280]{2,1,0:T(8,128)S(1)}) custom-call(f32[4,8,128]{2,1,0:T(8,128)S(1)} %get-tuple-element.28.notes, bf16[2,256,1280]{2,1,0:T(8,128)(2,1)S(1)} %get-tuple-element.29.turned_q, f32[2,8,1280]{2,1,0:T(8,128)S(1)} %get-tuple-element.45.sum_in, ...), custom_call_target="tpu_custom_call", output_to_operand_aliasing={{0}: (2, {}), {1}: (3, {})} | custom-call | flops 838860800 | bytes 4000000 | tf_op jit(solution)/shard_map/visits_of_2/pallas_call | solution.py:450
  29.3 0.3 collective-permute-done.11.refs_1_.refs_16_
  29.6 2.1 %last_visitor.1 = (bf16[2,320,512]{2,1,0:T(8,128)(2,1)}, f32[2,4,320]{2,1,0:T(4,128)}) custom-call(s32[8]{0:T(128)S(1)} %get-tuple-element.27.sb.sb_ref, f32[4,8,128]{2,1,0:T(8,128)S(1)} %get-tuple-element.28.notes, bf16[2,256,1280]{2,1,0:T(8,128)(2,1)S(1)} %get-tuple-element.29.turned_q, f32[2,8,1280]{2,1,0:T(8,128)S(1)} %get-tuple-element.30.top_ref, ...), custom_call_target="tpu_custom_call" | custom-call | flops 838860800 | bytes 7000000 | tf_op jit(solution)/shard_map/last_visitor/pallas_call | solution.py:501
Async XLA Ops:
  1.6 11.9 %collective-permute-start.1 = (bf16[2,320,128]{2,1,0:T(8,128)(2,1)S(1)}, bf16[2,320,128]{2,1,0:T(8,128)(2,1)S(1)}, u32[]{:S(2)}, u32[]{:S(2)}) collective-permute-start(bf16[2,320,128]{2,1,0:T(8,128)(2,1)S(1)} %get-tuple-element.32), channel_id=1, source_target_pairs={{0,8},{4,12},{8,0},{12,4},{1,9},{5,13},{9,1},{13,5},{2,10},{6,14},... | collective-permute-start | bytes 491528 | tf_op jit(solution)/shard_map/along_seq/ppermute | solution.py:377
  5.7 8.0 %collective-permute-start = (bf16[2,320,128]{2,1,0:T(8,128)(2,1)S(1)}, bf16[2,320,128]{2,1,0:T(8,128)(2,1)S(1)}, u32[]{:S(2)}, u32[]{:S(2)}) collective-permute-start(bf16[2,320,128]{2,1,0:T(8,128)(2,1)S(1)} %get-tuple-element.32), channel_id=1, source_target_pairs={{0,4},{4,0},{8,12},{12,8},{1,5},{5,1},{9,13},{13,9},{2,6},{6,2},{1... | collective-permute-start | bytes 491528 | tf_op jit(solution)/shard_map/along_seq/ppermute | solution.py:377
  13.7 4.0 %collective-permute-start.2 = (bf16[2,320,128]{2,1,0:T(8,128)(2,1)S(1)}, bf16[2,320,128]{2,1,0:T(8,128)(2,1)S(1)}, u32[]{:S(2)}, u32[]{:S(2)}) collective-permute-start(bf16[2,320,128]{2,1,0:T(8,128)(2,1)S(1)} %collective-permute-done.refs_0_.refs_5_), channel_id=1, source_target_pairs={{0,1},{1,0},{2,3},{3,2},{4,5},{5,4},{6,7},{7,6},{8,9},{9,8},{10,11... | collective-permute-start | bytes 491528 | tf_op jit(solution)/shard_map/along_inner/ppermute | solution.py:385
  13.7 4.0 %collective-permute-start.3 = (bf16[2,320,128]{2,1,0:T(8,128)(2,1)S(1)}, bf16[2,320,128]{2,1,0:T(8,128)(2,1)S(1)}, u32[]{:S(2)}, u32[]{:S(2)}) collective-permute-start(bf16[2,320,128]{2,1,0:T(8,128)(2,1)S(1)} %collective-permute-done.1.refs_2_.refs_9_), channel_id=1, source_target_pairs={{0,1},{1,0},{2,3},{3,2},{4,5},{5,4},{6,7},{7,6},{8,9},{9,8},{10,11... | collective-permute-start | bytes 491528 | tf_op jit(solution)/shard_map/along_inner/ppermute | solution.py:385
  14.2 7.1 %collective-permute-start.6 = (bf16[2,320,128]{2,1,0:T(8,128)(2,1)S(1)}, bf16[2,320,128]{2,1,0:T(8,128)(2,1)S(1)}, u32[]{:S(2)}, u32[]{:S(2)}) collective-permute-start(bf16[2,320,128]{2,1,0:T(8,128)(2,1)S(1)} %collective-permute-done.refs_0_.refs_5_), channel_id=1, source_target_pairs={{0,2},{2,0},{1,3},{3,1},{4,6},{6,4},{5,7},{7,5},{8,10},{10,8},{9,1... | collective-permute-start | bytes 491528 | tf_op jit(solution)/shard_map/along_head/ppermute | solution.py:381
  15.8 5.8 %collective-permute-start.5 = (bf16[2,320,128]{2,1,0:T(8,128)(2,1)S(1)}, bf16[2,320,128]{2,1,0:T(8,128)(2,1)S(1)}, u32[]{:S(2)}, u32[]{:S(2)}) collective-permute-start(bf16[2,320,128]{2,1,0:T(8,128)(2,1)S(1)} %collective-permute-done.1.refs_2_.refs_9_), channel_id=1, source_target_pairs={{0,4},{4,0},{8,12},{12,8},{1,5},{5,1},{9,13},{13,9},{2,6},{6,2},{1... | collective-permute-start | bytes 491528 | tf_op jit(solution)/shard_map/along_seq/ppermute | solution.py:377
  17.2 6.6 %collective-permute-start.4 = (bf16[2,320,128]{2,1,0:T(8,128)(2,1)S(1)}, bf16[2,320,128]{2,1,0:T(8,128)(2,1)S(1)}, u32[]{:S(2)}, u32[]{:S(2)}) collective-permute-start(bf16[2,320,128]{2,1,0:T(8,128)(2,1)S(1)} %collective-permute-done.1.refs_2_.refs_9_), channel_id=1, source_target_pairs={{0,2},{2,0},{1,3},{3,1},{4,6},{6,4},{5,7},{7,5},{8,10},{10,8},{9,1... | collective-permute-start | bytes 491528 | tf_op jit(solution)/shard_map/along_head/ppermute | solution.py:381
  21.6 2.3 %collective-permute-start.8 = (bf16[2,320,128]{2,1,0:T(8,128)(2,1)S(1)}, bf16[2,320,128]{2,1,0:T(8,128)(2,1)S(1)}, u32[]{:S(2)}, u32[]{:S(2)}) collective-permute-start(bf16[2,320,128]{2,1,0:T(8,128)(2,1)S(1)} %collective-permute-done.5.refs_2_.refs_13_), channel_id=1, source_target_pairs={{0,1},{1,0},{2,3},{3,2},{4,5},{5,4},{6,7},{7,6},{8,9},{9,8},{10,11... | collective-permute-start | bytes 491528 | tf_op jit(solution)/shard_map/along_inner/ppermute | solution.py:385
  21.6 2.3 %collective-permute-start.7 = (bf16[2,320,128]{2,1,0:T(8,128)(2,1)S(1)}, bf16[2,320,128]{2,1,0:T(8,128)(2,1)S(1)}, u32[]{:S(2)}, u32[]{:S(2)}) collective-permute-start(bf16[2,320,128]{2,1,0:T(8,128)(2,1)S(1)} %collective-permute-done.6.refs_0_.refs_7_), channel_id=1, source_target_pairs={{0,1},{1,0},{2,3},{3,2},{4,5},{5,4},{6,7},{7,6},{8,9},{9,8},{10,11... | collective-permute-start | bytes 491528 | tf_op jit(solution)/shard_map/along_inner/ppermute | solution.py:385
  22.1 6.1 %collective-permute-start.9 = (bf16[2,320,128]{2,1,0:T(8,128)(2,1)S(1)}, bf16[2,320,128]{2,1,0:T(8,128)(2,1)S(1)}, u32[]{:S(2)}, u32[]{:S(2)}) collective-permute-start(bf16[2,320,128]{2,1,0:T(8,128)(2,1)S(1)} %collective-permute-done.5.refs_2_.refs_13_), channel_id=1, source_target_pairs={{0,2},{2,0},{1,3},{3,1},{4,6},{6,4},{5,7},{7,5},{8,10},{10,8},{9,1... | collective-permute-start | bytes 491528 | tf_op jit(solution)/shard_map/along_head/ppermute | solution.py:381
  23.8 4.4 %collective-permute-start.10 = (bf16[2,320,128]{2,1,0:T(8,128)(2,1)S(1)}, bf16[2,320,128]{2,1,0:T(8,128)(2,1)S(1)}, u32[]{:S(2)}, u32[]{:S(2)}) collective-permute-start(bf16[2,320,128]{2,1,0:T(8,128)(2,1)S(1)} %collective-permute-done.4.refs_0_.refs_11_), channel_id=1, source_target_pairs={{0,1},{1,0},{2,3},{3,2},{4,5},{5,4},{6,7},{7,6},{8,9},{9,8},{10,11... | collective-permute-start | bytes 491528 | tf_op jit(solution)/shard_map/along_inner/ppermute | solution.py:385
  28.2 1.4 %collective-permute-start.11 = (bf16[2,320,128]{2,1,0:T(8,128)(2,1)S(1)}, bf16[2,320,128]{2,1,0:T(8,128)(2,1)S(1)}, u32[]{:S(2)}, u32[]{:S(2)}) collective-permute-start(bf16[2,320,128]{2,1,0:T(8,128)(2,1)S(1)} %collective-permute-done.9.refs_0_.refs_15_), channel_id=1, source_target_pairs={{0,1},{1,0},{2,3},{3,2},{4,5},{5,4},{6,7},{7,6},{8,9},{9,8},{10,11... | collective-permute-start | bytes 491528 | tf_op jit(solution)/shard_map/along_inner/ppermute | solution.py:385

commit v15 on v14

--- a/solution.py
+++ b/solution.py
@@ -117,7 +117,7 @@
     block_len = k_ref.shape[1]
     hi, _, _ = blocks_of(sb, lax.axis_index("seq"))
     slots = {HI: hi, LO: 1 - hi}
-    tiles = key_tiles(block_len)
+    tiles = [(0, block_len)]
     me, count = lax.axis_index("seq"), lax.axis_size("seq")
     notes[0] = jnp.full(notes.shape[1:], hi, jnp.int32).astype(jnp.float32)
     for distance in range(1, count):

time: 32 us -> 32 us (level)
  transfers between devices with their start and end apart: 12 -> 12, of which waited for: 7 -> 7; matrix products, arithmetic and copies ran while one was open for 0% -> 0% of each run, Pallas kernels for 34% -> 33%
where the time goes in v15:
time: 32 us; the launch traced here: 31.9 us
  Pallas kernels  13.7 us (43%)
  starting transfers between devices  11.5 us (36%)
  waiting for transfers between devices  5.84 us (18%)
  between operations  0.86 us (3%)
    ppermute x3, starting transfers between devices, along_seq(): return lax.ppermute(block, 'seq', route)  7.11 us
    pallas_call x1, Pallas kernels, body(): pl.pallas_call(functools.partial(local_kernel, coef, rows), in_specs=[sca...  5.45 us
    pallas_call x3, Pallas kernels, attended_with(): pl.pallas_call(functools.partial(middle_kernel, coef, [visit[0] for visit...  5.22 us
    ppermute x3, waiting for transfers between devices, along_head(): lax.ppermute(block, 'head', [(i, i ^ 1) for i in range(lax.axis_size('hea...  4.26 us
    ppermute x3, starting transfers between devices, along_head(): lax.ppermute(block, 'head', [(i, i ^ 1) for i in range(lax.axis_size('hea...  3.32 us
    pallas_call x1, Pallas kernels, body(): pl.pallas_call(functools.partial(last_kernel, coef, distances, final), in...  2.08 us
    ppermute x3, waiting for transfers between devices, along_seq(): return lax.ppermute(block, 'seq', route)  1.28 us
    ppermute x6, starting transfers between devices, along_inner(): return lax.ppermute(block, 'inner', [(0, 1), (1, 0)])  1.03 us
  transfers between devices with their start and end apart: 12, of which 7 were waited for; matrix products, arithmetic and copies ran while one was open for 0% of the time, Pallas kernels for 33%

profile of v15, /device:TPU:0, one launch (start us, length us, event | category | flops | bytes accessed | tf_op | source)
XLA Modules:
  0.0 31.9 jit_solution(6708462859746013060)
XLA Ops:
  0.6 1.0 %pick_piece.1 = (bf16[2,320,128]{2,1,0:T(8,128)(2,1)S(1)}, s32[8]{0:T(128)S(1)}) custom-call(bf16[2,640,128]{2,1,0:T(8,128)(2,1)} %refs_2_.1, bf16[2,640,128]{2,1,0:T(8,128)(2,1)} %refs_3_.1, s32[8]{0:T(128)} %sb_hbm.1), custom_call_target="tpu_custom_call" | custom-call | bytes 400000 | tf_op jit(solution)/shard_map/pick_piece/pallas_call | solution.py:405
  1.6 4.1 %collective-permute-start.1 = (bf16[2,320,128]{2,1,0:T(8,128)(2,1)S(1)}, bf16[2,320,128]{2,1,0:T(8,128)(2,1)S(1)}, u32[]{:S(2)}, u32[]{:S(2)}) collective-permute-start(bf16[2,320,128]{2,1,0:T(8,128)(2,1)S(1)} %get-tuple-element.32), channel_id=1, source_target_pairs={{0,8},{4,12},{8,0},{12,4},{1,9},{5,13},{9,1},{13,5},{2,10},{6,14},... | collective-permute-start | bytes 491528 | tf_op jit(solution)/shard_map/along_seq/ppermute | solution.py:377
  5.7 1.6 %collective-permute-start = (bf16[2,320,128]{2,1,0:T(8,128)(2,1)S(1)}, bf16[2,320,128]{2,1,0:T(8,128)(2,1)S(1)}, u32[]{:S(2)}, u32[]{:S(2)}) collective-permute-start(bf16[2,320,128]{2,1,0:T(8,128)(2,1)S(1)} %get-tuple-element.32), channel_id=1, source_target_pairs={{0,4},{4,0},{8,12},{12,8},{1,5},{5,1},{9,13},{13,9},{2,6},{6,2},{1... | collective-permute-start | bytes 491528 | tf_op jit(solution)/shard_map/along_seq/ppermute | solution.py:377
  7.3 5.4 %local_part.1 = (bf16[2,256,1280]{2,1,0:T(8,128)(2,1)S(1)}, f32[2,8,1280]{2,1,0:T(8,128)S(1)}, f32[2,8,1280]{2,1,0:T(8,128)S(1)}, f32[2,128,1280]{2,1,0:T(8,128)S(1)}, f32[4,8,128]{2,1,0:T(8,128)S(1)}) custom-call(s32[8]{0:T(128)S(1)} %get-tuple-element.27.sb.sb_ref, bf16[2,320,512]{2,1,0:T(8,128)(2,1)} %refs_4_.1, bf16[2,640,128]{2,1,0:T(8,128)(2,1)} %refs_2_.1, ...), custom_call_target="tpu_custom_call" | custom-call | flops 2516582400 | bytes 6000000 | tf_op jit(solution)/shard_map/local_part/pallas_call | solution.py:421
  12.7 0.8 %collective-permute-done.1.refs_2_.refs_9_ = bf16[2,320,128]{2,1,0:T(8,128)(2,1)S(1)} collective-permute-done((bf16[2,320,128]{2,1,0:T(8,128)(2,1)S(1)}, bf16[2,320,128]{2,1,0:T(8,128)(2,1)S(1)}, u32[]{:S(2)}, u32[]{:S(2)}) %collective-permute-start.1) | collective-permute-done | bytes 163872 | tf_op jit(solution)/shard_map/along_seq/ppermute | solution.py:377
  13.5 0.2 collective-permute-done.refs_0_.refs_5_
  13.7 0.0 collective-permute-start.2
  13.7 0.5 %collective-permute-start.3 = (bf16[2,320,128]{2,1,0:T(8,128)(2,1)S(1)}, bf16[2,320,128]{2,1,0:T(8,128)(2,1)S(1)}, u32[]{:S(2)}, u32[]{:S(2)}) collective-permute-start(bf16[2,320,128]{2,1,0:T(8,128)(2,1)S(1)} %collective-permute-done.1.refs_2_.refs_9_), channel_id=1, source_target_pairs={{0,1},{1,0},{2,3},{3,2},{4,5},{5,4},{6,7},{7,6},{8,9},{9,8},{10,11... | collective-permute-start | bytes 491528 | tf_op jit(solution)/shard_map/along_inner/ppermute | solution.py:385
  14.2 1.5 %collective-permute-start.6 = (bf16[2,320,128]{2,1,0:T(8,128)(2,1)S(1)}, bf16[2,320,128]{2,1,0:T(8,128)(2,1)S(1)}, u32[]{:S(2)}, u32[]{:S(2)}) collective-permute-start(bf16[2,320,128]{2,1,0:T(8,128)(2,1)S(1)} %collective-permute-done.refs_0_.refs_5_), channel_id=1, source_target_pairs={{0,2},{2,0},{1,3},{3,1},{4,6},{6,4},{5,7},{7,5},{8,10},{10,8},{9,1... | collective-permute-start | bytes 491528 | tf_op jit(solution)/shard_map/along_head/ppermute | solution.py:381
  15.8 1.4 %collective-permute-start.5 = (bf16[2,320,128]{2,1,0:T(8,128)(2,1)S(1)}, bf16[2,320,128]{2,1,0:T(8,128)(2,1)S(1)}, u32[]{:S(2)}, u32[]{:S(2)}) collective-permute-start(bf16[2,320,128]{2,1,0:T(8,128)(2,1)S(1)} %collective-permute-done.1.refs_2_.refs_9_), channel_id=1, source_target_pairs={{0,4},{4,0},{8,12},{12,8},{1,5},{5,1},{9,13},{13,9},{2,6},{6,2},{1... | collective-permute-start | bytes 491528 | tf_op jit(solution)/shard_map/along_seq/ppermute | solution.py:377
  17.2 0.5 %collective-permute-start.4 = (bf16[2,320,128]{2,1,0:T(8,128)(2,1)S(1)}, bf16[2,320,128]{2,1,0:T(8,128)(2,1)S(1)}, u32[]{:S(2)}, u32[]{:S(2)}) collective-permute-start(bf16[2,320,128]{2,1,0:T(8,128)(2,1)S(1)} %collective-permute-done.1.refs_2_.refs_9_), channel_id=1, source_target_pairs={{0,2},{2,0},{1,3},{3,1},{4,6},{6,4},{5,7},{7,5},{8,10},{10,8},{9,1... | collective-permute-start | bytes 491528 | tf_op jit(solution)/shard_map/along_head/ppermute | solution.py:381
  17.7 0.0 collective-permute-done.2.refs_1_.refs_6_
  17.7 0.0 collective-permute-done.3.refs_3_.refs_10_
  17.7 2.1 %visits_of_1_2.1 = (f32[2,8,1280]{2,1,0:T(8,128)S(1)}, f32[2,128,1280]{2,1,0:T(8,128)S(1)}) custom-call(f32[4,8,128]{2,1,0:T(8,128)S(1)} %get-tuple-element.28.notes, bf16[2,256,1280]{2,1,0:T(8,128)(2,1)S(1)} %get-tuple-element.29.turned_q, f32[2,8,1280]{2,1,0:T(8,128)S(1)} %get-tuple-element.31.sum_in, ...), custom_call_target="tpu_custom_call", output_to_operand_aliasing={{0}: (2, {}), {1}: (3, {})} | custom-call | flops 1677721600 | bytes 4000000 | tf_op jit(solution)/shard_map/visits_of_1_2/pallas_call | solution.py:450
  19.8 1.5 %collective-permute-done.6.refs_0_.refs_7_ = bf16[2,320,128]{2,1,0:T(8,128)(2,1)S(1)} collective-permute-done((bf16[2,320,128]{2,1,0:T(8,128)(2,1)S(1)}, bf16[2,320,128]{2,1,0:T(8,128)(2,1)S(1)}, u32[]{:S(2)}, u32[]{:S(2)}) %collective-permute-start.6) | collective-permute-done | bytes 163872 | tf_op jit(solution)/shard_map/along_head/ppermute | solution.py:381
  21.3 0.3 collective-permute-done.5.refs_2_.refs_13_
  21.6 0.0 collective-permute-start.8
  21.6 0.5 %collective-permute-start.7 = (bf16[2,320,128]{2,1,0:T(8,128)(2,1)S(1)}, bf16[2,320,128]{2,1,0:T(8,128)(2,1)S(1)}, u32[]{:S(2)}, u32[]{:S(2)}) collective-permute-start(bf16[2,320,128]{2,1,0:T(8,128)(2,1)S(1)} %collective-permute-done.6.refs_0_.refs_7_), channel_id=1, source_target_pairs={{0,1},{1,0},{2,3},{3,2},{4,5},{5,4},{6,7},{7,6},{8,9},{9,8},{10,11... | collective-permute-start | bytes 491528 | tf_op jit(solution)/shard_map/along_inner/ppermute | solution.py:385
  22.1 1.2 %collective-permute-start.9 = (bf16[2,320,128]{2,1,0:T(8,128)(2,1)S(1)}, bf16[2,320,128]{2,1,0:T(8,128)(2,1)S(1)}, u32[]{:S(2)}, u32[]{:S(2)}) collective-permute-start(bf16[2,320,128]{2,1,0:T(8,128)(2,1)S(1)} %collective-permute-done.5.refs_2_.refs_13_), channel_id=1, source_target_pairs={{0,2},{2,0},{1,3},{3,1},{4,6},{6,4},{5,7},{7,5},{8,10},{10,8},{9,1... | collective-permute-start | bytes 491528 | tf_op jit(solution)/shard_map/along_head/ppermute | solution.py:381
  23.3 0.5 %collective-permute-done.4.refs_0_.refs_11_ = bf16[2,320,128]{2,1,0:T(8,128)(2,1)S(1)} collective-permute-done((bf16[2,320,128]{2,1,0:T(8,128)(2,1)S(1)}, bf16[2,320,128]{2,1,0:T(8,128)(2,1)S(1)}, u32[]{:S(2)}, u32[]{:S(2)}) %collective-permute-start.4) | collective-permute-done | bytes 163872 | tf_op jit(solution)/shard_map/along_head/ppermute | solution.py:381
  23.8 0.0 collective-permute-start.10
  23.8 0.0 collective-permute-done.8.refs_3_.refs_14_
  23.8 0.0 collective-permute-done.7.refs_1_.refs_8_
  23.8 2.1 %visits_of_1_3.1 = (f32[2,8,1280]{2,1,0:T(8,128)S(1)}, f32[2,128,1280]{2,1,0:T(8,128)S(1)}) custom-call(f32[4,8,128]{2,1,0:T(8,128)S(1)} %get-tuple-element.28.notes, bf16[2,256,1280]{2,1,0:T(8,128)(2,1)S(1)} %get-tuple-element.29.turned_q, f32[2,8,1280]{2,1,0:T(8,128)S(1)} %get-tuple-element.38.sum_in, ...), custom_call_target="tpu_custom_call", output_to_operand_aliasing={{0}: (2, {}), {1}: (3, {})} | custom-call | flops 1677721600 | bytes 4000000 | tf_op jit(solution)/shard_map/visits_of_1_3/pallas_call | solution.py:450
  25.9 2.3 %collective-permute-done.9.refs_0_.refs_15_ = bf16[2,320,128]{2,1,0:T(8,128)(2,1)S(1)} collective-permute-done((bf16[2,320,128]{2,1,0:T(8,128)(2,1)S(1)}, bf16[2,320,128]{2,1,0:T(8,128)(2,1)S(1)}, u32[]{:S(2)}, u32[]{:S(2)}) %collective-permute-start.9) | collective-permute-done | bytes 163872 | tf_op jit(solution)/shard_map/along_head/ppermute | solution.py:381
  28.2 0.0 collective-permute-start.11
  28.2 0.0 collective-permute-done.10.refs_1_.refs_12_
  28.2 1.1 %visits_of_2.1 = (f32[2,8,1280]{2,1,0:T(8,128)S(1)}, f32[2,128,1280]{2,1,0:T(8,128)S(1)}) custom-call(f32[4,8,128]{2,1,0:T(8,128)S(1)} %get-tuple-element.28.notes, bf16[2,256,1280]{2,1,0:T(8,128)(2,1)S(1)} %get-tuple-element.29.turned_q, f32[2,8,1280]{2,1,0:T(8,128)S(1)} %get-tuple-element.45.sum_in, ...), custom_call_target="tpu_custom_call", output_to_operand_aliasing={{0}: (2, {}), {1}: (3, {})} | custom-call | flops 838860800 | bytes 4000000 | tf_op jit(solution)/shard_map/visits_of_2/pallas_call | solution.py:450
  29.3 0.3 collective-permute-done.11.refs_1_.refs_16_
  29.6 2.1 %last_visitor.1 = (bf16[2,320,512]{2,1,0:T(8,128)(2,1)}, f32[2,4,320]{2,1,0:T(4,128)}) custom-call(s32[8]{0:T(128)S(1)} %get-tuple-element.27.sb.sb_ref, f32[4,8,128]{2,1,0:T(8,128)S(1)} %get-tuple-element.28.notes, bf16[2,256,1280]{2,1,0:T(8,128)(2,1)S(1)} %get-tuple-element.29.turned_q, f32[2,8,1280]{2,1,0:T(8,128)S(1)} %get-tuple-element.30.top_ref, ...), custom_call_target="tpu_custom_call" | custom-call | flops 838860800 | bytes 7000000 | tf_op jit(solution)/shard_map/last_visitor/pallas_call | solution.py:501
Async XLA Ops:
  1.6 11.9 %collective-permute-start.1 = (bf16[2,320,128]{2,1,0:T(8,128)(2,1)S(1)}, bf16[2,320,128]{2,1,0:T(8,128)(2,1)S(1)}, u32[]{:S(2)}, u32[]{:S(2)}) collective-permute-start(bf16[2,320,128]{2,1,0:T(8,128)(2,1)S(1)} %get-tuple-element.32), channel_id=1, source_target_pairs={{0,8},{4,12},{8,0},{12,4},{1,9},{5,13},{9,1},{13,5},{2,10},{6,14},... | collective-permute-start | bytes 491528 | tf_op jit(solution)/shard_map/along_seq/ppermute | solution.py:377
  5.7 8.0 %collective-permute-start = (bf16[2,320,128]{2,1,0:T(8,128)(2,1)S(1)}, bf16[2,320,128]{2,1,0:T(8,128)(2,1)S(1)}, u32[]{:S(2)}, u32[]{:S(2)}) collective-permute-start(bf16[2,320,128]{2,1,0:T(8,128)(2,1)S(1)} %get-tuple-element.32), channel_id=1, source_target_pairs={{0,4},{4,0},{8,12},{12,8},{1,5},{5,1},{9,13},{13,9},{2,6},{6,2},{1... | collective-permute-start | bytes 491528 | tf_op jit(solution)/shard_map/along_seq/ppermute | solution.py:377
  13.7 4.0 %collective-permute-start.2 = (bf16[2,320,128]{2,1,0:T(8,128)(2,1)S(1)}, bf16[2,320,128]{2,1,0:T(8,128)(2,1)S(1)}, u32[]{:S(2)}, u32[]{:S(2)}) collective-permute-start(bf16[2,320,128]{2,1,0:T(8,128)(2,1)S(1)} %collective-permute-done.refs_0_.refs_5_), channel_id=1, source_target_pairs={{0,1},{1,0},{2,3},{3,2},{4,5},{5,4},{6,7},{7,6},{8,9},{9,8},{10,11... | collective-permute-start | bytes 491528 | tf_op jit(solution)/shard_map/along_inner/ppermute | solution.py:385
  13.7 4.0 %collective-permute-start.3 = (bf16[2,320,128]{2,1,0:T(8,128)(2,1)S(1)}, bf16[2,320,128]{2,1,0:T(8,128)(2,1)S(1)}, u32[]{:S(2)}, u32[]{:S(2)}) collective-permute-start(bf16[2,320,128]{2,1,0:T(8,128)(2,1)S(1)} %collective-permute-done.1.refs_2_.refs_9_), channel_id=1, source_target_pairs={{0,1},{1,0},{2,3},{3,2},{4,5},{5,4},{6,7},{7,6},{8,9},{9,8},{10,11... | collective-permute-start | bytes 491528 | tf_op jit(solution)/shard_map/along_inner/ppermute | solution.py:385
  14.2 7.1 %collective-permute-start.6 = (bf16[2,320,128]{2,1,0:T(8,128)(2,1)S(1)}, bf16[2,320,128]{2,1,0:T(8,128)(2,1)S(1)}, u32[]{:S(2)}, u32[]{:S(2)}) collective-permute-start(bf16[2,320,128]{2,1,0:T(8,128)(2,1)S(1)} %collective-permute-done.refs_0_.refs_5_), channel_id=1, source_target_pairs={{0,2},{2,0},{1,3},{3,1},{4,6},{6,4},{5,7},{7,5},{8,10},{10,8},{9,1... | collective-permute-start | bytes 491528 | tf_op jit(solution)/shard_map/along_head/ppermute | solution.py:381
  15.8 5.8 %collective-permute-start.5 = (bf16[2,320,128]{2,1,0:T(8,128)(2,1)S(1)}, bf16[2,320,128]{2,1,0:T(8,128)(2,1)S(1)}, u32[]{:S(2)}, u32[]{:S(2)}) collective-permute-start(bf16[2,320,128]{2,1,0:T(8,128)(2,1)S(1)} %collective-permute-done.1.refs_2_.refs_9_), channel_id=1, source_target_pairs={{0,4},{4,0},{8,12},{12,8},{1,5},{5,1},{9,13},{13,9},{2,6},{6,2},{1... | collective-permute-start | bytes 491528 | tf_op jit(solution)/shard_map/along_seq/ppermute | solution.py:377
  17.2 6.6 %collective-permute-start.4 = (bf16[2,320,128]{2,1,0:T(8,128)(2,1)S(1)}, bf16[2,320,128]{2,1,0:T(8,128)(2,1)S(1)}, u32[]{:S(2)}, u32[]{:S(2)}) collective-permute-start(bf16[2,320,128]{2,1,0:T(8,128)(2,1)S(1)} %collective-permute-done.1.refs_2_.refs_9_), channel_id=1, source_target_pairs={{0,2},{2,0},{1,3},{3,1},{4,6},{6,4},{5,7},{7,5},{8,10},{10,8},{9,1... | collective-permute-start | bytes 491528 | tf_op jit(solution)/shard_map/along_head/ppermute | solution.py:381
  21.6 2.3 %collective-permute-start.8 = (bf16[2,320,128]{2,1,0:T(8,128)(2,1)S(1)}, bf16[2,320,128]{2,1,0:T(8,128)(2,1)S(1)}, u32[]{:S(2)}, u32[]{:S(2)}) collective-permute-start(bf16[2,320,128]{2,1,0:T(8,128)(2,1)S(1)} %collective-permute-done.5.refs_2_.refs_13_), channel_id=1, source_target_pairs={{0,1},{1,0},{2,3},{3,2},{4,5},{5,4},{6,7},{7,6},{8,9},{9,8},{10,11... | collective-permute-start | bytes 491528 | tf_op jit(solution)/shard_map/along_inner/ppermute | solution.py:385
  21.6 2.3 %collective-permute-start.7 = (bf16[2,320,128]{2,1,0:T(8,128)(2,1)S(1)}, bf16[2,320,128]{2,1,0:T(8,128)(2,1)S(1)}, u32[]{:S(2)}, u32[]{:S(2)}) collective-permute-start(bf16[2,320,128]{2,1,0:T(8,128)(2,1)S(1)} %collective-permute-done.6.refs_0_.refs_7_), channel_id=1, source_target_pairs={{0,1},{1,0},{2,3},{3,2},{4,5},{5,4},{6,7},{7,6},{8,9},{9,8},{10,11... | collective-permute-start | bytes 491528 | tf_op jit(solution)/shard_map/along_inner/ppermute | solution.py:385
  22.1 6.1 %collective-permute-start.9 = (bf16[2,320,128]{2,1,0:T(8,128)(2,1)S(1)}, bf16[2,320,128]{2,1,0:T(8,128)(2,1)S(1)}, u32[]{:S(2)}, u32[]{:S(2)}) collective-permute-start(bf16[2,320,128]{2,1,0:T(8,128)(2,1)S(1)} %collective-permute-done.5.refs_2_.refs_13_), channel_id=1, source_target_pairs={{0,2},{2,0},{1,3},{3,1},{4,6},{6,4},{5,7},{7,5},{8,10},{10,8},{9,1... | collective-permute-start | bytes 491528 | tf_op jit(solution)/shard_map/along_head/ppermute | solution.py:381
  23.8 4.4 %collective-permute-start.10 = (bf16[2,320,128]{2,1,0:T(8,128)(2,1)S(1)}, bf16[2,320,128]{2,1,0:T(8,128)(2,1)S(1)}, u32[]{:S(2)}, u32[]{:S(2)}) collective-permute-start(bf16[2,320,128]{2,1,0:T(8,128)(2,1)S(1)} %collective-permute-done.4.refs_0_.refs_11_), channel_id=1, source_target_pairs={{0,1},{1,0},{2,3},{3,2},{4,5},{5,4},{6,7},{7,6},{8,9},{9,8},{10,11... | collective-permute-start | bytes 491528 | tf_op jit(solution)/shard_map/along_inner/ppermute | solution.py:385
  28.2 1.4 %collective-permute-start.11 = (bf16[2,320,128]{2,1,0:T(8,128)(2,1)S(1)}, bf16[2,320,128]{2,1,0:T(8,128)(2,1)S(1)}, u32[]{:S(2)}, u32[]{:S(2)}) collective-permute-start(bf16[2,320,128]{2,1,0:T(8,128)(2,1)S(1)} %collective-permute-done.9.refs_0_.refs_15_), channel_id=1, source_target_pairs={{0,1},{1,0},{2,3},{3,2},{4,5},{5,4},{6,7},{7,6},{8,9},{9,8},{10,11... | collective-permute-start | bytes 491528 | tf_op jit(solution)/shard_map/along_inner/ppermute | solution.py:385
